TPU v7x, 256 devices: a whole 4x4x8 slice. The times are simulated.
256 devices in a mesh: expert: 8 (over z), vocab: 8 (over x, core), batch: 4 (over y).
Axes of the slice: x: 4, y: 4, z: 8, core: 2. Of those that a mesh axis runs over, the one named last changes fastest.
Arguments:
- resid: bfloat16 [4, 512, 6144], P('batch', ('expert', 'vocab')), may hold values from -6 to 6
- moe_gain: float32 [6144], replicated, may hold values from 0.25 to 2.5
- final_gain: float32 [6144], replicated, may hold values from 0.5 to 1.5
- router: bfloat16 [6144, 8], replicated, may hold values from -0.078125 to 0.078125
- w_gate: bfloat16 [8, 6144, 8192], P('expert', None, ('vocab', 'batch')), may hold values from -0.078125 to 0.078125
- w_up: bfloat16 [8, 6144, 8192], P('expert', None, ('vocab', 'batch')), may hold values from -0.078125 to 0.078125
- w_down: bfloat16 [8, 8192, 6144], P('expert', ('vocab', 'batch')), may hold values from -0.0625 to 0.0625
- lm_head: bfloat16 [16384, 6144], P(('expert', 'vocab')), may hold values from -6 to 6
- expert_ids: int32 [4, 512, 2], P('batch', ('expert', 'vocab')), may hold values from 0 to 7, all different within a row; in each aligned block of 8 rows (0 to 7, 8 to 15, ..., all dimensions but the last counted through in order) at most 3 rows name the same one
- target_ids: int32 [4, 512], P('batch'), may hold values from 0 to 16383
- choice_len: int32 [4, 16], P('batch'), may hold values from 1 to 64, 512 in all within a row
- choice_question: int32 [4, 16], P('batch'), may hold values from 0 to 3, as said below
Outputs:
- token_logprob: float32 [4, 512], P('batch', ('expert', 'vocab'))
- choice_prob: float32 [4, 16], P('batch')
Inputs may be any that keep to these rules, and one draw needn't show every extreme that they name: `expert_ids`: A token's 2 experts differ; the rows of one device name each expert at most 3 times. `choice_len`: each group's lengths sum to 512. `choice_question`: in each group every question number appears exactly four times.
All inputs are finite; a program needn't handle non-finite values.
Results may differ from a plain program's by a relative error of at most 0.019.
Values may be sent and summed in bfloat16 or wider, within the bound.
No kernel may reach another device: no remote copies, remote signals or barrier semaphores. Data moves between devices by JAX's collectives and lax.ppermute only.
A program may use at most 128 MiB of HBM per device.

v0:
```python
import jax
import jax.numpy as jnp
from jax import lax
from jax.sharding import PartitionSpec as P

epsilon = 1e-05


def copy_for_each(array, axis):
    peers = lax.axis_size(axis)
    return lax.all_to_all(
        jnp.broadcast_to(array[None], (peers, *array.shape)), axis, 0, 0, tiled=True
    )


def gathered_once(array, axis):
    leaves = jax.tree.leaves(array)
    order = sorted(range(len(leaves)), key=lambda k: -leaves[k].size)
    width = (1, *leaves[order[0]].shape)[-1]
    lines = [
        jnp.pad(leaves[k].reshape(-1), (0, -leaves[k].size % width)).reshape(-1, width)
        for k in order
    ]
    both, at, found = (copy_for_each(jnp.concatenate(lines), axis), 0, {})
    for k, line in zip(order, lines):
        slab = both[:, at : at + len(line)].reshape(len(both), -1)
        found[k] = slab[:, : leaves[k].size].reshape(-1, *leaves[k].shape)
        at += len(line)
    numbers = iter(range(len(leaves)))
    return jax.tree.map(lambda _: found[next(numbers)], array)


def joined_by_halves(pieces, combine):
    while len(jax.tree.leaves(pieces)[0]) > 1:
        pieces = jax.vmap(combine)(
            *(jax.tree.map(lambda part: part[side::2], pieces) for side in (0, 1))
        )
    return jax.tree.map(lambda part: part[0], pieces)


def joined_all(array, axis, combine):
    pieces = gathered_once(array, axis)
    return joined_by_halves(pieces, combine)


def rms_scale(values, gain):
    mean_square = jnp.mean(values * values, axis=-1, keepdims=True)
    return values * lax.rsqrt(mean_square + epsilon) * gain


def route_gates(router_logit, route_ids):
    expert_count = router_logit.shape[1]
    matches = route_ids[:, :, None] == jnp.arange(expert_count, dtype=jnp.int32)[None, None, :]
    picked = jnp.sum(jnp.where(matches, router_logit[:, None, :], 0.0), axis=2)
    return 1.0 / jnp.sum(jnp.exp(picked[:, None, :] - picked[:, :, None]), axis=2)


def expand_rows(block_rows, gate_cols, up_cols):
    gate_part = jnp.dot(block_rows, gate_cols, preferred_element_type=jnp.float32)
    up_part = jnp.dot(block_rows, up_cols, preferred_element_type=jnp.float32)
    return (jax.nn.silu(gate_part) * up_part).astype(jnp.bfloat16)


def choice_member(lengths, positions):
    ends = jnp.cumsum(lengths, dtype=jnp.int32)
    starts = ends - lengths
    return (positions[None, :] >= starts[:, None]) & (positions[None, :] < ends[:, None])


def choice_softmax(choice_total, lengths, questions):
    average = choice_total / lengths.astype(jnp.float32)
    same_question = questions[:, None] == questions[None, :]
    question_top = jnp.max(jnp.where(same_question, average[None, :], -jnp.inf), axis=1)
    raised = jnp.exp(average - question_top)
    denominator = jnp.sum(jnp.where(same_question, raised[None, :], 0.0), axis=1)
    return raised / denominator


def merge_stats(first, second):
    top_value = jnp.maximum(first[0], second[0])
    summed = first[1] * jnp.exp(first[0] - top_value) + second[1] * jnp.exp(second[0] - top_value)
    return (top_value, summed, first[2] + second[2])


def on_device(
    resid,
    moe_gain,
    final_gain,
    router,
    w_gate,
    w_up,
    w_down,
    lm_head,
    expert_ids,
    target_ids,
    choice_len,
    choice_question,
):
    stream = resid[0].astype(jnp.float32)
    token_count, model_width = stream.shape
    normed_in = rms_scale(stream, moe_gain).astype(jnp.bfloat16)
    router_logit = jnp.dot(normed_in, router, preferred_element_type=jnp.float32)
    route_ids = expert_ids[0]
    route_count = route_ids.shape[1]
    gate_weights = route_gates(router_logit, route_ids)
    expert_count = lax.axis_size("expert")
    bucket_size = max(2, (token_count * route_count + expert_count - 1) // expert_count + 1)
    flat_ids = route_ids.reshape(-1)
    expert_match = (flat_ids[:, None] == jnp.arange(expert_count, dtype=jnp.int32)[None, :]).astype(
        jnp.int32
    )
    earlier = jnp.cumsum(expert_match, axis=0, dtype=jnp.int32) - expert_match
    slot_index = flat_ids * bucket_size + jnp.sum(earlier * expert_match, axis=1)
    slot_match = (
        slot_index[:, None] == jnp.arange(expert_count * bucket_size, dtype=jnp.int32)[None, :]
    ).astype(jnp.float32)
    slot_match = slot_match.reshape(token_count, route_count, -1)
    dispatch = jnp.sum(slot_match, axis=1).astype(jnp.bfloat16)
    combine_weights = jnp.sum(slot_match * gate_weights[:, :, None], axis=1)
    buckets = lax.dot_general(
        dispatch, normed_in, (((0,), (0,)), ((), ())), preferred_element_type=jnp.float32
    )
    buckets = buckets.astype(jnp.bfloat16).reshape(expert_count, bucket_size, model_width)
    gate_cols = w_gate[0]
    up_cols = w_up[0]
    down_rows = w_down[0]
    arrived = lax.all_to_all(buckets, "expert", split_axis=0, concat_axis=0, tiled=True).reshape(
        -1, model_width
    )
    hidden = expand_rows(
        lax.all_gather(arrived, ("vocab", "batch"), axis=0, tiled=True), gate_cols, up_cols
    )
    expert_sum = lax.psum_scatter(
        jnp.dot(hidden, down_rows, preferred_element_type=jnp.float32).astype(jnp.bfloat16),
        ("vocab", "batch"),
        scatter_dimension=0,
        tiled=True,
    )
    outgoing = expert_sum.reshape(expert_count, bucket_size, model_width)
    returned = lax.all_to_all(outgoing, "expert", split_axis=0, concat_axis=0, tiled=True)
    returned_rows = returned.reshape(-1, model_width).astype(jnp.float32)
    mixed_rows = stream + jnp.dot(combine_weights, returned_rows)
    normed_out = rms_scale(mixed_rows, final_gain).astype(jnp.bfloat16)
    head_index = lax.axis_index(("expert", "vocab"))
    vocab_share = lm_head.shape[0]
    vocab_ids = jnp.arange(vocab_share, dtype=jnp.int32) + head_index * vocab_share
    targets = target_ids[0]
    group_tokens = targets.shape[0]
    logits = lax.dot_general(
        lax.all_gather(normed_out, ("expert", "vocab"), axis=0, tiled=True),
        lm_head,
        (((1,), (1,)), ((), ())),
        preferred_element_type=jnp.float32,
    )
    block_top = jnp.max(logits, axis=1)
    block_sum = jnp.sum(jnp.exp(logits - block_top[:, None]), axis=1)
    block_hit = jnp.sum(jnp.where(targets[:, None] == vocab_ids[None, :], logits, 0.0), axis=1)
    fresh = (block_top, block_sum, block_hit)
    largest, spread_sum, chosen = tuple((fresh[slot] for slot in range(3)))
    lengths = choice_len[0]
    questions = choice_question[0]
    own_first = head_index * token_count
    group_positions = jnp.arange(group_tokens, dtype=jnp.int32)
    best, summed, target_sum = joined_all(
        (largest, spread_sum, chosen), ("expert", "vocab"), merge_stats
    )
    group_logprob = target_sum - (best + jnp.log(summed))
    choice_total = jnp.sum(
        jnp.where(choice_member(lengths, group_positions), group_logprob[None, :], 0.0), axis=1
    )
    own_logprob = lax.dynamic_slice_in_dim(group_logprob, own_first, token_count, 0)
    choice_prob = choice_softmax(choice_total, lengths, questions)
    return (own_logprob.reshape(1, -1), choice_prob.reshape(1, -1))


def solution(mesh):
    return jax.shard_map(
        on_device,
        mesh=mesh,
        in_specs=(
            P("batch", ("expert", "vocab"), None),
            P(),
            P(),
            P(),
            P("expert", None, ("vocab", "batch")),
            P("expert", None, ("vocab", "batch")),
            P("expert", ("vocab", "batch"), None),
            P(("expert", "vocab"), None),
            P("batch", ("expert", "vocab"), None),
            P("batch", None),
            P("batch", None),
            P("batch", None),
        ),
        out_specs=(P("batch", ("expert", "vocab")), P("batch", None)),
        check_vma=False,
    )
```

profile of v0, /device:TPU:1, one launch (start us, length us, event | category | flops | bytes accessed | tf_op | source)
XLA Modules:
  0.0 376.1 jit_solution(1491115489635027238)
XLA Ops:
  7.2 0.9 copy.31
  8.1 0.1 eq.72
  8.2 0.1 fusion.28
  8.3 0.2 select_reduce_fusion.4
  8.5 0.1 reduce_sum.106
  8.6 0.1 copy.32
  8.7 0.7 multiply_add_fusion.5
  9.4 1.1 fusion.19
  10.4 1.2 fusion.24
  11.6 0.8 select_reduce_fusion.3
  12.5 0.1 convert_reduce_fusion
  12.6 1.9 convolution_convert_fusion.1
  14.5 1.1 reshape.128
  15.6 22.4 %all_to_all.15 = bf16[8,3,6144]{2,1,0:T(4,128)(2,1)} all-to-all(bf16[8,3,6144]{2,1,0:T(4,128)(2,1)S(1)} %reshape.128), channel_id=1, replica_groups=mesh['expert'=8,'vocab'=8,'batch'=4] {'expert'}, dimensions={0} | all-to-all | bytes 589824 | tf_op jit(solution)/shard_map/all_to_all | solution.py:127
  38.1 2.0 reshape.129
  40.0 0.0 reduce-scatter.2.cloned.1.call-start
  40.1 58.8 %all-gather.3.cloned.1.call-done = bf16[768,6144]{1,0:T(8,128)(2,1)} async-done(((bf16[24,6144]{1,0:T(8,128)(2,1)}), bf16[768,6144]{1,0:T(8,128)(2,1)}) %all-gather.3.cloned.1.call-update) | async-done | bytes 9437200 | tf_op jit(solution)/shard_map/all_gather | solution.py:131
  98.9 8.1 %fusion.3 = f32[768,256]{1,0:T(8,128)} fusion(bf16[768,6144]{1,0:T(8,128)(2,1)} %all-gather.3.cloned.1.call-done, bf16[1,6144,256]{2,1,0:T(8,128)(2,1)} %param.16), kind=kOutput, calls=%fused_computation.6 | convolution fusion | flops 2415919104 | bytes 13369344 | tf_op jit(solution)/shard_map/dot_general | solution.py:59
  106.9 19.4 %convolution_convert_fusion = bf16[768,6144]{1,0:T(8,128)(2,1)} fusion(bf16[1,256,6144]{2,1,0:T(8,128)(2,1)S(1)} %copy-done, bf16[768,6144]{1,0:T(8,128)(2,1)} %all-gather.3.cloned.1.call-done, bf16[1,6144,256]{2,1,0:T(8,128)(2,1)} %param.17, f32[768,256]{1,0:T(8,128)} %fusion.3), kind=kOutput, calls=%fused_computation | convolution fusion | flops 4837736448 | bytes 25952256 | tf_op jit(solution)/shard_map/dot_general | solution.py:134
  126.3 0.0 all-gather.5.cloned.1.call-start
  126.4 100.8 %reduce-scatter.2.cloned.1.call-done = bf16[24,6144]{1,0:T(8,128)(2,1)} async-done(((bf16[768,6144]{1,0:T(8,128)(2,1)}), bf16[24,6144]{1,0:T(8,128)(2,1)}) %reduce-scatter.2.cloned.1.call-update) | async-done | bytes 294928 | tf_op jit(solution)/shard_map/reduce_scatter | solution.py:133
  227.2 1.1 reshape.130
  228.4 18.1 %all_to_all.16 = bf16[8,3,6144]{2,1,0:T(4,128)(2,1)} all-to-all(bf16[8,3,6144]{2,1,0:T(4,128)(2,1)S(1)} %reshape.130), channel_id=1, replica_groups=mesh['expert'=8,'vocab'=8,'batch'=4] {'expert'}, dimensions={0} | all-to-all | bytes 589824 | tf_op jit(solution)/shard_map/all_to_all | solution.py:140
  246.5 1.2 reshape.131
  247.7 1.2 multiply_reduce_fusion
  248.9 1.5 multiply_convert_fusion
  250.5 79.1 %all-gather.5.cloned.1.call-done = bf16[512,6144]{1,0:T(8,128)(2,1)} async-done(((bf16[8,6144]{1,0:T(8,128)(2,1)}), bf16[512,6144]{1,0:T(8,128)(2,1)}) %all-gather.5.cloned.1.call-update) | async-done | bytes 6291472 | tf_op jit(solution)/shard_map/all_gather | solution.py:150
  329.6 5.5 %fusion.37 = (f32[512]{0:T(512)S(1)}, f32[512,256]{0,1:T(8,128)S(1)}) fusion(bf16[512,6144]{1,0:T(8,128)(2,1)} %all-gather.5.cloned.1.call-done, bf16[256,6144]{1,0:T(8,128)(2,1)} %param.19), kind=kOutput, calls=%fused_computation.74 | convolution fusion | flops 1610743296 | bytes 9963520 | tf_op jit(solution)/shard_map/dot_general | solution.py:149
  335.2 0.1 exponential_reduce_fusion
  335.3 0.9 broadcast_in_dim.84
  336.2 5.9 %all-to-all-start.2 = ((f32[64,3,512]{2,1,0:T(4,128)}), f32[64,3,512]{2,1,0:T(4,128)}, u32[]{:S(2)}, u32[]{:S(2)}) async-start(f32[64,3,512]{2,1,0:T(4,128)} %broadcast_in_dim.84), calls=%async_computation.3 | async-start | bytes 1048576 | tf_op jit(solution)/shard_map/all_to_all | solution.py:11
  342.1 0.1 copy.35
  342.2 0.1 reduce
  342.3 0.5 bitcast_subtract_fusion.1
  342.8 16.9 %all-to-all-done.2 = f32[64,3,512]{2,1,0:T(4,128)} async-done(((f32[64,3,512]{2,1,0:T(4,128)}), f32[64,3,512]{2,1,0:T(4,128)}, u32[]{:S(2)}, u32[]{:S(2)}) %all-to-all-start.2) | async-done | bytes 393248 | tf_op jit(solution)/shard_map/all_to_all | solution.py:11
  359.7 1.8 fusion.36
  361.5 0.6 slice.124
  362.1 0.6 slice.125
  362.8 0.9 add.97
  363.9 0.6 slice.138
  364.6 0.6 slice.137
  365.2 0.9 multiply_add_fusion
  366.6 0.6 constant_dynamic-slice_fusion
  367.2 0.8 select_reduce_fusion.1
  368.0 0.7 bitcast_divide_fusion.1
  368.7 0.2 fusion.26
  368.9 0.2 fusion.27
  369.1 0.5 bitcast_divide_fusion
  (58 shorter events, 1.0 us)
Async XLA Ops:
  7.2 99.8 %copy-start = (bf16[1,256,6144]{2,1,0:T(8,128)(2,1)S(1)}, bf16[1,256,6144]{2,1,0:T(8,128)(2,1)}, u32[]{:S(2)}) copy-start(bf16[1,256,6144]{2,1,0:T(8,128)(2,1)} %param.18) | copy-start | bytes 9437188
  7.2 91.7 %all-gather.3.cloned.1.call-start = ((), (), s32[]{:S(2)}) async-start(), calls=%async_computation.4 | async-start | bytes 9732096 | tf_op jit(solution)/shard_map/all_gather | solution.py:131
  40.0 187.2 %reduce-scatter.2.cloned.1.call-start = ((), (), s32[]{:S(2)}) async-start(), calls=%async_computation.5 | async-start | bytes 9732096 | tf_op jit(solution)/shard_map/reduce_scatter | solution.py:133
  126.3 203.3 %all-gather.5.cloned.1.call-start = ((), (), s32[]{:S(2)}) async-start(), calls=%async_computation.6 | async-start | bytes 6389760 | tf_op jit(solution)/shard_map/all_gather | solution.py:150
  250.4 84.7 %copy-start.2 = (s32[1,512]{1,0:T(1,128)S(1)}, s32[1,512]{1,0:T(1,128)}, u32[]{:S(2)}) copy-start(s32[1,512]{1,0:T(1,128)} %param.21) | copy-start | bytes 6148
  250.5 91.6 %copy-start.3 = (s32[1,16]{1,0:T(1,128)S(1)}, s32[1,16]{1,0:T(1,128)}, u32[]{:S(2)}) copy-start(s32[1,16]{1,0:T(1,128)} %param.22) | copy-start | bytes 196
  335.2 33.5 %copy-start.1 = (s32[1,16]{1,0:T(1,128)S(1)}, s32[1,16]{1,0:T(1,128)}, u32[]{:S(2)}) copy-start(s32[1,16]{1,0:T(1,128)} %param.23) | copy-start | bytes 196
  336.2 23.5 %all-to-all-start.2 = ((f32[64,3,512]{2,1,0:T(4,128)}), f32[64,3,512]{2,1,0:T(4,128)}, u32[]{:S(2)}, u32[]{:S(2)}) async-start(f32[64,3,512]{2,1,0:T(4,128)} %broadcast_in_dim.84), calls=%async_computation.3 | async-start | bytes 1048576 | tf_op jit(solution)/shard_map/all_to_all | solution.py:11
Sparse Core Ops, SparseCore 0:
  40.2 58.6 all-gather.2
  126.5 100.7 reduce-scatter.1
  250.5 79.0 all-gather.4
where the time goes:
time: 377 us; the launch traced here: 376 us
  waiting for transfers between devices  256 us (68%)
  blocking collectives  40.6 us (11%)
  matrix products  37.3 us (10%)
  between operations  14 us (4%)
  local copies, waits for them, and re-layouts  13.1 us (3%)
  other arithmetic  9.63 us (3%)
  starting transfers between devices  5.98 us (2%)
    reduce_scatter x1, waiting for transfers between devices, on_device(): lax.psum_scatter(jnp.dot(hidden, down_rows, preferred_element_type=jnp.fl...  101 us
    all_gather x1, waiting for transfers between devices, on_device(): lax.all_gather(normed_out, ('expert', 'vocab'), axis=0, tiled=True)  79.1 us
    all_gather x1, waiting for transfers between devices, on_device(): lax.all_gather(arrived, ('vocab', 'batch'), axis=0, tiled=True)  58.8 us
    all_to_all x1, blocking collectives, on_device(): lax.all_to_all(buckets, 'expert', split_axis=0, concat_axis=0, tiled=True)  22.4 us
    dot_general x1, matrix products, on_device(): jnp.dot(hidden, down_rows, preferred_element_type=jnp.float32)  19.4 us
    all_to_all x1, blocking collectives, on_device(): lax.all_to_all(outgoing, 'expert', split_axis=0, concat_axis=0, tiled=True)  18.1 us
    all_to_all x1, waiting for transfers between devices, copy_for_each(): lax.all_to_all(jnp.broadcast_to(array[None], (peers, *array.shape)), axis...  16.9 us
    dot_general x1, matrix products, expand_rows(): jnp.dot(block_rows, gate_cols, preferred_element_type=jnp.float32)  8.09 us
  transfers between devices with their start and end apart: 4, of which 4 were waited for; matrix products, arithmetic and copies ran while one was open for 0% of the time, Pallas kernels for 0%

commit v1 on v0

v1 whole, which is shorter than its diff:
```python
import jax
import jax.numpy as jnp
from jax import lax
from jax.sharding import PartitionSpec as P

epsilon = 1e-05
bf16 = jnp.bfloat16
f32 = jnp.float32

NZ, NX, NC, NY = 8, 4, 2, 4
Z_ORDER = (0, -1, 1, -2, 2, -3, 3, 4)
X_ORDER = (0, -1, 1, 2)


def plane_perm(second, shift):
    pairs = []
    for x in range(NX):
        for c in range(NC):
            for y in range(NY):
                along_x = (c == 0) != second
                to_x = (x + shift) % NX if along_x else x
                to_y = y if along_x else (y + shift) % NY
                pairs.append(((x * NC + c) * NY + y, (to_x * NC + c) * NY + to_y))
    return pairs


def plane_shift(array, second, shift):
    return lax.ppermute(array, ("vocab", "batch"), plane_perm(second, shift))


def swap_cores(array):
    return lax.ppermute(array, "vocab", [(v, v ^ 1) for v in range(NX * NC)])


def x_shift(array, shift):
    return lax.ppermute(
        array,
        "vocab",
        [(v, ((v // NC + shift) % NX) * NC + v % NC) for v in range(NX * NC)],
    )


def z_shift(array, shift):
    return lax.ppermute(array, "expert", [(z, (z + shift) % NZ) for z in range(NZ)])


def gather_four(block, shift_by):
    return [block, shift_by(block, 1), shift_by(block, -1), shift_by(block, 2)]


def scatter_four(parts, shift_by):
    back = [shift_by(parts[1], -1), shift_by(parts[2], 1), shift_by(parts[3], 2)]
    return sum((piece.astype(f32) for piece in back), parts[0].astype(f32))


def copy_for_each(array, axis):
    peers = lax.axis_size(axis)
    return lax.all_to_all(
        jnp.broadcast_to(array[None], (peers, *array.shape)), axis, 0, 0, tiled=True
    )


def rms_scale(values, gain):
    mean_square = jnp.mean(values * values, axis=-1, keepdims=True)
    return values * lax.rsqrt(mean_square + epsilon) * gain


def route_gates(router_logit, route_ids):
    expert_count = router_logit.shape[1]
    matches = route_ids[:, :, None] == jnp.arange(expert_count, dtype=jnp.int32)[None, None, :]
    picked = jnp.sum(jnp.where(matches, router_logit[:, None, :], 0.0), axis=2)
    return 1.0 / jnp.sum(jnp.exp(picked[:, None, :] - picked[:, :, None]), axis=2)


def choice_member(lengths, positions):
    count = lengths.shape[0]
    upto = jnp.arange(count)[:, None] >= jnp.arange(count)[None, :]
    ends = jnp.sum(jnp.where(upto, lengths[None, :], 0), axis=1)
    starts = ends - lengths
    return (positions[None, :] >= starts[:, None]) & (positions[None, :] < ends[:, None])


def choice_softmax(choice_total, lengths, questions):
    average = choice_total / lengths.astype(f32)
    same_question = questions[:, None] == questions[None, :]
    question_top = jnp.max(jnp.where(same_question, average[None, :], -jnp.inf), axis=1)
    raised = jnp.exp(average - question_top)
    denominator = jnp.sum(jnp.where(same_question, raised[None, :], 0.0), axis=1)
    return raised / denominator


def on_device(
    resid,
    moe_gain,
    final_gain,
    router,
    w_gate,
    w_up,
    w_down,
    lm_head,
    expert_ids,
    target_ids,
    choice_len,
    choice_question,
):
    own_gate, own_up, own_down = w_gate[0], w_up[0], w_down[0]
    stream = resid[0].astype(f32)
    token_count, model_width = stream.shape

    other_gate = swap_cores(own_gate)
    other_up = swap_cores(own_up)
    other_down = swap_cores(own_down)
    other_head = swap_cores(lm_head)

    normed_in = rms_scale(stream, moe_gain).astype(bf16)
    router_logit = jnp.dot(normed_in, router, preferred_element_type=f32)
    route_ids = expert_ids[0]
    route_count = route_ids.shape[1]
    gate_weights = route_gates(router_logit, route_ids)
    bucket_size = 3
    flat_ids = route_ids.reshape(-1)
    picks = flat_ids.shape[0]
    before = jnp.arange(picks)[:, None] > jnp.arange(picks)[None, :]
    earlier = jnp.sum(
        (before & (flat_ids[:, None] == flat_ids[None, :])).astype(jnp.int32), axis=1
    )
    slot_index = flat_ids * bucket_size + earlier
    slot_match = (
        slot_index[:, None] == jnp.arange(NZ * bucket_size, dtype=jnp.int32)[None, :]
    ).astype(f32)
    slot_match = slot_match.reshape(token_count, route_count, -1)
    dispatch = jnp.sum(slot_match, axis=1).astype(bf16)
    combine_weights = jnp.sum(slot_match * gate_weights[:, :, None], axis=1)
    buckets = lax.dot_general(
        dispatch, normed_in, (((0,), (0,)), ((), ())), preferred_element_type=f32
    )
    buckets = buckets.astype(bf16).reshape(NZ, bucket_size, model_width)

    arrived = lax.all_to_all(buckets, "expert", split_axis=0, concat_axis=0, tiled=True).reshape(
        -1, model_width
    )
    column_rows = arrived.shape[0]

    def first(block, shift):
        return plane_shift(block, False, shift)

    def second(block, shift):
        return plane_shift(block, True, shift)

    line = jnp.concatenate(gather_four(arrived, first))
    rows = jnp.concatenate(gather_four(line, second))

    def expand(gate_cols, up_cols):
        gate_part = jnp.dot(rows, gate_cols, preferred_element_type=f32)
        up_part = jnp.dot(rows, up_cols, preferred_element_type=f32)
        return (jax.nn.silu(gate_part) * up_part).astype(bf16)

    hidden = jnp.concatenate([expand(own_gate, own_up), expand(other_gate, other_up)], axis=1)
    down = jnp.concatenate([own_down, other_down])
    parts = [
        jnp.dot(block, down, preferred_element_type=f32).astype(bf16)
        for block in jnp.split(hidden, 4)
    ]
    line_sum = scatter_four(parts, second).astype(bf16)
    expert_sum = scatter_four(jnp.split(line_sum, 4), first).astype(bf16)

    outgoing = expert_sum.reshape(NZ, bucket_size, model_width)
    returned = lax.all_to_all(outgoing, "expert", split_axis=0, concat_axis=0, tiled=True)
    returned_rows = returned.reshape(-1, model_width).astype(f32)
    mixed_rows = stream + jnp.sum(combine_weights[:, :, None] * returned_rows[None], axis=1)
    normed_out = rms_scale(mixed_rows, final_gain).astype(bf16)

    near = jnp.concatenate(gather_four(normed_out, x_shift))
    up_side, down_side = [near], [near]
    for _ in range(3):
        up_side.append(z_shift(up_side[-1], 1))
        down_side.append(z_shift(down_side[-1], -1))
    far = z_shift(up_side[-1], 1)
    blocks = [near]
    for step in range(1, 4):
        blocks += [up_side[step], down_side[step]]
    blocks.append(far)
    head_rows = jnp.concatenate(blocks)

    z_index = lax.axis_index("expert")
    v_index = lax.axis_index("vocab")
    x_index, c_index = v_index // NC, v_index % NC
    local = NZ * NX * token_count
    z_seen = (z_index + jnp.array(Z_ORDER, jnp.int32)) % NZ
    x_seen = (x_index + jnp.array(X_ORDER, jnp.int32)) % NX
    place = (
        (z_seen[:, None, None] * NX + x_seen[None, :, None]) * token_count
        + jnp.arange(token_count, dtype=jnp.int32)[None, None, :]
    ).reshape(-1)
    targets = target_ids[0]
    side_targets = lax.dynamic_slice_in_dim(
        targets.reshape(NZ * NX, NC, token_count), c_index, 1, 1
    ).reshape(-1)
    placed = place[:, None] == jnp.arange(local, dtype=jnp.int32)[None, :]
    seen_targets = jnp.sum(jnp.where(placed, side_targets[None, :], 0), axis=1)

    vocab_share = lm_head.shape[0]
    steps = jnp.arange(vocab_share, dtype=jnp.int32)
    own_base = (z_index * NX * NC + v_index) * vocab_share
    other_base = (z_index * NX * NC + (v_index ^ 1)) * vocab_share

    def head(rows_of, table, base):
        logits = lax.dot_general(
            rows_of, table, (((1,), (1,)), ((), ())), preferred_element_type=f32
        )
        top = jnp.max(logits, axis=1)
        total = jnp.sum(jnp.exp(logits - top[:, None]), axis=1)
        hit = jnp.sum(
            jnp.where(seen_targets[:, None] == (base + steps)[None, :], logits, 0.0), axis=1
        )
        return top, total, hit

    top_a, total_a, hit_a = head(head_rows, lm_head, own_base)
    top_b, total_b, hit_b = head(head_rows, other_head, other_base)
    top = jnp.maximum(top_a, top_b)
    total = total_a * jnp.exp(top_a - top) + total_b * jnp.exp(top_b - top)
    stats = jnp.stack([top, total, hit_a + hit_b])
    stats = jnp.sum(jnp.where(placed[None], stats[:, :, None], 0.0), axis=1)

    gathered = copy_for_each(stats, ("expert", "vocab")).reshape(NZ * NX, NC, 3, local)
    tops, totals, hits = gathered[:, :, 0], gathered[:, :, 1], gathered[:, :, 2]
    best = jnp.max(tops, axis=0)
    summed = jnp.sum(totals * jnp.exp(tops - best[None]), axis=0)
    logprob = jnp.sum(hits, axis=0) - (best + jnp.log(summed))
    group_logprob = logprob.reshape(NC, NZ * NX, token_count).transpose(1, 0, 2).reshape(-1)

    lengths = choice_len[0]
    questions = choice_question[0]
    positions = jnp.arange(group_logprob.shape[0], dtype=jnp.int32)
    choice_total = jnp.sum(
        jnp.where(choice_member(lengths, positions), group_logprob[None, :], 0.0), axis=1
    )
    own_first = (z_index * NX * NC + v_index) * token_count
    own_logprob = lax.dynamic_slice_in_dim(group_logprob, own_first, token_count, 0)
    choice_prob = choice_softmax(choice_total, lengths, questions)
    return (own_logprob.reshape(1, -1), choice_prob.reshape(1, -1))


def solution(mesh):
    return jax.shard_map(
        on_device,
        mesh=mesh,
        in_specs=(
            P("batch", ("expert", "vocab"), None),
            P(),
            P(),
            P(),
            P("expert", None, ("vocab", "batch")),
            P("expert", None, ("vocab", "batch")),
            P("expert", ("vocab", "batch"), None),
            P(("expert", "vocab"), None),
            P("batch", ("expert", "vocab"), None),
            P("batch", None),
            P("batch", None),
            P("batch", None),
        ),
        out_specs=(P("batch", ("expert", "vocab")), P("batch", None)),
        check_vma=False,
    )
```

time: 377 us -> 236 us (0.63)
  waiting for transfers between devices: 256 us -> 112 us
  starting transfers between devices: 5.98 us -> 57.2 us
  blocking collectives: 40.6 us -> 22.3 us
  between operations: 14 us -> 1.17 us
  matrix products: 37.3 us -> 27.7 us
  local copies, waits for them, and re-layouts: 13.1 us -> 6.85 us
    all_gather x2 -> x0, waiting for transfers between devices: 138 us -> none  [the longest x1 79.1 us: on_device(): lax.all_gather(normed_out, ('expert', 'vocab'), axis=0, tiled=True)]
    reduce_scatter x1 -> x0, waiting for transfers between devices: 101 us -> none  [on_device(): lax.psum_scatter(jnp.dot(hidden, down_rows, preferred_element_type=jnp.fl...]
    ppermute x0 -> x26, waiting for transfers between devices: none -> 89 us  [the longest x12 59.4 us: plane_shift(): return lax.ppermute(array, ('vocab', 'batch'), plane_perm(second, shift))]
    ppermute x0 -> x26, starting transfers between devices: none -> 35.1 us  [the longest x12 14.2 us: plane_shift(): return lax.ppermute(array, ('vocab', 'batch'), plane_perm(second, shift))]
    all_to_all x1 -> x0, blocking collectives: 18.1 us -> none  [on_device(): lax.all_to_all(outgoing, 'expert', split_axis=0, concat_axis=0, tiled=True)]
    all_to_all x1, starting transfers between devices: 5.85 us -> 18.6 us  [copy_for_each(): lax.all_to_all(jnp.broadcast_to(array[None], (peers, *array.shape)), axis...]
    all_to_all x0 -> x1, waiting for transfers between devices: none -> 10.2 us  [on_device(): lax.all_to_all(outgoing, 'expert', split_axis=0, concat_axis=0, tiled=True)]
    dot_general x5 -> x11, matrix products: 35.4 us -> 26.5 us  [the longest x4 12.2 us: on_device(): jnp.dot(block, down, preferred_element_type=f32).astype(bf16)]
  transfers between devices with their start and end apart: 4 -> 28, of which waited for: 4 -> 18; matrix products, arithmetic and copies ran while one was open for 0% -> 11% of each run, Pallas kernels for 0% -> 0%
where the time goes in v1:
time: 236 us; the launch traced here: 235 us
  waiting for transfers between devices  112 us (47%)
  starting transfers between devices  57.2 us (24%)
  matrix products  27.7 us (12%)
  blocking collectives  22.3 us (9%)
  other arithmetic  7.08 us (3%)
  local copies, waits for them, and re-layouts  6.85 us (3%)
    ppermute x12, waiting for transfers between devices, plane_shift(): return lax.ppermute(array, ('vocab', 'batch'), plane_perm(second, shift))  59.4 us
    ppermute x7, waiting for transfers between devices, z_shift(): lax.ppermute(array, 'expert', [(z, (z + shift) % NZ) for z in range(NZ)])  24.6 us
    all_to_all x1, blocking collectives, on_device(): lax.all_to_all(buckets, 'expert', split_axis=0, concat_axis=0, tiled=True)  22.3 us
    all_to_all x1, starting transfers between devices, copy_for_each(): lax.all_to_all(jnp.broadcast_to(array[None], (peers, *array.shape)), axis...  18.6 us
    ppermute x12, starting transfers between devices, plane_shift(): return lax.ppermute(array, ('vocab', 'batch'), plane_perm(second, shift))  14.2 us
    all_to_all x1, waiting for transfers between devices, copy_for_each(): lax.all_to_all(jnp.broadcast_to(array[None], (peers, *array.shape)), axis...  13.1 us
    dot_general x4, matrix products, on_device(): jnp.dot(block, down, preferred_element_type=f32).astype(bf16)  12.2 us
    all_to_all x1, waiting for transfers between devices, on_device(): lax.all_to_all(outgoing, 'expert', split_axis=0, concat_axis=0, tiled=True)  10.2 us
  transfers between devices with their start and end apart: 28, of which 18 were waited for; matrix products, arithmetic and copies ran while one was open for 11% of the time, Pallas kernels for 0%

profile of v1, /device:TPU:1, one launch (start us, length us, event | category | flops | bytes accessed | tf_op | source)
XLA Modules:
  0.0 234.6 jit_solution(17577022563303028512)
XLA Ops:
  0.6 1.1 fusion.5
  2.5 1.1 fusion.21
  5.7 1.2 convolution_convert_fusion.4
  7.1 22.3 %all_to_all.15 = bf16[8,3,6144]{2,1,0:T(4,128)(2,1)S(1)} all-to-all(bf16[8,3,6144]{2,1,0:T(4,128)(2,1)S(1)} %reshape.245), channel_id=1, replica_groups=mesh['expert'=8,'vocab'=8,'batch'=4] {'expert'}, dimensions={0} | all-to-all | bytes 589824 | tf_op jit(solution)/shard_map/all_to_all | solution.py:139
  29.7 1.4 collective-permute-start
  31.1 1.5 collective-permute-start.1
  32.7 1.6 collective-permute-start.2
  34.3 2.6 %collective-permute-done = bf16[24,6144]{1,0:T(8,128)(2,1)S(1)} collective-permute-done((bf16[24,6144]{1,0:T(8,128)(2,1)S(1)}, bf16[24,6144]{1,0:T(8,128)(2,1)S(1)}, u32[]{:S(2)}, u32[]{:S(2)}) %collective-permute-start) | collective-permute-done | bytes 294944 | tf_op jit(solution)/shard_map/ppermute | solution.py:28
  37.1 4.2 %collective-permute-done.2 = bf16[24,6144]{1,0:T(8,128)(2,1)S(1)} collective-permute-done((bf16[24,6144]{1,0:T(8,128)(2,1)S(1)}, bf16[24,6144]{1,0:T(8,128)(2,1)S(1)}, u32[]{:S(2)}, u32[]{:S(2)}) %collective-permute-start.2) | collective-permute-done | bytes 294944 | tf_op jit(solution)/shard_map/ppermute | solution.py:28
  42.3 1.8 collective-permute-start.4
  44.1 3.3 %collective-permute-start.6 = (bf16[6144,256]{1,0:T(8,128)(2,1)S(1)}, bf16[6144,256]{1,0:T(8,128)(2,1)S(1)}, u32[]{:S(2)}, u32[]{:S(2)}) collective-permute-start(bf16[6144,256]{1,0:T(8,128)(2,1)S(1)} %bitcast.84), channel_id=1, source_target_pairs={{0,4},{4,0},{8,12},{12,8},{16,20},{20,16},{24,28},{28,24},{1,5},{5... | collective-permute-start | bytes 9437192 | tf_op jit(solution)/shard_map/ppermute | solution.py:32
  47.8 10.1 %collective-permute-done.3 = bf16[96,6144]{1,0:T(8,128)(2,1)S(1)} collective-permute-done((bf16[96,6144]{1,0:T(8,128)(2,1)S(1)}, bf16[96,6144]{1,0:T(8,128)(2,1)S(1)}, u32[]{:S(2)}, u32[]{:S(2)}) %collective-permute-start.3) | collective-permute-done | bytes 1179680 | tf_op jit(solution)/shard_map/ppermute | solution.py:28
  58.0 1.2 collective-permute-start.5
  59.3 15.5 %collective-permute-done.5 = bf16[96,6144]{1,0:T(8,128)(2,1)S(1)} collective-permute-done((bf16[96,6144]{1,0:T(8,128)(2,1)S(1)}, bf16[96,6144]{1,0:T(8,128)(2,1)S(1)}, u32[]{:S(2)}, u32[]{:S(2)}) %collective-permute-start.5) | collective-permute-done | bytes 1179680 | tf_op jit(solution)/shard_map/ppermute | solution.py:28
  74.9 1.8 fusion.39
  76.8 1.8 multiply_convert_fusion.1
  78.6 1.8 fusion.45
  80.5 1.8 multiply_convert_fusion
  82.4 2.4 %convolution_convert_fusion.2 = bf16[96,6144]{1,0:T(8,128)(2,1)} fusion(bf16[384,256]{0,1:T(8,128)(2,1)S(1)} %multiply_convert_fusion.1, bf16[384,256]{0,1:T(8,128)(2,1)S(1)} %multiply_convert_fusion, bf16[256,6144]{1,0:T(8,128)(2,1)S(1)} %collective-permute-done.8, bf16[256,6144]{1,0:T(8,128)(2,1)S(1)} %bitcast.88), kind=kOutput, calls=%fused_computation.2 | convolution fusion | flops 617349120 | bytes 7864320 | tf_op jit(solution)/shard_map/dot_general | solution.py:161
  84.8 1.2 collective-permute-start.9
  86.0 2.4 %convolution_convert_fusion.1 = bf16[96,6144]{1,0:T(8,128)(2,1)} fusion(bf16[384,256]{0,1:T(8,128)(2,1)S(1)} %multiply_convert_fusion.1, bf16[384,256]{0,1:T(8,128)(2,1)S(1)} %multiply_convert_fusion, bf16[256,6144]{1,0:T(8,128)(2,1)S(1)} %collective-permute-done.8, bf16[256,6144]{1,0:T(8,128)(2,1)S(1)} %bitcast.89), kind=kOutput, calls=%fused_computation.1 | convolution fusion | flops 617349120 | bytes 7864320 | tf_op jit(solution)/shard_map/dot_general | solution.py:161
  88.6 2.4 %convolution_convert_fusion = bf16[96,6144]{1,0:T(8,128)(2,1)} fusion(bf16[384,256]{0,1:T(8,128)(2,1)S(1)} %multiply_convert_fusion, bf16[384,256]{0,1:T(8,128)(2,1)S(1)} %multiply_convert_fusion.1, bf16[256,6144]{1,0:T(8,128)(2,1)S(1)} %collective-permute-done.8, bf16[256,6144]{1,0:T(8,128)(2,1)S(1)} %bitcast.90), kind=kOutput, calls=%fused_computation | convolution fusion | flops 617349120 | bytes 7864320 | tf_op jit(solution)/shard_map/dot_general | solution.py:161
  91.0 1.2 collective-permute-start.11
  92.2 5.8 %collective-permute-start.25 = (bf16[256,6144]{1,0:T(8,128)(2,1)}, bf16[256,6144]{1,0:T(8,128)(2,1)}, u32[]{:S(2)}, u32[]{:S(2)}) collective-permute-start(bf16[256,6144]{1,0:T(8,128)(2,1)} %param.21), channel_id=1, source_target_pairs={{0,4},{4,0},{8,12},{12,8},{16,20},{20,16},{24,28},{28,24},{1,5},{5... | collective-permute-start | bytes 9437192 | tf_op jit(solution)/shard_map/ppermute | solution.py:32
  98.1 2.3 collective-permute-done.9
  100.3 17.6 %collective-permute-done.10 = bf16[96,6144]{1,0:T(8,128)(2,1)S(1)} collective-permute-done((bf16[96,6144]{1,0:T(8,128)(2,1)}, bf16[96,6144]{1,0:T(8,128)(2,1)S(1)}, u32[]{:S(2)}, u32[]{:S(2)}) %collective-permute-start.10) | collective-permute-done | bytes 1179680 | tf_op jit(solution)/shard_map/ppermute | solution.py:28
  117.9 1.1 copy-done.9
  119.0 5.1 %fusion.4 = bf16[96,6144]{1,0:T(8,128)(2,1)S(1)} fusion(bf16[96,6144]{1,0:T(8,128)(2,1)} %collective-permute-done.11, bf16[96,6144]{1,0:T(8,128)(2,1)} %copy-done.9, bf16[96,6144]{1,0:T(8,128)(2,1)S(1)} %collective-permute-done.9, bf16[384,256]{0,1:T(8,128)(2,1)S(1)} %multiply_convert_fusion.1, bf16[384,256]{0,1:T(8,128)(2,1)S(1)} %multiply_convert_fusion, ...), kind=kOutput, calls=%fused_computation.8 | convolution fusion | flops 622067712 | bytes 11403264 | tf_op jit(solution)/shard_map/dot_general | solution.py:161
  124.2 1.8 collective-permute-start.12
  125.9 1.3 collective-permute-start.14
  128.8 1.1 collective-permute-done.12
  129.8 6.1 %collective-permute-done.13 = bf16[24,6144]{1,0:T(8,128)(2,1)S(1)} collective-permute-done((bf16[24,6144]{1,0:T(8,128)(2,1)S(1)}, bf16[24,6144]{1,0:T(8,128)(2,1)S(1)}, u32[]{:S(2)}, u32[]{:S(2)}) %collective-permute-start.13) | collective-permute-done | bytes 294944 | tf_op jit(solution)/shard_map/ppermute | solution.py:28
  137.0 3.5 %all-to-all-start.1 = ((bf16[8,3,6144]{2,1,0:T(4,128)(2,1)}), bf16[8,3,6144]{2,1,0:T(4,128)(2,1)S(1)}, u32[]{:S(2)}, u32[]{:S(2)}) async-start(bf16[8,3,6144]{2,1,0:T(4,128)(2,1)} %reshape.247), calls=%async_computation.1 | async-start | bytes 786432 | tf_op jit(solution)/shard_map/all_to_all | solution.py:168
  140.9 10.2 %all-to-all-done.1 = bf16[8,3,6144]{2,1,0:T(4,128)(2,1)S(1)} async-done(((bf16[8,3,6144]{2,1,0:T(4,128)(2,1)}), bf16[8,3,6144]{2,1,0:T(4,128)(2,1)S(1)}, u32[]{:S(2)}, u32[]{:S(2)}) %all-to-all-start.1) | async-done | bytes 294944 | tf_op jit(solution)/shard_map/all_to_all | solution.py:168
  152.4 2.7 %collective-permute-start.16 = (bf16[8,6144]{1,0:T(8,128)(2,1)S(1)}, bf16[8,6144]{1,0:T(8,128)(2,1)S(1)}, u32[]{:S(2)}, u32[]{:S(2)}) collective-permute-start(bf16[8,6144]{1,0:T(8,128)(2,1)S(1)} %get-tuple-element.13), channel_id=1, source_target_pairs={{0,24},{4,28},{8,0},{12,4},{16,8},{20,12},{24,16},{28,20},{1,25},{... | collective-permute-start | bytes 294920 | tf_op jit(solution)/shard_map/ppermute | solution.py:36
  155.1 2.0 collective-permute-done.15
  157.7 2.4 %collective-permute-done.17 = bf16[8,6144]{1,0:T(8,128)(2,1)S(1)} collective-permute-done((bf16[8,6144]{1,0:T(8,128)(2,1)S(1)}, bf16[8,6144]{1,0:T(8,128)(2,1)S(1)}, u32[]{:S(2)}, u32[]{:S(2)}) %collective-permute-start.17) | collective-permute-done | bytes 98336 | tf_op jit(solution)/shard_map/ppermute | solution.py:36
  160.4 2.4 %collective-permute-start.19 = (bf16[32,6144]{1,0:T(8,128)(2,1)S(1)}, bf16[32,6144]{1,0:T(8,128)(2,1)S(1)}, u32[]{:S(2)}, u32[]{:S(2)}) collective-permute-start(bf16[32,6144]{1,0:T(8,128)(2,1)S(1)} %pad_maximum_fusion.1), channel_id=1, source_target_pairs={{0,224},{32,0},{64,32},{96,64},{128,96},{160,128},{192,160},{224,1... | collective-permute-start | bytes 1179656 | tf_op jit(solution)/shard_map/ppermute | solution.py:44
  162.9 5.1 %collective-permute-done.18 = bf16[32,6144]{1,0:T(8,128)(2,1)S(1)} collective-permute-done((bf16[32,6144]{1,0:T(8,128)(2,1)S(1)}, bf16[32,6144]{1,0:T(8,128)(2,1)S(1)}, u32[]{:S(2)}, u32[]{:S(2)}) %collective-permute-start.18) | collective-permute-done | bytes 393248 | tf_op jit(solution)/shard_map/ppermute | solution.py:44
  168.0 2.7 %collective-permute-start.21 = (bf16[32,6144]{1,0:T(8,128)(2,1)S(1)}, bf16[32,6144]{1,0:T(8,128)(2,1)S(1)}, u32[]{:S(2)}, u32[]{:S(2)}) collective-permute-start(bf16[32,6144]{1,0:T(8,128)(2,1)S(1)} %collective-permute-done.19), channel_id=1, source_target_pairs={{0,224},{32,0},{64,32},{96,64},{128,96},{160,128},{192,160},{224,1... | collective-permute-start | bytes 1179656 | tf_op jit(solution)/shard_map/ppermute | solution.py:44
  170.8 6.4 %collective-permute-done.20 = bf16[32,6144]{1,0:T(8,128)(2,1)S(1)} collective-permute-done((bf16[32,6144]{1,0:T(8,128)(2,1)S(1)}, bf16[32,6144]{1,0:T(8,128)(2,1)S(1)}, u32[]{:S(2)}, u32[]{:S(2)}) %collective-permute-start.20) | collective-permute-done | bytes 393248 | tf_op jit(solution)/shard_map/ppermute | solution.py:44
  177.2 3.0 %collective-permute-start.23 = (bf16[32,6144]{1,0:T(8,128)(2,1)S(1)}, bf16[32,6144]{1,0:T(8,128)(2,1)S(1)}, u32[]{:S(2)}, u32[]{:S(2)}) collective-permute-start(bf16[32,6144]{1,0:T(8,128)(2,1)S(1)} %collective-permute-done.21), channel_id=1, source_target_pairs={{0,224},{32,0},{64,32},{96,64},{128,96},{160,128},{192,160},{224,1... | collective-permute-start | bytes 1179656 | tf_op jit(solution)/shard_map/ppermute | solution.py:44
  180.3 5.2 %collective-permute-done.22 = bf16[32,6144]{1,0:T(8,128)(2,1)S(1)} collective-permute-done((bf16[32,6144]{1,0:T(8,128)(2,1)S(1)}, bf16[32,6144]{1,0:T(8,128)(2,1)S(1)}, u32[]{:S(2)}, u32[]{:S(2)}) %collective-permute-start.22) | collective-permute-done | bytes 393248 | tf_op jit(solution)/shard_map/ppermute | solution.py:44
  185.5 7.9 %collective-permute-done.24 = bf16[32,6144]{1,0:T(8,128)(2,1)S(1)} collective-permute-done((bf16[32,6144]{1,0:T(8,128)(2,1)S(1)}, bf16[32,6144]{1,0:T(8,128)(2,1)S(1)}, u32[]{:S(2)}, u32[]{:S(2)}) %collective-permute-start.24) | collective-permute-done | bytes 393248 | tf_op jit(solution)/shard_map/ppermute | solution.py:44
  193.5 2.9 %fusion.44 = (f32[256]{0:T(256)S(1)}, f32[256,256]{0,1:T(8,128)S(1)}) fusion(bf16[256,6144]{1,0:T(8,128)(2,1)S(1)} %constant_dynamic-update-slice_fusion.11, bf16[256,6144]{1,0:T(8,128)(2,1)} %param.21), kind=kOutput, calls=%fused_computation.131 | convolution fusion | flops 805371648 | bytes 6554624 | tf_op jit(solution)/shard_map/dot_general | solution.py:208
  196.5 2.9 %fusion.43 = (f32[256]{0:T(256)S(1)}, f32[256,256]{0,1:T(8,128)S(1)}) fusion(bf16[256,6144]{1,0:T(8,128)(2,1)S(1)} %constant_dynamic-update-slice_fusion.11, bf16[256,6144]{1,0:T(8,128)(2,1)} %collective-permute-done.25), kind=kOutput, calls=%fused_computation.130 | convolution fusion | flops 805371648 | bytes 6554624 | tf_op jit(solution)/shard_map/dot_general | solution.py:208
  200.5 18.6 %all-to-all-start.2 = ((f32[64,3,256]{2,1,0:T(4,128)}), f32[64,3,256]{2,1,0:T(4,128)S(1)}, u32[]{:S(2)}, u32[]{:S(2)}) async-start(f32[64,3,256]{2,1,0:T(4,128)} %broadcast_in_dim.152), calls=%async_computation.2 | async-start | bytes 524288 | tf_op jit(solution)/shard_map/all_to_all | solution.py:58
  219.3 13.1 %all-to-all-done.2 = f32[64,3,256]{2,1,0:T(4,128)S(1)} async-done(((f32[64,3,256]{2,1,0:T(4,128)}), f32[64,3,256]{2,1,0:T(4,128)S(1)}, u32[]{:S(2)}, u32[]{:S(2)}) %all-to-all-start.2) | async-done | bytes 196640 | tf_op jit(solution)/shard_map/all_to_all | solution.py:58
  (121 shorter events, 14.6 us)
Async XLA Ops:
  0.6 1.9 copy-start
  29.7 14.4 %copy-start.5 = (bf16[1,6144,256]{2,1,0:T(8,128)(2,1)S(1)}, bf16[1,6144,256]{2,1,0:T(8,128)(2,1)}, u32[]{:S(2)}) copy-start(bf16[1,6144,256]{2,1,0:T(8,128)(2,1)} %param.18) | copy-start | bytes 9437188
  29.7 7.3 %collective-permute-start = (bf16[24,6144]{1,0:T(8,128)(2,1)S(1)}, bf16[24,6144]{1,0:T(8,128)(2,1)S(1)}, u32[]{:S(2)}, u32[]{:S(2)}) collective-permute-start(bf16[24,6144]{1,0:T(8,128)(2,1)S(1)} %reshape.246), channel_id=1, source_target_pairs={{0,8},{1,9},{2,10},{3,11},{4,5},{5,6},{6,7},{7,4},{8,16},{9,17},{1... | collective-permute-start | bytes 884744 | tf_op jit(solution)/shard_map/ppermute | solution.py:28
  31.1 5.9 %collective-permute-start.1 = (bf16[24,6144]{1,0:T(8,128)(2,1)S(1)}, bf16[24,6144]{1,0:T(8,128)(2,1)S(1)}, u32[]{:S(2)}, u32[]{:S(2)}) collective-permute-start(bf16[24,6144]{1,0:T(8,128)(2,1)S(1)} %reshape.246), channel_id=1, source_target_pairs={{0,24},{1,25},{2,26},{3,27},{4,7},{5,4},{6,5},{7,6},{8,0},{9,1},{1... | collective-permute-start | bytes 884744 | tf_op jit(solution)/shard_map/ppermute | solution.py:28
  32.7 8.6 %collective-permute-start.2 = (bf16[24,6144]{1,0:T(8,128)(2,1)S(1)}, bf16[24,6144]{1,0:T(8,128)(2,1)S(1)}, u32[]{:S(2)}, u32[]{:S(2)}) collective-permute-start(bf16[24,6144]{1,0:T(8,128)(2,1)S(1)} %reshape.246), channel_id=1, source_target_pairs={{0,16},{1,17},{2,18},{3,19},{4,6},{5,7},{6,4},{7,5},{8,24},{9,25},... | collective-permute-start | bytes 884744 | tf_op jit(solution)/shard_map/ppermute | solution.py:28
  41.3 16.6 %collective-permute-start.3 = (bf16[96,6144]{1,0:T(8,128)(2,1)S(1)}, bf16[96,6144]{1,0:T(8,128)(2,1)S(1)}, u32[]{:S(2)}, u32[]{:S(2)}) collective-permute-start(bf16[96,6144]{1,0:T(8,128)(2,1)S(1)} %get-tuple-element.17), channel_id=1, source_target_pairs={{0,1},{1,2},{2,3},{3,0},{4,12},{5,13},{6,14},{7,15},{8,9},{9,10},{... | collective-permute-start | bytes 3538952 | tf_op jit(solution)/shard_map/ppermute | solution.py:28
  42.3 17.0 %collective-permute-start.4 = (bf16[96,6144]{1,0:T(8,128)(2,1)S(1)}, bf16[96,6144]{1,0:T(8,128)(2,1)S(1)}, u32[]{:S(2)}, u32[]{:S(2)}) collective-permute-start(bf16[96,6144]{1,0:T(8,128)(2,1)S(1)} %get-tuple-element.17), channel_id=1, source_target_pairs={{0,3},{1,0},{2,1},{3,2},{4,28},{5,29},{6,30},{7,31},{8,11},{9,8},{... | collective-permute-start | bytes 3538952 | tf_op jit(solution)/shard_map/ppermute | solution.py:28
  44.1 34.6 %collective-permute-start.6 = (bf16[6144,256]{1,0:T(8,128)(2,1)S(1)}, bf16[6144,256]{1,0:T(8,128)(2,1)S(1)}, u32[]{:S(2)}, u32[]{:S(2)}) collective-permute-start(bf16[6144,256]{1,0:T(8,128)(2,1)S(1)} %bitcast.84), channel_id=1, source_target_pairs={{0,4},{4,0},{8,12},{12,8},{16,20},{20,16},{24,28},{28,24},{1,5},{5... | collective-permute-start | bytes 9437192 | tf_op jit(solution)/shard_map/ppermute | solution.py:32
  47.3 33.2 %collective-permute-start.7 = (bf16[6144,256]{1,0:T(8,128)(2,1)}, bf16[6144,256]{1,0:T(8,128)(2,1)S(1)}, u32[]{:S(2)}, u32[]{:S(2)}) collective-permute-start(bf16[6144,256]{1,0:T(8,128)(2,1)} %bitcast.85), channel_id=1, source_target_pairs={{0,4},{4,0},{8,12},{12,8},{16,20},{20,16},{24,28},{28,24},{1,5},{5... | collective-permute-start | bytes 9437192 | tf_op jit(solution)/shard_map/ppermute | solution.py:32
  47.3 35.0 %collective-permute-start.8 = (bf16[256,6144]{1,0:T(8,128)(2,1)}, bf16[256,6144]{1,0:T(8,128)(2,1)S(1)}, u32[]{:S(2)}, u32[]{:S(2)}) collective-permute-start(bf16[256,6144]{1,0:T(8,128)(2,1)} %bitcast.86), channel_id=1, source_target_pairs={{0,4},{4,0},{8,12},{12,8},{16,20},{20,16},{24,28},{28,24},{1,5},{5... | collective-permute-start | bytes 9437192 | tf_op jit(solution)/shard_map/ppermute | solution.py:32
  58.0 16.9 %collective-permute-start.5 = (bf16[96,6144]{1,0:T(8,128)(2,1)S(1)}, bf16[96,6144]{1,0:T(8,128)(2,1)S(1)}, u32[]{:S(2)}, u32[]{:S(2)}) collective-permute-start(bf16[96,6144]{1,0:T(8,128)(2,1)S(1)} %get-tuple-element.17), channel_id=1, source_target_pairs={{0,2},{1,3},{2,0},{3,1},{4,20},{5,21},{6,22},{7,23},{8,10},{9,11},... | collective-permute-start | bytes 3538952 | tf_op jit(solution)/shard_map/ppermute | solution.py:28
  74.9 1.9 copy-start.6
  80.5 1.9 copy-start.7
  82.4 6.2 %copy-start.8 = (bf16[256,6144]{1,0:T(8,128)(2,1)}, bf16[256,6144]{1,0:T(8,128)(2,1)S(1)}, u32[]{:S(2)}) copy-start(bf16[256,6144]{1,0:T(8,128)(2,1)S(1)} %collective-permute-done.8) | copy-start | bytes 9437188
  84.8 15.6 %collective-permute-start.9 = (bf16[96,6144]{1,0:T(8,128)(2,1)}, bf16[96,6144]{1,0:T(8,128)(2,1)S(1)}, u32[]{:S(2)}, u32[]{:S(2)}) collective-permute-start(bf16[96,6144]{1,0:T(8,128)(2,1)} %convolution_convert_fusion.2), channel_id=1, source_target_pairs={{0,3},{1,0},{2,1},{3,2},{4,28},{5,29},{6,30},{7,31},{8,11},{9,8},{... | collective-permute-start | bytes 3538952 | tf_op jit(solution)/shard_map/ppermute | solution.py:28
  88.4 9.6 %copy-start.12 = (s32[4]{0:T(128)S(1)}, s32[4]{0:T(128)}, u32[]{:S(2)}) copy-start(s32[4]{0:T(128)} %constant.93.clone) | copy-start | bytes 52
  88.4 29.5 %collective-permute-start.10 = (bf16[96,6144]{1,0:T(8,128)(2,1)}, bf16[96,6144]{1,0:T(8,128)(2,1)S(1)}, u32[]{:S(2)}, u32[]{:S(2)}) collective-permute-start(bf16[96,6144]{1,0:T(8,128)(2,1)} %convolution_convert_fusion.1), channel_id=1, source_target_pairs={{0,1},{1,2},{2,3},{3,0},{4,12},{5,13},{6,14},{7,15},{8,9},{9,10},{... | collective-permute-start | bytes 3538952 | tf_op jit(solution)/shard_map/ppermute | solution.py:28
  91.0 28.0 %collective-permute-start.11 = (bf16[96,6144]{1,0:T(8,128)(2,1)}, bf16[96,6144]{1,0:T(8,128)(2,1)}, u32[]{:S(2)}, u32[]{:S(2)}) collective-permute-start(bf16[96,6144]{1,0:T(8,128)(2,1)} %convolution_convert_fusion), channel_id=1, source_target_pairs={{0,2},{1,3},{2,0},{3,1},{4,20},{5,21},{6,22},{7,23},{8,10},{9,11},... | collective-permute-start | bytes 3538952 | tf_op jit(solution)/shard_map/ppermute | solution.py:28
  92.2 104.3 %collective-permute-start.25 = (bf16[256,6144]{1,0:T(8,128)(2,1)}, bf16[256,6144]{1,0:T(8,128)(2,1)}, u32[]{:S(2)}, u32[]{:S(2)}) collective-permute-start(bf16[256,6144]{1,0:T(8,128)(2,1)} %param.21), channel_id=1, source_target_pairs={{0,4},{4,0},{8,12},{12,8},{16,20},{20,16},{24,28},{28,24},{1,5},{5... | collective-permute-start | bytes 9437192 | tf_op jit(solution)/shard_map/ppermute | solution.py:32
  98.0 29.2 %copy-start.11 = (s32[8]{0:T(128)S(1)}, s32[8]{0:T(128)}, u32[]{:S(2)}) copy-start(s32[8]{0:T(128)} %constant.92.clone) | copy-start | bytes 100
  98.1 29.7 %copy-start.4 = (s32[1,512]{1,0:T(1,128)S(1)}, s32[1,512]{1,0:T(1,128)}, u32[]{:S(2)}) copy-start(s32[1,512]{1,0:T(1,128)} %param.23) | copy-start | bytes 6148
  117.9 1.1 copy-start.9
  124.1 27.9 %copy-start.1 = (bf16[1,8,6144]{2,1,0:T(8,128)(2,1)S(1)}, bf16[1,8,6144]{2,1,0:T(8,128)(2,1)}, u32[]{:S(2)}) copy-start(bf16[1,8,6144]{2,1,0:T(8,128)(2,1)} %param.14) | copy-start | bytes 294916
  124.1 28.1 %copy-start.2 = (f32[6144]{0:T(1024)S(1)}, f32[6144]{0:T(1024)}, u32[]{:S(2)}) copy-start(f32[6144]{0:T(1024)} %param.16) | copy-start | bytes 73732
  124.2 5.7 %collective-permute-start.12 = (bf16[24,6144]{1,0:T(8,128)(2,1)S(1)}, bf16[24,6144]{1,0:T(8,128)(2,1)S(1)}, u32[]{:S(2)}, u32[]{:S(2)}) collective-permute-start(bf16[24,6144]{1,0:T(8,128)(2,1)S(1)} %get-tuple-element.14), channel_id=1, source_target_pairs={{0,24},{1,25},{2,26},{3,27},{4,7},{5,4},{6,5},{7,6},{8,0},{9,1},{1... | collective-permute-start | bytes 884744 | tf_op jit(solution)/shard_map/ppermute | solution.py:28
  125.9 9.9 %collective-permute-start.13 = (bf16[24,6144]{1,0:T(8,128)(2,1)S(1)}, bf16[24,6144]{1,0:T(8,128)(2,1)S(1)}, u32[]{:S(2)}, u32[]{:S(2)}) collective-permute-start(bf16[24,6144]{1,0:T(8,128)(2,1)S(1)} %get-tuple-element.16), channel_id=1, source_target_pairs={{0,8},{1,9},{2,10},{3,11},{4,5},{5,6},{6,7},{7,4},{8,16},{9,17},{1... | collective-permute-start | bytes 884744 | tf_op jit(solution)/shard_map/ppermute | solution.py:28
  125.9 9.9 %collective-permute-start.14 = (bf16[24,6144]{1,0:T(8,128)(2,1)S(1)}, bf16[24,6144]{1,0:T(8,128)(2,1)S(1)}, u32[]{:S(2)}, u32[]{:S(2)}) collective-permute-start(bf16[24,6144]{1,0:T(8,128)(2,1)S(1)} %get-tuple-element.15), channel_id=1, source_target_pairs={{0,16},{1,17},{2,18},{3,19},{4,6},{5,7},{6,4},{7,5},{8,24},{9,25},... | collective-permute-start | bytes 884744 | tf_op jit(solution)/shard_map/ppermute | solution.py:28
  137.0 14.1 %all-to-all-start.1 = ((bf16[8,3,6144]{2,1,0:T(4,128)(2,1)}), bf16[8,3,6144]{2,1,0:T(4,128)(2,1)S(1)}, u32[]{:S(2)}, u32[]{:S(2)}) async-start(bf16[8,3,6144]{2,1,0:T(4,128)(2,1)} %reshape.247), calls=%async_computation.1 | async-start | bytes 786432 | tf_op jit(solution)/shard_map/all_to_all | solution.py:168
  152.3 4.8 %collective-permute-start.15 = (bf16[8,6144]{1,0:T(8,128)(2,1)S(1)}, bf16[8,6144]{1,0:T(8,128)(2,1)S(1)}, u32[]{:S(2)}, u32[]{:S(2)}) collective-permute-start(bf16[8,6144]{1,0:T(8,128)(2,1)S(1)} %get-tuple-element.13), channel_id=1, source_target_pairs={{0,8},{4,12},{8,16},{12,20},{16,24},{20,28},{24,0},{28,4},{1,9},{5... | collective-permute-start | bytes 294920 | tf_op jit(solution)/shard_map/ppermute | solution.py:36
  152.4 5.3 %collective-permute-start.16 = (bf16[8,6144]{1,0:T(8,128)(2,1)S(1)}, bf16[8,6144]{1,0:T(8,128)(2,1)S(1)}, u32[]{:S(2)}, u32[]{:S(2)}) collective-permute-start(bf16[8,6144]{1,0:T(8,128)(2,1)S(1)} %get-tuple-element.13), channel_id=1, source_target_pairs={{0,24},{4,28},{8,0},{12,4},{16,8},{20,12},{24,16},{28,20},{1,25},{... | collective-permute-start | bytes 294920 | tf_op jit(solution)/shard_map/ppermute | solution.py:36
  155.1 5.0 %collective-permute-start.17 = (bf16[8,6144]{1,0:T(8,128)(2,1)S(1)}, bf16[8,6144]{1,0:T(8,128)(2,1)S(1)}, u32[]{:S(2)}, u32[]{:S(2)}) collective-permute-start(bf16[8,6144]{1,0:T(8,128)(2,1)S(1)} %get-tuple-element.13), channel_id=1, source_target_pairs={{0,16},{4,20},{8,24},{12,28},{16,0},{20,4},{24,8},{28,12},{1,17},{... | collective-permute-start | bytes 294920 | tf_op jit(solution)/shard_map/ppermute | solution.py:36
  160.1 7.9 %collective-permute-start.18 = (bf16[32,6144]{1,0:T(8,128)(2,1)S(1)}, bf16[32,6144]{1,0:T(8,128)(2,1)S(1)}, u32[]{:S(2)}, u32[]{:S(2)}) collective-permute-start(bf16[32,6144]{1,0:T(8,128)(2,1)S(1)} %pad_maximum_fusion.1), channel_id=1, source_target_pairs={{0,32},{32,64},{64,96},{96,128},{128,160},{160,192},{192,224},{224... | collective-permute-start | bytes 1179656 | tf_op jit(solution)/shard_map/ppermute | solution.py:44
  160.4 7.6 %collective-permute-start.19 = (bf16[32,6144]{1,0:T(8,128)(2,1)S(1)}, bf16[32,6144]{1,0:T(8,128)(2,1)S(1)}, u32[]{:S(2)}, u32[]{:S(2)}) collective-permute-start(bf16[32,6144]{1,0:T(8,128)(2,1)S(1)} %pad_maximum_fusion.1), channel_id=1, source_target_pairs={{0,224},{32,0},{64,32},{96,64},{128,96},{160,128},{192,160},{224,1... | collective-permute-start | bytes 1179656 | tf_op jit(solution)/shard_map/ppermute | solution.py:44
  168.0 9.2 %collective-permute-start.20 = (bf16[32,6144]{1,0:T(8,128)(2,1)S(1)}, bf16[32,6144]{1,0:T(8,128)(2,1)S(1)}, u32[]{:S(2)}, u32[]{:S(2)}) collective-permute-start(bf16[32,6144]{1,0:T(8,128)(2,1)S(1)} %collective-permute-done.18), channel_id=1, source_target_pairs={{0,32},{32,64},{64,96},{96,128},{128,160},{160,192},{192,224},{224... | collective-permute-start | bytes 1179656 | tf_op jit(solution)/shard_map/ppermute | solution.py:44
  168.0 9.2 %collective-permute-start.21 = (bf16[32,6144]{1,0:T(8,128)(2,1)S(1)}, bf16[32,6144]{1,0:T(8,128)(2,1)S(1)}, u32[]{:S(2)}, u32[]{:S(2)}) collective-permute-start(bf16[32,6144]{1,0:T(8,128)(2,1)S(1)} %collective-permute-done.19), channel_id=1, source_target_pairs={{0,224},{32,0},{64,32},{96,64},{128,96},{160,128},{192,160},{224,1... | collective-permute-start | bytes 1179656 | tf_op jit(solution)/shard_map/ppermute | solution.py:44
  177.2 8.3 %collective-permute-start.22 = (bf16[32,6144]{1,0:T(8,128)(2,1)S(1)}, bf16[32,6144]{1,0:T(8,128)(2,1)S(1)}, u32[]{:S(2)}, u32[]{:S(2)}) collective-permute-start(bf16[32,6144]{1,0:T(8,128)(2,1)S(1)} %collective-permute-done.20), channel_id=1, source_target_pairs={{0,32},{32,64},{64,96},{96,128},{128,160},{160,192},{192,224},{224... | collective-permute-start | bytes 1179656 | tf_op jit(solution)/shard_map/ppermute | solution.py:44
  177.2 8.3 %collective-permute-start.23 = (bf16[32,6144]{1,0:T(8,128)(2,1)S(1)}, bf16[32,6144]{1,0:T(8,128)(2,1)S(1)}, u32[]{:S(2)}, u32[]{:S(2)}) collective-permute-start(bf16[32,6144]{1,0:T(8,128)(2,1)S(1)} %collective-permute-done.21), channel_id=1, source_target_pairs={{0,224},{32,0},{64,32},{96,64},{128,96},{160,128},{192,160},{224,1... | collective-permute-start | bytes 1179656 | tf_op jit(solution)/shard_map/ppermute | solution.py:44
  185.4 8.0 %collective-permute-start.24 = (bf16[32,6144]{1,0:T(8,128)(2,1)S(1)}, bf16[32,6144]{1,0:T(8,128)(2,1)S(1)}, u32[]{:S(2)}, u32[]{:S(2)}) collective-permute-start(bf16[32,6144]{1,0:T(8,128)(2,1)S(1)} %collective-permute-done.22), channel_id=1, source_target_pairs={{0,32},{32,64},{64,96},{96,128},{128,160},{160,192},{192,224},{224... | collective-permute-start | bytes 1179656 | tf_op jit(solution)/shard_map/ppermute | solution.py:44
  196.4 22.7 %copy-start.10 = (s32[1,16]{1,0:T(1,128)S(1)}, s32[1,16]{1,0:T(1,128)}, u32[]{:S(2)}) copy-start(s32[1,16]{1,0:T(1,128)} %param.24) | copy-start | bytes 196
  196.4 36.7 %copy-start.3 = (s32[1,16]{1,0:T(1,128)S(1)}, s32[1,16]{1,0:T(1,128)}, u32[]{:S(2)}) copy-start(s32[1,16]{1,0:T(1,128)} %param.25) | copy-start | bytes 196
  200.5 31.9 %all-to-all-start.2 = ((f32[64,3,256]{2,1,0:T(4,128)}), f32[64,3,256]{2,1,0:T(4,128)S(1)}, u32[]{:S(2)}, u32[]{:S(2)}) async-start(f32[64,3,256]{2,1,0:T(4,128)} %broadcast_in_dim.152), calls=%async_computation.2 | async-start | bytes 524288 | tf_op jit(solution)/shard_map/all_to_all | solution.py:58

commit v2 on v0

v2 whole, which is shorter than its diff:
```python
import functools

import jax
import jax.numpy as jnp
from jax import lax
from jax.experimental import pallas as pl
from jax.experimental.pallas import tpu as pltpu
from jax.sharding import PartitionSpec as P

epsilon = 1e-05
bf16 = jnp.bfloat16
f32 = jnp.float32
i32 = jnp.int32

NZ, NX, NC, NY = 8, 4, 2, 4
SLOTS = 3
VMEM_LIMIT = 48 * 2**20


def two_axis_perm(sizes, coords, axis_of, shift):
    pairs = []
    for index in range(sizes):
        place = coords(index)
        axis, step, size = axis_of(place)
        to = dict(place)
        to[axis] = (place[axis] + shift * step) % size
        pairs.append((index, coords(to)))
    return pairs


def plane_coords(index):
    if isinstance(index, dict):
        return (index["x"] * NC + index["c"]) * NY + index["y"]
    return {"x": index // (NC * NY), "c": index // NY % NC, "y": index % NY}


def head_coords(index):
    if isinstance(index, dict):
        return (index["z"] * NX + index["x"]) * NC + index["c"]
    return {"z": index // (NX * NC), "x": index // NC % NX, "c": index % NC}


def plane_shift(array, second, shift):
    def axis_of(place):
        return ("x", 1, NX) if (place["c"] == 0) != second else ("y", 1, NY)

    perm = two_axis_perm(NX * NC * NY, plane_coords, axis_of, shift)
    return lax.ppermute(array, ("vocab", "batch"), perm)


def head_shift(array, second, shift):
    def axis_of(place):
        return ("z", 2, NZ) if (place["c"] == 0) != second else ("x", 1, NX)

    perm = two_axis_perm(NZ * NX * NC, head_coords, axis_of, shift)
    return lax.ppermute(array, ("expert", "vocab"), perm)


def swap_cores(array):
    return lax.ppermute(array, "vocab", [(v, v ^ 1) for v in range(NX * NC)])


def swap_planes(array):
    return lax.ppermute(array, "expert", [(z, z ^ 1) for z in range(NZ)])


def gather_four(block, shift_by):
    return [block, shift_by(block, 1), shift_by(block, -1), shift_by(block, 2)]


def rel_step(rel):
    return jnp.where(rel == 1, -1, jnp.where(rel == 2, 1, jnp.where(rel == 3, 2, 0)))


def tied(*arrays):
    return lax.optimization_barrier(arrays)


def shape(dims, dtype):
    return jax.ShapeDtypeStruct(dims, dtype)


def iota(dims, axis):
    return lax.broadcasted_iota(i32, dims, axis)


def params():
    return pltpu.CompilerParams(vmem_limit_bytes=VMEM_LIMIT)


def cost(flops, moved):
    return pl.CostEstimate(flops=flops, bytes_accessed=moved, transcendentals=0)


def prelude_kernel(ids_ref, resid_ref, gain_ref, router_ref, buckets_ref, weights_ref):
    values = resid_ref[...].astype(f32)
    tokens = values.shape[0]
    mean_square = jnp.mean(values * values, axis=-1, keepdims=True)
    normed = (values * lax.rsqrt(mean_square + epsilon) * gain_ref[...]).astype(bf16)
    logits = lax.dot_general(
        normed, router_ref[...], (((1,), (1,)), ((), ())), preferred_element_type=f32
    )
    ids = ids_ref[...]
    id_a, id_b = ids[:, 0:1], ids[:, 1:2]
    earlier = (iota((tokens, tokens), 0) > iota((tokens, tokens), 1)).astype(f32)

    def slots(width):
        column = iota((tokens, NZ * width), 1)
        owner, slot = column // width, column % width
        match_a, match_b = id_a == owner, id_b == owner
        named = (match_a | match_b).astype(f32)
        rank = jnp.dot(earlier, named, preferred_element_type=f32)
        chosen = named * (rank == slot.astype(f32)).astype(f32)
        return chosen, match_a, match_b

    wide, _, _ = slots(8)
    chosen, match_a, match_b = slots(SLOTS)
    entry = iota(logits.shape, 1)
    pick_a = jnp.sum(jnp.where(id_a == entry, logits, 0.0), axis=1, keepdims=True)
    pick_b = jnp.sum(jnp.where(id_b == entry, logits, 0.0), axis=1, keepdims=True)
    gate_a = 1.0 / (1.0 + jnp.exp(pick_b - pick_a))
    gate_b = 1.0 / (jnp.exp(pick_a - pick_b) + 1.0)
    weights_ref[...] = chosen * (
        jnp.where(match_a, gate_a, 0.0) + jnp.where(match_b, gate_b, 0.0)
    )
    rows = lax.dot_general(
        wide.astype(bf16), normed, (((0,), (0,)), ((), ())), preferred_element_type=f32
    )
    for e in range(NZ):
        buckets_ref[e] = rows[8 * e : 8 * e + SLOTS].astype(bf16)


def prelude(ids, resid, gain, router):
    tokens, width = resid.shape
    return pl.pallas_call(
        prelude_kernel,
        out_shape=(
            shape((NZ, SLOTS, width), bf16),
            shape((tokens, NZ * SLOTS), f32),
        ),
        compiler_params=params(),
        cost_estimate=cost(2 * 64 * 8 * width, 8 * width),
    )(ids, resid, gain, router)


def stack_kernel(*refs, chunk):
    *parts, out_ref = refs
    width = out_ref.shape[1]

    @pl.loop(0, width // chunk)
    def _(step):
        columns = pl.ds(pl.multiple_of(step * chunk, chunk), chunk)
        pieces = []
        for part in parts:
            if len(part.shape) == 3:
                pieces += [part[e, :, columns].astype(f32) for e in range(part.shape[0])]
            else:
                pieces.append(part[:, columns].astype(f32))
        out_ref[:, columns] = jnp.concatenate(pieces).astype(bf16)


def stack(parts):
    width = parts[0].shape[-1]
    rows = sum(part.size // width for part in parts)
    return pl.pallas_call(
        functools.partial(stack_kernel, chunk=512),
        out_shape=shape((rows, width), bf16),
        compiler_params=params(),
        cost_estimate=cost(0, 4 * rows * width),
    )(*parts)


def expand_kernel(*refs, count):
    rows = [ref[...] for ref in refs[:count]]
    gate_a, up_a, gate_b, up_b, out_ref, total = refs[count:]
    step = pl.program_id(0)

    @pl.when(step == 0)
    def _():
        total[...] = jnp.zeros_like(total)

    block = rows[0] if count == 1 else jnp.concatenate(rows)
    for j, weight in enumerate((gate_a, up_a, gate_b, up_b)):
        total[j] += jnp.dot(block, weight[...], preferred_element_type=f32)

    @pl.when(step == pl.num_programs(0) - 1)
    def _():
        share = total.shape[2]
        for j in range(2):
            gate = total[2 * j]
            out_ref[:, j * share : (j + 1) * share] = (
                gate / (1.0 + jnp.exp(-gate)) * total[2 * j + 1]
            ).astype(bf16)


def expand(rows, weights):
    depth = 768
    count = len(rows)
    each, width = rows[0].shape
    share = weights[0].shape[1]
    return pl.pallas_call(
        functools.partial(expand_kernel, count=count),
        grid=(width // depth,),
        in_specs=[pl.BlockSpec((each, depth), lambda k: (0, k))] * count
        + [pl.BlockSpec((depth, share), lambda k: (k, 0))] * 4,
        out_specs=pl.BlockSpec((count * each, 2 * share), lambda k: (0, 0)),
        out_shape=shape((count * each, 2 * share), bf16),
        scratch_shapes=[pltpu.VMEM((4, count * each, share), f32)],
        compiler_params=params(),
        cost_estimate=cost(8 * count * each * width * share, 8 * width * share),
    )(*rows, *weights)


def contract(hidden, down_a, down_b):
    share = down_a.shape[0]
    return jnp.dot(hidden[:, :share], down_a, preferred_element_type=f32) + jnp.dot(
        hidden[:, share:], down_b, preferred_element_type=f32
    )


def far_kernel(hidden_ref, down_a, down_b, before_ref, after_ref):
    part = contract(hidden_ref[...], down_a[...], down_b[...]).astype(bf16)
    half = before_ref.shape[0]
    before_ref[...] = part[:half]
    after_ref[...] = part[half:]


def near_kernel(hidden_ref, down_a, down_b, got_before, got_after, own_ref, before_ref, after_ref):
    part = contract(hidden_ref[...], down_a[...], down_b[...])
    rows = own_ref.shape[0]
    half = rows // 2
    own_ref[...] = part[:rows].astype(bf16)
    before_ref[:half] = (part[rows : rows + half] + got_before[...].astype(f32)).astype(bf16)
    before_ref[half:] = part[rows + half : 2 * rows].astype(bf16)
    after_ref[:half] = part[2 * rows : 2 * rows + half].astype(bf16)
    after_ref[half:] = (part[2 * rows + half :] + got_after[...].astype(f32)).astype(bf16)


def down_call(kernel, hidden, downs, got, out_rows):
    tile = 1024
    share, width = downs[0].shape
    return pl.pallas_call(
        kernel,
        grid=(width // tile,),
        in_specs=[pl.BlockSpec(hidden.shape, lambda n: (0, 0))]
        + [pl.BlockSpec((share, tile), lambda n: (0, n))] * 2
        + [pl.BlockSpec((g.shape[0], tile), lambda n: (0, n)) for g in got],
        out_specs=[pl.BlockSpec((rows, tile), lambda n: (0, n)) for rows in out_rows],
        out_shape=[shape((rows, width), bf16) for rows in out_rows],
        compiler_params=params(),
        cost_estimate=cost(4 * hidden.shape[0] * share * width, 4 * share * width),
    )(hidden, *downs, *got)


def line_sum_kernel(own_ref, before_ref, after_ref, *outs):
    total = own_ref[...].astype(f32) + before_ref[...].astype(f32) + after_ref[...].astype(f32)
    rows = outs[0].shape[0]
    for j, out in enumerate(outs):
        out[...] = total[j * rows : (j + 1) * rows].astype(bf16)


def line_sum(parts):
    tile = 1536
    rows, width = parts[0].shape
    return pl.pallas_call(
        line_sum_kernel,
        grid=(width // tile,),
        in_specs=[pl.BlockSpec((rows, tile), lambda n: (0, n))] * 3,
        out_specs=[pl.BlockSpec((rows // 4, tile), lambda n: (0, n))] * 4,
        out_shape=[shape((rows // 4, width), bf16)] * 4,
        compiler_params=params(),
        cost_estimate=cost(3 * rows * width, 8 * rows * width),
    )(*parts)


def expert_sum_kernel(a, b, c, d, out_ref, *, chunk):
    @pl.loop(0, out_ref.shape[2] // chunk)
    def _(step):
        columns = pl.ds(pl.multiple_of(step * chunk, chunk), chunk)
        total = (
            a[:, columns].astype(f32)
            + b[:, columns].astype(f32)
            + c[:, columns].astype(f32)
            + d[:, columns].astype(f32)
        )
        for e in range(NZ):
            out_ref[e, :, columns] = total[SLOTS * e : SLOTS * e + SLOTS].astype(bf16)


def expert_sum(parts):
    width = parts[0].shape[1]
    return pl.pallas_call(
        functools.partial(expert_sum_kernel, chunk=512),
        out_shape=shape((NZ, SLOTS, width), bf16),
        compiler_params=params(),
        cost_estimate=cost(96 * width, 240 * width),
    )(*parts)


def combine_kernel(weights_ref, rows_ref, resid_ref, gain_ref, out_ref):
    mixed = resid_ref[...].astype(f32)
    weights = weights_ref[...]
    for e in range(NZ):
        rows = rows_ref[e].astype(f32)
        for s in range(SLOTS):
            slot = SLOTS * e + s
            mixed += weights[:, slot : slot + 1] * rows[s : s + 1]
    mean_square = jnp.mean(mixed * mixed, axis=-1, keepdims=True)
    out_ref[...] = (mixed * lax.rsqrt(mean_square + epsilon) * gain_ref[...]).astype(bf16)


def combine(weights, rows, resid, gain):
    return pl.pallas_call(
        combine_kernel,
        out_shape=shape(resid.shape, bf16),
        compiler_params=params(),
        cost_estimate=cost(48 * resid.size, 8 * resid.size),
    )(weights, rows, resid, gain)


def head_kernel(place_ref, targets_ref, r0, r1, r2, r3, t0, t1, t2, t3, out_ref, total):
    step = pl.program_id(0)

    @pl.when(step == 0)
    def _():
        total[...] = jnp.zeros_like(total)

    rows = jnp.concatenate([r0[...], r1[...], r2[...], r3[...]])
    share = t0.shape[0]
    for j, table in enumerate((t0, t1, t2, t3)):
        total[:, j * share : (j + 1) * share] += lax.dot_general(
            rows, table[...], (((1,), (1,)), ((), ())), preferred_element_type=f32
        )

    @pl.when(step == pl.num_programs(0) - 1)
    def _():
        z, x, c = place_ref[0], place_ref[1], place_ref[2]
        count = rows.shape[0]
        row = iota((count, 1), 0)
        outer, inner, token = rel_step(row // 32), rel_step(row // 8 % 4), row % 8
        z_half = (z // 2 + 4 + jnp.where(c == 0, inner, outer)) % 4
        x_seen = (x + 4 + jnp.where(c == 0, outer, inner)) % 4
        place = (z_half * NX + x_seen) * 8 + token
        position = ((2 * z_half + z % 2) * NX + x_seen) * (NC * 8) + c * 8 + token
        targets = targets_ref[...]
        wanted = jnp.sum(
            jnp.where(position == iota((count, targets.shape[1]), 1), targets, 0),
            axis=1,
            keepdims=True,
        )
        logits = total[...]
        entry = iota((1, 4 * share), 1)
        table, offset = entry // share, entry % share
        z_of = jnp.where(table < 2, z, z + 1 - 2 * (z % 2))
        c_of = jnp.where(table % 2 == 0, c, 1 - c)
        entry_id = ((z_of * NX + x) * NC + c_of) * share + offset
        top = jnp.max(logits, axis=1, keepdims=True)
        spread = jnp.sum(jnp.exp(logits - top), axis=1, keepdims=True)
        hit = jnp.sum(jnp.where(wanted == entry_id, logits, 0.0), axis=1, keepdims=True)
        here = place == iota((count, count), 1)
        figures = [
            jnp.sum(jnp.where(here, value, 0.0), axis=0, keepdims=True)
            for value in (top, spread, hit, hit)
        ]
        figures = jnp.concatenate(figures)
        for peer in range(out_ref.shape[0]):
            out_ref[peer] = figures


def head(place, targets, rows, tables):
    depth = 768
    width = rows[0].shape[1]
    share = tables[0].shape[0]
    count = sum(r.shape[0] for r in rows)
    whole = pl.BlockSpec(memory_space=pltpu.SMEM)
    return pl.pallas_call(
        head_kernel,
        grid=(width // depth,),
        in_specs=[whole, pl.BlockSpec(targets.shape, lambda k: (0, 0))]
        + [pl.BlockSpec((rows[0].shape[0], depth), lambda k: (0, k))] * 4
        + [pl.BlockSpec((share, depth), lambda k: (0, k))] * 4,
        out_specs=pl.BlockSpec((NZ * NX * NC, 4, count), lambda k: (0, 0, 0)),
        out_shape=shape((NZ * NX * NC, 4, count), f32),
        scratch_shapes=[pltpu.VMEM((count, 4 * share), f32)],
        compiler_params=params(),
        cost_estimate=cost(8 * count * share * width, 8 * share * width),
    )(place, targets, *rows, *tables)


def finish_kernel(place_ref, stats_ref, lengths_ref, questions_ref, logprob_ref, prob_ref):
    z, x, c = place_ref[0], place_ref[1], place_ref[2]
    count = lengths_ref.shape[1]
    local = stats_ref.shape[2]
    lengths = lengths_ref[...].astype(f32)
    questions = questions_ref[...].astype(f32)
    square = (count, count)
    same_place = iota(square, 0) == iota(square, 1)
    ends = jnp.sum(
        jnp.where(iota(square, 1) <= iota(square, 0), lengths, 0.0), axis=1, keepdims=True
    )

    def as_column(line):
        return jnp.sum(jnp.where(same_place, line, 0.0), axis=1, keepdims=True)

    def as_line(column):
        return jnp.sum(jnp.where(same_place, column, 0.0), axis=0, keepdims=True)

    length_column = as_column(lengths)
    starts = ends - length_column
    lane = iota((1, local), 1)
    choice_total = jnp.zeros((count, 1), f32)
    own = jnp.zeros((1, local), f32)
    for parity in range(2):
        for core in range(NC):
            senders = [
                (zz * NX + xx) * NC + core for zz in range(parity, NZ, 2) for xx in range(NX)
            ]
            figures = [stats_ref[j] for j in senders]
            best = functools.reduce(jnp.maximum, [f[0:1] for f in figures])
            summed = sum(f[1:2] * jnp.exp(f[0:1] - best) for f in figures)
            logprob = sum(f[2:3] for f in figures) - (best + jnp.log(summed))
            position = (
                (2 * (lane // 32) + parity) * (NX * NC * 8)
                + lane // 8 % 4 * (NC * 8)
                + core * 8
                + lane % 8
            ).astype(f32)
            member = (position >= starts) & (position < ends)
            choice_total += jnp.sum(jnp.where(member, logprob, 0.0), axis=1, keepdims=True)
            mine = (z % 2 == parity) & (c == core)
            own += jnp.where(mine, logprob, 0.0)
    tokens = logprob_ref.shape[1]
    first = (z // 2 * NX + x) * tokens
    column = jnp.sum(
        jnp.where(iota((tokens, local), 1) == first + iota((tokens, local), 0), own, 0.0),
        axis=1,
        keepdims=True,
    )
    eye = iota((tokens, tokens), 0) == iota((tokens, tokens), 1)
    logprob_ref[...] = jnp.sum(jnp.where(eye, column, 0.0), axis=0, keepdims=True)

    average = choice_total / length_column
    same_question = as_column(questions) == questions
    top = jnp.max(
        jnp.where(same_question, as_line(average), -jnp.inf), axis=1, keepdims=True
    )
    raised = jnp.exp(average - top)
    denominator = jnp.sum(
        jnp.where(same_question, as_line(raised), 0.0), axis=1, keepdims=True
    )
    prob_ref[...] = as_line(raised / denominator)


def finish(place, stats, lengths, questions, tokens):
    smem, vmem = (pl.BlockSpec(memory_space=space) for space in (pltpu.SMEM, pltpu.VMEM))
    return pl.pallas_call(
        finish_kernel,
        in_specs=[smem, vmem, vmem, vmem],
        out_shape=(shape((1, tokens), f32), shape(lengths.shape, f32)),
        compiler_params=params(),
    )(place, stats, lengths, questions)


def on_device(
    resid,
    moe_gain,
    final_gain,
    router,
    w_gate,
    w_up,
    w_down,
    lm_head,
    expert_ids,
    target_ids,
    choice_len,
    choice_question,
):
    own_gate, own_up, own_down = w_gate[0], w_up[0], w_down[0]
    z_index = lax.axis_index("expert")
    v_index = lax.axis_index("vocab")
    place = jnp.stack([z_index, v_index // NC, v_index % NC]).astype(i32)

    other_gate = swap_cores(own_gate)
    other_up = swap_cores(own_up)
    other_down = swap_cores(own_down)
    other_head = swap_cores(lm_head)

    buckets, combine_weights = prelude(
        expert_ids[0], resid[0], moe_gain.reshape(1, -1), router.T
    )
    arrived = lax.all_to_all(buckets, "expert", split_axis=0, concat_axis=0, tiled=True)
    arrived, other_gate, other_up, other_down, other_head, own_head = tied(
        arrived, other_gate, other_up, other_down, other_head, lm_head
    )
    pair_head = swap_planes(own_head)
    pair_other = swap_cores(pair_head)

    def first(block, shift):
        return plane_shift(block, False, shift)

    def second(block, shift):
        return plane_shift(block, True, shift)

    line = stack(gather_four(arrived, first))
    rows = line.shape[0]
    half = rows // 2
    from_before = second(line, 1)
    from_after = second(line, -1)
    far_before = second(from_before[:half], 1)
    far_after = second(from_after[half:], -1)
    weights = (own_gate, own_up, other_gate, other_up)
    downs = (own_down, other_down)
    near_hidden = expand([line, from_before, from_after], weights)
    far_hidden = expand([far_before, far_after], weights)

    to_before, to_after = down_call(far_kernel, far_hidden, downs, (), (half, half))
    got_before = second(to_before, -1)
    got_after = second(to_after, 1)
    own_part, before_part, after_part = down_call(
        near_kernel, near_hidden, downs, (got_before, got_after), (rows, rows, rows)
    )
    pieces = line_sum([own_part, second(before_part, -1), second(after_part, 1)])
    outgoing = expert_sum(
        [pieces[0], first(pieces[1], -1), first(pieces[2], 1), first(pieces[3], 2)]
    )

    returned = lax.all_to_all(outgoing, "expert", split_axis=0, concat_axis=0, tiled=True)
    normed_out = combine(combine_weights, returned, resid[0], final_gain.reshape(1, -1))

    head_line = stack(gather_four(normed_out, lambda b, s: head_shift(b, False, s)))
    head_rows = gather_four(head_line, lambda b, s: head_shift(b, True, s))
    stats = head(place, target_ids, head_rows, (lm_head, other_head, pair_head, pair_other))
    gathered = lax.all_to_all(stats, ("expert", "vocab"), 0, 0, tiled=True)
    return finish(place, gathered, choice_len, choice_question, resid.shape[1])


def solution(mesh):
    return jax.shard_map(
        on_device,
        mesh=mesh,
        in_specs=(
            P("batch", ("expert", "vocab"), None),
            P(),
            P(),
            P(),
            P("expert", None, ("vocab", "batch")),
            P("expert", None, ("vocab", "batch")),
            P("expert", ("vocab", "batch"), None),
            P(("expert", "vocab"), None),
            P("batch", ("expert", "vocab"), None),
            P("batch", None),
            P("batch", None),
            P("batch", None),
        ),
        out_specs=(P("batch", ("expert", "vocab")), P("batch", None)),
        check_vma=False,
    )
```

time: 377 us -> 227 us (0.60)
  waiting for transfers between devices: 256 us -> 89.6 us
  Pallas kernels: 0 us -> 41.8 us
  matrix products: 37.3 us -> 0 us
  starting transfers between devices: 5.98 us -> 34.4 us
  blocking collectives: 40.6 us -> 56 us
  between operations: 14 us -> 0.86 us
  local copies, waits for them, and re-layouts: 13.1 us -> 3.39 us
  other arithmetic: 9.63 us -> 0.08 us
    all_gather x2 -> x0, waiting for transfers between devices: 138 us -> none  [the longest x1 79.1 us: on_device(): lax.all_gather(normed_out, ('expert', 'vocab'), axis=0, tiled=True)]
    reduce_scatter x1 -> x0, waiting for transfers between devices: 101 us -> none  [on_device(): lax.psum_scatter(jnp.dot(hidden, down_rows, preferred_element_type=jnp.fl...]
    ppermute x0 -> x26, waiting for transfers between devices: none -> 89.6 us  [the longest x14 55.7 us: plane_shift(): return lax.ppermute(array, ('vocab', 'batch'), perm)]
    pallas_call x0 -> x12, Pallas kernels: none -> 41.8 us  [the longest x2 16.9 us: expand(): pl.pallas_call(functools.partial(expand_kernel, count=count), grid=(width...]
    dot_general x6 -> x0, matrix products: 37.3 us -> none  [the longest x1 19.4 us: on_device(): jnp.dot(hidden, down_rows, preferred_element_type=jnp.float32)]
    ppermute x0 -> x26, starting transfers between devices: none -> 34.4 us  [the longest x14 19.5 us: plane_shift(): return lax.ppermute(array, ('vocab', 'batch'), perm)]
    all_to_all x0 -> x1, blocking collectives: none -> 22.3 us  [on_device(): gathered = lax.all_to_all(stats, ('expert', 'vocab'), 0, 0, tiled=True)]
    all_to_all x1 -> x0, waiting for transfers between devices: 16.9 us -> none  [copy_for_each(): lax.all_to_all(jnp.broadcast_to(array[None], (peers, *array.shape)), axis...]
  transfers between devices with their start and end apart: 4 -> 26, of which waited for: 4 -> 15; matrix products, arithmetic and copies ran while one was open for 0% -> 0% of each run, Pallas kernels for 0% -> 14%
where the time goes in v2:
time: 227 us; the launch traced here: 226 us
  waiting for transfers between devices  89.6 us (39%)
  blocking collectives  56 us (25%)
  Pallas kernels  41.8 us (18%)
  starting transfers between devices  34.4 us (15%)
  local copies, waits for them, and re-layouts  3.39 us (1%)
    ppermute x14, waiting for transfers between devices, plane_shift(): return lax.ppermute(array, ('vocab', 'batch'), perm)  55.7 us
    ppermute x6, waiting for transfers between devices, head_shift(): return lax.ppermute(array, ('expert', 'vocab'), perm)  22.4 us
    all_to_all x1, blocking collectives, on_device(): gathered = lax.all_to_all(stats, ('expert', 'vocab'), 0, 0, tiled=True)  22.3 us
    all_to_all x1, blocking collectives, on_device(): lax.all_to_all(buckets, 'expert', split_axis=0, concat_axis=0, tiled=True)  19.9 us
    ppermute x14, starting transfers between devices, plane_shift(): return lax.ppermute(array, ('vocab', 'batch'), perm)  19.5 us
    pallas_call x2, Pallas kernels, expand(): pl.pallas_call(functools.partial(expand_kernel, count=count), grid=(width...  16.9 us
    all_to_all x1, blocking collectives, on_device(): lax.all_to_all(outgoing, 'expert', split_axis=0, concat_axis=0, tiled=True)  13.8 us
    ppermute x1, waiting for transfers between devices, swap_planes(): return lax.ppermute(array, 'expert', [(z, z ^ 1) for z in range(NZ)])  11.5 us
  transfers between devices with their start and end apart: 26, of which 15 were waited for; matrix products, arithmetic and copies ran while one was open for 0% of the time, Pallas kernels for 14%

profile of v2, /device:TPU:1, one launch (start us, length us, event | category | flops | bytes accessed | tf_op | source)
XLA Modules:
  0.0 226.1 jit_solution(17765361206228822249)
XLA Ops:
  0.6 3.3 %collective-permute-start = (bf16[6144,256]{1,0:T(8,128)(2,1)}, bf16[6144,256]{1,0:T(8,128)(2,1)}, u32[]{:S(2)}, u32[]{:S(2)}) collective-permute-start(bf16[6144,256]{1,0:T(8,128)(2,1)} %bitcast.14), channel_id=1, source_target_pairs={{0,4},{4,0},{8,12},{12,8},{16,20},{20,16},{24,28},{28,24},{1,5},{5... | collective-permute-start | bytes 9437192 | tf_op jit(solution)/shard_map/ppermute | solution.py:60
  4.1 0.4 collective-permute-start.2
  4.6 0.8 copy.14.ids_ref
  5.3 0.9 copy-done.3
  6.2 0.9 copy-done.5
  7.1 0.7 copy-done.7
  7.9 0.6 shard_map.131
  8.5 19.9 %all_to_all.15.refs_0_ = bf16[8,3,6144]{2,1,0:T(4,128)(2,1)S(1)} all-to-all(bf16[8,3,6144]{2,1,0:T(4,128)(2,1)S(1)} %get-tuple-element.20), channel_id=1, replica_groups=mesh['expert'=8,'vocab'=8,'batch'=4] {'expert'}, dimensions={0} | all-to-all | bytes 589824 | tf_op jit(solution)/shard_map/all_to_all | solution.py:491
  28.4 0.4 collective-permute-start.24
  28.8 1.3 collective-permute-start.4
  30.1 1.4 collective-permute-start.5
  31.5 1.6 collective-permute-start.6
  33.2 3.8 %collective-permute-done.4.refs_1_ = bf16[8,3,6144]{2,1,0:T(4,128)(2,1)S(1)} collective-permute-done((bf16[8,3,6144]{2,1,0:T(4,128)(2,1)S(1)}, bf16[8,3,6144]{2,1,0:T(4,128)(2,1)S(1)}, u32[]{:S(2)}, u32[]{:S(2)}) %collective-permute-start.4) | collective-permute-done | bytes 294944 | tf_op jit(solution)/shard_map/ppermute | solution.py:48
  37.1 5.3 %collective-permute-done.6.refs_3_ = bf16[8,3,6144]{2,1,0:T(4,128)(2,1)S(1)} collective-permute-done((bf16[8,3,6144]{2,1,0:T(4,128)(2,1)S(1)}, bf16[8,3,6144]{2,1,0:T(4,128)(2,1)S(1)}, u32[]{:S(2)}, u32[]{:S(2)}) %collective-permute-start.6) | collective-permute-done | bytes 294944 | tf_op jit(solution)/shard_map/ppermute | solution.py:48
  42.4 0.6 shard_map.132.refs_0_
  43.0 1.0 collective-permute-start.7
  44.0 1.8 collective-permute-start.8
  45.8 13.9 %collective-permute-done.7.refs_1_ = bf16[96,6144]{1,0:T(8,128)(2,1)S(1)} collective-permute-done((bf16[96,6144]{1,0:T(8,128)(2,1)S(1)}, bf16[96,6144]{1,0:T(8,128)(2,1)S(1)}, u32[]{:S(2)}, u32[]{:S(2)}) %collective-permute-start.7) | collective-permute-done | bytes 1179680 | tf_op jit(solution)/shard_map/ppermute | solution.py:48
  59.9 2.7 %collective-permute-start.10 = (bf16[48,6144]{1,0:T(8,128)(2,1)S(1)}, bf16[48,6144]{1,0:T(8,128)(2,1)S(1)}, u32[]{:S(2)}, u32[]{:S(2)}) collective-permute-start(bf16[48,6144]{1,0:T(8,128)(2,1)S(1)} %slice.9), channel_id=1, source_target_pairs={{0,3},{1,0},{2,1},{3,2},{4,28},{5,29},{6,30},{7,31},{8,11},{9,8},{... | collective-permute-start | bytes 1769480 | tf_op jit(solution)/shard_map/ppermute | solution.py:48
  62.6 7.4 %collective-permute-done.9.refs_0_ = bf16[48,6144]{1,0:T(8,128)(2,1)S(1)} collective-permute-done((bf16[48,6144]{1,0:T(8,128)(2,1)S(1)}, bf16[48,6144]{1,0:T(8,128)(2,1)S(1)}, u32[]{:S(2)}, u32[]{:S(2)}) %collective-permute-start.9) | collective-permute-done | bytes 589856 | tf_op jit(solution)/shard_map/ppermute | solution.py:48
  70.0 7.4 %shard_map.134.hidden_ref = bf16[96,512]{1,0:T(8,128)(2,1)S(1)} custom-call(bf16[48,6144]{1,0:T(8,128)(2,1)S(1)} %collective-permute-done.9.refs_0_, bf16[48,6144]{1,0:T(8,128)(2,1)S(1)} %collective-permute-done.10.refs_1_, bf16[6144,256]{1,0:T(8,128)(2,1)S(1)} %bitcast.16, bf16[6144,256]{1,0:T(8,128)(2,1)} %bitcast.23, ...), custom_call_target="tpu_custom_call" | custom-call | flops 1207959552 | bytes 12582912 | tf_op jit(solution)/shard_map/pallas_call | solution.py:201
  77.5 4.7 %shard_map.135 = (bf16[48,6144]{1,0:T(8,128)(2,1)S(1)}, bf16[48,6144]{1,0:T(8,128)(2,1)S(1)}) custom-call(bf16[96,512]{1,0:T(8,128)(2,1)S(1)} %shard_map.134.hidden_ref, bf16[256,6144]{1,0:T(8,128)(2,1)S(1)} %bitcast.13, bf16[256,6144]{1,0:T(8,128)(2,1)} %collective-permute-done.2.down_b), custom_call_target="tpu_custom_call" | custom-call | flops 603979776 | bytes 6291456 | tf_op jit(solution)/shard_map/pallas_call | solution.py:242
  82.1 2.9 %collective-permute-start.11 = (bf16[48,6144]{1,0:T(8,128)(2,1)S(1)}, bf16[48,6144]{1,0:T(8,128)(2,1)S(1)}, u32[]{:S(2)}, u32[]{:S(2)}) collective-permute-start(bf16[48,6144]{1,0:T(8,128)(2,1)S(1)} %get-tuple-element.25), channel_id=1, source_target_pairs={{0,3},{1,0},{2,1},{3,2},{4,28},{5,29},{6,30},{7,31},{8,11},{9,8},{... | collective-permute-start | bytes 1769480 | tf_op jit(solution)/shard_map/ppermute | solution.py:48
  85.0 11.5 %collective-permute-done.24.t2 = bf16[256,6144]{1,0:T(8,128)(2,1)} collective-permute-done((bf16[256,6144]{1,0:T(8,128)(2,1)}, bf16[256,6144]{1,0:T(8,128)(2,1)}, u32[]{:S(2)}, u32[]{:S(2)}) %collective-permute-start.24) | collective-permute-done | bytes 3145760 | tf_op jit(solution)/shard_map/ppermute | solution.py:64
  96.5 2.9 %collective-permute-start.25 = (bf16[256,6144]{1,0:T(8,128)(2,1)}, bf16[256,6144]{1,0:T(8,128)(2,1)}, u32[]{:S(2)}, u32[]{:S(2)}) collective-permute-start(bf16[256,6144]{1,0:T(8,128)(2,1)} %collective-permute-done.24.t2), channel_id=1, source_target_pairs={{0,4},{4,0},{8,12},{12,8},{16,20},{20,16},{24,28},{28,24},{1,5},{5... | collective-permute-start | bytes 9437192 | tf_op jit(solution)/shard_map/ppermute | solution.py:60
  99.4 9.5 %shard_map.133.hidden_ref = bf16[288,512]{1,0:T(8,128)(2,1)S(1)} custom-call(bf16[96,6144]{1,0:T(8,128)(2,1)S(1)} %shard_map.132.refs_0_, bf16[96,6144]{1,0:T(8,128)(2,1)S(1)} %collective-permute-done.7.refs_1_, bf16[96,6144]{1,0:T(8,128)(2,1)S(1)} %collective-permute-done.8.refs_2_, bf16[6144,256]{1,0:T(8,128)(2,1)} %bitcast.15, ...), custom_call_target="tpu_custom_call" | custom-call | flops 3623878656 | bytes 12582912 | tf_op jit(solution)/shard_map/pallas_call | solution.py:201
  108.9 5.9 %shard_map.136 = (bf16[96,6144]{1,0:T(8,128)(2,1)S(1)}, bf16[96,6144]{1,0:T(8,128)(2,1)S(1)}, bf16[96,6144]{1,0:T(8,128)(2,1)S(1)}) custom-call(bf16[288,512]{1,0:T(8,128)(2,1)S(1)} %shard_map.133.hidden_ref, bf16[256,6144]{1,0:T(8,128)(2,1)} %bitcast.12, bf16[256,6144]{1,0:T(8,128)(2,1)} %collective-permute-done.2.down_b, ...), custom_call_target="tpu_custom_call" | custom-call | flops 1811939328 | bytes 6291456 | tf_op jit(solution)/shard_map/pallas_call | solution.py:242
  114.8 2.6 %collective-permute-start.13 = (bf16[96,6144]{1,0:T(8,128)(2,1)S(1)}, bf16[96,6144]{1,0:T(8,128)(2,1)S(1)}, u32[]{:S(2)}, u32[]{:S(2)}) collective-permute-start(bf16[96,6144]{1,0:T(8,128)(2,1)S(1)} %get-tuple-element.28), channel_id=1, source_target_pairs={{0,3},{1,0},{2,1},{3,2},{4,28},{5,29},{6,30},{7,31},{8,11},{9,8},{... | collective-permute-start | bytes 3538952 | tf_op jit(solution)/shard_map/ppermute | solution.py:48
  117.4 13.1 %collective-permute-done.13.before_ref = bf16[96,6144]{1,0:T(8,128)(2,1)S(1)} collective-permute-done((bf16[96,6144]{1,0:T(8,128)(2,1)S(1)}, bf16[96,6144]{1,0:T(8,128)(2,1)S(1)}, u32[]{:S(2)}, u32[]{:S(2)}) %collective-permute-start.13) | collective-permute-done | bytes 1179680 | tf_op jit(solution)/shard_map/ppermute | solution.py:48
  130.5 3.4 %collective-permute-done.14.after_ref = bf16[96,6144]{1,0:T(8,128)(2,1)S(1)} collective-permute-done((bf16[96,6144]{1,0:T(8,128)(2,1)S(1)}, bf16[96,6144]{1,0:T(8,128)(2,1)S(1)}, u32[]{:S(2)}, u32[]{:S(2)}) %collective-permute-start.14) | collective-permute-done | bytes 1179680 | tf_op jit(solution)/shard_map/ppermute | solution.py:48
  133.9 0.9 shard_map.137
  134.8 2.5 %collective-permute-start.15 = (bf16[24,6144]{1,0:T(8,128)(2,1)S(1)}, bf16[24,6144]{1,0:T(8,128)(2,1)S(1)}, u32[]{:S(2)}, u32[]{:S(2)}) collective-permute-start(bf16[24,6144]{1,0:T(8,128)(2,1)S(1)} %get-tuple-element.31), channel_id=1, source_target_pairs={{0,24},{1,25},{2,26},{3,27},{4,7},{5,4},{6,5},{7,6},{8,0},{9,1},{1... | collective-permute-start | bytes 884744 | tf_op jit(solution)/shard_map/ppermute | solution.py:48
  137.3 1.6 collective-permute-start.17
  139.0 2.0 collective-permute-done.15.b
  141.0 6.6 %collective-permute-done.16.c = bf16[24,6144]{1,0:T(8,128)(2,1)S(1)} collective-permute-done((bf16[24,6144]{1,0:T(8,128)(2,1)S(1)}, bf16[24,6144]{1,0:T(8,128)(2,1)S(1)}, u32[]{:S(2)}, u32[]{:S(2)}) %collective-permute-start.16) | collective-permute-done | bytes 294944 | tf_op jit(solution)/shard_map/ppermute | solution.py:48
  147.9 13.8 %all_to_all.16.rows_ref = bf16[8,3,6144]{2,1,0:T(4,128)(2,1)S(1)} all-to-all(bf16[8,3,6144]{2,1,0:T(4,128)(2,1)S(1)} %shard_map.138), channel_id=1, replica_groups=mesh['expert'=8,'vocab'=8,'batch'=4] {'expert'}, dimensions={0} | all-to-all | bytes 589824 | tf_op jit(solution)/shard_map/all_to_all | solution.py:527
  161.7 1.0 shard_map.139.refs_0_
  162.8 2.7 %collective-permute-start.19 = (bf16[8,6144]{1,0:T(8,128)(2,1)S(1)}, bf16[8,6144]{1,0:T(8,128)(2,1)S(1)}, u32[]{:S(2)}, u32[]{:S(2)}) collective-permute-start(bf16[8,6144]{1,0:T(8,128)(2,1)S(1)} %shard_map.139.refs_0_), channel_id=1, source_target_pairs={{0,192},{4,28},{8,200},{12,4},{16,208},{20,12},{24,216},{28,20},{3... | collective-permute-start | bytes 294920 | tf_op jit(solution)/shard_map/ppermute | solution.py:56
  165.5 2.0 collective-permute-done.18.refs_1_
  167.5 0.6 collective-permute-done.19.refs_2_
  168.1 2.4 %collective-permute-done.20.refs_3_ = bf16[8,6144]{1,0:T(8,128)(2,1)S(1)} collective-permute-done((bf16[8,6144]{1,0:T(8,128)(2,1)S(1)}, bf16[8,6144]{1,0:T(8,128)(2,1)S(1)}, u32[]{:S(2)}, u32[]{:S(2)}) %collective-permute-start.20) | collective-permute-done | bytes 98336 | tf_op jit(solution)/shard_map/ppermute | solution.py:56
  170.6 3.6 %collective-permute-start.22 = (bf16[32,6144]{1,0:T(8,128)(2,1)S(1)}, bf16[32,6144]{1,0:T(8,128)(2,1)}, u32[]{:S(2)}, u32[]{:S(2)}) collective-permute-start(bf16[32,6144]{1,0:T(8,128)(2,1)S(1)} %shard_map.140.r0), channel_id=1, source_target_pairs={{0,24},{4,196},{8,0},{12,204},{16,8},{20,212},{24,16},{28,220},{32... | collective-permute-start | bytes 1179656 | tf_op jit(solution)/shard_map/ppermute | solution.py:56
  174.2 1.2 collective-permute-start.23
  175.5 8.3 %collective-permute-done.21.r1 = bf16[32,6144]{1,0:T(8,128)(2,1)} collective-permute-done((bf16[32,6144]{1,0:T(8,128)(2,1)S(1)}, bf16[32,6144]{1,0:T(8,128)(2,1)}, u32[]{:S(2)}, u32[]{:S(2)}) %collective-permute-start.21) | collective-permute-done | bytes 393248 | tf_op jit(solution)/shard_map/ppermute | solution.py:56
  183.9 9.1 %collective-permute-done.22.r2 = bf16[32,6144]{1,0:T(8,128)(2,1)} collective-permute-done((bf16[32,6144]{1,0:T(8,128)(2,1)S(1)}, bf16[32,6144]{1,0:T(8,128)(2,1)}, u32[]{:S(2)}, u32[]{:S(2)}) %collective-permute-start.22) | collective-permute-done | bytes 393248 | tf_op jit(solution)/shard_map/ppermute | solution.py:56
  193.0 9.4 %shard_map.141 = f32[64,4,128]{2,1,0:T(4,128)S(1)} custom-call(s32[3]{0:T(128)S(1)} %pad_add_fusion.place_ref, s32[1,512]{1,0:T(1,128)S(1)} %copy-done.8, bf16[32,6144]{1,0:T(8,128)(2,1)S(1)} %shard_map.140.r0, bf16[32,6144]{1,0:T(8,128)(2,1)} %collective-permute-done.21.r1, bf16[32,6144]{1,0:T(8,128)(2,1)} %collective-permute-done.22.r2, ...), custom_call_target="tpu_custom_call" | custom-call | flops 1610612736 | bytes 12582912 | tf_op jit(solution)/shard_map/pallas_call | solution.py:376
  202.4 22.3 %all_to_all.17.stats_ref = f32[64,4,128]{2,1,0:T(4,128)S(1)} all-to-all(f32[64,4,128]{2,1,0:T(4,128)S(1)} %shard_map.141), channel_id=1, replica_groups=mesh['expert'=8,'vocab'=8,'batch'=4] {'expert','vocab'}, dimensions={0} | all-to-all | bytes 262144 | tf_op jit(solution)/shard_map/all_to_all | solution.py:533
  224.7 1.4 shard_map.142
  (45 shorter events, 1.3 us)
Async XLA Ops:
  0.6 69.4 %copy-start.1 = (bf16[1,6144,256]{2,1,0:T(8,128)(2,1)S(1)}, bf16[1,6144,256]{2,1,0:T(8,128)(2,1)}, u32[]{:S(2)}) copy-start(bf16[1,6144,256]{2,1,0:T(8,128)(2,1)} %param.16) | copy-start | bytes 9437188
  0.6 27.8 %collective-permute-start = (bf16[6144,256]{1,0:T(8,128)(2,1)}, bf16[6144,256]{1,0:T(8,128)(2,1)}, u32[]{:S(2)}, u32[]{:S(2)}) collective-permute-start(bf16[6144,256]{1,0:T(8,128)(2,1)} %bitcast.14), channel_id=1, source_target_pairs={{0,4},{4,0},{8,12},{12,8},{16,20},{20,16},{24,28},{28,24},{1,5},{5... | collective-permute-start | bytes 9437192 | tf_op jit(solution)/shard_map/ppermute | solution.py:60
  4.0 24.5 %collective-permute-start.1 = (bf16[6144,256]{1,0:T(8,128)(2,1)}, bf16[6144,256]{1,0:T(8,128)(2,1)}, u32[]{:S(2)}, u32[]{:S(2)}) collective-permute-start(bf16[6144,256]{1,0:T(8,128)(2,1)} %bitcast.22), channel_id=1, source_target_pairs={{0,4},{4,0},{8,12},{12,8},{16,20},{20,16},{24,28},{28,24},{1,5},{5... | collective-permute-start | bytes 9437192 | tf_op jit(solution)/shard_map/ppermute | solution.py:60
  4.1 24.4 %collective-permute-start.2 = (bf16[256,6144]{1,0:T(8,128)(2,1)}, bf16[256,6144]{1,0:T(8,128)(2,1)}, u32[]{:S(2)}, u32[]{:S(2)}) collective-permute-start(bf16[256,6144]{1,0:T(8,128)(2,1)} %bitcast.11), channel_id=1, source_target_pairs={{0,4},{4,0},{8,12},{12,8},{16,20},{20,16},{24,28},{28,24},{1,5},{5... | collective-permute-start | bytes 9437192 | tf_op jit(solution)/shard_map/ppermute | solution.py:60
  4.5 24.0 %collective-permute-start.3 = (bf16[256,6144]{1,0:T(8,128)(2,1)}, bf16[256,6144]{1,0:T(8,128)(2,1)}, u32[]{:S(2)}, u32[]{:S(2)}) collective-permute-start(bf16[256,6144]{1,0:T(8,128)(2,1)} %t0.1), channel_id=1, source_target_pairs={{0,4},{4,0},{8,12},{12,8},{16,20},{20,16},{24,28},{28,24},{1,5},{5... | collective-permute-start | bytes 9437192 | tf_op jit(solution)/shard_map/ppermute | solution.py:60
  5.3 0.9 copy-start.3
  6.2 0.9 copy-start.5
  7.1 0.7 copy-start.7
  28.4 68.0 %collective-permute-start.24 = (bf16[256,6144]{1,0:T(8,128)(2,1)}, bf16[256,6144]{1,0:T(8,128)(2,1)}, u32[]{:S(2)}, u32[]{:S(2)}) collective-permute-start(bf16[256,6144]{1,0:T(8,128)(2,1)} %t0.1), channel_id=1, source_target_pairs={{0,32},{32,0},{64,96},{96,64},{128,160},{160,128},{192,224},{224,1... | collective-permute-start | bytes 9437192 | tf_op jit(solution)/shard_map/ppermute | solution.py:64
  28.8 8.2 %collective-permute-start.4 = (bf16[8,3,6144]{2,1,0:T(4,128)(2,1)S(1)}, bf16[8,3,6144]{2,1,0:T(4,128)(2,1)S(1)}, u32[]{:S(2)}, u32[]{:S(2)}) collective-permute-start(bf16[8,3,6144]{2,1,0:T(4,128)(2,1)S(1)} %all_to_all.15.refs_0_), channel_id=1, source_target_pairs={{0,8},{1,9},{2,10},{3,11},{4,5},{5,6},{6,7},{7,4},{8,16},{9,17},{1... | collective-permute-start | bytes 884744 | tf_op jit(solution)/shard_map/ppermute | solution.py:48
  30.1 7.0 %collective-permute-start.5 = (bf16[8,3,6144]{2,1,0:T(4,128)(2,1)S(1)}, bf16[8,3,6144]{2,1,0:T(4,128)(2,1)S(1)}, u32[]{:S(2)}, u32[]{:S(2)}) collective-permute-start(bf16[8,3,6144]{2,1,0:T(4,128)(2,1)S(1)} %all_to_all.15.refs_0_), channel_id=1, source_target_pairs={{0,24},{1,25},{2,26},{3,27},{4,7},{5,4},{6,5},{7,6},{8,0},{9,1},{1... | collective-permute-start | bytes 884744 | tf_op jit(solution)/shard_map/ppermute | solution.py:48
  31.5 10.8 %collective-permute-start.6 = (bf16[8,3,6144]{2,1,0:T(4,128)(2,1)S(1)}, bf16[8,3,6144]{2,1,0:T(4,128)(2,1)S(1)}, u32[]{:S(2)}, u32[]{:S(2)}) collective-permute-start(bf16[8,3,6144]{2,1,0:T(4,128)(2,1)S(1)} %all_to_all.15.refs_0_), channel_id=1, source_target_pairs={{0,16},{1,17},{2,18},{3,19},{4,6},{5,7},{6,4},{7,5},{8,24},{9,25},... | collective-permute-start | bytes 884744 | tf_op jit(solution)/shard_map/ppermute | solution.py:48
  43.0 16.6 %collective-permute-start.7 = (bf16[96,6144]{1,0:T(8,128)(2,1)S(1)}, bf16[96,6144]{1,0:T(8,128)(2,1)S(1)}, u32[]{:S(2)}, u32[]{:S(2)}) collective-permute-start(bf16[96,6144]{1,0:T(8,128)(2,1)S(1)} %shard_map.132.refs_0_), channel_id=1, source_target_pairs={{0,1},{1,2},{2,3},{3,0},{4,12},{5,13},{6,14},{7,15},{8,9},{9,10},{... | collective-permute-start | bytes 3538952 | tf_op jit(solution)/shard_map/ppermute | solution.py:48
  44.0 15.8 %collective-permute-start.8 = (bf16[96,6144]{1,0:T(8,128)(2,1)S(1)}, bf16[96,6144]{1,0:T(8,128)(2,1)S(1)}, u32[]{:S(2)}, u32[]{:S(2)}) collective-permute-start(bf16[96,6144]{1,0:T(8,128)(2,1)S(1)} %shard_map.132.refs_0_), channel_id=1, source_target_pairs={{0,3},{1,0},{2,1},{3,2},{4,28},{5,29},{6,30},{7,31},{8,11},{9,8},{... | collective-permute-start | bytes 3538952 | tf_op jit(solution)/shard_map/ppermute | solution.py:48
  59.7 10.3 %collective-permute-start.9 = (bf16[48,6144]{1,0:T(8,128)(2,1)S(1)}, bf16[48,6144]{1,0:T(8,128)(2,1)S(1)}, u32[]{:S(2)}, u32[]{:S(2)}) collective-permute-start(bf16[48,6144]{1,0:T(8,128)(2,1)S(1)} %slice.8), channel_id=1, source_target_pairs={{0,1},{1,2},{2,3},{3,0},{4,12},{5,13},{6,14},{7,15},{8,9},{9,10},{... | collective-permute-start | bytes 1769480 | tf_op jit(solution)/shard_map/ppermute | solution.py:48
  59.9 17.6 %copy-start = (bf16[1,256,6144]{2,1,0:T(8,128)(2,1)S(1)}, bf16[1,256,6144]{2,1,0:T(8,128)(2,1)}, u32[]{:S(2)}) copy-start(bf16[1,256,6144]{2,1,0:T(8,128)(2,1)} %param.18) | copy-start | bytes 9437188
  59.9 10.2 %collective-permute-start.10 = (bf16[48,6144]{1,0:T(8,128)(2,1)S(1)}, bf16[48,6144]{1,0:T(8,128)(2,1)S(1)}, u32[]{:S(2)}, u32[]{:S(2)}) collective-permute-start(bf16[48,6144]{1,0:T(8,128)(2,1)S(1)} %slice.9), channel_id=1, source_target_pairs={{0,3},{1,0},{2,1},{3,2},{4,28},{5,29},{6,30},{7,31},{8,11},{9,8},{... | collective-permute-start | bytes 1769480 | tf_op jit(solution)/shard_map/ppermute | solution.py:48
  82.1 26.7 %collective-permute-start.11 = (bf16[48,6144]{1,0:T(8,128)(2,1)S(1)}, bf16[48,6144]{1,0:T(8,128)(2,1)S(1)}, u32[]{:S(2)}, u32[]{:S(2)}) collective-permute-start(bf16[48,6144]{1,0:T(8,128)(2,1)S(1)} %get-tuple-element.25), channel_id=1, source_target_pairs={{0,3},{1,0},{2,1},{3,2},{4,28},{5,29},{6,30},{7,31},{8,11},{9,8},{... | collective-permute-start | bytes 1769480 | tf_op jit(solution)/shard_map/ppermute | solution.py:48
  85.0 23.9 %collective-permute-start.12 = (bf16[48,6144]{1,0:T(8,128)(2,1)S(1)}, bf16[48,6144]{1,0:T(8,128)(2,1)S(1)}, u32[]{:S(2)}, u32[]{:S(2)}) collective-permute-start(bf16[48,6144]{1,0:T(8,128)(2,1)S(1)} %get-tuple-element.26), channel_id=1, source_target_pairs={{0,1},{1,2},{2,3},{3,0},{4,12},{5,13},{6,14},{7,15},{8,9},{9,10},{... | collective-permute-start | bytes 1769480 | tf_op jit(solution)/shard_map/ppermute | solution.py:48
  96.5 96.5 %collective-permute-start.25 = (bf16[256,6144]{1,0:T(8,128)(2,1)}, bf16[256,6144]{1,0:T(8,128)(2,1)}, u32[]{:S(2)}, u32[]{:S(2)}) collective-permute-start(bf16[256,6144]{1,0:T(8,128)(2,1)} %collective-permute-done.24.t2), channel_id=1, source_target_pairs={{0,4},{4,0},{8,12},{12,8},{16,20},{20,16},{24,28},{28,24},{1,5},{5... | collective-permute-start | bytes 9437192 | tf_op jit(solution)/shard_map/ppermute | solution.py:60
  114.8 46.9 %copy-start.4 = (bf16[1,8,6144]{2,1,0:T(8,128)(2,1)S(1)}, bf16[1,8,6144]{2,1,0:T(8,128)(2,1)}, u32[]{:S(2)}) copy-start(bf16[1,8,6144]{2,1,0:T(8,128)(2,1)} %param.12) | copy-start | bytes 294916
  114.8 46.9 %copy-start.6 = (f32[6144]{0:T(1024)S(1)}, f32[6144]{0:T(1024)}, u32[]{:S(2)}) copy-start(f32[6144]{0:T(1024)} %param.14) | copy-start | bytes 73732
  114.8 15.7 %collective-permute-start.13 = (bf16[96,6144]{1,0:T(8,128)(2,1)S(1)}, bf16[96,6144]{1,0:T(8,128)(2,1)S(1)}, u32[]{:S(2)}, u32[]{:S(2)}) collective-permute-start(bf16[96,6144]{1,0:T(8,128)(2,1)S(1)} %get-tuple-element.28), channel_id=1, source_target_pairs={{0,3},{1,0},{2,1},{3,2},{4,28},{5,29},{6,30},{7,31},{8,11},{9,8},{... | collective-permute-start | bytes 3538952 | tf_op jit(solution)/shard_map/ppermute | solution.py:48
  117.4 16.6 %collective-permute-start.14 = (bf16[96,6144]{1,0:T(8,128)(2,1)S(1)}, bf16[96,6144]{1,0:T(8,128)(2,1)S(1)}, u32[]{:S(2)}, u32[]{:S(2)}) collective-permute-start(bf16[96,6144]{1,0:T(8,128)(2,1)S(1)} %get-tuple-element.29), channel_id=1, source_target_pairs={{0,1},{1,2},{2,3},{3,0},{4,12},{5,13},{6,14},{7,15},{8,9},{9,10},{... | collective-permute-start | bytes 3538952 | tf_op jit(solution)/shard_map/ppermute | solution.py:48
  133.9 59.1 %copy-start.2 = (bf16[256,6144]{1,0:T(8,128)(2,1)S(1)}, bf16[256,6144]{1,0:T(8,128)(2,1)}, u32[]{:S(2)}) copy-start(bf16[256,6144]{1,0:T(8,128)(2,1)} %t0.1) | copy-start | bytes 9437188
  133.9 59.1 %copy-start.8 = (s32[1,512]{1,0:T(1,128)S(1)}, s32[1,512]{1,0:T(1,128)}, u32[]{:S(2)}) copy-start(s32[1,512]{1,0:T(1,128)} %targets_ref.1) | copy-start | bytes 6148
  134.8 6.2 %collective-permute-start.15 = (bf16[24,6144]{1,0:T(8,128)(2,1)S(1)}, bf16[24,6144]{1,0:T(8,128)(2,1)S(1)}, u32[]{:S(2)}, u32[]{:S(2)}) collective-permute-start(bf16[24,6144]{1,0:T(8,128)(2,1)S(1)} %get-tuple-element.31), channel_id=1, source_target_pairs={{0,24},{1,25},{2,26},{3,27},{4,7},{5,4},{6,5},{7,6},{8,0},{9,1},{1... | collective-permute-start | bytes 884744 | tf_op jit(solution)/shard_map/ppermute | solution.py:48
  137.3 10.2 %collective-permute-start.16 = (bf16[24,6144]{1,0:T(8,128)(2,1)S(1)}, bf16[24,6144]{1,0:T(8,128)(2,1)S(1)}, u32[]{:S(2)}, u32[]{:S(2)}) collective-permute-start(bf16[24,6144]{1,0:T(8,128)(2,1)S(1)} %get-tuple-element.32), channel_id=1, source_target_pairs={{0,8},{1,9},{2,10},{3,11},{4,5},{5,6},{6,7},{7,4},{8,16},{9,17},{1... | collective-permute-start | bytes 884744 | tf_op jit(solution)/shard_map/ppermute | solution.py:48
  137.3 10.2 %collective-permute-start.17 = (bf16[24,6144]{1,0:T(8,128)(2,1)S(1)}, bf16[24,6144]{1,0:T(8,128)(2,1)S(1)}, u32[]{:S(2)}, u32[]{:S(2)}) collective-permute-start(bf16[24,6144]{1,0:T(8,128)(2,1)S(1)} %get-tuple-element.33), channel_id=1, source_target_pairs={{0,16},{1,17},{2,18},{3,19},{4,6},{5,7},{6,4},{7,5},{8,24},{9,25},... | collective-permute-start | bytes 884744 | tf_op jit(solution)/shard_map/ppermute | solution.py:48
  162.7 4.8 %collective-permute-start.18 = (bf16[8,6144]{1,0:T(8,128)(2,1)S(1)}, bf16[8,6144]{1,0:T(8,128)(2,1)S(1)}, u32[]{:S(2)}, u32[]{:S(2)}) collective-permute-start(bf16[8,6144]{1,0:T(8,128)(2,1)S(1)} %shard_map.139.refs_0_), channel_id=1, source_target_pairs={{0,64},{4,12},{8,72},{12,20},{16,80},{20,28},{24,88},{28,4},{32,96... | collective-permute-start | bytes 294920 | tf_op jit(solution)/shard_map/ppermute | solution.py:56
  162.8 5.3 %collective-permute-start.19 = (bf16[8,6144]{1,0:T(8,128)(2,1)S(1)}, bf16[8,6144]{1,0:T(8,128)(2,1)S(1)}, u32[]{:S(2)}, u32[]{:S(2)}) collective-permute-start(bf16[8,6144]{1,0:T(8,128)(2,1)S(1)} %shard_map.139.refs_0_), channel_id=1, source_target_pairs={{0,192},{4,28},{8,200},{12,4},{16,208},{20,12},{24,216},{28,20},{3... | collective-permute-start | bytes 294920 | tf_op jit(solution)/shard_map/ppermute | solution.py:56
  165.5 5.0 %collective-permute-start.20 = (bf16[8,6144]{1,0:T(8,128)(2,1)S(1)}, bf16[8,6144]{1,0:T(8,128)(2,1)S(1)}, u32[]{:S(2)}, u32[]{:S(2)}) collective-permute-start(bf16[8,6144]{1,0:T(8,128)(2,1)S(1)} %shard_map.139.refs_0_), channel_id=1, source_target_pairs={{0,128},{4,20},{8,136},{12,28},{16,144},{20,4},{24,152},{28,12},{3... | collective-permute-start | bytes 294920 | tf_op jit(solution)/shard_map/ppermute | solution.py:56
  170.5 13.3 %collective-permute-start.21 = (bf16[32,6144]{1,0:T(8,128)(2,1)S(1)}, bf16[32,6144]{1,0:T(8,128)(2,1)}, u32[]{:S(2)}, u32[]{:S(2)}) collective-permute-start(bf16[32,6144]{1,0:T(8,128)(2,1)S(1)} %shard_map.140.r0), channel_id=1, source_target_pairs={{0,8},{4,68},{8,16},{12,76},{16,24},{20,84},{24,0},{28,92},{32,40}... | collective-permute-start | bytes 1179656 | tf_op jit(solution)/shard_map/ppermute | solution.py:56
  170.6 22.4 %collective-permute-start.22 = (bf16[32,6144]{1,0:T(8,128)(2,1)S(1)}, bf16[32,6144]{1,0:T(8,128)(2,1)}, u32[]{:S(2)}, u32[]{:S(2)}) collective-permute-start(bf16[32,6144]{1,0:T(8,128)(2,1)S(1)} %shard_map.140.r0), channel_id=1, source_target_pairs={{0,24},{4,196},{8,0},{12,204},{16,8},{20,212},{24,16},{28,220},{32... | collective-permute-start | bytes 1179656 | tf_op jit(solution)/shard_map/ppermute | solution.py:56
  174.2 18.8 %collective-permute-start.23 = (bf16[32,6144]{1,0:T(8,128)(2,1)S(1)}, bf16[32,6144]{1,0:T(8,128)(2,1)}, u32[]{:S(2)}, u32[]{:S(2)}) collective-permute-start(bf16[32,6144]{1,0:T(8,128)(2,1)S(1)} %shard_map.140.r0), channel_id=1, source_target_pairs={{0,16},{4,132},{8,24},{12,140},{16,0},{20,148},{24,8},{28,156},{32... | collective-permute-start | bytes 1179656 | tf_op jit(solution)/shard_map/ppermute | solution.py:56
  175.5 49.2 %copy-start.9 = (s32[1,16]{1,0:T(1,128)S(1)}, s32[1,16]{1,0:T(1,128)}, u32[]{:S(2)}) copy-start(s32[1,16]{1,0:T(1,128)} %lengths_ref.1) | copy-start | bytes 196
  175.5 49.2 %copy-start.10 = (s32[1,16]{1,0:T(1,128)S(1)}, s32[1,16]{1,0:T(1,128)}, u32[]{:S(2)}) copy-start(s32[1,16]{1,0:T(1,128)} %questions_ref.1) | copy-start | bytes 196

commit v3 on v2

--- a/solution.py
+++ b/solution.py
@@ -14,7 +14,7 @@
 
 NZ, NX, NC, NY = 8, 4, 2, 4
 SLOTS = 3
-VMEM_LIMIT = 48 * 2**20
+VMEM_LIMIT = 14 * 2**20
 
 
 def two_axis_perm(sizes, coords, axis_of, shift):
@@ -493,7 +493,6 @@
         arrived, other_gate, other_up, other_down, other_head, lm_head
     )
     pair_head = swap_planes(own_head)
-    pair_other = swap_cores(pair_head)
 
     def first(block, shift):
         return plane_shift(block, False, shift)
@@ -511,6 +510,7 @@
     weights = (own_gate, own_up, other_gate, other_up)
     downs = (own_down, other_down)
     near_hidden = expand([line, from_before, from_after], weights)
+    near_hidden, far_before, far_after = tied(near_hidden, far_before, far_after)
     far_hidden = expand([far_before, far_after], weights)
 
     to_before, to_after = down_call(far_kernel, far_hidden, downs, (), (half, half))
@@ -520,6 +520,8 @@
         near_kernel, near_hidden, downs, (got_before, got_after), (rows, rows, rows)
     )
     pieces = line_sum([own_part, second(before_part, -1), second(after_part, 1)])
+    pair_head, *pieces = tied(pair_head, *pieces)
+    pair_other = swap_cores(pair_head)
     outgoing = expert_sum(
         [pieces[0], first(pieces[1], -1), first(pieces[2], 1), first(pieces[3], 2)]
     )

time: 227 us -> 215 us (0.947)
  waiting for transfers between devices: 89.6 us -> 75.5 us
  Pallas kernels: 41.8 us -> 35.9 us
  blocking collectives: 56 us -> 59.9 us
    ppermute x1, waiting for transfers between devices: 11.5 us -> 0.01 us  [swap_planes(): return lax.ppermute(array, 'expert', [(z, z ^ 1) for z in range(NZ)])]
    pallas_call x2, Pallas kernels: 10.6 us -> 6.09 us  [down_call(): pl.pallas_call(kernel, grid=(width // tile,), in_specs=[pl.BlockSpec(hidd...]
    all_to_all x1, blocking collectives: 22.3 us -> 26.4 us  [on_device(): gathered = lax.all_to_all(stats, ('expert', 'vocab'), 0, 0, tiled=True)]
    ppermute x14, starting transfers between devices: 19.5 us -> 15.5 us  [plane_shift(): return lax.ppermute(array, ('vocab', 'batch'), perm)]
    ppermute x5, starting transfers between devices: 6.81 us -> 10.2 us  [swap_cores(): return lax.ppermute(array, 'vocab', [(v, v ^ 1) for v in range(NX * NC)])]
    ppermute x6, starting transfers between devices: 7.64 us -> 10.6 us  [head_shift(): return lax.ppermute(array, ('expert', 'vocab'), perm)]
    unnamed x22 -> x26, local copies, waits for them, and re-layouts: 2.56 us -> 4.6 us
  transfers between devices with their start and end apart: 26 -> 26, of which waited for: 15 -> 15; matrix products, arithmetic and copies ran while one was open for 0% -> 0% of each run, Pallas kernels for 14% -> 11%
where the time goes in v3:
time: 215 us; the launch traced here: 214 us
  waiting for transfers between devices  75.5 us (35%)
  blocking collectives  59.9 us (28%)
  starting transfers between devices  36.6 us (17%)
  Pallas kernels  35.9 us (17%)
  local copies, waits for them, and re-layouts  5.43 us (3%)
    ppermute x14, waiting for transfers between devices, plane_shift(): return lax.ppermute(array, ('vocab', 'batch'), perm)  54.9 us
    all_to_all x1, blocking collectives, on_device(): gathered = lax.all_to_all(stats, ('expert', 'vocab'), 0, 0, tiled=True)  26.4 us
    ppermute x6, waiting for transfers between devices, head_shift(): return lax.ppermute(array, ('expert', 'vocab'), perm)  20.5 us
    all_to_all x1, blocking collectives, on_device(): lax.all_to_all(buckets, 'expert', split_axis=0, concat_axis=0, tiled=True)  19.9 us
    ppermute x14, starting transfers between devices, plane_shift(): return lax.ppermute(array, ('vocab', 'batch'), perm)  15.5 us
    pallas_call x2, Pallas kernels, expand(): pl.pallas_call(functools.partial(expand_kernel, count=count), grid=(width...  15.5 us
    all_to_all x1, blocking collectives, on_device(): lax.all_to_all(outgoing, 'expert', split_axis=0, concat_axis=0, tiled=True)  13.6 us
    ppermute x6, starting transfers between devices, head_shift(): return lax.ppermute(array, ('expert', 'vocab'), perm)  10.6 us
  transfers between devices with their start and end apart: 26, of which 15 were waited for; matrix products, arithmetic and copies ran while one was open for 0% of the time, Pallas kernels for 11%

profile of v3, /device:TPU:1, one launch (start us, length us, event | category | flops | bytes accessed | tf_op | source)
XLA Modules:
  0.0 214.2 jit_solution(5813590231971444994)
XLA Ops:
  0.6 3.3 %collective-permute-start = (bf16[6144,256]{1,0:T(8,128)(2,1)}, bf16[6144,256]{1,0:T(8,128)(2,1)}, u32[]{:S(2)}, u32[]{:S(2)}) collective-permute-start(bf16[6144,256]{1,0:T(8,128)(2,1)} %bitcast.14), channel_id=1, source_target_pairs={{0,4},{4,0},{8,12},{12,8},{16,20},{20,16},{24,28},{28,24},{1,5},{5... | collective-permute-start | bytes 9437192 | tf_op jit(solution)/shard_map/ppermute | solution.py:60
  4.6 0.8 copy.14.ids_ref
  5.3 1.0 copy-done.5
  6.4 0.9 copy-done.7
  7.3 0.7 copy-done.9
  8.0 0.6 shard_map.131
  8.6 19.9 %all_to_all.15.refs_0_ = bf16[8,3,6144]{2,1,0:T(4,128)(2,1)S(1)} all-to-all(bf16[8,3,6144]{2,1,0:T(4,128)(2,1)S(1)} %get-tuple-element.28), channel_id=1, replica_groups=mesh['expert'=8,'vocab'=8,'batch'=4] {'expert'}, dimensions={0} | all-to-all | bytes 589824 | tf_op jit(solution)/shard_map/all_to_all | solution.py:491
  28.6 1.4 collective-permute-start.5
  30.0 1.5 collective-permute-start.6
  31.5 1.6 collective-permute-start.7
  33.0 3.8 %collective-permute-done.5.refs_1_ = bf16[8,3,6144]{2,1,0:T(4,128)(2,1)S(1)} collective-permute-done((bf16[8,3,6144]{2,1,0:T(4,128)(2,1)S(1)}, bf16[8,3,6144]{2,1,0:T(4,128)(2,1)S(1)}, u32[]{:S(2)}, u32[]{:S(2)}) %collective-permute-start.5) | collective-permute-done | bytes 294944 | tf_op jit(solution)/shard_map/ppermute | solution.py:48
  36.9 3.6 %collective-permute-done.6.refs_2_ = bf16[8,3,6144]{2,1,0:T(4,128)(2,1)S(1)} collective-permute-done((bf16[8,3,6144]{2,1,0:T(4,128)(2,1)S(1)}, bf16[8,3,6144]{2,1,0:T(4,128)(2,1)S(1)}, u32[]{:S(2)}, u32[]{:S(2)}) %collective-permute-start.6) | collective-permute-done | bytes 294944 | tf_op jit(solution)/shard_map/ppermute | solution.py:48
  40.4 1.8 collective-permute-done.7.refs_3_
  42.2 0.6 shard_map.132.refs_0_
  42.9 1.0 collective-permute-start.8
  43.9 1.8 collective-permute-start.9
  45.9 13.6 %collective-permute-done.8.refs_1_ = bf16[96,6144]{1,0:T(8,128)(2,1)S(1)} collective-permute-done((bf16[96,6144]{1,0:T(8,128)(2,1)S(1)}, bf16[96,6144]{1,0:T(8,128)(2,1)S(1)}, u32[]{:S(2)}, u32[]{:S(2)}) %collective-permute-start.8) | collective-permute-done | bytes 1179680 | tf_op jit(solution)/shard_map/ppermute | solution.py:48
  59.7 2.7 %collective-permute-start.11 = (bf16[48,6144]{1,0:T(8,128)(2,1)S(1)}, bf16[48,6144]{1,0:T(8,128)(2,1)S(1)}, u32[]{:S(2)}, u32[]{:S(2)}) collective-permute-start(bf16[48,6144]{1,0:T(8,128)(2,1)S(1)} %slice.9), channel_id=1, source_target_pairs={{0,3},{1,0},{2,1},{3,2},{4,28},{5,29},{6,30},{7,31},{8,11},{9,8},{... | collective-permute-start | bytes 1769480 | tf_op jit(solution)/shard_map/ppermute | solution.py:48
  62.4 1.9 copy-done.2
  64.3 8.5 %shard_map.133.hidden_ref = bf16[288,512]{1,0:T(8,128)(2,1)S(1)} custom-call(bf16[96,6144]{1,0:T(8,128)(2,1)S(1)} %shard_map.132.refs_0_, bf16[96,6144]{1,0:T(8,128)(2,1)S(1)} %collective-permute-done.8.refs_1_, bf16[96,6144]{1,0:T(8,128)(2,1)S(1)} %collective-permute-done.9.refs_2_, bf16[6144,256]{1,0:T(8,128)(2,1)S(1)} %bitcast.15, ...), custom_call_target="tpu_custom_call" | custom-call | flops 3623878656 | bytes 12582912 | tf_op jit(solution)/shard_map/pallas_call | solution.py:201
  72.9 7.0 %shard_map.134.hidden_ref = bf16[96,512]{1,0:T(8,128)(2,1)S(1)} custom-call(bf16[48,6144]{1,0:T(8,128)(2,1)S(1)} %collective-permute-done.10.refs_0_, bf16[48,6144]{1,0:T(8,128)(2,1)S(1)} %collective-permute-done.11.refs_1_, bf16[6144,256]{1,0:T(8,128)(2,1)S(1)} %bitcast.16, bf16[6144,256]{1,0:T(8,128)(2,1)S(1)} %bitcast.19, ...), custom_call_target="tpu_custom_call" | custom-call | flops 1207959552 | bytes 12582912 | tf_op jit(solution)/shard_map/pallas_call | solution.py:201
  79.9 2.4 %shard_map.135 = (bf16[48,6144]{1,0:T(8,128)(2,1)S(1)}, bf16[48,6144]{1,0:T(8,128)(2,1)S(1)}) custom-call(bf16[96,512]{1,0:T(8,128)(2,1)S(1)} %shard_map.134.hidden_ref, bf16[256,6144]{1,0:T(8,128)(2,1)S(1)} %bitcast.12, bf16[256,6144]{1,0:T(8,128)(2,1)S(1)} %collective-permute-done.2.down_b), custom_call_target="tpu_custom_call" | custom-call | flops 603979776 | bytes 6291456 | tf_op jit(solution)/shard_map/pallas_call | solution.py:242
  82.5 1.3 collective-permute-start.13
  83.8 7.7 %collective-permute-done.12.got_before = bf16[48,6144]{1,0:T(8,128)(2,1)S(1)} collective-permute-done((bf16[48,6144]{1,0:T(8,128)(2,1)S(1)}, bf16[48,6144]{1,0:T(8,128)(2,1)S(1)}, u32[]{:S(2)}, u32[]{:S(2)}) %collective-permute-start.12) | collective-permute-done | bytes 589856 | tf_op jit(solution)/shard_map/ppermute | solution.py:48
  91.5 1.3 collective-permute-done.13.got_after
  92.8 3.7 %shard_map.136 = (bf16[96,6144]{1,0:T(8,128)(2,1)S(1)}, bf16[96,6144]{1,0:T(8,128)(2,1)S(1)}, bf16[96,6144]{1,0:T(8,128)(2,1)S(1)}) custom-call(bf16[288,512]{1,0:T(8,128)(2,1)S(1)} %shard_map.133.hidden_ref, bf16[256,6144]{1,0:T(8,128)(2,1)S(1)} %bitcast.13, bf16[256,6144]{1,0:T(8,128)(2,1)S(1)} %collective-permute-done.2.down_b, ...), custom_call_target="tpu_custom_call" | custom-call | flops 1811939328 | bytes 6291456 | tf_op jit(solution)/shard_map/pallas_call | solution.py:242
  96.8 1.5 collective-permute-start.15
  98.2 14.0 %collective-permute-done.14.before_ref = bf16[96,6144]{1,0:T(8,128)(2,1)S(1)} collective-permute-done((bf16[96,6144]{1,0:T(8,128)(2,1)S(1)}, bf16[96,6144]{1,0:T(8,128)(2,1)S(1)}, u32[]{:S(2)}, u32[]{:S(2)}) %collective-permute-start.14) | collective-permute-done | bytes 1179680 | tf_op jit(solution)/shard_map/ppermute | solution.py:48
  112.2 1.2 collective-permute-done.15.after_ref
  113.4 0.9 shard_map.137
  114.3 6.2 %collective-permute-start.25 = (bf16[256,6144]{1,0:T(8,128)(2,1)}, bf16[256,6144]{1,0:T(8,128)(2,1)}, u32[]{:S(2)}, u32[]{:S(2)}) collective-permute-start(bf16[256,6144]{1,0:T(8,128)(2,1)} %collective-permute-done.4.t2), channel_id=1, source_target_pairs={{0,4},{4,0},{8,12},{12,8},{16,20},{20,16},{24,28},{28,24},{1,5},{5... | collective-permute-start | bytes 9437192 | tf_op jit(solution)/shard_map/ppermute | solution.py:60
  120.5 1.5 collective-permute-start.17
  122.0 0.8 collective-permute-start.18
  122.7 3.6 %collective-permute-done.16.b = bf16[24,6144]{1,0:T(8,128)(2,1)S(1)} collective-permute-done((bf16[24,6144]{1,0:T(8,128)(2,1)S(1)}, bf16[24,6144]{1,0:T(8,128)(2,1)S(1)}, u32[]{:S(2)}, u32[]{:S(2)}) %collective-permute-start.16) | collective-permute-done | bytes 294944 | tf_op jit(solution)/shard_map/ppermute | solution.py:48
  126.4 4.4 %collective-permute-done.17.c = bf16[24,6144]{1,0:T(8,128)(2,1)S(1)} collective-permute-done((bf16[24,6144]{1,0:T(8,128)(2,1)S(1)}, bf16[24,6144]{1,0:T(8,128)(2,1)S(1)}, u32[]{:S(2)}, u32[]{:S(2)}) %collective-permute-start.17) | collective-permute-done | bytes 294944 | tf_op jit(solution)/shard_map/ppermute | solution.py:48
  131.1 13.6 %all_to_all.16.rows_ref = bf16[8,3,6144]{2,1,0:T(4,128)(2,1)S(1)} all-to-all(bf16[8,3,6144]{2,1,0:T(4,128)(2,1)S(1)} %shard_map.138), channel_id=1, replica_groups=mesh['expert'=8,'vocab'=8,'batch'=4] {'expert'}, dimensions={0} | all-to-all | bytes 589824 | tf_op jit(solution)/shard_map/all_to_all | solution.py:529
  144.7 1.0 shard_map.139.refs_0_
  145.7 4.9 %collective-permute-start.19 = (bf16[8,6144]{1,0:T(8,128)(2,1)S(1)}, bf16[8,6144]{1,0:T(8,128)(2,1)S(1)}, u32[]{:S(2)}, u32[]{:S(2)}) collective-permute-start(bf16[8,6144]{1,0:T(8,128)(2,1)S(1)} %shard_map.139.refs_0_), channel_id=1, source_target_pairs={{0,64},{4,12},{8,72},{12,20},{16,80},{20,28},{24,88},{28,4},{32,96... | collective-permute-start | bytes 294920 | tf_op jit(solution)/shard_map/ppermute | solution.py:56
  150.6 1.9 collective-permute-start.21
  152.5 1.6 collective-permute-done.20.refs_2_
  154.1 1.8 collective-permute-done.21.refs_3_
  156.1 3.6 %collective-permute-start.23 = (bf16[32,6144]{1,0:T(8,128)(2,1)S(1)}, bf16[32,6144]{1,0:T(8,128)(2,1)}, u32[]{:S(2)}, u32[]{:S(2)}) collective-permute-start(bf16[32,6144]{1,0:T(8,128)(2,1)S(1)} %shard_map.140.r0), channel_id=1, source_target_pairs={{0,24},{4,196},{8,0},{12,204},{16,8},{20,212},{24,16},{28,220},{32... | collective-permute-start | bytes 1179656 | tf_op jit(solution)/shard_map/ppermute | solution.py:56
  159.9 7.7 %collective-permute-done.22.r1 = bf16[32,6144]{1,0:T(8,128)(2,1)} collective-permute-done((bf16[32,6144]{1,0:T(8,128)(2,1)S(1)}, bf16[32,6144]{1,0:T(8,128)(2,1)}, u32[]{:S(2)}, u32[]{:S(2)}) %collective-permute-start.22) | collective-permute-done | bytes 393248 | tf_op jit(solution)/shard_map/ppermute | solution.py:56
  167.6 8.6 %collective-permute-done.23.r2 = bf16[32,6144]{1,0:T(8,128)(2,1)} collective-permute-done((bf16[32,6144]{1,0:T(8,128)(2,1)S(1)}, bf16[32,6144]{1,0:T(8,128)(2,1)}, u32[]{:S(2)}, u32[]{:S(2)}) %collective-permute-start.23) | collective-permute-done | bytes 393248 | tf_op jit(solution)/shard_map/ppermute | solution.py:56
  176.2 0.8 collective-permute-done.24.r3
  177.0 9.4 %shard_map.141 = f32[64,4,128]{2,1,0:T(4,128)S(1)} custom-call(s32[3]{0:T(128)S(1)} %pad_add_fusion.place_ref, s32[1,512]{1,0:T(1,128)S(1)} %copy-done.10, bf16[32,6144]{1,0:T(8,128)(2,1)S(1)} %shard_map.140.r0, bf16[32,6144]{1,0:T(8,128)(2,1)} %collective-permute-done.22.r1, bf16[32,6144]{1,0:T(8,128)(2,1)} %collective-permute-done.23.r2, ...), custom_call_target="tpu_custom_call" | custom-call | flops 1610612736 | bytes 12582912 | tf_op jit(solution)/shard_map/pallas_call | solution.py:376
  186.4 26.4 %all_to_all.17.stats_ref = f32[64,4,128]{2,1,0:T(4,128)S(1)} all-to-all(f32[64,4,128]{2,1,0:T(4,128)S(1)} %shard_map.141), channel_id=1, replica_groups=mesh['expert'=8,'vocab'=8,'batch'=4] {'expert','vocab'}, dimensions={0} | all-to-all | bytes 262144 | tf_op jit(solution)/shard_map/all_to_all | solution.py:535
  212.8 1.4 shard_map.142
  (49 shorter events, 2.4 us)
Async XLA Ops:
  0.6 27.9 %collective-permute-start = (bf16[6144,256]{1,0:T(8,128)(2,1)}, bf16[6144,256]{1,0:T(8,128)(2,1)}, u32[]{:S(2)}, u32[]{:S(2)}) collective-permute-start(bf16[6144,256]{1,0:T(8,128)(2,1)} %bitcast.14), channel_id=1, source_target_pairs={{0,4},{4,0},{8,12},{12,8},{16,20},{20,16},{24,28},{28,24},{1,5},{5... | collective-permute-start | bytes 9437192 | tf_op jit(solution)/shard_map/ppermute | solution.py:60
  4.0 24.6 %collective-permute-start.1 = (bf16[6144,256]{1,0:T(8,128)(2,1)}, bf16[6144,256]{1,0:T(8,128)(2,1)}, u32[]{:S(2)}, u32[]{:S(2)}) collective-permute-start(bf16[6144,256]{1,0:T(8,128)(2,1)} %bitcast.17), channel_id=1, source_target_pairs={{0,4},{4,0},{8,12},{12,8},{16,20},{20,16},{24,28},{28,24},{1,5},{5... | collective-permute-start | bytes 9437192 | tf_op jit(solution)/shard_map/ppermute | solution.py:60
  4.1 24.5 %collective-permute-start.2 = (bf16[256,6144]{1,0:T(8,128)(2,1)}, bf16[256,6144]{1,0:T(8,128)(2,1)S(1)}, u32[]{:S(2)}, u32[]{:S(2)}) collective-permute-start(bf16[256,6144]{1,0:T(8,128)(2,1)} %bitcast.11), channel_id=1, source_target_pairs={{0,4},{4,0},{8,12},{12,8},{16,20},{20,16},{24,28},{28,24},{1,5},{5... | collective-permute-start | bytes 9437192 | tf_op jit(solution)/shard_map/ppermute | solution.py:60
  4.5 24.1 %collective-permute-start.3 = (bf16[256,6144]{1,0:T(8,128)(2,1)}, bf16[256,6144]{1,0:T(8,128)(2,1)}, u32[]{:S(2)}, u32[]{:S(2)}) collective-permute-start(bf16[256,6144]{1,0:T(8,128)(2,1)} %t0.1), channel_id=1, source_target_pairs={{0,4},{4,0},{8,12},{12,8},{16,20},{20,16},{24,28},{28,24},{1,5},{5... | collective-permute-start | bytes 9437192 | tf_op jit(solution)/shard_map/ppermute | solution.py:60
  5.3 57.1 %copy-start.1 = (bf16[1,6144,256]{2,1,0:T(8,128)(2,1)S(1)}, bf16[1,6144,256]{2,1,0:T(8,128)(2,1)}, u32[]{:S(2)}) copy-start(bf16[1,6144,256]{2,1,0:T(8,128)(2,1)} %param.16) | copy-start | bytes 9437188
  5.3 1.0 copy-start.5
  6.4 0.9 copy-start.7
  7.3 0.7 copy-start.9
  28.6 8.3 %collective-permute-start.5 = (bf16[8,3,6144]{2,1,0:T(4,128)(2,1)S(1)}, bf16[8,3,6144]{2,1,0:T(4,128)(2,1)S(1)}, u32[]{:S(2)}, u32[]{:S(2)}) collective-permute-start(bf16[8,3,6144]{2,1,0:T(4,128)(2,1)S(1)} %all_to_all.15.refs_0_), channel_id=1, source_target_pairs={{0,8},{1,9},{2,10},{3,11},{4,5},{5,6},{6,7},{7,4},{8,16},{9,17},{1... | collective-permute-start | bytes 884744 | tf_op jit(solution)/shard_map/ppermute | solution.py:48
  30.0 10.5 %collective-permute-start.6 = (bf16[8,3,6144]{2,1,0:T(4,128)(2,1)S(1)}, bf16[8,3,6144]{2,1,0:T(4,128)(2,1)S(1)}, u32[]{:S(2)}, u32[]{:S(2)}) collective-permute-start(bf16[8,3,6144]{2,1,0:T(4,128)(2,1)S(1)} %all_to_all.15.refs_0_), channel_id=1, source_target_pairs={{0,24},{1,25},{2,26},{3,27},{4,7},{5,4},{6,5},{7,6},{8,0},{9,1},{1... | collective-permute-start | bytes 884744 | tf_op jit(solution)/shard_map/ppermute | solution.py:48
  31.5 10.8 %collective-permute-start.7 = (bf16[8,3,6144]{2,1,0:T(4,128)(2,1)S(1)}, bf16[8,3,6144]{2,1,0:T(4,128)(2,1)S(1)}, u32[]{:S(2)}, u32[]{:S(2)}) collective-permute-start(bf16[8,3,6144]{2,1,0:T(4,128)(2,1)S(1)} %all_to_all.15.refs_0_), channel_id=1, source_target_pairs={{0,16},{1,17},{2,18},{3,19},{4,6},{5,7},{6,4},{7,5},{8,24},{9,25},... | collective-permute-start | bytes 884744 | tf_op jit(solution)/shard_map/ppermute | solution.py:48
  42.9 16.6 %collective-permute-start.8 = (bf16[96,6144]{1,0:T(8,128)(2,1)S(1)}, bf16[96,6144]{1,0:T(8,128)(2,1)S(1)}, u32[]{:S(2)}, u32[]{:S(2)}) collective-permute-start(bf16[96,6144]{1,0:T(8,128)(2,1)S(1)} %shard_map.132.refs_0_), channel_id=1, source_target_pairs={{0,1},{1,2},{2,3},{3,0},{4,12},{5,13},{6,14},{7,15},{8,9},{9,10},{... | collective-permute-start | bytes 3538952 | tf_op jit(solution)/shard_map/ppermute | solution.py:48
  43.9 15.8 %collective-permute-start.9 = (bf16[96,6144]{1,0:T(8,128)(2,1)S(1)}, bf16[96,6144]{1,0:T(8,128)(2,1)S(1)}, u32[]{:S(2)}, u32[]{:S(2)}) collective-permute-start(bf16[96,6144]{1,0:T(8,128)(2,1)S(1)} %shard_map.132.refs_0_), channel_id=1, source_target_pairs={{0,3},{1,0},{2,1},{3,2},{4,28},{5,29},{6,30},{7,31},{8,11},{9,8},{... | collective-permute-start | bytes 3538952 | tf_op jit(solution)/shard_map/ppermute | solution.py:48
  45.6 68.6 %collective-permute-start.4 = (bf16[256,6144]{1,0:T(8,128)(2,1)}, bf16[256,6144]{1,0:T(8,128)(2,1)}, u32[]{:S(2)}, u32[]{:S(2)}) collective-permute-start(bf16[256,6144]{1,0:T(8,128)(2,1)} %t0.1), channel_id=1, source_target_pairs={{0,32},{32,0},{64,96},{96,64},{128,160},{160,128},{192,224},{224,1... | collective-permute-start | bytes 9437192 | tf_op jit(solution)/shard_map/ppermute | solution.py:64
  59.6 13.3 %collective-permute-start.10 = (bf16[48,6144]{1,0:T(8,128)(2,1)S(1)}, bf16[48,6144]{1,0:T(8,128)(2,1)S(1)}, u32[]{:S(2)}, u32[]{:S(2)}) collective-permute-start(bf16[48,6144]{1,0:T(8,128)(2,1)S(1)} %slice.8), channel_id=1, source_target_pairs={{0,1},{1,2},{2,3},{3,0},{4,12},{5,13},{6,14},{7,15},{8,9},{9,10},{... | collective-permute-start | bytes 1769480 | tf_op jit(solution)/shard_map/ppermute | solution.py:48
  59.7 13.2 %collective-permute-start.11 = (bf16[48,6144]{1,0:T(8,128)(2,1)S(1)}, bf16[48,6144]{1,0:T(8,128)(2,1)S(1)}, u32[]{:S(2)}, u32[]{:S(2)}) collective-permute-start(bf16[48,6144]{1,0:T(8,128)(2,1)S(1)} %slice.9), channel_id=1, source_target_pairs={{0,3},{1,0},{2,1},{3,2},{4,28},{5,29},{6,30},{7,31},{8,11},{9,8},{... | collective-permute-start | bytes 1769480 | tf_op jit(solution)/shard_map/ppermute | solution.py:48
  62.4 1.9 copy-start.2
  64.3 8.5 %copy-start.3 = (bf16[1,6144,256]{2,1,0:T(8,128)(2,1)S(1)}, bf16[1,6144,256]{2,1,0:T(8,128)(2,1)}, u32[]{:S(2)}) copy-start(bf16[1,6144,256]{2,1,0:T(8,128)(2,1)} %param.17) | copy-start | bytes 9437188
  72.8 7.0 %copy-start = (bf16[1,256,6144]{2,1,0:T(8,128)(2,1)S(1)}, bf16[1,256,6144]{2,1,0:T(8,128)(2,1)}, u32[]{:S(2)}) copy-start(bf16[1,256,6144]{2,1,0:T(8,128)(2,1)} %param.18) | copy-start | bytes 9437188
  82.3 9.2 %collective-permute-start.12 = (bf16[48,6144]{1,0:T(8,128)(2,1)S(1)}, bf16[48,6144]{1,0:T(8,128)(2,1)S(1)}, u32[]{:S(2)}, u32[]{:S(2)}) collective-permute-start(bf16[48,6144]{1,0:T(8,128)(2,1)S(1)} %get-tuple-element.37), channel_id=1, source_target_pairs={{0,3},{1,0},{2,1},{3,2},{4,28},{5,29},{6,30},{7,31},{8,11},{9,8},{... | collective-permute-start | bytes 1769480 | tf_op jit(solution)/shard_map/ppermute | solution.py:48
  82.5 10.2 %collective-permute-start.13 = (bf16[48,6144]{1,0:T(8,128)(2,1)S(1)}, bf16[48,6144]{1,0:T(8,128)(2,1)S(1)}, u32[]{:S(2)}, u32[]{:S(2)}) collective-permute-start(bf16[48,6144]{1,0:T(8,128)(2,1)S(1)} %get-tuple-element.38), channel_id=1, source_target_pairs={{0,1},{1,2},{2,3},{3,0},{4,12},{5,13},{6,14},{7,15},{8,9},{9,10},{... | collective-permute-start | bytes 1769480 | tf_op jit(solution)/shard_map/ppermute | solution.py:48
  96.5 48.2 %copy-start.6 = (bf16[1,8,6144]{2,1,0:T(8,128)(2,1)S(1)}, bf16[1,8,6144]{2,1,0:T(8,128)(2,1)}, u32[]{:S(2)}) copy-start(bf16[1,8,6144]{2,1,0:T(8,128)(2,1)} %param.12) | copy-start | bytes 294916
  96.5 48.2 %copy-start.8 = (f32[6144]{0:T(1024)S(1)}, f32[6144]{0:T(1024)}, u32[]{:S(2)}) copy-start(f32[6144]{0:T(1024)} %param.14) | copy-start | bytes 73732
  96.5 15.7 %collective-permute-start.14 = (bf16[96,6144]{1,0:T(8,128)(2,1)S(1)}, bf16[96,6144]{1,0:T(8,128)(2,1)S(1)}, u32[]{:S(2)}, u32[]{:S(2)}) collective-permute-start(bf16[96,6144]{1,0:T(8,128)(2,1)S(1)} %get-tuple-element.40), channel_id=1, source_target_pairs={{0,3},{1,0},{2,1},{3,2},{4,28},{5,29},{6,30},{7,31},{8,11},{9,8},{... | collective-permute-start | bytes 3538952 | tf_op jit(solution)/shard_map/ppermute | solution.py:48
  96.8 16.6 %collective-permute-start.15 = (bf16[96,6144]{1,0:T(8,128)(2,1)S(1)}, bf16[96,6144]{1,0:T(8,128)(2,1)S(1)}, u32[]{:S(2)}, u32[]{:S(2)}) collective-permute-start(bf16[96,6144]{1,0:T(8,128)(2,1)S(1)} %get-tuple-element.41), channel_id=1, source_target_pairs={{0,1},{1,2},{2,3},{3,0},{4,12},{5,13},{6,14},{7,15},{8,9},{9,10},{... | collective-permute-start | bytes 3538952 | tf_op jit(solution)/shard_map/ppermute | solution.py:48
  113.4 63.6 %copy-start.4 = (bf16[256,6144]{1,0:T(8,128)(2,1)S(1)}, bf16[256,6144]{1,0:T(8,128)(2,1)}, u32[]{:S(2)}) copy-start(bf16[256,6144]{1,0:T(8,128)(2,1)} %t0.1) | copy-start | bytes 9437188
  113.4 63.6 %copy-start.10 = (s32[1,512]{1,0:T(1,128)S(1)}, s32[1,512]{1,0:T(1,128)}, u32[]{:S(2)}) copy-start(s32[1,512]{1,0:T(1,128)} %targets_ref.1) | copy-start | bytes 6148
  114.3 62.7 %collective-permute-start.25 = (bf16[256,6144]{1,0:T(8,128)(2,1)}, bf16[256,6144]{1,0:T(8,128)(2,1)}, u32[]{:S(2)}, u32[]{:S(2)}) collective-permute-start(bf16[256,6144]{1,0:T(8,128)(2,1)} %collective-permute-done.4.t2), channel_id=1, source_target_pairs={{0,4},{4,0},{8,12},{12,8},{16,20},{20,16},{24,28},{28,24},{1,5},{5... | collective-permute-start | bytes 9437192 | tf_op jit(solution)/shard_map/ppermute | solution.py:60
  120.5 5.9 %collective-permute-start.16 = (bf16[24,6144]{1,0:T(8,128)(2,1)S(1)}, bf16[24,6144]{1,0:T(8,128)(2,1)S(1)}, u32[]{:S(2)}, u32[]{:S(2)}) collective-permute-start(bf16[24,6144]{1,0:T(8,128)(2,1)S(1)} %get-tuple-element.47), channel_id=1, source_target_pairs={{0,24},{1,25},{2,26},{3,27},{4,7},{5,4},{6,5},{7,6},{8,0},{9,1},{1... | collective-permute-start | bytes 884744 | tf_op jit(solution)/shard_map/ppermute | solution.py:48
  120.5 10.2 %collective-permute-start.17 = (bf16[24,6144]{1,0:T(8,128)(2,1)S(1)}, bf16[24,6144]{1,0:T(8,128)(2,1)S(1)}, u32[]{:S(2)}, u32[]{:S(2)}) collective-permute-start(bf16[24,6144]{1,0:T(8,128)(2,1)S(1)} %get-tuple-element.48), channel_id=1, source_target_pairs={{0,8},{1,9},{2,10},{3,11},{4,5},{5,6},{6,7},{7,4},{8,16},{9,17},{1... | collective-permute-start | bytes 884744 | tf_op jit(solution)/shard_map/ppermute | solution.py:48
  122.0 8.8 %collective-permute-start.18 = (bf16[24,6144]{1,0:T(8,128)(2,1)S(1)}, bf16[24,6144]{1,0:T(8,128)(2,1)S(1)}, u32[]{:S(2)}, u32[]{:S(2)}) collective-permute-start(bf16[24,6144]{1,0:T(8,128)(2,1)S(1)} %get-tuple-element.49), channel_id=1, source_target_pairs={{0,16},{1,17},{2,18},{3,19},{4,6},{5,7},{6,4},{7,5},{8,24},{9,25},... | collective-permute-start | bytes 884744 | tf_op jit(solution)/shard_map/ppermute | solution.py:48
  145.7 6.8 %collective-permute-start.19 = (bf16[8,6144]{1,0:T(8,128)(2,1)S(1)}, bf16[8,6144]{1,0:T(8,128)(2,1)S(1)}, u32[]{:S(2)}, u32[]{:S(2)}) collective-permute-start(bf16[8,6144]{1,0:T(8,128)(2,1)S(1)} %shard_map.139.refs_0_), channel_id=1, source_target_pairs={{0,64},{4,12},{8,72},{12,20},{16,80},{20,28},{24,88},{28,4},{32,96... | collective-permute-start | bytes 294920 | tf_op jit(solution)/shard_map/ppermute | solution.py:56
  150.6 3.5 %collective-permute-start.20 = (bf16[8,6144]{1,0:T(8,128)(2,1)S(1)}, bf16[8,6144]{1,0:T(8,128)(2,1)S(1)}, u32[]{:S(2)}, u32[]{:S(2)}) collective-permute-start(bf16[8,6144]{1,0:T(8,128)(2,1)S(1)} %shard_map.139.refs_0_), channel_id=1, source_target_pairs={{0,192},{4,28},{8,200},{12,4},{16,208},{20,12},{24,216},{28,20},{3... | collective-permute-start | bytes 294920 | tf_op jit(solution)/shard_map/ppermute | solution.py:56
  150.6 5.3 %collective-permute-start.21 = (bf16[8,6144]{1,0:T(8,128)(2,1)S(1)}, bf16[8,6144]{1,0:T(8,128)(2,1)S(1)}, u32[]{:S(2)}, u32[]{:S(2)}) collective-permute-start(bf16[8,6144]{1,0:T(8,128)(2,1)S(1)} %shard_map.139.refs_0_), channel_id=1, source_target_pairs={{0,128},{4,20},{8,136},{12,28},{16,144},{20,4},{24,152},{28,12},{3... | collective-permute-start | bytes 294920 | tf_op jit(solution)/shard_map/ppermute | solution.py:56
  156.0 11.6 %collective-permute-start.22 = (bf16[32,6144]{1,0:T(8,128)(2,1)S(1)}, bf16[32,6144]{1,0:T(8,128)(2,1)}, u32[]{:S(2)}, u32[]{:S(2)}) collective-permute-start(bf16[32,6144]{1,0:T(8,128)(2,1)S(1)} %shard_map.140.r0), channel_id=1, source_target_pairs={{0,8},{4,68},{8,16},{12,76},{16,24},{20,84},{24,0},{28,92},{32,40}... | collective-permute-start | bytes 1179656 | tf_op jit(solution)/shard_map/ppermute | solution.py:56
  156.1 20.1 %collective-permute-start.23 = (bf16[32,6144]{1,0:T(8,128)(2,1)S(1)}, bf16[32,6144]{1,0:T(8,128)(2,1)}, u32[]{:S(2)}, u32[]{:S(2)}) collective-permute-start(bf16[32,6144]{1,0:T(8,128)(2,1)S(1)} %shard_map.140.r0), channel_id=1, source_target_pairs={{0,24},{4,196},{8,0},{12,204},{16,8},{20,212},{24,16},{28,220},{32... | collective-permute-start | bytes 1179656 | tf_op jit(solution)/shard_map/ppermute | solution.py:56
  159.6 17.4 %collective-permute-start.24 = (bf16[32,6144]{1,0:T(8,128)(2,1)S(1)}, bf16[32,6144]{1,0:T(8,128)(2,1)}, u32[]{:S(2)}, u32[]{:S(2)}) collective-permute-start(bf16[32,6144]{1,0:T(8,128)(2,1)S(1)} %shard_map.140.r0), channel_id=1, source_target_pairs={{0,16},{4,132},{8,24},{12,140},{16,0},{20,148},{24,8},{28,156},{32... | collective-permute-start | bytes 1179656 | tf_op jit(solution)/shard_map/ppermute | solution.py:56
  159.9 52.9 %copy-start.11 = (s32[1,16]{1,0:T(1,128)S(1)}, s32[1,16]{1,0:T(1,128)}, u32[]{:S(2)}) copy-start(s32[1,16]{1,0:T(1,128)} %lengths_ref.1) | copy-start | bytes 196
  159.9 52.9 %copy-start.12 = (s32[1,16]{1,0:T(1,128)S(1)}, s32[1,16]{1,0:T(1,128)}, u32[]{:S(2)}) copy-start(s32[1,16]{1,0:T(1,128)} %questions_ref.1) | copy-start | bytes 196

commit v4 on v3

--- a/solution.py
+++ b/solution.py
@@ -14,7 +14,7 @@
 
 NZ, NX, NC, NY = 8, 4, 2, 4
 SLOTS = 3
-VMEM_LIMIT = 14 * 2**20
+VMEM_LIMIT = 16 * 2**20
 
 
 def two_axis_perm(sizes, coords, axis_of, shift):
@@ -92,54 +92,72 @@
     return pl.CostEstimate(flops=flops, bytes_accessed=moved, transcendentals=0)
 
 
-def prelude_kernel(ids_ref, resid_ref, gain_ref, router_ref, buckets_ref, weights_ref):
+def normed_rows(resid_ref, gain_ref):
     values = resid_ref[...].astype(f32)
-    tokens = values.shape[0]
     mean_square = jnp.mean(values * values, axis=-1, keepdims=True)
-    normed = (values * lax.rsqrt(mean_square + epsilon) * gain_ref[...]).astype(bf16)
+    return (values * lax.rsqrt(mean_square + epsilon) * gain_ref[...]).astype(bf16)
+
+
+def slots(ids, width):
+    tokens = ids.shape[0]
+    earlier = (iota((tokens, tokens), 0) > iota((tokens, tokens), 1)).astype(f32)
+    column = iota((tokens, NZ * width), 1)
+    owner, slot = column // width, column % width
+    match_a, match_b = ids[:, 0:1] == owner, ids[:, 1:2] == owner
+    named = (match_a | match_b).astype(f32)
+    rank = jnp.dot(earlier, named, preferred_element_type=f32)
+    chosen = named * (rank == slot.astype(f32)).astype(f32)
+    return chosen, match_a, match_b
+
+
+def bucket_kernel(ids_ref, resid_ref, gain_ref, buckets_ref):
+    chosen, _, _ = slots(ids_ref[...], 8)
+    rows = lax.dot_general(
+        chosen.astype(bf16),
+        normed_rows(resid_ref, gain_ref),
+        (((0,), (0,)), ((), ())),
+        preferred_element_type=f32,
+    )
+    for e in range(NZ):
+        buckets_ref[e] = rows[8 * e : 8 * e + SLOTS].astype(bf16)
+
+
+def bucket_rows(ids, resid, gain):
+    tokens, width = resid.shape
+    return pl.pallas_call(
+        bucket_kernel,
+        out_shape=shape((NZ, SLOTS, width), bf16),
+        compiler_params=params(),
+        cost_estimate=cost(2 * 64 * tokens * width, 8 * width),
+    )(ids, resid, gain)
+
+
+def gate_kernel(ids_ref, resid_ref, gain_ref, router_ref, weights_ref):
     logits = lax.dot_general(
-        normed, router_ref[...], (((1,), (1,)), ((), ())), preferred_element_type=f32
+        normed_rows(resid_ref, gain_ref),
+        router_ref[...],
+        (((1,), (1,)), ((), ())),
+        preferred_element_type=f32,
     )
     ids = ids_ref[...]
-    id_a, id_b = ids[:, 0:1], ids[:, 1:2]
-    earlier = (iota((tokens, tokens), 0) > iota((tokens, tokens), 1)).astype(f32)
-
-    def slots(width):
-        column = iota((tokens, NZ * width), 1)
-        owner, slot = column // width, column % width
-        match_a, match_b = id_a == owner, id_b == owner
-        named = (match_a | match_b).astype(f32)
-        rank = jnp.dot(earlier, named, preferred_element_type=f32)
-        chosen = named * (rank == slot.astype(f32)).astype(f32)
-        return chosen, match_a, match_b
-
-    wide, _, _ = slots(8)
-    chosen, match_a, match_b = slots(SLOTS)
+    chosen, match_a, match_b = slots(ids, SLOTS)
     entry = iota(logits.shape, 1)
-    pick_a = jnp.sum(jnp.where(id_a == entry, logits, 0.0), axis=1, keepdims=True)
-    pick_b = jnp.sum(jnp.where(id_b == entry, logits, 0.0), axis=1, keepdims=True)
+    pick_a = jnp.sum(jnp.where(ids[:, 0:1] == entry, logits, 0.0), axis=1, keepdims=True)
+    pick_b = jnp.sum(jnp.where(ids[:, 1:2] == entry, logits, 0.0), axis=1, keepdims=True)
     gate_a = 1.0 / (1.0 + jnp.exp(pick_b - pick_a))
     gate_b = 1.0 / (jnp.exp(pick_a - pick_b) + 1.0)
     weights_ref[...] = chosen * (
         jnp.where(match_a, gate_a, 0.0) + jnp.where(match_b, gate_b, 0.0)
     )
-    rows = lax.dot_general(
-        wide.astype(bf16), normed, (((0,), (0,)), ((), ())), preferred_element_type=f32
-    )
-    for e in range(NZ):
-        buckets_ref[e] = rows[8 * e : 8 * e + SLOTS].astype(bf16)
-
-
-def prelude(ids, resid, gain, router):
+
+
+def slot_gates(ids, resid, gain, router):
     tokens, width = resid.shape
     return pl.pallas_call(
-        prelude_kernel,
-        out_shape=(
-            shape((NZ, SLOTS, width), bf16),
-            shape((tokens, NZ * SLOTS), f32),
-        ),
-        compiler_params=params(),
-        cost_estimate=cost(2 * 64 * 8 * width, 8 * width),
+        gate_kernel,
+        out_shape=shape((tokens, NZ * SLOTS), f32),
+        compiler_params=params(),
+        cost_estimate=cost(16 * tokens * width, 8 * width),
     )(ids, resid, gain, router)
 
 
@@ -194,7 +212,7 @@
 
 
 def expand(rows, weights):
-    depth = 768
+    depth = 1536
     count = len(rows)
     each, width = rows[0].shape
     share = weights[0].shape[1]
@@ -328,8 +346,8 @@
     rows = jnp.concatenate([r0[...], r1[...], r2[...], r3[...]])
     share = t0.shape[0]
     for j, table in enumerate((t0, t1, t2, t3)):
-        total[:, j * share : (j + 1) * share] += lax.dot_general(
-            rows, table[...], (((1,), (1,)), ((), ())), preferred_element_type=f32
+        total[j * share : (j + 1) * share] += lax.dot_general(
+            table[...], rows, (((1,), (1,)), ((), ())), preferred_element_type=f32
         )
 
     @pl.when(step == pl.num_programs(0) - 1)
@@ -348,27 +366,29 @@
             axis=1,
             keepdims=True,
         )
+        same = iota((count, count), 0) == iota((count, count), 1)
+        here = place == iota((count, count), 1)
+        wanted = jnp.sum(jnp.where(same, wanted, 0), axis=0, keepdims=True)
         logits = total[...]
-        entry = iota((1, 4 * share), 1)
+        entry = iota((4 * share, 1), 0)
         table, offset = entry // share, entry % share
         z_of = jnp.where(table < 2, z, z + 1 - 2 * (z % 2))
         c_of = jnp.where(table % 2 == 0, c, 1 - c)
         entry_id = ((z_of * NX + x) * NC + c_of) * share + offset
-        top = jnp.max(logits, axis=1, keepdims=True)
-        spread = jnp.sum(jnp.exp(logits - top), axis=1, keepdims=True)
-        hit = jnp.sum(jnp.where(wanted == entry_id, logits, 0.0), axis=1, keepdims=True)
-        here = place == iota((count, count), 1)
-        figures = [
-            jnp.sum(jnp.where(here, value, 0.0), axis=0, keepdims=True)
-            for value in (top, spread, hit, hit)
-        ]
+        top = jnp.max(logits, axis=0, keepdims=True)
+        spread = jnp.sum(jnp.exp(logits - top), axis=0, keepdims=True)
+        hit = jnp.sum(jnp.where(wanted == entry_id, logits, 0.0), axis=0, keepdims=True)
+        figures = []
+        for value in (top + jnp.log(spread), hit):
+            column = jnp.sum(jnp.where(same, value, 0.0), axis=1, keepdims=True)
+            figures.append(jnp.sum(jnp.where(here, column, 0.0), axis=0, keepdims=True))
         figures = jnp.concatenate(figures)
         for peer in range(out_ref.shape[0]):
             out_ref[peer] = figures
 
 
 def head(place, targets, rows, tables):
-    depth = 768
+    depth = 1536
     width = rows[0].shape[1]
     share = tables[0].shape[0]
     count = sum(r.shape[0] for r in rows)
@@ -379,12 +399,37 @@
         in_specs=[whole, pl.BlockSpec(targets.shape, lambda k: (0, 0))]
         + [pl.BlockSpec((rows[0].shape[0], depth), lambda k: (0, k))] * 4
         + [pl.BlockSpec((share, depth), lambda k: (0, k))] * 4,
-        out_specs=pl.BlockSpec((NZ * NX * NC, 4, count), lambda k: (0, 0, 0)),
-        out_shape=shape((NZ * NX * NC, 4, count), f32),
-        scratch_shapes=[pltpu.VMEM((count, 4 * share), f32)],
+        out_specs=pl.BlockSpec((NZ * NX * NC, 2, count), lambda k: (0, 0, 0)),
+        out_shape=shape((NZ * NX * NC, 2, count), f32),
+        scratch_shapes=[pltpu.VMEM((4 * share, count), f32)],
         compiler_params=params(),
         cost_estimate=cost(8 * count * share * width, 8 * share * width),
     )(place, targets, *rows, *tables)
+
+
+def hold_kernel(*refs, count):
+    sources, kept, sems = refs[:count], refs[count : 2 * count], refs[2 * count]
+    copies = [
+        pltpu.make_async_copy(source, keep, sems.at[j])
+        for j, (source, keep) in enumerate(zip(sources, kept))
+    ]
+    for copy in copies:
+        copy.start()
+    for copy in copies:
+        copy.wait()
+
+
+def hold(arrays):
+    count = len(arrays)
+    return pl.pallas_call(
+        functools.partial(hold_kernel, count=count),
+        in_specs=[pl.BlockSpec(memory_space=pl.ANY)] * count,
+        out_specs=[pl.BlockSpec(memory_space=pltpu.VMEM)] * count,
+        out_shape=[pltpu.VMEM(a.shape, a.dtype) for a in arrays],
+        scratch_shapes=[pltpu.SemaphoreType.DMA((count,))],
+        compiler_params=params(),
+        cost_estimate=cost(0, sum(2 * a.size for a in arrays)),
+    )(*arrays)
 
 
 def finish_kernel(place_ref, stats_ref, lengths_ref, questions_ref, logprob_ref, prob_ref):
@@ -417,8 +462,8 @@
             ]
             figures = [stats_ref[j] for j in senders]
             best = functools.reduce(jnp.maximum, [f[0:1] for f in figures])
-            summed = sum(f[1:2] * jnp.exp(f[0:1] - best) for f in figures)
-            logprob = sum(f[2:3] for f in figures) - (best + jnp.log(summed))
+            summed = sum(jnp.exp(f[0:1] - best) for f in figures)
+            logprob = sum(f[1:2] for f in figures) - (best + jnp.log(summed))
             position = (
                 (2 * (lane // 32) + parity) * (NX * NC * 8)
                 + lane // 8 % 4 * (NC * 8)
@@ -485,13 +530,12 @@
     other_down = swap_cores(own_down)
     other_head = swap_cores(lm_head)
 
-    buckets, combine_weights = prelude(
-        expert_ids[0], resid[0], moe_gain.reshape(1, -1), router.T
-    )
+    buckets = bucket_rows(expert_ids[0], resid[0], moe_gain.reshape(1, -1))
     arrived = lax.all_to_all(buckets, "expert", split_axis=0, concat_axis=0, tiled=True)
-    arrived, other_gate, other_up, other_down, other_head, own_head = tied(
-        arrived, other_gate, other_up, other_down, other_head, lm_head
-    )
+    arrived, other_gate, other_up, other_down, other_head, own_head, router = tied(
+        arrived, other_gate, other_up, other_down, other_head, lm_head, router
+    )
+    combine_weights = slot_gates(expert_ids[0], resid[0], moe_gain.reshape(1, -1), router.T)
     pair_head = swap_planes(own_head)
 
     def first(block, shift):
@@ -505,9 +549,12 @@
     half = rows // 2
     from_before = second(line, 1)
     from_after = second(line, -1)
+    weights = hold(tied(line, own_gate, own_up, other_gate, other_up)[1:])
+    from_before, from_after, combine_weights, *weights = tied(
+        from_before, from_after, combine_weights, *weights
+    )
     far_before = second(from_before[:half], 1)
     far_after = second(from_after[half:], -1)
-    weights = (own_gate, own_up, other_gate, other_up)
     downs = (own_down, other_down)
     near_hidden = expand([line, from_before, from_after], weights)
     near_hidden, far_before, far_after = tied(near_hidden, far_before, far_after)
@@ -520,18 +567,17 @@
         near_kernel, near_hidden, downs, (got_before, got_after), (rows, rows, rows)
     )
     pieces = line_sum([own_part, second(before_part, -1), second(after_part, 1)])
-    pair_head, *pieces = tied(pair_head, *pieces)
+    back = (first(pieces[1], -1), first(pieces[2], 1), first(pieces[3], 2))
+    *back, pair_head = tied(*back, pair_head)
     pair_other = swap_cores(pair_head)
-    outgoing = expert_sum(
-        [pieces[0], first(pieces[1], -1), first(pieces[2], 1), first(pieces[3], 2)]
-    )
+    outgoing = expert_sum([pieces[0], *back])
 
     returned = lax.all_to_all(outgoing, "expert", split_axis=0, concat_axis=0, tiled=True)
     normed_out = combine(combine_weights, returned, resid[0], final_gain.reshape(1, -1))
 
     head_line = stack(gather_four(normed_out, lambda b, s: head_shift(b, False, s)))
     head_rows = gather_four(head_line, lambda b, s: head_shift(b, True, s))
-    stats = head(place, target_ids, head_rows, (lm_head, other_head, pair_head, pair_other))
+    stats = head(place, target_ids, head_rows, hold([lm_head, other_head, pair_head, pair_other]))
     gathered = lax.all_to_all(stats, ("expert", "vocab"), 0, 0, tiled=True)
     return finish(place, gathered, choice_len, choice_question, resid.shape[1])
 

time: 215 us -> 205 us (0.953)
  blocking collectives: 59.9 us -> 55.2 us
  Pallas kernels: 35.9 us -> 32.8 us
  waiting for transfers between devices: 75.5 us -> 72.5 us
    all_to_all x1, blocking collectives: 26.4 us -> 17.8 us  [on_device(): gathered = lax.all_to_all(stats, ('expert', 'vocab'), 0, 0, tiled=True)]
    pallas_call x1 -> x4, Pallas kernels: 0.61 us -> 8.28 us  [the longest x2 7.3 us: hold(): pl.pallas_call(functools.partial(hold_kernel, count=count), in_specs=[pl....]
    pallas_call x2, Pallas kernels: 15.5 us -> 7.9 us  [expand(): pl.pallas_call(functools.partial(expand_kernel, count=count), grid=(width...]
    ppermute x6, starting transfers between devices: 10.6 us -> 6.4 us  [head_shift(): return lax.ppermute(array, ('expert', 'vocab'), perm)]
    all_to_all x1, blocking collectives: 13.6 us -> 17.6 us  [on_device(): lax.all_to_all(outgoing, 'expert', split_axis=0, concat_axis=0, tiled=True)]
    ppermute x5, starting transfers between devices: 10.2 us -> 14.1 us  [swap_cores(): return lax.ppermute(array, 'vocab', [(v, v ^ 1) for v in range(NX * NC)])]
    pallas_call x1, Pallas kernels: 9.36 us -> 6.16 us  [head(): pl.pallas_call(head_kernel, grid=(width // depth,), in_specs=[whole, pl.B...]
    ppermute x6, waiting for transfers between devices: 20.5 us -> 17.4 us  [head_shift(): return lax.ppermute(array, ('expert', 'vocab'), perm)]
  transfers between devices with their start and end apart: 26 -> 26, of which waited for: 15 -> 18; matrix products, arithmetic and copies ran while one was open for 0% -> 0% of each run, Pallas kernels for 11% -> 12%
where the time goes in v4:
time: 205 us; the launch traced here: 203 us
  waiting for transfers between devices  72.5 us (35%)
  blocking collectives  55.2 us (27%)
  starting transfers between devices  36.9 us (18%)
  Pallas kernels  32.8 us (16%)
  local copies, waits for them, and re-layouts  4.57 us (2%)
    ppermute x14, waiting for transfers between devices, plane_shift(): return lax.ppermute(array, ('vocab', 'batch'), perm)  55.2 us
    all_to_all x1, blocking collectives, on_device(): lax.all_to_all(buckets, 'expert', split_axis=0, concat_axis=0, tiled=True)  19.9 us
    all_to_all x1, blocking collectives, on_device(): gathered = lax.all_to_all(stats, ('expert', 'vocab'), 0, 0, tiled=True)  17.8 us
    all_to_all x1, blocking collectives, on_device(): lax.all_to_all(outgoing, 'expert', split_axis=0, concat_axis=0, tiled=True)  17.6 us
    ppermute x6, waiting for transfers between devices, head_shift(): return lax.ppermute(array, ('expert', 'vocab'), perm)  17.4 us
    ppermute x14, starting transfers between devices, plane_shift(): return lax.ppermute(array, ('vocab', 'batch'), perm)  16.1 us
    ppermute x5, starting transfers between devices, swap_cores(): return lax.ppermute(array, 'vocab', [(v, v ^ 1) for v in range(NX * NC)])  14.1 us
    pallas_call x2, Pallas kernels, expand(): pl.pallas_call(functools.partial(expand_kernel, count=count), grid=(width...  7.9 us
  transfers between devices with their start and end apart: 26, of which 18 were waited for; matrix products, arithmetic and copies ran while one was open for 0% of the time, Pallas kernels for 12%

profile of v4, /device:TPU:1, one launch (start us, length us, event | category | flops | bytes accessed | tf_op | source)
XLA Modules:
  0.0 203.0 jit_solution(16579554427703587089)
XLA Ops:
  0.6 3.3 %collective-permute-start.2 = (bf16[256,6144]{1,0:T(8,128)(2,1)}, bf16[256,6144]{1,0:T(8,128)(2,1)S(1)}, u32[]{:S(2)}, u32[]{:S(2)}) collective-permute-start(bf16[256,6144]{1,0:T(8,128)(2,1)} %bitcast.11), channel_id=1, source_target_pairs={{0,4},{4,0},{8,12},{12,8},{16,20},{20,16},{24,28},{28,24},{1,5},{5... | collective-permute-start | bytes 9437192 | tf_op jit(solution)/shard_map/ppermute | solution.py:60
  4.6 0.8 copy.14.ids_ref
  5.3 1.0 copy-done.4
  6.4 0.7 copy-done.6
  7.7 19.9 %all_to_all.15.refs_0_ = bf16[8,3,6144]{2,1,0:T(4,128)(2,1)S(1)} all-to-all(bf16[8,3,6144]{2,1,0:T(4,128)(2,1)S(1)} %shard_map.131), channel_id=1, replica_groups=mesh['expert'=8,'vocab'=8,'batch'=4] {'expert'}, dimensions={0} | all-to-all | bytes 589824 | tf_op jit(solution)/shard_map/all_to_all | solution.py:534
  27.6 1.3 collective-permute-start.4
  28.9 1.6 collective-permute-start.5
  30.6 1.6 collective-permute-start.6
  32.1 3.8 %collective-permute-done.4.refs_1_ = bf16[8,3,6144]{2,1,0:T(4,128)(2,1)S(1)} collective-permute-done((bf16[8,3,6144]{2,1,0:T(4,128)(2,1)S(1)}, bf16[8,3,6144]{2,1,0:T(4,128)(2,1)S(1)}, u32[]{:S(2)}, u32[]{:S(2)}) %collective-permute-start.4) | collective-permute-done | bytes 294944 | tf_op jit(solution)/shard_map/ppermute | solution.py:48
  35.9 3.6 %collective-permute-done.5.refs_2_ = bf16[8,3,6144]{2,1,0:T(4,128)(2,1)S(1)} collective-permute-done((bf16[8,3,6144]{2,1,0:T(4,128)(2,1)S(1)}, bf16[8,3,6144]{2,1,0:T(4,128)(2,1)S(1)}, u32[]{:S(2)}, u32[]{:S(2)}) %collective-permute-start.5) | collective-permute-done | bytes 294944 | tf_op jit(solution)/shard_map/ppermute | solution.py:48
  39.5 1.8 collective-permute-done.6.refs_3_
  42.0 0.9 collective-permute-start.7
  42.9 1.8 collective-permute-start.8
  45.5 1.9 copy-done.2
  47.3 3.3 %shard_map.134 = (bf16[6144,256]{1,0:T(8,128)(2,1)S(1)}, bf16[6144,256]{1,0:T(8,128)(2,1)S(1)}, bf16[6144,256]{1,0:T(8,128)(2,1)S(1)}, bf16[6144,256]{1,0:T(8,128)(2,1)S(1)}) custom-call(bf16[6144,256]{1,0:T(8,128)(2,1)S(1)} %bitcast.15, bf16[6144,256]{1,0:T(8,128)(2,1)S(1)} %bitcast.17, bf16[6144,256]{1,0:T(8,128)(2,1)} %collective-permute-done.refs_2_, ...), custom_call_target="tpu_custom_call" | custom-call | bytes 12582912 | tf_op jit(solution)/shard_map/pallas_call | solution.py:424
  50.6 7.9 %collective-permute-done.7.refs_1_ = bf16[96,6144]{1,0:T(8,128)(2,1)S(1)} collective-permute-done((bf16[96,6144]{1,0:T(8,128)(2,1)S(1)}, bf16[96,6144]{1,0:T(8,128)(2,1)S(1)}, u32[]{:S(2)}, u32[]{:S(2)}) %collective-permute-start.7) | collective-permute-done | bytes 1179680 | tf_op jit(solution)/shard_map/ppermute | solution.py:48
  58.6 2.8 %collective-permute-start.10 = (bf16[48,6144]{1,0:T(8,128)(2,1)S(1)}, bf16[48,6144]{1,0:T(8,128)(2,1)S(1)}, u32[]{:S(2)}, u32[]{:S(2)}) collective-permute-start(bf16[48,6144]{1,0:T(8,128)(2,1)S(1)} %slice.7), channel_id=1, source_target_pairs={{0,3},{1,0},{2,1},{3,2},{4,28},{5,29},{6,30},{7,31},{8,11},{9,8},{... | collective-permute-start | bytes 1769480 | tf_op jit(solution)/shard_map/ppermute | solution.py:48
  61.5 5.1 %shard_map.135.hidden_ref = bf16[288,512]{1,0:T(8,128)(2,1)S(1)} custom-call(bf16[96,6144]{1,0:T(8,128)(2,1)S(1)} %shard_map.132.refs_0_, bf16[96,6144]{1,0:T(8,128)(2,1)S(1)} %collective-permute-done.7.refs_1_, bf16[96,6144]{1,0:T(8,128)(2,1)S(1)} %collective-permute-done.8.refs_2_, bf16[6144,256]{1,0:T(8,128)(2,1)S(1)} %get-tuple-element.59.refs_3_.refs_2_, ...), custom_call_target="tpu_custom_call" | custom-call | flops 3623878656 | bytes 12582912 | tf_op jit(solution)/shard_map/pallas_call | solution.py:219
  66.6 1.6 collective-permute-done.10.refs_1_
  68.2 3.5 %collective-permute-done.9.refs_0_ = bf16[48,6144]{1,0:T(8,128)(2,1)S(1)} collective-permute-done((bf16[48,6144]{1,0:T(8,128)(2,1)S(1)}, bf16[48,6144]{1,0:T(8,128)(2,1)S(1)}, u32[]{:S(2)}, u32[]{:S(2)}) %collective-permute-start.9) | collective-permute-done | bytes 589856 | tf_op jit(solution)/shard_map/ppermute | solution.py:48
  71.7 2.8 %shard_map.136.hidden_ref = bf16[96,512]{1,0:T(8,128)(2,1)S(1)} custom-call(bf16[48,6144]{1,0:T(8,128)(2,1)S(1)} %collective-permute-done.9.refs_0_, bf16[48,6144]{1,0:T(8,128)(2,1)S(1)} %collective-permute-done.10.refs_1_, bf16[6144,256]{1,0:T(8,128)(2,1)S(1)} %get-tuple-element.59.refs_3_.refs_2_, bf16[6144,256]{1,0:T(8,128)(2,1)S(1)} %get-tuple-element.60.refs_4_.refs_3_, ...), custom_call_target="tpu_custom_call" | custom-call | flops 1207959552 | bytes 12582912 | tf_op jit(solution)/shard_map/pallas_call | solution.py:219
  74.6 2.4 %shard_map.137 = (bf16[48,6144]{1,0:T(8,128)(2,1)S(1)}, bf16[48,6144]{1,0:T(8,128)(2,1)S(1)}) custom-call(bf16[96,512]{1,0:T(8,128)(2,1)S(1)} %shard_map.136.hidden_ref, bf16[256,6144]{1,0:T(8,128)(2,1)S(1)} %bitcast.12, bf16[256,6144]{1,0:T(8,128)(2,1)S(1)} %collective-permute-done.2.down_b), custom_call_target="tpu_custom_call" | custom-call | flops 603979776 | bytes 6291456 | tf_op jit(solution)/shard_map/pallas_call | solution.py:260
  77.1 1.5 collective-permute-start.12
  78.6 7.7 %collective-permute-done.11.got_before = bf16[48,6144]{1,0:T(8,128)(2,1)S(1)} collective-permute-done((bf16[48,6144]{1,0:T(8,128)(2,1)S(1)}, bf16[48,6144]{1,0:T(8,128)(2,1)S(1)}, u32[]{:S(2)}, u32[]{:S(2)}) %collective-permute-start.11) | collective-permute-done | bytes 589856 | tf_op jit(solution)/shard_map/ppermute | solution.py:48
  86.2 1.4 collective-permute-done.12.got_after
  87.6 3.7 %shard_map.138 = (bf16[96,6144]{1,0:T(8,128)(2,1)S(1)}, bf16[96,6144]{1,0:T(8,128)(2,1)S(1)}, bf16[96,6144]{1,0:T(8,128)(2,1)S(1)}) custom-call(bf16[288,512]{1,0:T(8,128)(2,1)S(1)} %shard_map.135.hidden_ref, bf16[256,6144]{1,0:T(8,128)(2,1)S(1)} %bitcast.13, bf16[256,6144]{1,0:T(8,128)(2,1)S(1)} %collective-permute-done.2.down_b, ...), custom_call_target="tpu_custom_call" | custom-call | flops 1811939328 | bytes 6291456 | tf_op jit(solution)/shard_map/pallas_call | solution.py:260
  91.4 1.5 collective-permute-start.14
  92.9 14.0 %collective-permute-done.13.before_ref = bf16[96,6144]{1,0:T(8,128)(2,1)S(1)} collective-permute-done((bf16[96,6144]{1,0:T(8,128)(2,1)S(1)}, bf16[96,6144]{1,0:T(8,128)(2,1)S(1)}, u32[]{:S(2)}, u32[]{:S(2)}) %collective-permute-start.13) | collective-permute-done | bytes 1179680 | tf_op jit(solution)/shard_map/ppermute | solution.py:48
  106.8 1.2 collective-permute-done.14.after_ref
  108.0 0.9 shard_map.139
  108.9 1.7 collective-permute-start.15
  110.6 1.3 collective-permute-start.17
  111.8 3.9 %collective-permute-done.15.b = bf16[24,6144]{1,0:T(8,128)(2,1)S(1)} collective-permute-done((bf16[24,6144]{1,0:T(8,128)(2,1)S(1)}, bf16[24,6144]{1,0:T(8,128)(2,1)S(1)}, u32[]{:S(2)}, u32[]{:S(2)}) %collective-permute-start.15) | collective-permute-done | bytes 294944 | tf_op jit(solution)/shard_map/ppermute | solution.py:48
  115.7 4.8 %collective-permute-done.16.c = bf16[24,6144]{1,0:T(8,128)(2,1)S(1)} collective-permute-done((bf16[24,6144]{1,0:T(8,128)(2,1)S(1)}, bf16[24,6144]{1,0:T(8,128)(2,1)S(1)}, u32[]{:S(2)}, u32[]{:S(2)}) %collective-permute-start.16) | collective-permute-done | bytes 294944 | tf_op jit(solution)/shard_map/ppermute | solution.py:48
  120.5 10.2 %collective-permute-start.25 = (bf16[256,6144]{1,0:T(8,128)(2,1)}, bf16[256,6144]{1,0:T(8,128)(2,1)}, u32[]{:S(2)}, u32[]{:S(2)}) collective-permute-start(bf16[256,6144]{1,0:T(8,128)(2,1)} %collective-permute-done.18.refs_2_), channel_id=1, source_target_pairs={{0,4},{4,0},{8,12},{12,8},{16,20},{20,16},{24,28},{28,24},{1,5},{5... | collective-permute-start | bytes 9437192 | tf_op jit(solution)/shard_map/ppermute | solution.py:60
  131.1 17.6 %all_to_all.16.rows_ref = bf16[8,3,6144]{2,1,0:T(4,128)(2,1)S(1)} all-to-all(bf16[8,3,6144]{2,1,0:T(4,128)(2,1)S(1)} %shard_map.140), channel_id=1, replica_groups=mesh['expert'=8,'vocab'=8,'batch'=4] {'expert'}, dimensions={0} | all-to-all | bytes 589824 | tf_op jit(solution)/shard_map/all_to_all | solution.py:575
  148.7 1.0 shard_map.141.refs_0_
  149.8 2.7 %collective-permute-start.20 = (bf16[8,6144]{1,0:T(8,128)(2,1)S(1)}, bf16[8,6144]{1,0:T(8,128)(2,1)S(1)}, u32[]{:S(2)}, u32[]{:S(2)}) collective-permute-start(bf16[8,6144]{1,0:T(8,128)(2,1)S(1)} %shard_map.141.refs_0_), channel_id=1, source_target_pairs={{0,192},{4,28},{8,200},{12,4},{16,208},{20,12},{24,216},{28,20},{3... | collective-permute-start | bytes 294920 | tf_op jit(solution)/shard_map/ppermute | solution.py:56
  152.5 2.0 collective-permute-done.19.refs_1_
  155.1 2.4 %collective-permute-done.21.refs_3_ = bf16[8,6144]{1,0:T(8,128)(2,1)S(1)} collective-permute-done((bf16[8,6144]{1,0:T(8,128)(2,1)S(1)}, bf16[8,6144]{1,0:T(8,128)(2,1)S(1)}, u32[]{:S(2)}, u32[]{:S(2)}) %collective-permute-start.21) | collective-permute-done | bytes 98336 | tf_op jit(solution)/shard_map/ppermute | solution.py:56
  157.6 3.6 %collective-permute-start.23 = (bf16[32,6144]{1,0:T(8,128)(2,1)S(1)}, bf16[32,6144]{1,0:T(8,128)(2,1)}, u32[]{:S(2)}, u32[]{:S(2)}) collective-permute-start(bf16[32,6144]{1,0:T(8,128)(2,1)S(1)} %shard_map.142.r0), channel_id=1, source_target_pairs={{0,24},{4,196},{8,0},{12,204},{16,8},{20,212},{24,16},{28,220},{32... | collective-permute-start | bytes 1179656 | tf_op jit(solution)/shard_map/ppermute | solution.py:56
  161.3 4.0 %shard_map.143 = (bf16[256,6144]{1,0:T(8,128)(2,1)S(1)}, bf16[256,6144]{1,0:T(8,128)(2,1)S(1)}, bf16[256,6144]{1,0:T(8,128)(2,1)S(1)}, bf16[256,6144]{1,0:T(8,128)(2,1)S(1)}) custom-call(bf16[256,6144]{1,0:T(8,128)(2,1)S(1)} %copy-done.3, bf16[256,6144]{1,0:T(8,128)(2,1)} %collective-permute-done.3.refs_1_, ...), custom_call_target="tpu_custom_call" | custom-call | bytes 12582912 | tf_op jit(solution)/shard_map/pallas_call | solution.py:424
  165.3 3.7 %collective-permute-done.22.r1 = bf16[32,6144]{1,0:T(8,128)(2,1)} collective-permute-done((bf16[32,6144]{1,0:T(8,128)(2,1)S(1)}, bf16[32,6144]{1,0:T(8,128)(2,1)}, u32[]{:S(2)}, u32[]{:S(2)}) %collective-permute-start.22) | collective-permute-done | bytes 393248 | tf_op jit(solution)/shard_map/ppermute | solution.py:56
  169.0 7.7 %collective-permute-done.23.r2 = bf16[32,6144]{1,0:T(8,128)(2,1)} collective-permute-done((bf16[32,6144]{1,0:T(8,128)(2,1)S(1)}, bf16[32,6144]{1,0:T(8,128)(2,1)}, u32[]{:S(2)}, u32[]{:S(2)}) %collective-permute-start.23) | collective-permute-done | bytes 393248 | tf_op jit(solution)/shard_map/ppermute | solution.py:56
  176.7 1.0 collective-permute-done.24.r3
  177.7 6.2 %shard_map.144 = f32[64,2,128]{2,1,0:T(2,128)S(1)} custom-call(s32[3]{0:T(128)S(1)} %pad_add_fusion.place_ref, s32[1,512]{1,0:T(1,128)S(1)} %copy-done.10, bf16[32,6144]{1,0:T(8,128)(2,1)S(1)} %shard_map.142.r0, bf16[32,6144]{1,0:T(8,128)(2,1)} %collective-permute-done.22.r1, bf16[32,6144]{1,0:T(8,128)(2,1)} %collective-permute-done.23.r2, ...), custom_call_target="tpu_custom_call" | custom-call | flops 1610612736 | bytes 12582912 | tf_op jit(solution)/shard_map/pallas_call | solution.py:396
  183.9 17.8 %all_to_all.17.stats_ref = f32[64,2,128]{2,1,0:T(2,128)S(1)} all-to-all(f32[64,2,128]{2,1,0:T(2,128)S(1)} %shard_map.144), channel_id=1, replica_groups=mesh['expert'=8,'vocab'=8,'batch'=4] {'expert','vocab'}, dimensions={0} | all-to-all | bytes 131072 | tf_op jit(solution)/shard_map/all_to_all | solution.py:581
  201.6 1.4 shard_map.145
  (52 shorter events, 4.2 us)
Async XLA Ops:
  0.6 26.9 %collective-permute-start.2 = (bf16[256,6144]{1,0:T(8,128)(2,1)}, bf16[256,6144]{1,0:T(8,128)(2,1)S(1)}, u32[]{:S(2)}, u32[]{:S(2)}) collective-permute-start(bf16[256,6144]{1,0:T(8,128)(2,1)} %bitcast.11), channel_id=1, source_target_pairs={{0,4},{4,0},{8,12},{12,8},{16,20},{20,16},{24,28},{28,24},{1,5},{5... | collective-permute-start | bytes 9437192 | tf_op jit(solution)/shard_map/ppermute | solution.py:60
  4.0 23.6 %collective-permute-start = (bf16[6144,256]{1,0:T(8,128)(2,1)}, bf16[6144,256]{1,0:T(8,128)(2,1)}, u32[]{:S(2)}, u32[]{:S(2)}) collective-permute-start(bf16[6144,256]{1,0:T(8,128)(2,1)} %bitcast.14), channel_id=1, source_target_pairs={{0,4},{4,0},{8,12},{12,8},{16,20},{20,16},{24,28},{28,24},{1,5},{5... | collective-permute-start | bytes 9437192 | tf_op jit(solution)/shard_map/ppermute | solution.py:60
  4.1 23.5 %collective-permute-start.1 = (bf16[6144,256]{1,0:T(8,128)(2,1)}, bf16[6144,256]{1,0:T(8,128)(2,1)}, u32[]{:S(2)}, u32[]{:S(2)}) collective-permute-start(bf16[6144,256]{1,0:T(8,128)(2,1)} %bitcast.16), channel_id=1, source_target_pairs={{0,4},{4,0},{8,12},{12,8},{16,20},{20,16},{24,28},{28,24},{1,5},{5... | collective-permute-start | bytes 9437192 | tf_op jit(solution)/shard_map/ppermute | solution.py:60
  4.5 23.1 %collective-permute-start.3 = (bf16[256,6144]{1,0:T(8,128)(2,1)}, bf16[256,6144]{1,0:T(8,128)(2,1)}, u32[]{:S(2)}, u32[]{:S(2)}) collective-permute-start(bf16[256,6144]{1,0:T(8,128)(2,1)} %refs_0_.1), channel_id=1, source_target_pairs={{0,4},{4,0},{8,12},{12,8},{16,20},{20,16},{24,28},{28,24},{1,5},{5... | collective-permute-start | bytes 9437192 | tf_op jit(solution)/shard_map/ppermute | solution.py:60
  5.3 40.1 %copy-start.1 = (bf16[1,6144,256]{2,1,0:T(8,128)(2,1)S(1)}, bf16[1,6144,256]{2,1,0:T(8,128)(2,1)}, u32[]{:S(2)}) copy-start(bf16[1,6144,256]{2,1,0:T(8,128)(2,1)} %param.16) | copy-start | bytes 9437188
  5.3 1.0 copy-start.4
  6.4 0.7 copy-start.6
  7.1 37.9 %copy-start.7 = (f32[6144]{0:T(1024)S(1)}, f32[6144]{0:T(1024)}, u32[]{:S(2)}) copy-start(f32[6144]{0:T(1024)} %param.13) | copy-start | bytes 73732
  7.1 37.9 %copy-start.8 = (bf16[6144,8]{0,1:T(8,128)(2,1)S(1)}, bf16[6144,8]{0,1:T(8,128)(2,1)}, u32[]{:S(2)}) copy-start(bf16[6144,8]{0,1:T(8,128)(2,1)} %param.15) | copy-start | bytes 294916
  27.6 8.3 %collective-permute-start.4 = (bf16[8,3,6144]{2,1,0:T(4,128)(2,1)S(1)}, bf16[8,3,6144]{2,1,0:T(4,128)(2,1)S(1)}, u32[]{:S(2)}, u32[]{:S(2)}) collective-permute-start(bf16[8,3,6144]{2,1,0:T(4,128)(2,1)S(1)} %all_to_all.15.refs_0_), channel_id=1, source_target_pairs={{0,8},{1,9},{2,10},{3,11},{4,5},{5,6},{6,7},{7,4},{8,16},{9,17},{1... | collective-permute-start | bytes 884744 | tf_op jit(solution)/shard_map/ppermute | solution.py:48
  28.9 10.5 %collective-permute-start.5 = (bf16[8,3,6144]{2,1,0:T(4,128)(2,1)S(1)}, bf16[8,3,6144]{2,1,0:T(4,128)(2,1)S(1)}, u32[]{:S(2)}, u32[]{:S(2)}) collective-permute-start(bf16[8,3,6144]{2,1,0:T(4,128)(2,1)S(1)} %all_to_all.15.refs_0_), channel_id=1, source_target_pairs={{0,24},{1,25},{2,26},{3,27},{4,7},{5,4},{6,5},{7,6},{8,0},{9,1},{1... | collective-permute-start | bytes 884744 | tf_op jit(solution)/shard_map/ppermute | solution.py:48
  30.6 10.8 %collective-permute-start.6 = (bf16[8,3,6144]{2,1,0:T(4,128)(2,1)S(1)}, bf16[8,3,6144]{2,1,0:T(4,128)(2,1)S(1)}, u32[]{:S(2)}, u32[]{:S(2)}) collective-permute-start(bf16[8,3,6144]{2,1,0:T(4,128)(2,1)S(1)} %all_to_all.15.refs_0_), channel_id=1, source_target_pairs={{0,16},{1,17},{2,18},{3,19},{4,6},{5,7},{6,4},{7,5},{8,24},{9,25},... | collective-permute-start | bytes 884744 | tf_op jit(solution)/shard_map/ppermute | solution.py:48
  42.0 16.6 %collective-permute-start.7 = (bf16[96,6144]{1,0:T(8,128)(2,1)S(1)}, bf16[96,6144]{1,0:T(8,128)(2,1)S(1)}, u32[]{:S(2)}, u32[]{:S(2)}) collective-permute-start(bf16[96,6144]{1,0:T(8,128)(2,1)S(1)} %shard_map.132.refs_0_), channel_id=1, source_target_pairs={{0,1},{1,2},{2,3},{3,0},{4,12},{5,13},{6,14},{7,15},{8,9},{9,10},{... | collective-permute-start | bytes 3538952 | tf_op jit(solution)/shard_map/ppermute | solution.py:48
  42.9 15.7 %collective-permute-start.8 = (bf16[96,6144]{1,0:T(8,128)(2,1)S(1)}, bf16[96,6144]{1,0:T(8,128)(2,1)S(1)}, u32[]{:S(2)}, u32[]{:S(2)}) collective-permute-start(bf16[96,6144]{1,0:T(8,128)(2,1)S(1)} %shard_map.132.refs_0_), channel_id=1, source_target_pairs={{0,3},{1,0},{2,1},{3,2},{4,28},{5,29},{6,30},{7,31},{8,11},{9,8},{... | collective-permute-start | bytes 3538952 | tf_op jit(solution)/shard_map/ppermute | solution.py:48
  44.7 67.1 %collective-permute-start.18 = (bf16[256,6144]{1,0:T(8,128)(2,1)}, bf16[256,6144]{1,0:T(8,128)(2,1)}, u32[]{:S(2)}, u32[]{:S(2)}) collective-permute-start(bf16[256,6144]{1,0:T(8,128)(2,1)} %refs_0_.1), channel_id=1, source_target_pairs={{0,32},{32,0},{64,96},{96,64},{128,160},{160,128},{192,224},{224,1... | collective-permute-start | bytes 9437192 | tf_op jit(solution)/shard_map/ppermute | solution.py:64
  45.4 1.9 copy-start.2
  58.6 9.6 %collective-permute-start.10 = (bf16[48,6144]{1,0:T(8,128)(2,1)S(1)}, bf16[48,6144]{1,0:T(8,128)(2,1)S(1)}, u32[]{:S(2)}, u32[]{:S(2)}) collective-permute-start(bf16[48,6144]{1,0:T(8,128)(2,1)S(1)} %slice.7), channel_id=1, source_target_pairs={{0,3},{1,0},{2,1},{3,2},{4,28},{5,29},{6,30},{7,31},{8,11},{9,8},{... | collective-permute-start | bytes 1769480 | tf_op jit(solution)/shard_map/ppermute | solution.py:48
  61.4 10.3 %collective-permute-start.9 = (bf16[48,6144]{1,0:T(8,128)(2,1)S(1)}, bf16[48,6144]{1,0:T(8,128)(2,1)S(1)}, u32[]{:S(2)}, u32[]{:S(2)}) collective-permute-start(bf16[48,6144]{1,0:T(8,128)(2,1)S(1)} %slice.6), channel_id=1, source_target_pairs={{0,1},{1,2},{2,3},{3,0},{4,12},{5,13},{6,14},{7,15},{8,9},{9,10},{... | collective-permute-start | bytes 1769480 | tf_op jit(solution)/shard_map/ppermute | solution.py:48
  66.6 8.0 %copy-start = (bf16[1,256,6144]{2,1,0:T(8,128)(2,1)S(1)}, bf16[1,256,6144]{2,1,0:T(8,128)(2,1)}, u32[]{:S(2)}) copy-start(bf16[1,256,6144]{2,1,0:T(8,128)(2,1)} %param.18) | copy-start | bytes 9437188
  77.0 9.2 %collective-permute-start.11 = (bf16[48,6144]{1,0:T(8,128)(2,1)S(1)}, bf16[48,6144]{1,0:T(8,128)(2,1)S(1)}, u32[]{:S(2)}, u32[]{:S(2)}) collective-permute-start(bf16[48,6144]{1,0:T(8,128)(2,1)S(1)} %get-tuple-element.67), channel_id=1, source_target_pairs={{0,3},{1,0},{2,1},{3,2},{4,28},{5,29},{6,30},{7,31},{8,11},{9,8},{... | collective-permute-start | bytes 1769480 | tf_op jit(solution)/shard_map/ppermute | solution.py:48
  77.1 10.5 %collective-permute-start.12 = (bf16[48,6144]{1,0:T(8,128)(2,1)S(1)}, bf16[48,6144]{1,0:T(8,128)(2,1)S(1)}, u32[]{:S(2)}, u32[]{:S(2)}) collective-permute-start(bf16[48,6144]{1,0:T(8,128)(2,1)S(1)} %get-tuple-element.68), channel_id=1, source_target_pairs={{0,1},{1,2},{2,3},{3,0},{4,12},{5,13},{6,14},{7,15},{8,9},{9,10},{... | collective-permute-start | bytes 1769480 | tf_op jit(solution)/shard_map/ppermute | solution.py:48
  91.3 57.4 %copy-start.5 = (bf16[1,8,6144]{2,1,0:T(8,128)(2,1)S(1)}, bf16[1,8,6144]{2,1,0:T(8,128)(2,1)}, u32[]{:S(2)}) copy-start(bf16[1,8,6144]{2,1,0:T(8,128)(2,1)} %param.12) | copy-start | bytes 294916
  91.3 57.4 %copy-start.9 = (f32[6144]{0:T(1024)S(1)}, f32[6144]{0:T(1024)}, u32[]{:S(2)}) copy-start(f32[6144]{0:T(1024)} %param.14) | copy-start | bytes 73732
  91.3 15.5 %collective-permute-start.13 = (bf16[96,6144]{1,0:T(8,128)(2,1)S(1)}, bf16[96,6144]{1,0:T(8,128)(2,1)S(1)}, u32[]{:S(2)}, u32[]{:S(2)}) collective-permute-start(bf16[96,6144]{1,0:T(8,128)(2,1)S(1)} %get-tuple-element.70), channel_id=1, source_target_pairs={{0,3},{1,0},{2,1},{3,2},{4,28},{5,29},{6,30},{7,31},{8,11},{9,8},{... | collective-permute-start | bytes 3538952 | tf_op jit(solution)/shard_map/ppermute | solution.py:48
  91.4 16.6 %collective-permute-start.14 = (bf16[96,6144]{1,0:T(8,128)(2,1)S(1)}, bf16[96,6144]{1,0:T(8,128)(2,1)S(1)}, u32[]{:S(2)}, u32[]{:S(2)}) collective-permute-start(bf16[96,6144]{1,0:T(8,128)(2,1)S(1)} %get-tuple-element.71), channel_id=1, source_target_pairs={{0,1},{1,2},{2,3},{3,0},{4,12},{5,13},{6,14},{7,15},{8,9},{9,10},{... | collective-permute-start | bytes 3538952 | tf_op jit(solution)/shard_map/ppermute | solution.py:48
  108.0 53.2 %copy-start.3 = (bf16[256,6144]{1,0:T(8,128)(2,1)S(1)}, bf16[256,6144]{1,0:T(8,128)(2,1)}, u32[]{:S(2)}) copy-start(bf16[256,6144]{1,0:T(8,128)(2,1)} %refs_0_.1) | copy-start | bytes 9437188
  108.9 6.8 %collective-permute-start.15 = (bf16[24,6144]{1,0:T(8,128)(2,1)S(1)}, bf16[24,6144]{1,0:T(8,128)(2,1)S(1)}, u32[]{:S(2)}, u32[]{:S(2)}) collective-permute-start(bf16[24,6144]{1,0:T(8,128)(2,1)S(1)} %get-tuple-element.73), channel_id=1, source_target_pairs={{0,24},{1,25},{2,26},{3,27},{4,7},{5,4},{6,5},{7,6},{8,0},{9,1},{1... | collective-permute-start | bytes 884744 | tf_op jit(solution)/shard_map/ppermute | solution.py:48
  110.6 9.9 %collective-permute-start.16 = (bf16[24,6144]{1,0:T(8,128)(2,1)S(1)}, bf16[24,6144]{1,0:T(8,128)(2,1)S(1)}, u32[]{:S(2)}, u32[]{:S(2)}) collective-permute-start(bf16[24,6144]{1,0:T(8,128)(2,1)S(1)} %get-tuple-element.74), channel_id=1, source_target_pairs={{0,8},{1,9},{2,10},{3,11},{4,5},{5,6},{6,7},{7,4},{8,16},{9,17},{1... | collective-permute-start | bytes 884744 | tf_op jit(solution)/shard_map/ppermute | solution.py:48
  110.6 9.9 %collective-permute-start.17 = (bf16[24,6144]{1,0:T(8,128)(2,1)S(1)}, bf16[24,6144]{1,0:T(8,128)(2,1)S(1)}, u32[]{:S(2)}, u32[]{:S(2)}) collective-permute-start(bf16[24,6144]{1,0:T(8,128)(2,1)S(1)} %get-tuple-element.75), channel_id=1, source_target_pairs={{0,16},{1,17},{2,18},{3,19},{4,6},{5,7},{6,4},{7,5},{8,24},{9,25},... | collective-permute-start | bytes 884744 | tf_op jit(solution)/shard_map/ppermute | solution.py:48
  120.5 40.8 %collective-permute-start.25 = (bf16[256,6144]{1,0:T(8,128)(2,1)}, bf16[256,6144]{1,0:T(8,128)(2,1)}, u32[]{:S(2)}, u32[]{:S(2)}) collective-permute-start(bf16[256,6144]{1,0:T(8,128)(2,1)} %collective-permute-done.18.refs_2_), channel_id=1, source_target_pairs={{0,4},{4,0},{8,12},{12,8},{16,20},{20,16},{24,28},{28,24},{1,5},{5... | collective-permute-start | bytes 9437192 | tf_op jit(solution)/shard_map/ppermute | solution.py:60
  149.7 4.8 %collective-permute-start.19 = (bf16[8,6144]{1,0:T(8,128)(2,1)S(1)}, bf16[8,6144]{1,0:T(8,128)(2,1)S(1)}, u32[]{:S(2)}, u32[]{:S(2)}) collective-permute-start(bf16[8,6144]{1,0:T(8,128)(2,1)S(1)} %shard_map.141.refs_0_), channel_id=1, source_target_pairs={{0,64},{4,12},{8,72},{12,20},{16,80},{20,28},{24,88},{28,4},{32,96... | collective-permute-start | bytes 294920 | tf_op jit(solution)/shard_map/ppermute | solution.py:56
  149.8 5.3 %collective-permute-start.20 = (bf16[8,6144]{1,0:T(8,128)(2,1)S(1)}, bf16[8,6144]{1,0:T(8,128)(2,1)S(1)}, u32[]{:S(2)}, u32[]{:S(2)}) collective-permute-start(bf16[8,6144]{1,0:T(8,128)(2,1)S(1)} %shard_map.141.refs_0_), channel_id=1, source_target_pairs={{0,192},{4,28},{8,200},{12,4},{16,208},{20,12},{24,216},{28,20},{3... | collective-permute-start | bytes 294920 | tf_op jit(solution)/shard_map/ppermute | solution.py:56
  152.5 5.0 %collective-permute-start.21 = (bf16[8,6144]{1,0:T(8,128)(2,1)S(1)}, bf16[8,6144]{1,0:T(8,128)(2,1)S(1)}, u32[]{:S(2)}, u32[]{:S(2)}) collective-permute-start(bf16[8,6144]{1,0:T(8,128)(2,1)S(1)} %shard_map.141.refs_0_), channel_id=1, source_target_pairs={{0,128},{4,20},{8,136},{12,28},{16,144},{20,4},{24,152},{28,12},{3... | collective-permute-start | bytes 294920 | tf_op jit(solution)/shard_map/ppermute | solution.py:56
  157.5 11.5 %collective-permute-start.22 = (bf16[32,6144]{1,0:T(8,128)(2,1)S(1)}, bf16[32,6144]{1,0:T(8,128)(2,1)}, u32[]{:S(2)}, u32[]{:S(2)}) collective-permute-start(bf16[32,6144]{1,0:T(8,128)(2,1)S(1)} %shard_map.142.r0), channel_id=1, source_target_pairs={{0,8},{4,68},{8,16},{12,76},{16,24},{20,84},{24,0},{28,92},{32,40}... | collective-permute-start | bytes 1179656 | tf_op jit(solution)/shard_map/ppermute | solution.py:56
  157.6 19.1 %collective-permute-start.23 = (bf16[32,6144]{1,0:T(8,128)(2,1)S(1)}, bf16[32,6144]{1,0:T(8,128)(2,1)}, u32[]{:S(2)}, u32[]{:S(2)}) collective-permute-start(bf16[32,6144]{1,0:T(8,128)(2,1)S(1)} %shard_map.142.r0), channel_id=1, source_target_pairs={{0,24},{4,196},{8,0},{12,204},{16,8},{20,212},{24,16},{28,220},{32... | collective-permute-start | bytes 1179656 | tf_op jit(solution)/shard_map/ppermute | solution.py:56
  161.2 16.5 %collective-permute-start.24 = (bf16[32,6144]{1,0:T(8,128)(2,1)S(1)}, bf16[32,6144]{1,0:T(8,128)(2,1)}, u32[]{:S(2)}, u32[]{:S(2)}) collective-permute-start(bf16[32,6144]{1,0:T(8,128)(2,1)S(1)} %shard_map.142.r0), channel_id=1, source_target_pairs={{0,16},{4,132},{8,24},{12,140},{16,0},{20,148},{24,8},{28,156},{32... | collective-permute-start | bytes 1179656 | tf_op jit(solution)/shard_map/ppermute | solution.py:56
  161.3 16.4 %copy-start.10 = (s32[1,512]{1,0:T(1,128)S(1)}, s32[1,512]{1,0:T(1,128)}, u32[]{:S(2)}) copy-start(s32[1,512]{1,0:T(1,128)} %targets_ref.1) | copy-start | bytes 6148
  177.7 23.9 %copy-start.11 = (s32[1,16]{1,0:T(1,128)S(1)}, s32[1,16]{1,0:T(1,128)}, u32[]{:S(2)}) copy-start(s32[1,16]{1,0:T(1,128)} %lengths_ref.1) | copy-start | bytes 196
  177.7 23.9 %copy-start.12 = (s32[1,16]{1,0:T(1,128)S(1)}, s32[1,16]{1,0:T(1,128)}, u32[]{:S(2)}) copy-start(s32[1,16]{1,0:T(1,128)} %questions_ref.1) | copy-start | bytes 196

commit v5 on v4

--- a/solution.py
+++ b/solution.py
@@ -60,8 +60,8 @@
     return lax.ppermute(array, "vocab", [(v, v ^ 1) for v in range(NX * NC)])
 
 
-def swap_planes(array):
-    return lax.ppermute(array, "expert", [(z, z ^ 1) for z in range(NZ)])
+def z_shift(array, shift):
+    return lax.ppermute(array, "expert", [(z, (z + shift) % NZ) for z in range(NZ)])
 
 
 def gather_four(block, shift_by):
@@ -243,15 +243,19 @@
     after_ref[...] = part[half:]
 
 
-def near_kernel(hidden_ref, down_a, down_b, got_before, got_after, own_ref, before_ref, after_ref):
-    part = contract(hidden_ref[...], down_a[...], down_b[...])
+def near_kernel(hidden_ref, down_a, down_b, got_before, got_after, before_ref, after_ref):
+    rows = before_ref.shape[0]
+    half = rows // 2
+    part = contract(hidden_ref[rows:], down_a[...], down_b[...])
+    before_ref[:half] = (part[:half] + got_before[...].astype(f32)).astype(bf16)
+    before_ref[half:] = part[half:rows].astype(bf16)
+    after_ref[:half] = part[rows : rows + half].astype(bf16)
+    after_ref[half:] = (part[rows + half :] + got_after[...].astype(f32)).astype(bf16)
+
+
+def own_kernel(hidden_ref, down_a, down_b, own_ref):
     rows = own_ref.shape[0]
-    half = rows // 2
-    own_ref[...] = part[:rows].astype(bf16)
-    before_ref[:half] = (part[rows : rows + half] + got_before[...].astype(f32)).astype(bf16)
-    before_ref[half:] = part[rows + half : 2 * rows].astype(bf16)
-    after_ref[:half] = part[2 * rows : 2 * rows + half].astype(bf16)
-    after_ref[half:] = (part[2 * rows + half :] + got_after[...].astype(f32)).astype(bf16)
+    own_ref[...] = contract(hidden_ref[:rows], down_a[...], down_b[...]).astype(bf16)
 
 
 def down_call(kernel, hidden, downs, got, out_rows):
@@ -336,7 +340,8 @@
     )(weights, rows, resid, gain)
 
 
-def head_kernel(place_ref, targets_ref, r0, r1, r2, r3, t0, t1, t2, t3, out_ref, total):
+def head_kernel(place_ref, targets_ref, r0, r1, r2, r3, *refs):
+    *tables, out_ref, total = refs
     step = pl.program_id(0)
 
     @pl.when(step == 0)
@@ -344,11 +349,13 @@
         total[...] = jnp.zeros_like(total)
 
     rows = jnp.concatenate([r0[...], r1[...], r2[...], r3[...]])
-    share = t0.shape[0]
-    for j, table in enumerate((t0, t1, t2, t3)):
-        total[j * share : (j + 1) * share] += lax.dot_general(
+    share = tables[0].shape[0]
+    at = 0
+    for table in tables:
+        total[at : at + table.shape[0]] += lax.dot_general(
             table[...], rows, (((1,), (1,)), ((), ())), preferred_element_type=f32
         )
+        at += table.shape[0]
 
     @pl.when(step == pl.num_programs(0) - 1)
     def _():
@@ -370,10 +377,16 @@
         here = place == iota((count, count), 1)
         wanted = jnp.sum(jnp.where(same, wanted, 0), axis=0, keepdims=True)
         logits = total[...]
+        half = share // 2
         entry = iota((4 * share, 1), 0)
-        table, offset = entry // share, entry % share
-        z_of = jnp.where(table < 2, z, z + 1 - 2 * (z % 2))
-        c_of = jnp.where(table % 2 == 0, c, 1 - c)
+        part = entry // half
+        shared, upper = part >= 4, part >= 6
+        z_of = jnp.where(shared, (z + NZ + jnp.where(upper, 1, -1)) % NZ, z)
+        other = jnp.where(shared, part % 2, jnp.where(part >= 2, 1, 0))
+        c_of = c + other * (1 - 2 * c)
+        offset = jnp.where(
+            shared, entry % half + jnp.where(upper, half, 0), entry % share
+        )
         entry_id = ((z_of * NX + x) * NC + c_of) * share + offset
         top = jnp.max(logits, axis=0, keepdims=True)
         spread = jnp.sum(jnp.exp(logits - top), axis=0, keepdims=True)
@@ -398,7 +411,7 @@
         grid=(width // depth,),
         in_specs=[whole, pl.BlockSpec(targets.shape, lambda k: (0, 0))]
         + [pl.BlockSpec((rows[0].shape[0], depth), lambda k: (0, k))] * 4
-        + [pl.BlockSpec((share, depth), lambda k: (0, k))] * 4,
+        + [pl.BlockSpec((t.shape[0], depth), lambda k: (0, k)) for t in tables],
         out_specs=pl.BlockSpec((NZ * NX * NC, 2, count), lambda k: (0, 0, 0)),
         out_shape=shape((NZ * NX * NC, 2, count), f32),
         scratch_shapes=[pltpu.VMEM((4 * share, count), f32)],
@@ -536,7 +549,9 @@
         arrived, other_gate, other_up, other_down, other_head, lm_head, router
     )
     combine_weights = slot_gates(expert_ids[0], resid[0], moe_gain.reshape(1, -1), router.T)
-    pair_head = swap_planes(own_head)
+    head_half = own_head.shape[0] // 2
+    low_head = z_shift(own_head[:head_half], 1)
+    high_head = z_shift(own_head[head_half:], -1)
 
     def first(block, shift):
         return plane_shift(block, False, shift)
@@ -563,13 +578,16 @@
     to_before, to_after = down_call(far_kernel, far_hidden, downs, (), (half, half))
     got_before = second(to_before, -1)
     got_after = second(to_after, 1)
-    own_part, before_part, after_part = down_call(
-        near_kernel, near_hidden, downs, (got_before, got_after), (rows, rows, rows)
-    )
+    got_before, low_head, high_head = tied(got_before, low_head, high_head)
+    before_part, after_part = down_call(
+        near_kernel, near_hidden, downs, (got_before, got_after), (rows, rows)
+    )
+    (own_part,) = down_call(own_kernel, near_hidden, downs, (), (rows,))
+    own_part, low_head, high_head = tied(own_part, low_head, high_head)
+    low_other = swap_cores(low_head)
+    high_other = swap_cores(high_head)
     pieces = line_sum([own_part, second(before_part, -1), second(after_part, 1)])
     back = (first(pieces[1], -1), first(pieces[2], 1), first(pieces[3], 2))
-    *back, pair_head = tied(*back, pair_head)
-    pair_other = swap_cores(pair_head)
     outgoing = expert_sum([pieces[0], *back])
 
     returned = lax.all_to_all(outgoing, "expert", split_axis=0, concat_axis=0, tiled=True)
@@ -577,7 +595,7 @@
 
     head_line = stack(gather_four(normed_out, lambda b, s: head_shift(b, False, s)))
     head_rows = gather_four(head_line, lambda b, s: head_shift(b, True, s))
-    stats = head(place, target_ids, head_rows, hold([lm_head, other_head, pair_head, pair_other]))
+    stats = head(place, target_ids, head_rows, hold([lm_head, other_head, low_head, low_other, high_head, high_other]))
     gathered = lax.all_to_all(stats, ("expert", "vocab"), 0, 0, tiled=True)
     return finish(place, gathered, choice_len, choice_question, resid.shape[1])
 

time: 205 us -> 207 us (level)
  blocking collectives: 55.2 us -> 63.8 us
  waiting for transfers between devices: 72.5 us -> 67.7 us
    all_to_all x1, blocking collectives: 17.8 us -> 30.3 us  [on_device(): gathered = lax.all_to_all(stats, ('expert', 'vocab'), 0, 0, tiled=True)]
    ppermute x14, waiting for transfers between devices: 55.2 us -> 45.4 us  [plane_shift(): return lax.ppermute(array, ('vocab', 'batch'), perm)]
    ppermute x6, waiting for transfers between devices: 17.4 us -> 22 us  [head_shift(): return lax.ppermute(array, ('expert', 'vocab'), perm)]
    all_to_all x1, blocking collectives: 17.6 us -> 13.3 us  [on_device(): lax.all_to_all(outgoing, 'expert', split_axis=0, concat_axis=0, tiled=True)]
    ppermute x5 -> x6, starting transfers between devices: 14.1 us -> 10.2 us  [swap_cores(): return lax.ppermute(array, 'vocab', [(v, v ^ 1) for v in range(NX * NC)])]
    ppermute x1 -> x2, starting transfers between devices: 0.28 us -> 2.75 us  [z_shift(): lax.ppermute(array, 'expert', [(z, (z + shift) % NZ) for z in range(NZ)])]
    pallas_call x2 -> x3, Pallas kernels: 6.09 us -> 7.87 us  [down_call(): pl.pallas_call(kernel, grid=(width // tile,), in_specs=[pl.BlockSpec(hidd...]
  transfers between devices with their start and end apart: 26 -> 28, of which waited for: 18 -> 18; matrix products, arithmetic and copies ran while one was open for 0% -> 1% of each run, Pallas kernels for 12% -> 11%
where the time goes in v5:
time: 207 us; the launch traced here: 206 us
  waiting for transfers between devices  67.7 us (33%)
  blocking collectives  63.8 us (31%)
  starting transfers between devices  36 us (17%)
  Pallas kernels  34.7 us (17%)
  local copies, waits for them, and re-layouts  2.86 us (1%)
    ppermute x14, waiting for transfers between devices, plane_shift(): return lax.ppermute(array, ('vocab', 'batch'), perm)  45.4 us
    all_to_all x1, blocking collectives, on_device(): gathered = lax.all_to_all(stats, ('expert', 'vocab'), 0, 0, tiled=True)  30.3 us
    ppermute x6, waiting for transfers between devices, head_shift(): return lax.ppermute(array, ('expert', 'vocab'), perm)  22 us
    all_to_all x1, blocking collectives, on_device(): lax.all_to_all(buckets, 'expert', split_axis=0, concat_axis=0, tiled=True)  20.3 us
    ppermute x14, starting transfers between devices, plane_shift(): return lax.ppermute(array, ('vocab', 'batch'), perm)  16.2 us
    all_to_all x1, blocking collectives, on_device(): lax.all_to_all(outgoing, 'expert', split_axis=0, concat_axis=0, tiled=True)  13.3 us
    ppermute x6, starting transfers between devices, swap_cores(): return lax.ppermute(array, 'vocab', [(v, v ^ 1) for v in range(NX * NC)])  10.2 us
    pallas_call x2, Pallas kernels, expand(): pl.pallas_call(functools.partial(expand_kernel, count=count), grid=(width...  7.89 us
  transfers between devices with their start and end apart: 28, of which 18 were waited for; matrix products, arithmetic and copies ran while one was open for 1% of the time, Pallas kernels for 11%

profile of v5, /device:TPU:1, one launch (start us, length us, event | category | flops | bytes accessed | tf_op | source)
XLA Modules:
  0.0 206.0 jit_solution(15785548113434963923)
XLA Ops:
  0.6 3.3 %collective-permute-start.2 = (bf16[256,6144]{1,0:T(8,128)(2,1)}, bf16[256,6144]{1,0:T(8,128)(2,1)S(1)}, u32[]{:S(2)}, u32[]{:S(2)}) collective-permute-start(bf16[256,6144]{1,0:T(8,128)(2,1)} %bitcast.11), channel_id=1, source_target_pairs={{0,4},{4,0},{8,12},{12,8},{16,20},{20,16},{24,28},{28,24},{1,5},{5... | collective-permute-start | bytes 9437192 | tf_op jit(solution)/shard_map/ppermute | solution.py:60
  4.6 0.8 copy.14.ids_ref
  5.3 0.9 copy-done.5
  6.2 0.7 copy-done.7
  7.5 20.3 %all_to_all.15.refs_0_ = bf16[8,3,6144]{2,1,0:T(4,128)(2,1)S(1)} all-to-all(bf16[8,3,6144]{2,1,0:T(4,128)(2,1)S(1)} %shard_map.131), channel_id=1, replica_groups=mesh['expert'=8,'vocab'=8,'batch'=4] {'expert'}, dimensions={0} | all-to-all | bytes 589824 | tf_op jit(solution)/shard_map/all_to_all | solution.py:547
  27.8 1.4 collective-permute-start.4
  29.2 1.5 collective-permute-start.5
  30.7 1.6 collective-permute-start.6
  32.2 3.8 %collective-permute-done.4.refs_1_ = bf16[8,3,6144]{2,1,0:T(4,128)(2,1)S(1)} collective-permute-done((bf16[8,3,6144]{2,1,0:T(4,128)(2,1)S(1)}, bf16[8,3,6144]{2,1,0:T(4,128)(2,1)S(1)}, u32[]{:S(2)}, u32[]{:S(2)}) %collective-permute-start.4) | collective-permute-done | bytes 294944 | tf_op jit(solution)/shard_map/ppermute | solution.py:48
  36.1 5.3 %collective-permute-done.6.refs_3_ = bf16[8,3,6144]{2,1,0:T(4,128)(2,1)S(1)} collective-permute-done((bf16[8,3,6144]{2,1,0:T(4,128)(2,1)S(1)}, bf16[8,3,6144]{2,1,0:T(4,128)(2,1)S(1)}, u32[]{:S(2)}, u32[]{:S(2)}) %collective-permute-start.6) | collective-permute-done | bytes 294944 | tf_op jit(solution)/shard_map/ppermute | solution.py:48
  42.1 1.0 collective-permute-start.7
  43.2 1.7 collective-permute-start.8
  45.6 2.4 %collective-permute-start.13 = (bf16[128,6144]{1,0:T(8,128)(2,1)S(1)}, bf16[128,6144]{1,0:T(8,128)(2,1)}, u32[]{:S(2)}, u32[]{:S(2)}) collective-permute-start(bf16[128,6144]{1,0:T(8,128)(2,1)S(1)} %get-tuple-element.92), channel_id=1, source_target_pairs={{0,224},{32,0},{64,32},{96,64},{128,96},{160,128},{192,160},{224,1... | collective-permute-start | bytes 4718600 | tf_op jit(solution)/shard_map/ppermute | solution.py:64
  48.4 3.3 %shard_map.134 = (bf16[6144,256]{1,0:T(8,128)(2,1)S(1)}, bf16[6144,256]{1,0:T(8,128)(2,1)S(1)}, bf16[6144,256]{1,0:T(8,128)(2,1)S(1)}, bf16[6144,256]{1,0:T(8,128)(2,1)S(1)}) custom-call(bf16[6144,256]{1,0:T(8,128)(2,1)S(1)} %bitcast.16, bf16[6144,256]{1,0:T(8,128)(2,1)S(1)} %bitcast.18, bf16[6144,256]{1,0:T(8,128)(2,1)} %collective-permute-done.refs_2_, ...), custom_call_target="tpu_custom_call" | custom-call | bytes 12582912 | tf_op jit(solution)/shard_map/pallas_call | solution.py:437
  51.7 7.1 %collective-permute-done.7.refs_1_ = bf16[96,6144]{1,0:T(8,128)(2,1)S(1)} collective-permute-done((bf16[96,6144]{1,0:T(8,128)(2,1)S(1)}, bf16[96,6144]{1,0:T(8,128)(2,1)S(1)}, u32[]{:S(2)}, u32[]{:S(2)}) %collective-permute-start.7) | collective-permute-done | bytes 1179680 | tf_op jit(solution)/shard_map/ppermute | solution.py:48
  58.9 2.8 %collective-permute-start.10 = (bf16[48,6144]{1,0:T(8,128)(2,1)S(1)}, bf16[48,6144]{1,0:T(8,128)(2,1)S(1)}, u32[]{:S(2)}, u32[]{:S(2)}) collective-permute-start(bf16[48,6144]{1,0:T(8,128)(2,1)S(1)} %slice.13), channel_id=1, source_target_pairs={{0,3},{1,0},{2,1},{3,2},{4,28},{5,29},{6,30},{7,31},{8,11},{9,8},{... | collective-permute-start | bytes 1769480 | tf_op jit(solution)/shard_map/ppermute | solution.py:48
  61.8 5.1 %shard_map.135.hidden_ref = bf16[288,512]{1,0:T(8,128)(2,1)S(1)} custom-call(bf16[96,6144]{1,0:T(8,128)(2,1)S(1)} %shard_map.132.refs_0_, bf16[96,6144]{1,0:T(8,128)(2,1)S(1)} %collective-permute-done.7.refs_1_, bf16[96,6144]{1,0:T(8,128)(2,1)S(1)} %collective-permute-done.8.refs_2_, bf16[6144,256]{1,0:T(8,128)(2,1)S(1)} %get-tuple-element.62.refs_3_.refs_2_, ...), custom_call_target="tpu_custom_call" | custom-call | flops 3623878656 | bytes 12582912 | tf_op jit(solution)/shard_map/pallas_call | solution.py:219
  66.9 1.6 collective-permute-done.10.refs_1_
  68.5 3.6 %collective-permute-done.9.refs_0_ = bf16[48,6144]{1,0:T(8,128)(2,1)S(1)} collective-permute-done((bf16[48,6144]{1,0:T(8,128)(2,1)S(1)}, bf16[48,6144]{1,0:T(8,128)(2,1)S(1)}, u32[]{:S(2)}, u32[]{:S(2)}) %collective-permute-start.9) | collective-permute-done | bytes 589856 | tf_op jit(solution)/shard_map/ppermute | solution.py:48
  72.1 2.8 %shard_map.137.hidden_ref = bf16[96,512]{1,0:T(8,128)(2,1)S(1)} custom-call(bf16[48,6144]{1,0:T(8,128)(2,1)S(1)} %collective-permute-done.9.refs_0_, bf16[48,6144]{1,0:T(8,128)(2,1)S(1)} %collective-permute-done.10.refs_1_, bf16[6144,256]{1,0:T(8,128)(2,1)S(1)} %get-tuple-element.62.refs_3_.refs_2_, bf16[6144,256]{1,0:T(8,128)(2,1)S(1)} %get-tuple-element.63.refs_4_.refs_3_, ...), custom_call_target="tpu_custom_call" | custom-call | flops 1207959552 | bytes 12582912 | tf_op jit(solution)/shard_map/pallas_call | solution.py:219
  75.0 2.4 %shard_map.138 = (bf16[48,6144]{1,0:T(8,128)(2,1)S(1)}, bf16[48,6144]{1,0:T(8,128)(2,1)S(1)}) custom-call(bf16[96,512]{1,0:T(8,128)(2,1)S(1)} %shard_map.137.hidden_ref, bf16[256,6144]{1,0:T(8,128)(2,1)S(1)} %bitcast.12, bf16[256,6144]{1,0:T(8,128)(2,1)S(1)} %collective-permute-done.2.down_b), custom_call_target="tpu_custom_call" | custom-call | flops 603979776 | bytes 6291456 | tf_op jit(solution)/shard_map/pallas_call | solution.py:264
  77.7 1.5 collective-permute-start.14
  79.4 7.3 %collective-permute-done.11.got_before = bf16[48,6144]{1,0:T(8,128)(2,1)S(1)} collective-permute-done((bf16[48,6144]{1,0:T(8,128)(2,1)S(1)}, bf16[48,6144]{1,0:T(8,128)(2,1)S(1)}, u32[]{:S(2)}, u32[]{:S(2)}) %collective-permute-start.11) | collective-permute-done | bytes 589856 | tf_op jit(solution)/shard_map/ppermute | solution.py:48
  86.7 1.3 collective-permute-done.14.got_after
  88.0 3.1 %shard_map.139 = (bf16[96,6144]{1,0:T(8,128)(2,1)S(1)}, bf16[96,6144]{1,0:T(8,128)(2,1)S(1)}) custom-call(bf16[288,512]{1,0:T(8,128)(2,1)S(1)} %shard_map.135.hidden_ref, bf16[256,6144]{1,0:T(8,128)(2,1)S(1)} %bitcast.13, bf16[256,6144]{1,0:T(8,128)(2,1)S(1)} %collective-permute-done.2.down_b, bf16[48,6144]{1,0:T(8,128)(2,1)S(1)} %collective-permute-done.11.got_before, ...), custom_call_target="tpu_custom_call" | custom-call | flops 1811939328 | bytes 6291456 | tf_op jit(solution)/shard_map/pallas_call | solution.py:264
  91.1 1.5 collective-permute-start.16
  92.6 2.4 %shard_map.136.own_ref = bf16[96,6144]{1,0:T(8,128)(2,1)S(1)} custom-call(bf16[288,512]{1,0:T(8,128)(2,1)S(1)} %shard_map.135.hidden_ref, bf16[256,6144]{1,0:T(8,128)(2,1)S(1)} %bitcast.14, bf16[256,6144]{1,0:T(8,128)(2,1)S(1)} %collective-permute-done.2.down_b), custom_call_target="tpu_custom_call" | custom-call | flops 1811939328 | bytes 6291456 | tf_op jit(solution)/shard_map/pallas_call | solution.py:264
  95.0 6.2 %collective-permute-start.26 = (bf16[128,6144]{1,0:T(8,128)(2,1)}, bf16[128,6144]{1,0:T(8,128)(2,1)}, u32[]{:S(2)}, u32[]{:S(2)}) collective-permute-start(bf16[128,6144]{1,0:T(8,128)(2,1)} %collective-permute-done.12.refs_2_), channel_id=1, source_target_pairs={{0,4},{4,0},{8,12},{12,8},{16,20},{20,16},{24,28},{28,24},{1,5},{5... | collective-permute-start | bytes 4718600 | tf_op jit(solution)/shard_map/ppermute | solution.py:60
  101.2 5.2 %collective-permute-done.15.before_ref = bf16[96,6144]{1,0:T(8,128)(2,1)S(1)} collective-permute-done((bf16[96,6144]{1,0:T(8,128)(2,1)S(1)}, bf16[96,6144]{1,0:T(8,128)(2,1)S(1)}, u32[]{:S(2)}, u32[]{:S(2)}) %collective-permute-start.15) | collective-permute-done | bytes 1179680 | tf_op jit(solution)/shard_map/ppermute | solution.py:48
  106.5 1.3 collective-permute-done.16.after_ref
  107.8 0.9 shard_map.140
  108.6 1.7 collective-permute-start.17
  110.3 1.3 collective-permute-start.19
  111.6 3.7 %collective-permute-done.17.b = bf16[24,6144]{1,0:T(8,128)(2,1)S(1)} collective-permute-done((bf16[24,6144]{1,0:T(8,128)(2,1)S(1)}, bf16[24,6144]{1,0:T(8,128)(2,1)S(1)}, u32[]{:S(2)}, u32[]{:S(2)}) %collective-permute-start.17) | collective-permute-done | bytes 294944 | tf_op jit(solution)/shard_map/ppermute | solution.py:48
  115.3 5.0 %collective-permute-done.18.c = bf16[24,6144]{1,0:T(8,128)(2,1)S(1)} collective-permute-done((bf16[24,6144]{1,0:T(8,128)(2,1)S(1)}, bf16[24,6144]{1,0:T(8,128)(2,1)S(1)}, u32[]{:S(2)}, u32[]{:S(2)}) %collective-permute-start.18) | collective-permute-done | bytes 294944 | tf_op jit(solution)/shard_map/ppermute | solution.py:48
  120.6 13.3 %all_to_all.16.rows_ref = bf16[8,3,6144]{2,1,0:T(4,128)(2,1)S(1)} all-to-all(bf16[8,3,6144]{2,1,0:T(4,128)(2,1)S(1)} %shard_map.141), channel_id=1, replica_groups=mesh['expert'=8,'vocab'=8,'batch'=4] {'expert'}, dimensions={0} | all-to-all | bytes 589824 | tf_op jit(solution)/shard_map/all_to_all | solution.py:593
  133.9 1.0 shard_map.142.refs_0_
  134.9 0.7 collective-permute-start.20
  135.7 2.0 collective-permute-start.21
  137.7 2.3 %collective-permute-done.20.refs_1_ = bf16[8,6144]{1,0:T(8,128)(2,1)S(1)} collective-permute-done((bf16[8,6144]{1,0:T(8,128)(2,1)S(1)}, bf16[8,6144]{1,0:T(8,128)(2,1)S(1)}, u32[]{:S(2)}, u32[]{:S(2)}) %collective-permute-start.20) | collective-permute-done | bytes 98336 | tf_op jit(solution)/shard_map/ppermute | solution.py:56
  140.3 2.4 %collective-permute-done.22.refs_3_ = bf16[8,6144]{1,0:T(8,128)(2,1)S(1)} collective-permute-done((bf16[8,6144]{1,0:T(8,128)(2,1)S(1)}, bf16[8,6144]{1,0:T(8,128)(2,1)S(1)}, u32[]{:S(2)}, u32[]{:S(2)}) %collective-permute-start.22) | collective-permute-done | bytes 98336 | tf_op jit(solution)/shard_map/ppermute | solution.py:56
  142.9 3.6 %collective-permute-start.24 = (bf16[32,6144]{1,0:T(8,128)(2,1)S(1)}, bf16[32,6144]{1,0:T(8,128)(2,1)}, u32[]{:S(2)}, u32[]{:S(2)}) collective-permute-start(bf16[32,6144]{1,0:T(8,128)(2,1)S(1)} %shard_map.143.r0), channel_id=1, source_target_pairs={{0,24},{4,196},{8,0},{12,204},{16,8},{20,212},{24,16},{28,220},{32... | collective-permute-start | bytes 1179656 | tf_op jit(solution)/shard_map/ppermute | solution.py:56
  147.0 4.0 %shard_map.144 = (bf16[256,6144]{1,0:T(8,128)(2,1)S(1)}, bf16[256,6144]{1,0:T(8,128)(2,1)S(1)}, bf16[128,6144]{1,0:T(8,128)(2,1)S(1)}, bf16[128,6144]{1,0:T(8,12...) custom-call(bf16[256,6144]{1,0:T(8,128)(2,1)S(1)} %copy-done.2, ...), custom_call_target="tpu_custom_call" | custom-call | bytes 12582912 | tf_op jit(solution)/shard_map/pallas_call | solution.py:437
  151.0 11.0 %collective-permute-done.23.r1 = bf16[32,6144]{1,0:T(8,128)(2,1)} collective-permute-done((bf16[32,6144]{1,0:T(8,128)(2,1)S(1)}, bf16[32,6144]{1,0:T(8,128)(2,1)}, u32[]{:S(2)}, u32[]{:S(2)}) %collective-permute-start.23) | collective-permute-done | bytes 393248 | tf_op jit(solution)/shard_map/ppermute | solution.py:56
  162.0 6.0 %collective-permute-done.24.r2 = bf16[32,6144]{1,0:T(8,128)(2,1)} collective-permute-done((bf16[32,6144]{1,0:T(8,128)(2,1)S(1)}, bf16[32,6144]{1,0:T(8,128)(2,1)}, u32[]{:S(2)}, u32[]{:S(2)}) %collective-permute-start.24) | collective-permute-done | bytes 393248 | tf_op jit(solution)/shard_map/ppermute | solution.py:56
  168.1 6.3 %shard_map.145 = f32[64,2,128]{2,1,0:T(2,128)S(1)} custom-call(s32[3]{0:T(128)S(1)} %pad_add_fusion.place_ref, s32[1,512]{1,0:T(1,128)S(1)} %copy-done.11, bf16[32,6144]{1,0:T(8,128)(2,1)S(1)} %shard_map.143.r0, bf16[32,6144]{1,0:T(8,128)(2,1)} %collective-permute-done.23.r1, bf16[32,6144]{1,0:T(8,128)(2,1)} %collective-permute-done.24.r2, ...), custom_call_target="tpu_custom_call" | custom-call | flops 1610612736 | bytes 12582912 | tf_op jit(solution)/shard_map/pallas_call | solution.py:409
  174.3 30.3 %all_to_all.17.stats_ref = f32[64,2,128]{2,1,0:T(2,128)S(1)} all-to-all(f32[64,2,128]{2,1,0:T(2,128)S(1)} %shard_map.145), channel_id=1, replica_groups=mesh['expert'=8,'vocab'=8,'batch'=4] {'expert','vocab'}, dimensions={0} | all-to-all | bytes 131072 | tf_op jit(solution)/shard_map/all_to_all | solution.py:599
  204.6 1.4 shard_map.146
  (60 shorter events, 5.3 us)
Async XLA Ops:
  0.6 27.2 %collective-permute-start.2 = (bf16[256,6144]{1,0:T(8,128)(2,1)}, bf16[256,6144]{1,0:T(8,128)(2,1)S(1)}, u32[]{:S(2)}, u32[]{:S(2)}) collective-permute-start(bf16[256,6144]{1,0:T(8,128)(2,1)} %bitcast.11), channel_id=1, source_target_pairs={{0,4},{4,0},{8,12},{12,8},{16,20},{20,16},{24,28},{28,24},{1,5},{5... | collective-permute-start | bytes 9437192 | tf_op jit(solution)/shard_map/ppermute | solution.py:60
  4.0 23.8 %collective-permute-start = (bf16[6144,256]{1,0:T(8,128)(2,1)}, bf16[6144,256]{1,0:T(8,128)(2,1)}, u32[]{:S(2)}, u32[]{:S(2)}) collective-permute-start(bf16[6144,256]{1,0:T(8,128)(2,1)} %bitcast.15), channel_id=1, source_target_pairs={{0,4},{4,0},{8,12},{12,8},{16,20},{20,16},{24,28},{28,24},{1,5},{5... | collective-permute-start | bytes 9437192 | tf_op jit(solution)/shard_map/ppermute | solution.py:60
  4.1 23.7 %collective-permute-start.1 = (bf16[6144,256]{1,0:T(8,128)(2,1)}, bf16[6144,256]{1,0:T(8,128)(2,1)}, u32[]{:S(2)}, u32[]{:S(2)}) collective-permute-start(bf16[6144,256]{1,0:T(8,128)(2,1)} %bitcast.17), channel_id=1, source_target_pairs={{0,4},{4,0},{8,12},{12,8},{16,20},{20,16},{24,28},{28,24},{1,5},{5... | collective-permute-start | bytes 9437192 | tf_op jit(solution)/shard_map/ppermute | solution.py:60
  4.5 23.3 %collective-permute-start.3 = (bf16[256,6144]{1,0:T(8,128)(2,1)}, bf16[256,6144]{1,0:T(8,128)(2,1)}, u32[]{:S(2)}, u32[]{:S(2)}) collective-permute-start(bf16[256,6144]{1,0:T(8,128)(2,1)} %refs_0_.1), channel_id=1, source_target_pairs={{0,4},{4,0},{8,12},{12,8},{16,20},{20,16},{24,28},{28,24},{1,5},{5... | collective-permute-start | bytes 9437192 | tf_op jit(solution)/shard_map/ppermute | solution.py:60
  5.3 0.9 copy-start.5
  6.2 0.7 copy-start.7
  7.5 37.3 %copy-start.1 = (bf16[256,6144]{1,0:T(8,128)(2,1)S(1)}, bf16[256,6144]{1,0:T(8,128)(2,1)}, u32[]{:S(2)}) copy-start(bf16[256,6144]{1,0:T(8,128)(2,1)} %refs_0_.1) | copy-start | bytes 9437188
  27.8 8.2 %collective-permute-start.4 = (bf16[8,3,6144]{2,1,0:T(4,128)(2,1)S(1)}, bf16[8,3,6144]{2,1,0:T(4,128)(2,1)S(1)}, u32[]{:S(2)}, u32[]{:S(2)}) collective-permute-start(bf16[8,3,6144]{2,1,0:T(4,128)(2,1)S(1)} %all_to_all.15.refs_0_), channel_id=1, source_target_pairs={{0,8},{1,9},{2,10},{3,11},{4,5},{5,6},{6,7},{7,4},{8,16},{9,17},{1... | collective-permute-start | bytes 884744 | tf_op jit(solution)/shard_map/ppermute | solution.py:48
  29.2 6.9 %collective-permute-start.5 = (bf16[8,3,6144]{2,1,0:T(4,128)(2,1)S(1)}, bf16[8,3,6144]{2,1,0:T(4,128)(2,1)S(1)}, u32[]{:S(2)}, u32[]{:S(2)}) collective-permute-start(bf16[8,3,6144]{2,1,0:T(4,128)(2,1)S(1)} %all_to_all.15.refs_0_), channel_id=1, source_target_pairs={{0,24},{1,25},{2,26},{3,27},{4,7},{5,4},{6,5},{7,6},{8,0},{9,1},{1... | collective-permute-start | bytes 884744 | tf_op jit(solution)/shard_map/ppermute | solution.py:48
  30.7 10.8 %collective-permute-start.6 = (bf16[8,3,6144]{2,1,0:T(4,128)(2,1)S(1)}, bf16[8,3,6144]{2,1,0:T(4,128)(2,1)S(1)}, u32[]{:S(2)}, u32[]{:S(2)}) collective-permute-start(bf16[8,3,6144]{2,1,0:T(4,128)(2,1)S(1)} %all_to_all.15.refs_0_), channel_id=1, source_target_pairs={{0,16},{1,17},{2,18},{3,19},{4,6},{5,7},{6,4},{7,5},{8,24},{9,25},... | collective-permute-start | bytes 884744 | tf_op jit(solution)/shard_map/ppermute | solution.py:48
  42.1 5.9 %copy-start.6 = (bf16[1,8,6144]{2,1,0:T(8,128)(2,1)S(1)}, bf16[1,8,6144]{2,1,0:T(8,128)(2,1)}, u32[]{:S(2)}) copy-start(bf16[1,8,6144]{2,1,0:T(8,128)(2,1)} %param.12) | copy-start | bytes 294916
  42.1 5.9 %copy-start.8 = (f32[6144]{0:T(1024)S(1)}, f32[6144]{0:T(1024)}, u32[]{:S(2)}) copy-start(f32[6144]{0:T(1024)} %param.13) | copy-start | bytes 73732
  42.1 5.9 %copy-start.9 = (bf16[6144,8]{0,1:T(8,128)(2,1)S(1)}, bf16[6144,8]{0,1:T(8,128)(2,1)}, u32[]{:S(2)}) copy-start(bf16[6144,8]{0,1:T(8,128)(2,1)} %param.15) | copy-start | bytes 294916
  42.1 16.7 %collective-permute-start.7 = (bf16[96,6144]{1,0:T(8,128)(2,1)S(1)}, bf16[96,6144]{1,0:T(8,128)(2,1)S(1)}, u32[]{:S(2)}, u32[]{:S(2)}) collective-permute-start(bf16[96,6144]{1,0:T(8,128)(2,1)S(1)} %shard_map.132.refs_0_), channel_id=1, source_target_pairs={{0,1},{1,2},{2,3},{3,0},{4,12},{5,13},{6,14},{7,15},{8,9},{9,10},{... | collective-permute-start | bytes 3538952 | tf_op jit(solution)/shard_map/ppermute | solution.py:48
  43.2 15.7 %collective-permute-start.8 = (bf16[96,6144]{1,0:T(8,128)(2,1)S(1)}, bf16[96,6144]{1,0:T(8,128)(2,1)S(1)}, u32[]{:S(2)}, u32[]{:S(2)}) collective-permute-start(bf16[96,6144]{1,0:T(8,128)(2,1)S(1)} %shard_map.132.refs_0_), channel_id=1, source_target_pairs={{0,3},{1,0},{2,1},{3,2},{4,28},{5,29},{6,30},{7,31},{8,11},{9,8},{... | collective-permute-start | bytes 3538952 | tf_op jit(solution)/shard_map/ppermute | solution.py:48
  44.9 3.5 %copy-start.3 = (bf16[1,6144,256]{2,1,0:T(8,128)(2,1)S(1)}, bf16[1,6144,256]{2,1,0:T(8,128)(2,1)}, u32[]{:S(2)}) copy-start(bf16[1,6144,256]{2,1,0:T(8,128)(2,1)} %param.16) | copy-start | bytes 9437188
  44.9 3.5 %copy-start.4 = (bf16[1,6144,256]{2,1,0:T(8,128)(2,1)S(1)}, bf16[1,6144,256]{2,1,0:T(8,128)(2,1)}, u32[]{:S(2)}) copy-start(bf16[1,6144,256]{2,1,0:T(8,128)(2,1)} %param.17) | copy-start | bytes 9437188
  45.2 34.2 %collective-permute-start.12 = (bf16[128,6144]{1,0:T(8,128)(2,1)S(1)}, bf16[128,6144]{1,0:T(8,128)(2,1)}, u32[]{:S(2)}, u32[]{:S(2)}) collective-permute-start(bf16[128,6144]{1,0:T(8,128)(2,1)S(1)} %get-tuple-element.93), channel_id=1, source_target_pairs={{0,32},{32,64},{64,96},{96,128},{128,160},{160,192},{192,224},{224... | collective-permute-start | bytes 4718600 | tf_op jit(solution)/shard_map/ppermute | solution.py:64
  45.6 33.8 %collective-permute-start.13 = (bf16[128,6144]{1,0:T(8,128)(2,1)S(1)}, bf16[128,6144]{1,0:T(8,128)(2,1)}, u32[]{:S(2)}, u32[]{:S(2)}) collective-permute-start(bf16[128,6144]{1,0:T(8,128)(2,1)S(1)} %get-tuple-element.92), channel_id=1, source_target_pairs={{0,224},{32,0},{64,32},{96,64},{128,96},{160,128},{192,160},{224,1... | collective-permute-start | bytes 4718600 | tf_op jit(solution)/shard_map/ppermute | solution.py:64
  58.9 9.6 %collective-permute-start.10 = (bf16[48,6144]{1,0:T(8,128)(2,1)S(1)}, bf16[48,6144]{1,0:T(8,128)(2,1)S(1)}, u32[]{:S(2)}, u32[]{:S(2)}) collective-permute-start(bf16[48,6144]{1,0:T(8,128)(2,1)S(1)} %slice.13), channel_id=1, source_target_pairs={{0,3},{1,0},{2,1},{3,2},{4,28},{5,29},{6,30},{7,31},{8,11},{9,8},{... | collective-permute-start | bytes 1769480 | tf_op jit(solution)/shard_map/ppermute | solution.py:48
  61.7 10.4 %collective-permute-start.9 = (bf16[48,6144]{1,0:T(8,128)(2,1)S(1)}, bf16[48,6144]{1,0:T(8,128)(2,1)S(1)}, u32[]{:S(2)}, u32[]{:S(2)}) collective-permute-start(bf16[48,6144]{1,0:T(8,128)(2,1)S(1)} %slice.12), channel_id=1, source_target_pairs={{0,1},{1,2},{2,3},{3,0},{4,12},{5,13},{6,14},{7,15},{8,9},{9,10},{... | collective-permute-start | bytes 1769480 | tf_op jit(solution)/shard_map/ppermute | solution.py:48
  72.1 2.8 %copy-start = (bf16[1,256,6144]{2,1,0:T(8,128)(2,1)S(1)}, bf16[1,256,6144]{2,1,0:T(8,128)(2,1)}, u32[]{:S(2)}) copy-start(bf16[1,256,6144]{2,1,0:T(8,128)(2,1)} %param.18) | copy-start | bytes 9437188
  77.4 9.3 %collective-permute-start.11 = (bf16[48,6144]{1,0:T(8,128)(2,1)S(1)}, bf16[48,6144]{1,0:T(8,128)(2,1)S(1)}, u32[]{:S(2)}, u32[]{:S(2)}) collective-permute-start(bf16[48,6144]{1,0:T(8,128)(2,1)S(1)} %get-tuple-element.70), channel_id=1, source_target_pairs={{0,3},{1,0},{2,1},{3,2},{4,28},{5,29},{6,30},{7,31},{8,11},{9,8},{... | collective-permute-start | bytes 1769480 | tf_op jit(solution)/shard_map/ppermute | solution.py:48
  77.7 10.3 %collective-permute-start.14 = (bf16[48,6144]{1,0:T(8,128)(2,1)S(1)}, bf16[48,6144]{1,0:T(8,128)(2,1)S(1)}, u32[]{:S(2)}, u32[]{:S(2)}) collective-permute-start(bf16[48,6144]{1,0:T(8,128)(2,1)S(1)} %get-tuple-element.76), channel_id=1, source_target_pairs={{0,1},{1,2},{2,3},{3,0},{4,12},{5,13},{6,14},{7,15},{8,9},{9,10},{... | collective-permute-start | bytes 1769480 | tf_op jit(solution)/shard_map/ppermute | solution.py:48
  91.0 15.4 %collective-permute-start.15 = (bf16[96,6144]{1,0:T(8,128)(2,1)S(1)}, bf16[96,6144]{1,0:T(8,128)(2,1)S(1)}, u32[]{:S(2)}, u32[]{:S(2)}) collective-permute-start(bf16[96,6144]{1,0:T(8,128)(2,1)S(1)} %get-tuple-element.77), channel_id=1, source_target_pairs={{0,3},{1,0},{2,1},{3,2},{4,28},{5,29},{6,30},{7,31},{8,11},{9,8},{... | collective-permute-start | bytes 3538952 | tf_op jit(solution)/shard_map/ppermute | solution.py:48
  91.1 16.6 %collective-permute-start.16 = (bf16[96,6144]{1,0:T(8,128)(2,1)S(1)}, bf16[96,6144]{1,0:T(8,128)(2,1)S(1)}, u32[]{:S(2)}, u32[]{:S(2)}) collective-permute-start(bf16[96,6144]{1,0:T(8,128)(2,1)S(1)} %get-tuple-element.78), channel_id=1, source_target_pairs={{0,1},{1,2},{2,3},{3,0},{4,12},{5,13},{6,14},{7,15},{8,9},{9,10},{... | collective-permute-start | bytes 3538952 | tf_op jit(solution)/shard_map/ppermute | solution.py:48
  95.0 52.0 %collective-permute-start.26 = (bf16[128,6144]{1,0:T(8,128)(2,1)}, bf16[128,6144]{1,0:T(8,128)(2,1)}, u32[]{:S(2)}, u32[]{:S(2)}) collective-permute-start(bf16[128,6144]{1,0:T(8,128)(2,1)} %collective-permute-done.12.refs_2_), channel_id=1, source_target_pairs={{0,4},{4,0},{8,12},{12,8},{16,20},{20,16},{24,28},{28,24},{1,5},{5... | collective-permute-start | bytes 4718600 | tf_op jit(solution)/shard_map/ppermute | solution.py:60
  101.1 45.9 %collective-permute-start.27 = (bf16[128,6144]{1,0:T(8,128)(2,1)}, bf16[128,6144]{1,0:T(8,128)(2,1)}, u32[]{:S(2)}, u32[]{:S(2)}) collective-permute-start(bf16[128,6144]{1,0:T(8,128)(2,1)} %collective-permute-done.13.refs_4_), channel_id=1, source_target_pairs={{0,4},{4,0},{8,12},{12,8},{16,20},{20,16},{24,28},{28,24},{1,5},{5... | collective-permute-start | bytes 4718600 | tf_op jit(solution)/shard_map/ppermute | solution.py:60
  108.6 25.3 %copy-start.10 = (f32[6144]{0:T(1024)S(1)}, f32[6144]{0:T(1024)}, u32[]{:S(2)}) copy-start(f32[6144]{0:T(1024)} %param.14) | copy-start | bytes 73732
  108.6 6.7 %collective-permute-start.17 = (bf16[24,6144]{1,0:T(8,128)(2,1)S(1)}, bf16[24,6144]{1,0:T(8,128)(2,1)S(1)}, u32[]{:S(2)}, u32[]{:S(2)}) collective-permute-start(bf16[24,6144]{1,0:T(8,128)(2,1)S(1)} %get-tuple-element.80), channel_id=1, source_target_pairs={{0,24},{1,25},{2,26},{3,27},{4,7},{5,4},{6,5},{7,6},{8,0},{9,1},{1... | collective-permute-start | bytes 884744 | tf_op jit(solution)/shard_map/ppermute | solution.py:48
  110.3 9.9 %collective-permute-start.18 = (bf16[24,6144]{1,0:T(8,128)(2,1)S(1)}, bf16[24,6144]{1,0:T(8,128)(2,1)S(1)}, u32[]{:S(2)}, u32[]{:S(2)}) collective-permute-start(bf16[24,6144]{1,0:T(8,128)(2,1)S(1)} %get-tuple-element.81), channel_id=1, source_target_pairs={{0,8},{1,9},{2,10},{3,11},{4,5},{5,6},{6,7},{7,4},{8,16},{9,17},{1... | collective-permute-start | bytes 884744 | tf_op jit(solution)/shard_map/ppermute | solution.py:48
  110.3 9.9 %collective-permute-start.19 = (bf16[24,6144]{1,0:T(8,128)(2,1)S(1)}, bf16[24,6144]{1,0:T(8,128)(2,1)S(1)}, u32[]{:S(2)}, u32[]{:S(2)}) collective-permute-start(bf16[24,6144]{1,0:T(8,128)(2,1)S(1)} %get-tuple-element.82), channel_id=1, source_target_pairs={{0,16},{1,17},{2,18},{3,19},{4,6},{5,7},{6,4},{7,5},{8,24},{9,25},... | collective-permute-start | bytes 884744 | tf_op jit(solution)/shard_map/ppermute | solution.py:48
  120.3 26.8 %copy-start.2 = (bf16[256,6144]{1,0:T(8,128)(2,1)S(1)}, bf16[256,6144]{1,0:T(8,128)(2,1)}, u32[]{:S(2)}) copy-start(bf16[256,6144]{1,0:T(8,128)(2,1)} %refs_0_.1) | copy-start | bytes 9437188
  134.9 5.1 %collective-permute-start.20 = (bf16[8,6144]{1,0:T(8,128)(2,1)S(1)}, bf16[8,6144]{1,0:T(8,128)(2,1)S(1)}, u32[]{:S(2)}, u32[]{:S(2)}) collective-permute-start(bf16[8,6144]{1,0:T(8,128)(2,1)S(1)} %shard_map.142.refs_0_), channel_id=1, source_target_pairs={{0,64},{4,12},{8,72},{12,20},{16,80},{20,28},{24,88},{28,4},{32,96... | collective-permute-start | bytes 294920 | tf_op jit(solution)/shard_map/ppermute | solution.py:56
  135.7 4.7 %collective-permute-start.21 = (bf16[8,6144]{1,0:T(8,128)(2,1)S(1)}, bf16[8,6144]{1,0:T(8,128)(2,1)S(1)}, u32[]{:S(2)}, u32[]{:S(2)}) collective-permute-start(bf16[8,6144]{1,0:T(8,128)(2,1)S(1)} %shard_map.142.refs_0_), channel_id=1, source_target_pairs={{0,192},{4,28},{8,200},{12,4},{16,208},{20,12},{24,216},{28,20},{3... | collective-permute-start | bytes 294920 | tf_op jit(solution)/shard_map/ppermute | solution.py:56
  137.7 5.0 %collective-permute-start.22 = (bf16[8,6144]{1,0:T(8,128)(2,1)S(1)}, bf16[8,6144]{1,0:T(8,128)(2,1)S(1)}, u32[]{:S(2)}, u32[]{:S(2)}) collective-permute-start(bf16[8,6144]{1,0:T(8,128)(2,1)S(1)} %shard_map.142.refs_0_), channel_id=1, source_target_pairs={{0,128},{4,20},{8,136},{12,28},{16,144},{20,4},{24,152},{28,12},{3... | collective-permute-start | bytes 294920 | tf_op jit(solution)/shard_map/ppermute | solution.py:56
  142.8 19.2 %collective-permute-start.23 = (bf16[32,6144]{1,0:T(8,128)(2,1)S(1)}, bf16[32,6144]{1,0:T(8,128)(2,1)}, u32[]{:S(2)}, u32[]{:S(2)}) collective-permute-start(bf16[32,6144]{1,0:T(8,128)(2,1)S(1)} %shard_map.143.r0), channel_id=1, source_target_pairs={{0,8},{4,68},{8,16},{12,76},{16,24},{20,84},{24,0},{28,92},{32,40}... | collective-permute-start | bytes 1179656 | tf_op jit(solution)/shard_map/ppermute | solution.py:56
  142.9 25.1 %collective-permute-start.24 = (bf16[32,6144]{1,0:T(8,128)(2,1)S(1)}, bf16[32,6144]{1,0:T(8,128)(2,1)}, u32[]{:S(2)}, u32[]{:S(2)}) collective-permute-start(bf16[32,6144]{1,0:T(8,128)(2,1)S(1)} %shard_map.143.r0), channel_id=1, source_target_pairs={{0,24},{4,196},{8,0},{12,204},{16,8},{20,212},{24,16},{28,220},{32... | collective-permute-start | bytes 1179656 | tf_op jit(solution)/shard_map/ppermute | solution.py:56
  146.5 21.6 %collective-permute-start.25 = (bf16[32,6144]{1,0:T(8,128)(2,1)S(1)}, bf16[32,6144]{1,0:T(8,128)(2,1)}, u32[]{:S(2)}, u32[]{:S(2)}) collective-permute-start(bf16[32,6144]{1,0:T(8,128)(2,1)S(1)} %shard_map.143.r0), channel_id=1, source_target_pairs={{0,16},{4,132},{8,24},{12,140},{16,0},{20,148},{24,8},{28,156},{32... | collective-permute-start | bytes 1179656 | tf_op jit(solution)/shard_map/ppermute | solution.py:56
  147.0 21.0 %copy-start.11 = (s32[1,512]{1,0:T(1,128)S(1)}, s32[1,512]{1,0:T(1,128)}, u32[]{:S(2)}) copy-start(s32[1,512]{1,0:T(1,128)} %targets_ref.1) | copy-start | bytes 6148
  168.0 36.6 %copy-start.12 = (s32[1,16]{1,0:T(1,128)S(1)}, s32[1,16]{1,0:T(1,128)}, u32[]{:S(2)}) copy-start(s32[1,16]{1,0:T(1,128)} %lengths_ref.1) | copy-start | bytes 196
  168.0 36.6 %copy-start.13 = (s32[1,16]{1,0:T(1,128)S(1)}, s32[1,16]{1,0:T(1,128)}, u32[]{:S(2)}) copy-start(s32[1,16]{1,0:T(1,128)} %questions_ref.1) | copy-start | bytes 196

commit v6 on v5

--- a/solution.py
+++ b/solution.py
@@ -50,7 +50,7 @@
 
 def head_shift(array, second, shift):
     def axis_of(place):
-        return ("z", 2, NZ) if (place["c"] == 0) != second else ("x", 1, NX)
+        return ("x", 1, NX) if second else ("z", 2, NZ)
 
     perm = two_axis_perm(NZ * NX * NC, head_coords, axis_of, shift)
     return lax.ppermute(array, ("expert", "vocab"), perm)
@@ -363,8 +363,8 @@
         count = rows.shape[0]
         row = iota((count, 1), 0)
         outer, inner, token = rel_step(row // 32), rel_step(row // 8 % 4), row % 8
-        z_half = (z // 2 + 4 + jnp.where(c == 0, inner, outer)) % 4
-        x_seen = (x + 4 + jnp.where(c == 0, outer, inner)) % 4
+        z_half = (z // 2 + 4 + inner) % 4
+        x_seen = (x + 4 + outer) % 4
         place = (z_half * NX + x_seen) * 8 + token
         position = ((2 * z_half + z % 2) * NX + x_seen) * (NC * 8) + c * 8 + token
         targets = targets_ref[...]

time: 207 us -> 200 us (0.966)
  waiting for transfers between devices: 67.7 us -> 58.7 us
  blocking collectives: 63.8 us -> 66.4 us
    ppermute x6, waiting for transfers between devices: 22 us -> 13 us  [head_shift(): return lax.ppermute(array, ('expert', 'vocab'), perm)]
    all_to_all x1, blocking collectives: 30.3 us -> 32.8 us  [on_device(): gathered = lax.all_to_all(stats, ('expert', 'vocab'), 0, 0, tiled=True)]
  transfers between devices with their start and end apart: 28 -> 28, of which waited for: 18 -> 16; matrix products, arithmetic and copies ran while one was open for 1% -> 1% of each run, Pallas kernels for 11% -> 12%
where the time goes in v6:
time: 200 us; the launch traced here: 199 us
  blocking collectives  66.4 us (33%)
  waiting for transfers between devices  58.7 us (29%)
  starting transfers between devices  35.8 us (18%)
  Pallas kernels  34.6 us (17%)
  local copies, waits for them, and re-layouts  2.86 us (1%)
    ppermute x14, waiting for transfers between devices, plane_shift(): return lax.ppermute(array, ('vocab', 'batch'), perm)  45.4 us
    all_to_all x1, blocking collectives, on_device(): gathered = lax.all_to_all(stats, ('expert', 'vocab'), 0, 0, tiled=True)  32.8 us
    all_to_all x1, blocking collectives, on_device(): lax.all_to_all(buckets, 'expert', split_axis=0, concat_axis=0, tiled=True)  20.3 us
    ppermute x14, starting transfers between devices, plane_shift(): return lax.ppermute(array, ('vocab', 'batch'), perm)  16.2 us
    all_to_all x1, blocking collectives, on_device(): lax.all_to_all(outgoing, 'expert', split_axis=0, concat_axis=0, tiled=True)  13.3 us
    ppermute x6, waiting for transfers between devices, head_shift(): return lax.ppermute(array, ('expert', 'vocab'), perm)  13 us
    ppermute x6, starting transfers between devices, swap_cores(): return lax.ppermute(array, 'vocab', [(v, v ^ 1) for v in range(NX * NC)])  10.2 us
    pallas_call x2, Pallas kernels, expand(): pl.pallas_call(functools.partial(expand_kernel, count=count), grid=(width...  7.89 us
  transfers between devices with their start and end apart: 28, of which 16 were waited for; matrix products, arithmetic and copies ran while one was open for 1% of the time, Pallas kernels for 12%

profile of v6, /device:TPU:1, one launch (start us, length us, event | category | flops | bytes accessed | tf_op | source)
XLA Modules:
  0.0 199.3 jit_solution(10856386956460961261)
XLA Ops:
  0.6 3.3 %collective-permute-start.2 = (bf16[256,6144]{1,0:T(8,128)(2,1)}, bf16[256,6144]{1,0:T(8,128)(2,1)S(1)}, u32[]{:S(2)}, u32[]{:S(2)}) collective-permute-start(bf16[256,6144]{1,0:T(8,128)(2,1)} %bitcast.11), channel_id=1, source_target_pairs={{0,4},{4,0},{8,12},{12,8},{16,20},{20,16},{24,28},{28,24},{1,5},{5... | collective-permute-start | bytes 9437192 | tf_op jit(solution)/shard_map/ppermute | solution.py:60
  4.6 0.8 copy.14.ids_ref
  5.3 0.9 copy-done.5
  6.2 0.7 copy-done.7
  7.0 0.6 shard_map.131
  7.5 20.3 %all_to_all.15.refs_0_ = bf16[8,3,6144]{2,1,0:T(4,128)(2,1)S(1)} all-to-all(bf16[8,3,6144]{2,1,0:T(4,128)(2,1)S(1)} %shard_map.131), channel_id=1, replica_groups=mesh['expert'=8,'vocab'=8,'batch'=4] {'expert'}, dimensions={0} | all-to-all | bytes 589824 | tf_op jit(solution)/shard_map/all_to_all | solution.py:547
  27.8 1.4 collective-permute-start.4
  29.2 1.5 collective-permute-start.5
  30.7 1.6 collective-permute-start.6
  32.2 3.8 %collective-permute-done.4.refs_1_ = bf16[8,3,6144]{2,1,0:T(4,128)(2,1)S(1)} collective-permute-done((bf16[8,3,6144]{2,1,0:T(4,128)(2,1)S(1)}, bf16[8,3,6144]{2,1,0:T(4,128)(2,1)S(1)}, u32[]{:S(2)}, u32[]{:S(2)}) %collective-permute-start.4) | collective-permute-done | bytes 294944 | tf_op jit(solution)/shard_map/ppermute | solution.py:48
  36.1 5.3 %collective-permute-done.6.refs_3_ = bf16[8,3,6144]{2,1,0:T(4,128)(2,1)S(1)} collective-permute-done((bf16[8,3,6144]{2,1,0:T(4,128)(2,1)S(1)}, bf16[8,3,6144]{2,1,0:T(4,128)(2,1)S(1)}, u32[]{:S(2)}, u32[]{:S(2)}) %collective-permute-start.6) | collective-permute-done | bytes 294944 | tf_op jit(solution)/shard_map/ppermute | solution.py:48
  41.4 0.6 shard_map.132.refs_0_
  42.1 1.0 collective-permute-start.7
  43.2 1.7 collective-permute-start.8
  45.6 2.4 %collective-permute-start.13 = (bf16[128,6144]{1,0:T(8,128)(2,1)S(1)}, bf16[128,6144]{1,0:T(8,128)(2,1)}, u32[]{:S(2)}, u32[]{:S(2)}) collective-permute-start(bf16[128,6144]{1,0:T(8,128)(2,1)S(1)} %get-tuple-element.92), channel_id=1, source_target_pairs={{0,224},{32,0},{64,32},{96,64},{128,96},{160,128},{192,160},{224,1... | collective-permute-start | bytes 4718600 | tf_op jit(solution)/shard_map/ppermute | solution.py:64
  48.4 3.3 %shard_map.134 = (bf16[6144,256]{1,0:T(8,128)(2,1)S(1)}, bf16[6144,256]{1,0:T(8,128)(2,1)S(1)}, bf16[6144,256]{1,0:T(8,128)(2,1)S(1)}, bf16[6144,256]{1,0:T(8,128)(2,1)S(1)}) custom-call(bf16[6144,256]{1,0:T(8,128)(2,1)S(1)} %bitcast.16, bf16[6144,256]{1,0:T(8,128)(2,1)S(1)} %bitcast.18, bf16[6144,256]{1,0:T(8,128)(2,1)} %collective-permute-done.refs_2_, ...), custom_call_target="tpu_custom_call" | custom-call | bytes 12582912 | tf_op jit(solution)/shard_map/pallas_call | solution.py:437
  51.7 7.1 %collective-permute-done.7.refs_1_ = bf16[96,6144]{1,0:T(8,128)(2,1)S(1)} collective-permute-done((bf16[96,6144]{1,0:T(8,128)(2,1)S(1)}, bf16[96,6144]{1,0:T(8,128)(2,1)S(1)}, u32[]{:S(2)}, u32[]{:S(2)}) %collective-permute-start.7) | collective-permute-done | bytes 1179680 | tf_op jit(solution)/shard_map/ppermute | solution.py:48
  58.9 2.8 %collective-permute-start.10 = (bf16[48,6144]{1,0:T(8,128)(2,1)S(1)}, bf16[48,6144]{1,0:T(8,128)(2,1)S(1)}, u32[]{:S(2)}, u32[]{:S(2)}) collective-permute-start(bf16[48,6144]{1,0:T(8,128)(2,1)S(1)} %slice.13), channel_id=1, source_target_pairs={{0,3},{1,0},{2,1},{3,2},{4,28},{5,29},{6,30},{7,31},{8,11},{9,8},{... | collective-permute-start | bytes 1769480 | tf_op jit(solution)/shard_map/ppermute | solution.py:48
  61.8 5.1 %shard_map.135.hidden_ref = bf16[288,512]{1,0:T(8,128)(2,1)S(1)} custom-call(bf16[96,6144]{1,0:T(8,128)(2,1)S(1)} %shard_map.132.refs_0_, bf16[96,6144]{1,0:T(8,128)(2,1)S(1)} %collective-permute-done.7.refs_1_, bf16[96,6144]{1,0:T(8,128)(2,1)S(1)} %collective-permute-done.8.refs_2_, bf16[6144,256]{1,0:T(8,128)(2,1)S(1)} %get-tuple-element.62.refs_3_.refs_2_, ...), custom_call_target="tpu_custom_call" | custom-call | flops 3623878656 | bytes 12582912 | tf_op jit(solution)/shard_map/pallas_call | solution.py:219
  66.9 1.6 collective-permute-done.10.refs_1_
  68.5 3.6 %collective-permute-done.9.refs_0_ = bf16[48,6144]{1,0:T(8,128)(2,1)S(1)} collective-permute-done((bf16[48,6144]{1,0:T(8,128)(2,1)S(1)}, bf16[48,6144]{1,0:T(8,128)(2,1)S(1)}, u32[]{:S(2)}, u32[]{:S(2)}) %collective-permute-start.9) | collective-permute-done | bytes 589856 | tf_op jit(solution)/shard_map/ppermute | solution.py:48
  72.1 2.8 %shard_map.137.hidden_ref = bf16[96,512]{1,0:T(8,128)(2,1)S(1)} custom-call(bf16[48,6144]{1,0:T(8,128)(2,1)S(1)} %collective-permute-done.9.refs_0_, bf16[48,6144]{1,0:T(8,128)(2,1)S(1)} %collective-permute-done.10.refs_1_, bf16[6144,256]{1,0:T(8,128)(2,1)S(1)} %get-tuple-element.62.refs_3_.refs_2_, bf16[6144,256]{1,0:T(8,128)(2,1)S(1)} %get-tuple-element.63.refs_4_.refs_3_, ...), custom_call_target="tpu_custom_call" | custom-call | flops 1207959552 | bytes 12582912 | tf_op jit(solution)/shard_map/pallas_call | solution.py:219
  75.0 2.4 %shard_map.138 = (bf16[48,6144]{1,0:T(8,128)(2,1)S(1)}, bf16[48,6144]{1,0:T(8,128)(2,1)S(1)}) custom-call(bf16[96,512]{1,0:T(8,128)(2,1)S(1)} %shard_map.137.hidden_ref, bf16[256,6144]{1,0:T(8,128)(2,1)S(1)} %bitcast.12, bf16[256,6144]{1,0:T(8,128)(2,1)S(1)} %collective-permute-done.2.down_b), custom_call_target="tpu_custom_call" | custom-call | flops 603979776 | bytes 6291456 | tf_op jit(solution)/shard_map/pallas_call | solution.py:264
  77.7 1.5 collective-permute-start.14
  79.4 7.3 %collective-permute-done.11.got_before = bf16[48,6144]{1,0:T(8,128)(2,1)S(1)} collective-permute-done((bf16[48,6144]{1,0:T(8,128)(2,1)S(1)}, bf16[48,6144]{1,0:T(8,128)(2,1)S(1)}, u32[]{:S(2)}, u32[]{:S(2)}) %collective-permute-start.11) | collective-permute-done | bytes 589856 | tf_op jit(solution)/shard_map/ppermute | solution.py:48
  86.7 1.3 collective-permute-done.14.got_after
  88.0 3.1 %shard_map.139 = (bf16[96,6144]{1,0:T(8,128)(2,1)S(1)}, bf16[96,6144]{1,0:T(8,128)(2,1)S(1)}) custom-call(bf16[288,512]{1,0:T(8,128)(2,1)S(1)} %shard_map.135.hidden_ref, bf16[256,6144]{1,0:T(8,128)(2,1)S(1)} %bitcast.13, bf16[256,6144]{1,0:T(8,128)(2,1)S(1)} %collective-permute-done.2.down_b, bf16[48,6144]{1,0:T(8,128)(2,1)S(1)} %collective-permute-done.11.got_before, ...), custom_call_target="tpu_custom_call" | custom-call | flops 1811939328 | bytes 6291456 | tf_op jit(solution)/shard_map/pallas_call | solution.py:264
  91.1 1.5 collective-permute-start.16
  92.6 2.4 %shard_map.136.own_ref = bf16[96,6144]{1,0:T(8,128)(2,1)S(1)} custom-call(bf16[288,512]{1,0:T(8,128)(2,1)S(1)} %shard_map.135.hidden_ref, bf16[256,6144]{1,0:T(8,128)(2,1)S(1)} %bitcast.14, bf16[256,6144]{1,0:T(8,128)(2,1)S(1)} %collective-permute-done.2.down_b), custom_call_target="tpu_custom_call" | custom-call | flops 1811939328 | bytes 6291456 | tf_op jit(solution)/shard_map/pallas_call | solution.py:264
  95.0 6.2 %collective-permute-start.26 = (bf16[128,6144]{1,0:T(8,128)(2,1)}, bf16[128,6144]{1,0:T(8,128)(2,1)}, u32[]{:S(2)}, u32[]{:S(2)}) collective-permute-start(bf16[128,6144]{1,0:T(8,128)(2,1)} %collective-permute-done.12.refs_2_), channel_id=1, source_target_pairs={{0,4},{4,0},{8,12},{12,8},{16,20},{20,16},{24,28},{28,24},{1,5},{5... | collective-permute-start | bytes 4718600 | tf_op jit(solution)/shard_map/ppermute | solution.py:60
  101.2 5.2 %collective-permute-done.15.before_ref = bf16[96,6144]{1,0:T(8,128)(2,1)S(1)} collective-permute-done((bf16[96,6144]{1,0:T(8,128)(2,1)S(1)}, bf16[96,6144]{1,0:T(8,128)(2,1)S(1)}, u32[]{:S(2)}, u32[]{:S(2)}) %collective-permute-start.15) | collective-permute-done | bytes 1179680 | tf_op jit(solution)/shard_map/ppermute | solution.py:48
  106.5 1.3 collective-permute-done.16.after_ref
  107.8 0.9 shard_map.140
  108.6 1.7 collective-permute-start.17
  110.3 1.3 collective-permute-start.19
  111.6 3.7 %collective-permute-done.17.b = bf16[24,6144]{1,0:T(8,128)(2,1)S(1)} collective-permute-done((bf16[24,6144]{1,0:T(8,128)(2,1)S(1)}, bf16[24,6144]{1,0:T(8,128)(2,1)S(1)}, u32[]{:S(2)}, u32[]{:S(2)}) %collective-permute-start.17) | collective-permute-done | bytes 294944 | tf_op jit(solution)/shard_map/ppermute | solution.py:48
  115.3 5.0 %collective-permute-done.18.c = bf16[24,6144]{1,0:T(8,128)(2,1)S(1)} collective-permute-done((bf16[24,6144]{1,0:T(8,128)(2,1)S(1)}, bf16[24,6144]{1,0:T(8,128)(2,1)S(1)}, u32[]{:S(2)}, u32[]{:S(2)}) %collective-permute-start.18) | collective-permute-done | bytes 294944 | tf_op jit(solution)/shard_map/ppermute | solution.py:48
  120.6 13.3 %all_to_all.16.rows_ref = bf16[8,3,6144]{2,1,0:T(4,128)(2,1)S(1)} all-to-all(bf16[8,3,6144]{2,1,0:T(4,128)(2,1)S(1)} %shard_map.141), channel_id=1, replica_groups=mesh['expert'=8,'vocab'=8,'batch'=4] {'expert'}, dimensions={0} | all-to-all | bytes 589824 | tf_op jit(solution)/shard_map/all_to_all | solution.py:593
  133.9 1.0 shard_map.142.refs_0_
  135.0 3.6 %collective-permute-start.21 = (bf16[8,6144]{1,0:T(8,128)(2,1)S(1)}, bf16[8,6144]{1,0:T(8,128)(2,1)S(1)}, u32[]{:S(2)}, u32[]{:S(2)}) collective-permute-start(bf16[8,6144]{1,0:T(8,128)(2,1)S(1)} %shard_map.142.refs_0_), channel_id=1, source_target_pairs={{0,192},{4,196},{8,200},{12,204},{16,208},{20,212},{24,216},{28,22... | collective-permute-start | bytes 294920 | tf_op jit(solution)/shard_map/ppermute | solution.py:56
  138.9 4.6 %collective-permute-done.20.refs_1_ = bf16[8,6144]{1,0:T(8,128)(2,1)S(1)} collective-permute-done((bf16[8,6144]{1,0:T(8,128)(2,1)S(1)}, bf16[8,6144]{1,0:T(8,128)(2,1)S(1)}, u32[]{:S(2)}, u32[]{:S(2)}) %collective-permute-start.20) | collective-permute-done | bytes 98336 | tf_op jit(solution)/shard_map/ppermute | solution.py:56
  143.5 3.0 %collective-permute-done.22.refs_3_ = bf16[8,6144]{1,0:T(8,128)(2,1)S(1)} collective-permute-done((bf16[8,6144]{1,0:T(8,128)(2,1)S(1)}, bf16[8,6144]{1,0:T(8,128)(2,1)S(1)}, u32[]{:S(2)}, u32[]{:S(2)}) %collective-permute-start.22) | collective-permute-done | bytes 98336 | tf_op jit(solution)/shard_map/ppermute | solution.py:56
  147.2 2.2 %collective-permute-start.24 = (bf16[32,6144]{1,0:T(8,128)(2,1)S(1)}, bf16[32,6144]{1,0:T(8,128)(2,1)}, u32[]{:S(2)}, u32[]{:S(2)}) collective-permute-start(bf16[32,6144]{1,0:T(8,128)(2,1)S(1)} %shard_map.143.r0), channel_id=1, source_target_pairs={{0,24},{4,28},{8,0},{12,4},{16,8},{20,12},{24,16},{28,20},{32,56},... | collective-permute-start | bytes 1179656 | tf_op jit(solution)/shard_map/ppermute | solution.py:56
  149.4 4.0 %shard_map.144 = (bf16[256,6144]{1,0:T(8,128)(2,1)S(1)}, bf16[256,6144]{1,0:T(8,128)(2,1)S(1)}, bf16[128,6144]{1,0:T(8,128)(2,1)S(1)}, bf16[128,6144]{1,0:T(8,12...) custom-call(bf16[256,6144]{1,0:T(8,128)(2,1)S(1)} %copy-done.2, ...), custom_call_target="tpu_custom_call" | custom-call | bytes 12582912 | tf_op jit(solution)/shard_map/pallas_call | solution.py:437
  153.4 5.4 %collective-permute-done.23.r1 = bf16[32,6144]{1,0:T(8,128)(2,1)} collective-permute-done((bf16[32,6144]{1,0:T(8,128)(2,1)S(1)}, bf16[32,6144]{1,0:T(8,128)(2,1)}, u32[]{:S(2)}, u32[]{:S(2)}) %collective-permute-start.23) | collective-permute-done | bytes 393248 | tf_op jit(solution)/shard_map/ppermute | solution.py:56
  158.9 6.2 %shard_map.145 = f32[64,2,128]{2,1,0:T(2,128)S(1)} custom-call(s32[3]{0:T(128)S(1)} %pad_add_fusion.place_ref, s32[1,512]{1,0:T(1,128)S(1)} %copy-done.11, bf16[32,6144]{1,0:T(8,128)(2,1)S(1)} %shard_map.143.r0, bf16[32,6144]{1,0:T(8,128)(2,1)} %collective-permute-done.23.r1, bf16[32,6144]{1,0:T(8,128)(2,1)} %collective-permute-done.24.r2, ...), custom_call_target="tpu_custom_call" | custom-call | flops 1610612736 | bytes 12582912 | tf_op jit(solution)/shard_map/pallas_call | solution.py:409
  165.1 32.8 %all_to_all.17.stats_ref = f32[64,2,128]{2,1,0:T(2,128)S(1)} all-to-all(f32[64,2,128]{2,1,0:T(2,128)S(1)} %shard_map.145), channel_id=1, replica_groups=mesh['expert'=8,'vocab'=8,'batch'=4] {'expert','vocab'}, dimensions={0} | all-to-all | bytes 131072 | tf_op jit(solution)/shard_map/all_to_all | solution.py:599
  197.9 1.4 shard_map.146
  (60 shorter events, 4.2 us)
Async XLA Ops:
  0.6 27.2 %collective-permute-start.2 = (bf16[256,6144]{1,0:T(8,128)(2,1)}, bf16[256,6144]{1,0:T(8,128)(2,1)S(1)}, u32[]{:S(2)}, u32[]{:S(2)}) collective-permute-start(bf16[256,6144]{1,0:T(8,128)(2,1)} %bitcast.11), channel_id=1, source_target_pairs={{0,4},{4,0},{8,12},{12,8},{16,20},{20,16},{24,28},{28,24},{1,5},{5... | collective-permute-start | bytes 9437192 | tf_op jit(solution)/shard_map/ppermute | solution.py:60
  4.0 23.8 %collective-permute-start = (bf16[6144,256]{1,0:T(8,128)(2,1)}, bf16[6144,256]{1,0:T(8,128)(2,1)}, u32[]{:S(2)}, u32[]{:S(2)}) collective-permute-start(bf16[6144,256]{1,0:T(8,128)(2,1)} %bitcast.15), channel_id=1, source_target_pairs={{0,4},{4,0},{8,12},{12,8},{16,20},{20,16},{24,28},{28,24},{1,5},{5... | collective-permute-start | bytes 9437192 | tf_op jit(solution)/shard_map/ppermute | solution.py:60
  4.1 23.7 %collective-permute-start.1 = (bf16[6144,256]{1,0:T(8,128)(2,1)}, bf16[6144,256]{1,0:T(8,128)(2,1)}, u32[]{:S(2)}, u32[]{:S(2)}) collective-permute-start(bf16[6144,256]{1,0:T(8,128)(2,1)} %bitcast.17), channel_id=1, source_target_pairs={{0,4},{4,0},{8,12},{12,8},{16,20},{20,16},{24,28},{28,24},{1,5},{5... | collective-permute-start | bytes 9437192 | tf_op jit(solution)/shard_map/ppermute | solution.py:60
  4.5 23.3 %collective-permute-start.3 = (bf16[256,6144]{1,0:T(8,128)(2,1)}, bf16[256,6144]{1,0:T(8,128)(2,1)}, u32[]{:S(2)}, u32[]{:S(2)}) collective-permute-start(bf16[256,6144]{1,0:T(8,128)(2,1)} %refs_0_.1), channel_id=1, source_target_pairs={{0,4},{4,0},{8,12},{12,8},{16,20},{20,16},{24,28},{28,24},{1,5},{5... | collective-permute-start | bytes 9437192 | tf_op jit(solution)/shard_map/ppermute | solution.py:60
  5.3 0.9 copy-start.5
  6.2 0.7 copy-start.7
  7.5 37.3 %copy-start.1 = (bf16[256,6144]{1,0:T(8,128)(2,1)S(1)}, bf16[256,6144]{1,0:T(8,128)(2,1)}, u32[]{:S(2)}) copy-start(bf16[256,6144]{1,0:T(8,128)(2,1)} %refs_0_.1) | copy-start | bytes 9437188
  27.8 8.2 %collective-permute-start.4 = (bf16[8,3,6144]{2,1,0:T(4,128)(2,1)S(1)}, bf16[8,3,6144]{2,1,0:T(4,128)(2,1)S(1)}, u32[]{:S(2)}, u32[]{:S(2)}) collective-permute-start(bf16[8,3,6144]{2,1,0:T(4,128)(2,1)S(1)} %all_to_all.15.refs_0_), channel_id=1, source_target_pairs={{0,8},{1,9},{2,10},{3,11},{4,5},{5,6},{6,7},{7,4},{8,16},{9,17},{1... | collective-permute-start | bytes 884744 | tf_op jit(solution)/shard_map/ppermute | solution.py:48
  29.2 6.9 %collective-permute-start.5 = (bf16[8,3,6144]{2,1,0:T(4,128)(2,1)S(1)}, bf16[8,3,6144]{2,1,0:T(4,128)(2,1)S(1)}, u32[]{:S(2)}, u32[]{:S(2)}) collective-permute-start(bf16[8,3,6144]{2,1,0:T(4,128)(2,1)S(1)} %all_to_all.15.refs_0_), channel_id=1, source_target_pairs={{0,24},{1,25},{2,26},{3,27},{4,7},{5,4},{6,5},{7,6},{8,0},{9,1},{1... | collective-permute-start | bytes 884744 | tf_op jit(solution)/shard_map/ppermute | solution.py:48
  30.7 10.8 %collective-permute-start.6 = (bf16[8,3,6144]{2,1,0:T(4,128)(2,1)S(1)}, bf16[8,3,6144]{2,1,0:T(4,128)(2,1)S(1)}, u32[]{:S(2)}, u32[]{:S(2)}) collective-permute-start(bf16[8,3,6144]{2,1,0:T(4,128)(2,1)S(1)} %all_to_all.15.refs_0_), channel_id=1, source_target_pairs={{0,16},{1,17},{2,18},{3,19},{4,6},{5,7},{6,4},{7,5},{8,24},{9,25},... | collective-permute-start | bytes 884744 | tf_op jit(solution)/shard_map/ppermute | solution.py:48
  42.1 5.9 %copy-start.6 = (bf16[1,8,6144]{2,1,0:T(8,128)(2,1)S(1)}, bf16[1,8,6144]{2,1,0:T(8,128)(2,1)}, u32[]{:S(2)}) copy-start(bf16[1,8,6144]{2,1,0:T(8,128)(2,1)} %param.12) | copy-start | bytes 294916
  42.1 5.9 %copy-start.8 = (f32[6144]{0:T(1024)S(1)}, f32[6144]{0:T(1024)}, u32[]{:S(2)}) copy-start(f32[6144]{0:T(1024)} %param.13) | copy-start | bytes 73732
  42.1 5.9 %copy-start.9 = (bf16[6144,8]{0,1:T(8,128)(2,1)S(1)}, bf16[6144,8]{0,1:T(8,128)(2,1)}, u32[]{:S(2)}) copy-start(bf16[6144,8]{0,1:T(8,128)(2,1)} %param.15) | copy-start | bytes 294916
  42.1 16.7 %collective-permute-start.7 = (bf16[96,6144]{1,0:T(8,128)(2,1)S(1)}, bf16[96,6144]{1,0:T(8,128)(2,1)S(1)}, u32[]{:S(2)}, u32[]{:S(2)}) collective-permute-start(bf16[96,6144]{1,0:T(8,128)(2,1)S(1)} %shard_map.132.refs_0_), channel_id=1, source_target_pairs={{0,1},{1,2},{2,3},{3,0},{4,12},{5,13},{6,14},{7,15},{8,9},{9,10},{... | collective-permute-start | bytes 3538952 | tf_op jit(solution)/shard_map/ppermute | solution.py:48
  43.2 15.7 %collective-permute-start.8 = (bf16[96,6144]{1,0:T(8,128)(2,1)S(1)}, bf16[96,6144]{1,0:T(8,128)(2,1)S(1)}, u32[]{:S(2)}, u32[]{:S(2)}) collective-permute-start(bf16[96,6144]{1,0:T(8,128)(2,1)S(1)} %shard_map.132.refs_0_), channel_id=1, source_target_pairs={{0,3},{1,0},{2,1},{3,2},{4,28},{5,29},{6,30},{7,31},{8,11},{9,8},{... | collective-permute-start | bytes 3538952 | tf_op jit(solution)/shard_map/ppermute | solution.py:48
  44.9 3.5 %copy-start.3 = (bf16[1,6144,256]{2,1,0:T(8,128)(2,1)S(1)}, bf16[1,6144,256]{2,1,0:T(8,128)(2,1)}, u32[]{:S(2)}) copy-start(bf16[1,6144,256]{2,1,0:T(8,128)(2,1)} %param.16) | copy-start | bytes 9437188
  44.9 3.5 %copy-start.4 = (bf16[1,6144,256]{2,1,0:T(8,128)(2,1)S(1)}, bf16[1,6144,256]{2,1,0:T(8,128)(2,1)}, u32[]{:S(2)}) copy-start(bf16[1,6144,256]{2,1,0:T(8,128)(2,1)} %param.17) | copy-start | bytes 9437188
  45.2 34.2 %collective-permute-start.12 = (bf16[128,6144]{1,0:T(8,128)(2,1)S(1)}, bf16[128,6144]{1,0:T(8,128)(2,1)}, u32[]{:S(2)}, u32[]{:S(2)}) collective-permute-start(bf16[128,6144]{1,0:T(8,128)(2,1)S(1)} %get-tuple-element.93), channel_id=1, source_target_pairs={{0,32},{32,64},{64,96},{96,128},{128,160},{160,192},{192,224},{224... | collective-permute-start | bytes 4718600 | tf_op jit(solution)/shard_map/ppermute | solution.py:64
  45.6 33.8 %collective-permute-start.13 = (bf16[128,6144]{1,0:T(8,128)(2,1)S(1)}, bf16[128,6144]{1,0:T(8,128)(2,1)}, u32[]{:S(2)}, u32[]{:S(2)}) collective-permute-start(bf16[128,6144]{1,0:T(8,128)(2,1)S(1)} %get-tuple-element.92), channel_id=1, source_target_pairs={{0,224},{32,0},{64,32},{96,64},{128,96},{160,128},{192,160},{224,1... | collective-permute-start | bytes 4718600 | tf_op jit(solution)/shard_map/ppermute | solution.py:64
  58.9 9.6 %collective-permute-start.10 = (bf16[48,6144]{1,0:T(8,128)(2,1)S(1)}, bf16[48,6144]{1,0:T(8,128)(2,1)S(1)}, u32[]{:S(2)}, u32[]{:S(2)}) collective-permute-start(bf16[48,6144]{1,0:T(8,128)(2,1)S(1)} %slice.13), channel_id=1, source_target_pairs={{0,3},{1,0},{2,1},{3,2},{4,28},{5,29},{6,30},{7,31},{8,11},{9,8},{... | collective-permute-start | bytes 1769480 | tf_op jit(solution)/shard_map/ppermute | solution.py:48
  61.7 10.4 %collective-permute-start.9 = (bf16[48,6144]{1,0:T(8,128)(2,1)S(1)}, bf16[48,6144]{1,0:T(8,128)(2,1)S(1)}, u32[]{:S(2)}, u32[]{:S(2)}) collective-permute-start(bf16[48,6144]{1,0:T(8,128)(2,1)S(1)} %slice.12), channel_id=1, source_target_pairs={{0,1},{1,2},{2,3},{3,0},{4,12},{5,13},{6,14},{7,15},{8,9},{9,10},{... | collective-permute-start | bytes 1769480 | tf_op jit(solution)/shard_map/ppermute | solution.py:48
  72.1 2.8 %copy-start = (bf16[1,256,6144]{2,1,0:T(8,128)(2,1)S(1)}, bf16[1,256,6144]{2,1,0:T(8,128)(2,1)}, u32[]{:S(2)}) copy-start(bf16[1,256,6144]{2,1,0:T(8,128)(2,1)} %param.18) | copy-start | bytes 9437188
  77.4 9.3 %collective-permute-start.11 = (bf16[48,6144]{1,0:T(8,128)(2,1)S(1)}, bf16[48,6144]{1,0:T(8,128)(2,1)S(1)}, u32[]{:S(2)}, u32[]{:S(2)}) collective-permute-start(bf16[48,6144]{1,0:T(8,128)(2,1)S(1)} %get-tuple-element.70), channel_id=1, source_target_pairs={{0,3},{1,0},{2,1},{3,2},{4,28},{5,29},{6,30},{7,31},{8,11},{9,8},{... | collective-permute-start | bytes 1769480 | tf_op jit(solution)/shard_map/ppermute | solution.py:48
  77.7 10.3 %collective-permute-start.14 = (bf16[48,6144]{1,0:T(8,128)(2,1)S(1)}, bf16[48,6144]{1,0:T(8,128)(2,1)S(1)}, u32[]{:S(2)}, u32[]{:S(2)}) collective-permute-start(bf16[48,6144]{1,0:T(8,128)(2,1)S(1)} %get-tuple-element.76), channel_id=1, source_target_pairs={{0,1},{1,2},{2,3},{3,0},{4,12},{5,13},{6,14},{7,15},{8,9},{9,10},{... | collective-permute-start | bytes 1769480 | tf_op jit(solution)/shard_map/ppermute | solution.py:48
  91.0 15.4 %collective-permute-start.15 = (bf16[96,6144]{1,0:T(8,128)(2,1)S(1)}, bf16[96,6144]{1,0:T(8,128)(2,1)S(1)}, u32[]{:S(2)}, u32[]{:S(2)}) collective-permute-start(bf16[96,6144]{1,0:T(8,128)(2,1)S(1)} %get-tuple-element.77), channel_id=1, source_target_pairs={{0,3},{1,0},{2,1},{3,2},{4,28},{5,29},{6,30},{7,31},{8,11},{9,8},{... | collective-permute-start | bytes 3538952 | tf_op jit(solution)/shard_map/ppermute | solution.py:48
  91.1 16.6 %collective-permute-start.16 = (bf16[96,6144]{1,0:T(8,128)(2,1)S(1)}, bf16[96,6144]{1,0:T(8,128)(2,1)S(1)}, u32[]{:S(2)}, u32[]{:S(2)}) collective-permute-start(bf16[96,6144]{1,0:T(8,128)(2,1)S(1)} %get-tuple-element.78), channel_id=1, source_target_pairs={{0,1},{1,2},{2,3},{3,0},{4,12},{5,13},{6,14},{7,15},{8,9},{9,10},{... | collective-permute-start | bytes 3538952 | tf_op jit(solution)/shard_map/ppermute | solution.py:48
  95.0 54.4 %collective-permute-start.26 = (bf16[128,6144]{1,0:T(8,128)(2,1)}, bf16[128,6144]{1,0:T(8,128)(2,1)}, u32[]{:S(2)}, u32[]{:S(2)}) collective-permute-start(bf16[128,6144]{1,0:T(8,128)(2,1)} %collective-permute-done.12.refs_2_), channel_id=1, source_target_pairs={{0,4},{4,0},{8,12},{12,8},{16,20},{20,16},{24,28},{28,24},{1,5},{5... | collective-permute-start | bytes 4718600 | tf_op jit(solution)/shard_map/ppermute | solution.py:60
  101.1 48.3 %collective-permute-start.27 = (bf16[128,6144]{1,0:T(8,128)(2,1)}, bf16[128,6144]{1,0:T(8,128)(2,1)}, u32[]{:S(2)}, u32[]{:S(2)}) collective-permute-start(bf16[128,6144]{1,0:T(8,128)(2,1)} %collective-permute-done.13.refs_4_), channel_id=1, source_target_pairs={{0,4},{4,0},{8,12},{12,8},{16,20},{20,16},{24,28},{28,24},{1,5},{5... | collective-permute-start | bytes 4718600 | tf_op jit(solution)/shard_map/ppermute | solution.py:60
  108.6 25.3 %copy-start.10 = (f32[6144]{0:T(1024)S(1)}, f32[6144]{0:T(1024)}, u32[]{:S(2)}) copy-start(f32[6144]{0:T(1024)} %param.14) | copy-start | bytes 73732
  108.6 6.7 %collective-permute-start.17 = (bf16[24,6144]{1,0:T(8,128)(2,1)S(1)}, bf16[24,6144]{1,0:T(8,128)(2,1)S(1)}, u32[]{:S(2)}, u32[]{:S(2)}) collective-permute-start(bf16[24,6144]{1,0:T(8,128)(2,1)S(1)} %get-tuple-element.80), channel_id=1, source_target_pairs={{0,24},{1,25},{2,26},{3,27},{4,7},{5,4},{6,5},{7,6},{8,0},{9,1},{1... | collective-permute-start | bytes 884744 | tf_op jit(solution)/shard_map/ppermute | solution.py:48
  110.3 9.9 %collective-permute-start.18 = (bf16[24,6144]{1,0:T(8,128)(2,1)S(1)}, bf16[24,6144]{1,0:T(8,128)(2,1)S(1)}, u32[]{:S(2)}, u32[]{:S(2)}) collective-permute-start(bf16[24,6144]{1,0:T(8,128)(2,1)S(1)} %get-tuple-element.81), channel_id=1, source_target_pairs={{0,8},{1,9},{2,10},{3,11},{4,5},{5,6},{6,7},{7,4},{8,16},{9,17},{1... | collective-permute-start | bytes 884744 | tf_op jit(solution)/shard_map/ppermute | solution.py:48
  110.3 9.9 %collective-permute-start.19 = (bf16[24,6144]{1,0:T(8,128)(2,1)S(1)}, bf16[24,6144]{1,0:T(8,128)(2,1)S(1)}, u32[]{:S(2)}, u32[]{:S(2)}) collective-permute-start(bf16[24,6144]{1,0:T(8,128)(2,1)S(1)} %get-tuple-element.82), channel_id=1, source_target_pairs={{0,16},{1,17},{2,18},{3,19},{4,6},{5,7},{6,4},{7,5},{8,24},{9,25},... | collective-permute-start | bytes 884744 | tf_op jit(solution)/shard_map/ppermute | solution.py:48
  120.3 29.2 %copy-start.2 = (bf16[256,6144]{1,0:T(8,128)(2,1)S(1)}, bf16[256,6144]{1,0:T(8,128)(2,1)}, u32[]{:S(2)}) copy-start(bf16[256,6144]{1,0:T(8,128)(2,1)} %refs_0_.1) | copy-start | bytes 9437188
  134.9 8.5 %collective-permute-start.20 = (bf16[8,6144]{1,0:T(8,128)(2,1)S(1)}, bf16[8,6144]{1,0:T(8,128)(2,1)S(1)}, u32[]{:S(2)}, u32[]{:S(2)}) collective-permute-start(bf16[8,6144]{1,0:T(8,128)(2,1)S(1)} %shard_map.142.refs_0_), channel_id=1, source_target_pairs={{0,64},{4,68},{8,72},{12,76},{16,80},{20,84},{24,88},{28,92},{32,9... | collective-permute-start | bytes 294920 | tf_op jit(solution)/shard_map/ppermute | solution.py:56
  135.0 8.4 %collective-permute-start.21 = (bf16[8,6144]{1,0:T(8,128)(2,1)S(1)}, bf16[8,6144]{1,0:T(8,128)(2,1)S(1)}, u32[]{:S(2)}, u32[]{:S(2)}) collective-permute-start(bf16[8,6144]{1,0:T(8,128)(2,1)S(1)} %shard_map.142.refs_0_), channel_id=1, source_target_pairs={{0,192},{4,196},{8,200},{12,204},{16,208},{20,212},{24,216},{28,22... | collective-permute-start | bytes 294920 | tf_op jit(solution)/shard_map/ppermute | solution.py:56
  138.6 7.9 %collective-permute-start.22 = (bf16[8,6144]{1,0:T(8,128)(2,1)S(1)}, bf16[8,6144]{1,0:T(8,128)(2,1)S(1)}, u32[]{:S(2)}, u32[]{:S(2)}) collective-permute-start(bf16[8,6144]{1,0:T(8,128)(2,1)S(1)} %shard_map.142.refs_0_), channel_id=1, source_target_pairs={{0,128},{4,132},{8,136},{12,140},{16,144},{20,148},{24,152},{28,15... | collective-permute-start | bytes 294920 | tf_op jit(solution)/shard_map/ppermute | solution.py:56
  146.6 12.2 %collective-permute-start.23 = (bf16[32,6144]{1,0:T(8,128)(2,1)S(1)}, bf16[32,6144]{1,0:T(8,128)(2,1)}, u32[]{:S(2)}, u32[]{:S(2)}) collective-permute-start(bf16[32,6144]{1,0:T(8,128)(2,1)S(1)} %shard_map.143.r0), channel_id=1, source_target_pairs={{0,8},{4,12},{8,16},{12,20},{16,24},{20,28},{24,0},{28,4},{32,40},... | collective-permute-start | bytes 1179656 | tf_op jit(solution)/shard_map/ppermute | solution.py:56
  147.2 11.7 %collective-permute-start.24 = (bf16[32,6144]{1,0:T(8,128)(2,1)S(1)}, bf16[32,6144]{1,0:T(8,128)(2,1)}, u32[]{:S(2)}, u32[]{:S(2)}) collective-permute-start(bf16[32,6144]{1,0:T(8,128)(2,1)S(1)} %shard_map.143.r0), channel_id=1, source_target_pairs={{0,24},{4,28},{8,0},{12,4},{16,8},{20,12},{24,16},{28,20},{32,56},... | collective-permute-start | bytes 1179656 | tf_op jit(solution)/shard_map/ppermute | solution.py:56
  149.3 9.5 %collective-permute-start.25 = (bf16[32,6144]{1,0:T(8,128)(2,1)S(1)}, bf16[32,6144]{1,0:T(8,128)(2,1)}, u32[]{:S(2)}, u32[]{:S(2)}) collective-permute-start(bf16[32,6144]{1,0:T(8,128)(2,1)S(1)} %shard_map.143.r0), channel_id=1, source_target_pairs={{0,16},{4,20},{8,24},{12,28},{16,0},{20,4},{24,8},{28,12},{32,48},... | collective-permute-start | bytes 1179656 | tf_op jit(solution)/shard_map/ppermute | solution.py:56
  149.4 9.4 %copy-start.11 = (s32[1,512]{1,0:T(1,128)S(1)}, s32[1,512]{1,0:T(1,128)}, u32[]{:S(2)}) copy-start(s32[1,512]{1,0:T(1,128)} %targets_ref.1) | copy-start | bytes 6148
  158.8 39.1 %copy-start.12 = (s32[1,16]{1,0:T(1,128)S(1)}, s32[1,16]{1,0:T(1,128)}, u32[]{:S(2)}) copy-start(s32[1,16]{1,0:T(1,128)} %lengths_ref.1) | copy-start | bytes 196
  158.8 39.1 %copy-start.13 = (s32[1,16]{1,0:T(1,128)S(1)}, s32[1,16]{1,0:T(1,128)}, u32[]{:S(2)}) copy-start(s32[1,16]{1,0:T(1,128)} %questions_ref.1) | copy-start | bytes 196

commit v7 on v6

--- a/solution.py
+++ b/solution.py
@@ -236,42 +236,58 @@
     )
 
 
-def far_kernel(hidden_ref, down_a, down_b, before_ref, after_ref):
-    part = contract(hidden_ref[...], down_a[...], down_b[...]).astype(bf16)
+def rows_from(near_ref, far_ref, places):
+    near, far = near_ref[...].astype(f32), far_ref[...].astype(f32)
+    block = far.shape[0]
+    each = block // 4
+    pieces = []
+    for place in places:
+        at = place * each
+        pieces += [near[q * block + at : q * block + at + each] for q in range(3)]
+        pieces.append(far[at : at + each])
+    return jnp.concatenate(pieces).astype(bf16)
+
+
+def far_kernel(near_ref, far_ref, down_a, down_b, before_ref, after_ref):
+    part = contract(rows_from(near_ref, far_ref, (3,)), down_a[...], down_b[...]).astype(bf16)
     half = before_ref.shape[0]
     before_ref[...] = part[:half]
     after_ref[...] = part[half:]
 
 
-def near_kernel(hidden_ref, down_a, down_b, got_before, got_after, before_ref, after_ref):
+def near_kernel(
+    near_ref, far_ref, down_a, down_b, got_before, got_after, before_ref, after_ref
+):
     rows = before_ref.shape[0]
     half = rows // 2
-    part = contract(hidden_ref[rows:], down_a[...], down_b[...])
+    part = contract(rows_from(near_ref, far_ref, (1, 2)), down_a[...], down_b[...])
     before_ref[:half] = (part[:half] + got_before[...].astype(f32)).astype(bf16)
     before_ref[half:] = part[half:rows].astype(bf16)
     after_ref[:half] = part[rows : rows + half].astype(bf16)
     after_ref[half:] = (part[rows + half :] + got_after[...].astype(f32)).astype(bf16)
 
 
-def own_kernel(hidden_ref, down_a, down_b, own_ref):
-    rows = own_ref.shape[0]
-    own_ref[...] = contract(hidden_ref[:rows], down_a[...], down_b[...]).astype(bf16)
+def own_kernel(near_ref, far_ref, down_a, down_b, own_ref):
+    own_ref[...] = contract(
+        rows_from(near_ref, far_ref, (0,)), down_a[...], down_b[...]
+    ).astype(bf16)
 
 
 def down_call(kernel, hidden, downs, got, out_rows):
-    tile = 1024
+    tile = 1536
     share, width = downs[0].shape
+    total = sum(out_rows)
     return pl.pallas_call(
         kernel,
         grid=(width // tile,),
-        in_specs=[pl.BlockSpec(hidden.shape, lambda n: (0, 0))]
+        in_specs=[pl.BlockSpec(h.shape, lambda n: (0, 0)) for h in hidden]
         + [pl.BlockSpec((share, tile), lambda n: (0, n))] * 2
         + [pl.BlockSpec((g.shape[0], tile), lambda n: (0, n)) for g in got],
         out_specs=[pl.BlockSpec((rows, tile), lambda n: (0, n)) for rows in out_rows],
         out_shape=[shape((rows, width), bf16) for rows in out_rows],
         compiler_params=params(),
-        cost_estimate=cost(4 * hidden.shape[0] * share * width, 4 * share * width),
-    )(hidden, *downs, *got)
+        cost_estimate=cost(4 * total * share * width, 4 * share * width),
+    )(*hidden, *downs, *got)
 
 
 def line_sum_kernel(own_ref, before_ref, after_ref, *outs):
@@ -575,19 +591,20 @@
     near_hidden, far_before, far_after = tied(near_hidden, far_before, far_after)
     far_hidden = expand([far_before, far_after], weights)
 
-    to_before, to_after = down_call(far_kernel, far_hidden, downs, (), (half, half))
-    got_before = second(to_before, -1)
-    got_after = second(to_after, 1)
+    hidden = (near_hidden, far_hidden)
+    to_before, to_after = down_call(far_kernel, hidden, downs, (), (half, half))
+    got_before = first(to_before, -1)
+    got_after = first(to_after, 1)
     got_before, low_head, high_head = tied(got_before, low_head, high_head)
     before_part, after_part = down_call(
-        near_kernel, near_hidden, downs, (got_before, got_after), (rows, rows)
-    )
-    (own_part,) = down_call(own_kernel, near_hidden, downs, (), (rows,))
+        near_kernel, hidden, downs, (got_before, got_after), (rows, rows)
+    )
+    (own_part,) = down_call(own_kernel, hidden, downs, (), (rows,))
     own_part, low_head, high_head = tied(own_part, low_head, high_head)
     low_other = swap_cores(low_head)
     high_other = swap_cores(high_head)
-    pieces = line_sum([own_part, second(before_part, -1), second(after_part, 1)])
-    back = (first(pieces[1], -1), first(pieces[2], 1), first(pieces[3], 2))
+    pieces = line_sum([own_part, first(before_part, -1), first(after_part, 1)])
+    back = (second(pieces[1], -1), second(pieces[2], 1), second(pieces[3], 2))
     outgoing = expert_sum([pieces[0], *back])
 
     returned = lax.all_to_all(outgoing, "expert", split_axis=0, concat_axis=0, tiled=True)

time: 200 us -> 198 us (0.990)
  blocking collectives: 66.4 us -> 63.7 us
    all_to_all x1, blocking collectives: 32.8 us -> 30.2 us  [on_device(): gathered = lax.all_to_all(stats, ('expert', 'vocab'), 0, 0, tiled=True)]
    ppermute x14, waiting for transfers between devices: 45.4 us -> 47.8 us  [plane_shift(): return lax.ppermute(array, ('vocab', 'batch'), perm)]
  transfers between devices with their start and end apart: 28 -> 28, of which waited for: 16 -> 17; matrix products, arithmetic and copies ran while one was open for 1% -> 1% of each run, Pallas kernels for 12% -> 11%
where the time goes in v7:
time: 198 us
  blocking collectives  63.7 us (32%)
  waiting for transfers between devices  60.6 us (31%)
  starting transfers between devices  36 us (18%)
  Pallas kernels  33.6 us (17%)
  local copies, waits for them, and re-layouts  2.86 us (1%)
    ppermute x14, waiting for transfers between devices, plane_shift(): return lax.ppermute(array, ('vocab', 'batch'), perm)  47.8 us
    all_to_all x1, blocking collectives, on_device(): gathered = lax.all_to_all(stats, ('expert', 'vocab'), 0, 0, tiled=True)  30.2 us
    all_to_all x1, blocking collectives, on_device(): lax.all_to_all(buckets, 'expert', split_axis=0, concat_axis=0, tiled=True)  20.3 us
    ppermute x14, starting transfers between devices, plane_shift(): return lax.ppermute(array, ('vocab', 'batch'), perm)  14.9 us
    all_to_all x1, blocking collectives, on_device(): lax.all_to_all(outgoing, 'expert', split_axis=0, concat_axis=0, tiled=True)  13.3 us
    ppermute x6, waiting for transfers between devices, head_shift(): return lax.ppermute(array, ('expert', 'vocab'), perm)  12.4 us
    ppermute x6, starting transfers between devices, swap_cores(): return lax.ppermute(array, 'vocab', [(v, v ^ 1) for v in range(NX * NC)])  10.8 us
    pallas_call x2, Pallas kernels, expand(): pl.pallas_call(functools.partial(expand_kernel, count=count), grid=(width...  7.89 us
  transfers between devices with their start and end apart: 28, of which 17 were waited for; matrix products, arithmetic and copies ran while one was open for 1% of the time, Pallas kernels for 11%

profile of v7, /device:TPU:1, one launch (start us, length us, event | category | flops | bytes accessed | tf_op | source)
XLA Modules:
  0.0 197.7 jit_solution(5709928176472607899)
XLA Ops:
  0.6 3.3 %collective-permute-start.2 = (bf16[256,6144]{1,0:T(8,128)(2,1)}, bf16[256,6144]{1,0:T(8,128)(2,1)S(1)}, u32[]{:S(2)}, u32[]{:S(2)}) collective-permute-start(bf16[256,6144]{1,0:T(8,128)(2,1)} %bitcast.11), channel_id=1, source_target_pairs={{0,4},{4,0},{8,12},{12,8},{16,20},{20,16},{24,28},{28,24},{1,5},{5... | collective-permute-start | bytes 9437192 | tf_op jit(solution)/shard_map/ppermute | solution.py:60
  4.6 0.8 copy.14.ids_ref
  5.3 0.9 copy-done.5
  6.2 0.7 copy-done.7
  7.5 20.3 %all_to_all.15.refs_0_ = bf16[8,3,6144]{2,1,0:T(4,128)(2,1)S(1)} all-to-all(bf16[8,3,6144]{2,1,0:T(4,128)(2,1)S(1)} %shard_map.131), channel_id=1, replica_groups=mesh['expert'=8,'vocab'=8,'batch'=4] {'expert'}, dimensions={0} | all-to-all | bytes 589824 | tf_op jit(solution)/shard_map/all_to_all | solution.py:563
  27.8 1.4 collective-permute-start.4
  29.2 1.5 collective-permute-start.5
  30.7 1.6 collective-permute-start.6
  32.2 3.8 %collective-permute-done.4.refs_1_ = bf16[8,3,6144]{2,1,0:T(4,128)(2,1)S(1)} collective-permute-done((bf16[8,3,6144]{2,1,0:T(4,128)(2,1)S(1)}, bf16[8,3,6144]{2,1,0:T(4,128)(2,1)S(1)}, u32[]{:S(2)}, u32[]{:S(2)}) %collective-permute-start.4) | collective-permute-done | bytes 294944 | tf_op jit(solution)/shard_map/ppermute | solution.py:48
  36.1 5.3 %collective-permute-done.6.refs_3_ = bf16[8,3,6144]{2,1,0:T(4,128)(2,1)S(1)} collective-permute-done((bf16[8,3,6144]{2,1,0:T(4,128)(2,1)S(1)}, bf16[8,3,6144]{2,1,0:T(4,128)(2,1)S(1)}, u32[]{:S(2)}, u32[]{:S(2)}) %collective-permute-start.6) | collective-permute-done | bytes 294944 | tf_op jit(solution)/shard_map/ppermute | solution.py:48
  41.4 0.6 shard_map.132.refs_0_
  42.1 1.0 collective-permute-start.7
  43.2 1.7 collective-permute-start.8
  45.6 2.4 %collective-permute-start.13 = (bf16[128,6144]{1,0:T(8,128)(2,1)S(1)}, bf16[128,6144]{1,0:T(8,128)(2,1)}, u32[]{:S(2)}, u32[]{:S(2)}) collective-permute-start(bf16[128,6144]{1,0:T(8,128)(2,1)S(1)} %get-tuple-element.92), channel_id=1, source_target_pairs={{0,224},{32,0},{64,32},{96,64},{128,96},{160,128},{192,160},{224,1... | collective-permute-start | bytes 4718600 | tf_op jit(solution)/shard_map/ppermute | solution.py:64
  48.4 3.3 %shard_map.134 = (bf16[6144,256]{1,0:T(8,128)(2,1)S(1)}, bf16[6144,256]{1,0:T(8,128)(2,1)S(1)}, bf16[6144,256]{1,0:T(8,128)(2,1)S(1)}, bf16[6144,256]{1,0:T(8,128)(2,1)S(1)}) custom-call(bf16[6144,256]{1,0:T(8,128)(2,1)S(1)} %bitcast.16, bf16[6144,256]{1,0:T(8,128)(2,1)S(1)} %bitcast.18, bf16[6144,256]{1,0:T(8,128)(2,1)} %collective-permute-done.refs_2_, ...), custom_call_target="tpu_custom_call" | custom-call | bytes 12582912 | tf_op jit(solution)/shard_map/pallas_call | solution.py:453
  51.7 7.1 %collective-permute-done.7.refs_1_ = bf16[96,6144]{1,0:T(8,128)(2,1)S(1)} collective-permute-done((bf16[96,6144]{1,0:T(8,128)(2,1)S(1)}, bf16[96,6144]{1,0:T(8,128)(2,1)S(1)}, u32[]{:S(2)}, u32[]{:S(2)}) %collective-permute-start.7) | collective-permute-done | bytes 1179680 | tf_op jit(solution)/shard_map/ppermute | solution.py:48
  58.9 2.8 %collective-permute-start.10 = (bf16[48,6144]{1,0:T(8,128)(2,1)S(1)}, bf16[48,6144]{1,0:T(8,128)(2,1)S(1)}, u32[]{:S(2)}, u32[]{:S(2)}) collective-permute-start(bf16[48,6144]{1,0:T(8,128)(2,1)S(1)} %slice.13), channel_id=1, source_target_pairs={{0,3},{1,0},{2,1},{3,2},{4,28},{5,29},{6,30},{7,31},{8,11},{9,8},{... | collective-permute-start | bytes 1769480 | tf_op jit(solution)/shard_map/ppermute | solution.py:48
  61.8 5.1 %shard_map.135.near_ref = bf16[288,512]{1,0:T(8,128)(2,1)S(1)} custom-call(bf16[96,6144]{1,0:T(8,128)(2,1)S(1)} %shard_map.132.refs_0_, bf16[96,6144]{1,0:T(8,128)(2,1)S(1)} %collective-permute-done.7.refs_1_, bf16[96,6144]{1,0:T(8,128)(2,1)S(1)} %collective-permute-done.8.refs_2_, bf16[6144,256]{1,0:T(8,128)(2,1)S(1)} %get-tuple-element.62.refs_3_.refs_2_, ...), custom_call_target="tpu_custom_call" | custom-call | flops 3623878656 | bytes 12582912 | tf_op jit(solution)/shard_map/pallas_call | solution.py:219
  66.9 1.6 collective-permute-done.10.refs_1_
  68.5 3.6 %collective-permute-done.9.refs_0_ = bf16[48,6144]{1,0:T(8,128)(2,1)S(1)} collective-permute-done((bf16[48,6144]{1,0:T(8,128)(2,1)S(1)}, bf16[48,6144]{1,0:T(8,128)(2,1)S(1)}, u32[]{:S(2)}, u32[]{:S(2)}) %collective-permute-start.9) | collective-permute-done | bytes 589856 | tf_op jit(solution)/shard_map/ppermute | solution.py:48
  72.1 2.8 %shard_map.136.far_ref = bf16[96,512]{1,0:T(8,128)(2,1)S(1)} custom-call(bf16[48,6144]{1,0:T(8,128)(2,1)S(1)} %collective-permute-done.9.refs_0_, bf16[48,6144]{1,0:T(8,128)(2,1)S(1)} %collective-permute-done.10.refs_1_, bf16[6144,256]{1,0:T(8,128)(2,1)S(1)} %get-tuple-element.62.refs_3_.refs_2_, bf16[6144,256]{1,0:T(8,128)(2,1)S(1)} %get-tuple-element.63.refs_4_.refs_3_, ...), custom_call_target="tpu_custom_call" | custom-call | flops 1207959552 | bytes 12582912 | tf_op jit(solution)/shard_map/pallas_call | solution.py:219
  75.0 2.1 %shard_map.138 = (bf16[48,6144]{1,0:T(8,128)(2,1)S(1)}, bf16[48,6144]{1,0:T(8,128)(2,1)S(1)}) custom-call(bf16[288,512]{1,0:T(8,128)(2,1)S(1)} %shard_map.135.near_ref, bf16[96,512]{1,0:T(8,128)(2,1)S(1)} %shard_map.136.far_ref, bf16[256,6144]{1,0:T(8,128)(2,1)S(1)} %bitcast.12, bf16[256,6144]{1,0:T(8,128)(2,1)S(1)} %collective-permute-done.2.down_b), custom_call_target="tpu_custom_call" | custom-call | flops 603979776 | bytes 6291456 | tf_op jit(solution)/shard_map/pallas_call | solution.py:280
  77.1 1.8 collective-permute-start.11
  79.4 7.0 %collective-permute-done.11.got_before = bf16[48,6144]{1,0:T(8,128)(2,1)S(1)} collective-permute-done((bf16[48,6144]{1,0:T(8,128)(2,1)S(1)}, bf16[48,6144]{1,0:T(8,128)(2,1)S(1)}, u32[]{:S(2)}, u32[]{:S(2)}) %collective-permute-start.11) | collective-permute-done | bytes 589856 | tf_op jit(solution)/shard_map/ppermute | solution.py:48
  86.4 2.8 %collective-permute-done.14.got_after = bf16[48,6144]{1,0:T(8,128)(2,1)S(1)} collective-permute-done((bf16[48,6144]{1,0:T(8,128)(2,1)S(1)}, bf16[48,6144]{1,0:T(8,128)(2,1)S(1)}, u32[]{:S(2)}, u32[]{:S(2)}) %collective-permute-start.14) | collective-permute-done | bytes 589856 | tf_op jit(solution)/shard_map/ppermute | solution.py:48
  89.2 2.6 %shard_map.139 = (bf16[96,6144]{1,0:T(8,128)(2,1)S(1)}, bf16[96,6144]{1,0:T(8,128)(2,1)S(1)}) custom-call(bf16[288,512]{1,0:T(8,128)(2,1)S(1)} %shard_map.135.near_ref, bf16[96,512]{1,0:T(8,128)(2,1)S(1)} %shard_map.136.far_ref, bf16[256,6144]{1,0:T(8,128)(2,1)S(1)} %bitcast.13, bf16[256,6144]{1,0:T(8,128)(2,1)S(1)} %collective-permute-done.2.down_b, ...), custom_call_target="tpu_custom_call" | custom-call | flops 1207959552 | bytes 6291456 | tf_op jit(solution)/shard_map/pallas_call | solution.py:280
  91.9 1.5 collective-permute-start.16
  93.3 2.1 %shard_map.137.own_ref = bf16[96,6144]{1,0:T(8,128)(2,1)S(1)} custom-call(bf16[288,512]{1,0:T(8,128)(2,1)S(1)} %shard_map.135.near_ref, bf16[96,512]{1,0:T(8,128)(2,1)S(1)} %shard_map.136.far_ref, bf16[256,6144]{1,0:T(8,128)(2,1)S(1)} %bitcast.14, bf16[256,6144]{1,0:T(8,128)(2,1)S(1)} %collective-permute-done.2.down_b), custom_call_target="tpu_custom_call" | custom-call | flops 603979776 | bytes 6291456 | tf_op jit(solution)/shard_map/pallas_call | solution.py:280
  95.4 6.8 %collective-permute-start.26 = (bf16[128,6144]{1,0:T(8,128)(2,1)}, bf16[128,6144]{1,0:T(8,128)(2,1)}, u32[]{:S(2)}, u32[]{:S(2)}) collective-permute-start(bf16[128,6144]{1,0:T(8,128)(2,1)} %collective-permute-done.12.refs_2_), channel_id=1, source_target_pairs={{0,4},{4,0},{8,12},{12,8},{16,20},{20,16},{24,28},{28,24},{1,5},{5... | collective-permute-start | bytes 4718600 | tf_op jit(solution)/shard_map/ppermute | solution.py:60
  102.3 4.9 %collective-permute-done.15.before_ref = bf16[96,6144]{1,0:T(8,128)(2,1)S(1)} collective-permute-done((bf16[96,6144]{1,0:T(8,128)(2,1)S(1)}, bf16[96,6144]{1,0:T(8,128)(2,1)S(1)}, u32[]{:S(2)}, u32[]{:S(2)}) %collective-permute-start.15) | collective-permute-done | bytes 1179680 | tf_op jit(solution)/shard_map/ppermute | solution.py:48
  107.2 1.3 collective-permute-done.16.after_ref
  108.5 0.9 shard_map.140
  109.5 1.5 collective-permute-start.18
  111.0 5.7 %collective-permute-done.17.b = bf16[24,6144]{1,0:T(8,128)(2,1)S(1)} collective-permute-done((bf16[24,6144]{1,0:T(8,128)(2,1)S(1)}, bf16[24,6144]{1,0:T(8,128)(2,1)S(1)}, u32[]{:S(2)}, u32[]{:S(2)}) %collective-permute-start.17) | collective-permute-done | bytes 294944 | tf_op jit(solution)/shard_map/ppermute | solution.py:48
  116.7 4.5 %collective-permute-done.18.c = bf16[24,6144]{1,0:T(8,128)(2,1)S(1)} collective-permute-done((bf16[24,6144]{1,0:T(8,128)(2,1)S(1)}, bf16[24,6144]{1,0:T(8,128)(2,1)S(1)}, u32[]{:S(2)}, u32[]{:S(2)}) %collective-permute-start.18) | collective-permute-done | bytes 294944 | tf_op jit(solution)/shard_map/ppermute | solution.py:48
  121.5 13.3 %all_to_all.16.rows_ref = bf16[8,3,6144]{2,1,0:T(4,128)(2,1)S(1)} all-to-all(bf16[8,3,6144]{2,1,0:T(4,128)(2,1)S(1)} %shard_map.141), channel_id=1, replica_groups=mesh['expert'=8,'vocab'=8,'batch'=4] {'expert'}, dimensions={0} | all-to-all | bytes 589824 | tf_op jit(solution)/shard_map/all_to_all | solution.py:610
  134.8 1.0 shard_map.142.refs_0_
  135.9 3.6 %collective-permute-start.21 = (bf16[8,6144]{1,0:T(8,128)(2,1)S(1)}, bf16[8,6144]{1,0:T(8,128)(2,1)S(1)}, u32[]{:S(2)}, u32[]{:S(2)}) collective-permute-start(bf16[8,6144]{1,0:T(8,128)(2,1)S(1)} %shard_map.142.refs_0_), channel_id=1, source_target_pairs={{0,192},{4,196},{8,200},{12,204},{16,208},{20,212},{24,216},{28,22... | collective-permute-start | bytes 294920 | tf_op jit(solution)/shard_map/ppermute | solution.py:56
  139.8 3.7 %collective-permute-done.20.refs_1_ = bf16[8,6144]{1,0:T(8,128)(2,1)S(1)} collective-permute-done((bf16[8,6144]{1,0:T(8,128)(2,1)S(1)}, bf16[8,6144]{1,0:T(8,128)(2,1)S(1)}, u32[]{:S(2)}, u32[]{:S(2)}) %collective-permute-start.20) | collective-permute-done | bytes 98336 | tf_op jit(solution)/shard_map/ppermute | solution.py:56
  143.5 0.7 collective-permute-done.21.refs_2_
  144.2 3.2 %collective-permute-done.22.refs_3_ = bf16[8,6144]{1,0:T(8,128)(2,1)S(1)} collective-permute-done((bf16[8,6144]{1,0:T(8,128)(2,1)S(1)}, bf16[8,6144]{1,0:T(8,128)(2,1)S(1)}, u32[]{:S(2)}, u32[]{:S(2)}) %collective-permute-start.22) | collective-permute-done | bytes 98336 | tf_op jit(solution)/shard_map/ppermute | solution.py:56
  147.5 2.7 %collective-permute-start.24 = (bf16[32,6144]{1,0:T(8,128)(2,1)S(1)}, bf16[32,6144]{1,0:T(8,128)(2,1)}, u32[]{:S(2)}, u32[]{:S(2)}) collective-permute-start(bf16[32,6144]{1,0:T(8,128)(2,1)S(1)} %shard_map.143.r0), channel_id=1, source_target_pairs={{0,24},{4,28},{8,0},{12,4},{16,8},{20,12},{24,16},{28,20},{32,56},... | collective-permute-start | bytes 1179656 | tf_op jit(solution)/shard_map/ppermute | solution.py:56
  150.2 0.8 collective-permute-start.25
  151.1 4.0 %shard_map.144 = (bf16[256,6144]{1,0:T(8,128)(2,1)S(1)}, bf16[256,6144]{1,0:T(8,128)(2,1)S(1)}, bf16[128,6144]{1,0:T(8,128)(2,1)S(1)}, bf16[128,6144]{1,0:T(8,12...) custom-call(bf16[256,6144]{1,0:T(8,128)(2,1)S(1)} %copy-done.2, ...), custom_call_target="tpu_custom_call" | custom-call | bytes 12582912 | tf_op jit(solution)/shard_map/pallas_call | solution.py:453
  155.1 4.8 %collective-permute-done.23.r1 = bf16[32,6144]{1,0:T(8,128)(2,1)} collective-permute-done((bf16[32,6144]{1,0:T(8,128)(2,1)S(1)}, bf16[32,6144]{1,0:T(8,128)(2,1)}, u32[]{:S(2)}, u32[]{:S(2)}) %collective-permute-start.23) | collective-permute-done | bytes 393248 | tf_op jit(solution)/shard_map/ppermute | solution.py:56
  159.9 6.2 %shard_map.145 = f32[64,2,128]{2,1,0:T(2,128)S(1)} custom-call(s32[3]{0:T(128)S(1)} %pad_add_fusion.place_ref, s32[1,512]{1,0:T(1,128)S(1)} %copy-done.11, bf16[32,6144]{1,0:T(8,128)(2,1)S(1)} %shard_map.143.r0, bf16[32,6144]{1,0:T(8,128)(2,1)} %collective-permute-done.23.r1, bf16[32,6144]{1,0:T(8,128)(2,1)} %collective-permute-done.24.r2, ...), custom_call_target="tpu_custom_call" | custom-call | flops 1610612736 | bytes 12582912 | tf_op jit(solution)/shard_map/pallas_call | solution.py:425
  166.1 30.2 %all_to_all.17.stats_ref = f32[64,2,128]{2,1,0:T(2,128)S(1)} all-to-all(f32[64,2,128]{2,1,0:T(2,128)S(1)} %shard_map.145), channel_id=1, replica_groups=mesh['expert'=8,'vocab'=8,'batch'=4] {'expert','vocab'}, dimensions={0} | all-to-all | bytes 131072 | tf_op jit(solution)/shard_map/all_to_all | solution.py:616
  196.3 1.4 shard_map.146
  (60 shorter events, 4.3 us)
Async XLA Ops:
  0.6 27.2 %collective-permute-start.2 = (bf16[256,6144]{1,0:T(8,128)(2,1)}, bf16[256,6144]{1,0:T(8,128)(2,1)S(1)}, u32[]{:S(2)}, u32[]{:S(2)}) collective-permute-start(bf16[256,6144]{1,0:T(8,128)(2,1)} %bitcast.11), channel_id=1, source_target_pairs={{0,4},{4,0},{8,12},{12,8},{16,20},{20,16},{24,28},{28,24},{1,5},{5... | collective-permute-start | bytes 9437192 | tf_op jit(solution)/shard_map/ppermute | solution.py:60
  4.0 23.8 %collective-permute-start = (bf16[6144,256]{1,0:T(8,128)(2,1)}, bf16[6144,256]{1,0:T(8,128)(2,1)}, u32[]{:S(2)}, u32[]{:S(2)}) collective-permute-start(bf16[6144,256]{1,0:T(8,128)(2,1)} %bitcast.15), channel_id=1, source_target_pairs={{0,4},{4,0},{8,12},{12,8},{16,20},{20,16},{24,28},{28,24},{1,5},{5... | collective-permute-start | bytes 9437192 | tf_op jit(solution)/shard_map/ppermute | solution.py:60
  4.1 23.7 %collective-permute-start.1 = (bf16[6144,256]{1,0:T(8,128)(2,1)}, bf16[6144,256]{1,0:T(8,128)(2,1)}, u32[]{:S(2)}, u32[]{:S(2)}) collective-permute-start(bf16[6144,256]{1,0:T(8,128)(2,1)} %bitcast.17), channel_id=1, source_target_pairs={{0,4},{4,0},{8,12},{12,8},{16,20},{20,16},{24,28},{28,24},{1,5},{5... | collective-permute-start | bytes 9437192 | tf_op jit(solution)/shard_map/ppermute | solution.py:60
  4.5 23.3 %collective-permute-start.3 = (bf16[256,6144]{1,0:T(8,128)(2,1)}, bf16[256,6144]{1,0:T(8,128)(2,1)}, u32[]{:S(2)}, u32[]{:S(2)}) collective-permute-start(bf16[256,6144]{1,0:T(8,128)(2,1)} %refs_0_.1), channel_id=1, source_target_pairs={{0,4},{4,0},{8,12},{12,8},{16,20},{20,16},{24,28},{28,24},{1,5},{5... | collective-permute-start | bytes 9437192 | tf_op jit(solution)/shard_map/ppermute | solution.py:60
  5.3 0.9 copy-start.5
  6.2 0.7 copy-start.7
  7.5 37.3 %copy-start.1 = (bf16[256,6144]{1,0:T(8,128)(2,1)S(1)}, bf16[256,6144]{1,0:T(8,128)(2,1)}, u32[]{:S(2)}) copy-start(bf16[256,6144]{1,0:T(8,128)(2,1)} %refs_0_.1) | copy-start | bytes 9437188
  27.8 8.2 %collective-permute-start.4 = (bf16[8,3,6144]{2,1,0:T(4,128)(2,1)S(1)}, bf16[8,3,6144]{2,1,0:T(4,128)(2,1)S(1)}, u32[]{:S(2)}, u32[]{:S(2)}) collective-permute-start(bf16[8,3,6144]{2,1,0:T(4,128)(2,1)S(1)} %all_to_all.15.refs_0_), channel_id=1, source_target_pairs={{0,8},{1,9},{2,10},{3,11},{4,5},{5,6},{6,7},{7,4},{8,16},{9,17},{1... | collective-permute-start | bytes 884744 | tf_op jit(solution)/shard_map/ppermute | solution.py:48
  29.2 6.9 %collective-permute-start.5 = (bf16[8,3,6144]{2,1,0:T(4,128)(2,1)S(1)}, bf16[8,3,6144]{2,1,0:T(4,128)(2,1)S(1)}, u32[]{:S(2)}, u32[]{:S(2)}) collective-permute-start(bf16[8,3,6144]{2,1,0:T(4,128)(2,1)S(1)} %all_to_all.15.refs_0_), channel_id=1, source_target_pairs={{0,24},{1,25},{2,26},{3,27},{4,7},{5,4},{6,5},{7,6},{8,0},{9,1},{1... | collective-permute-start | bytes 884744 | tf_op jit(solution)/shard_map/ppermute | solution.py:48
  30.7 10.8 %collective-permute-start.6 = (bf16[8,3,6144]{2,1,0:T(4,128)(2,1)S(1)}, bf16[8,3,6144]{2,1,0:T(4,128)(2,1)S(1)}, u32[]{:S(2)}, u32[]{:S(2)}) collective-permute-start(bf16[8,3,6144]{2,1,0:T(4,128)(2,1)S(1)} %all_to_all.15.refs_0_), channel_id=1, source_target_pairs={{0,16},{1,17},{2,18},{3,19},{4,6},{5,7},{6,4},{7,5},{8,24},{9,25},... | collective-permute-start | bytes 884744 | tf_op jit(solution)/shard_map/ppermute | solution.py:48
  42.1 5.9 %copy-start.6 = (bf16[1,8,6144]{2,1,0:T(8,128)(2,1)S(1)}, bf16[1,8,6144]{2,1,0:T(8,128)(2,1)}, u32[]{:S(2)}) copy-start(bf16[1,8,6144]{2,1,0:T(8,128)(2,1)} %param.12) | copy-start | bytes 294916
  42.1 5.9 %copy-start.8 = (f32[6144]{0:T(1024)S(1)}, f32[6144]{0:T(1024)}, u32[]{:S(2)}) copy-start(f32[6144]{0:T(1024)} %param.13) | copy-start | bytes 73732
  42.1 5.9 %copy-start.9 = (bf16[6144,8]{0,1:T(8,128)(2,1)S(1)}, bf16[6144,8]{0,1:T(8,128)(2,1)}, u32[]{:S(2)}) copy-start(bf16[6144,8]{0,1:T(8,128)(2,1)} %param.15) | copy-start | bytes 294916
  42.1 16.7 %collective-permute-start.7 = (bf16[96,6144]{1,0:T(8,128)(2,1)S(1)}, bf16[96,6144]{1,0:T(8,128)(2,1)S(1)}, u32[]{:S(2)}, u32[]{:S(2)}) collective-permute-start(bf16[96,6144]{1,0:T(8,128)(2,1)S(1)} %shard_map.132.refs_0_), channel_id=1, source_target_pairs={{0,1},{1,2},{2,3},{3,0},{4,12},{5,13},{6,14},{7,15},{8,9},{9,10},{... | collective-permute-start | bytes 3538952 | tf_op jit(solution)/shard_map/ppermute | solution.py:48
  43.2 15.7 %collective-permute-start.8 = (bf16[96,6144]{1,0:T(8,128)(2,1)S(1)}, bf16[96,6144]{1,0:T(8,128)(2,1)S(1)}, u32[]{:S(2)}, u32[]{:S(2)}) collective-permute-start(bf16[96,6144]{1,0:T(8,128)(2,1)S(1)} %shard_map.132.refs_0_), channel_id=1, source_target_pairs={{0,3},{1,0},{2,1},{3,2},{4,28},{5,29},{6,30},{7,31},{8,11},{9,8},{... | collective-permute-start | bytes 3538952 | tf_op jit(solution)/shard_map/ppermute | solution.py:48
  44.9 3.5 %copy-start.3 = (bf16[1,6144,256]{2,1,0:T(8,128)(2,1)S(1)}, bf16[1,6144,256]{2,1,0:T(8,128)(2,1)}, u32[]{:S(2)}) copy-start(bf16[1,6144,256]{2,1,0:T(8,128)(2,1)} %param.16) | copy-start | bytes 9437188
  44.9 3.5 %copy-start.4 = (bf16[1,6144,256]{2,1,0:T(8,128)(2,1)S(1)}, bf16[1,6144,256]{2,1,0:T(8,128)(2,1)}, u32[]{:S(2)}) copy-start(bf16[1,6144,256]{2,1,0:T(8,128)(2,1)} %param.17) | copy-start | bytes 9437188
  45.2 34.2 %collective-permute-start.12 = (bf16[128,6144]{1,0:T(8,128)(2,1)S(1)}, bf16[128,6144]{1,0:T(8,128)(2,1)}, u32[]{:S(2)}, u32[]{:S(2)}) collective-permute-start(bf16[128,6144]{1,0:T(8,128)(2,1)S(1)} %get-tuple-element.93), channel_id=1, source_target_pairs={{0,32},{32,64},{64,96},{96,128},{128,160},{160,192},{192,224},{224... | collective-permute-start | bytes 4718600 | tf_op jit(solution)/shard_map/ppermute | solution.py:64
  45.6 33.8 %collective-permute-start.13 = (bf16[128,6144]{1,0:T(8,128)(2,1)S(1)}, bf16[128,6144]{1,0:T(8,128)(2,1)}, u32[]{:S(2)}, u32[]{:S(2)}) collective-permute-start(bf16[128,6144]{1,0:T(8,128)(2,1)S(1)} %get-tuple-element.92), channel_id=1, source_target_pairs={{0,224},{32,0},{64,32},{96,64},{128,96},{160,128},{192,160},{224,1... | collective-permute-start | bytes 4718600 | tf_op jit(solution)/shard_map/ppermute | solution.py:64
  58.9 9.6 %collective-permute-start.10 = (bf16[48,6144]{1,0:T(8,128)(2,1)S(1)}, bf16[48,6144]{1,0:T(8,128)(2,1)S(1)}, u32[]{:S(2)}, u32[]{:S(2)}) collective-permute-start(bf16[48,6144]{1,0:T(8,128)(2,1)S(1)} %slice.13), channel_id=1, source_target_pairs={{0,3},{1,0},{2,1},{3,2},{4,28},{5,29},{6,30},{7,31},{8,11},{9,8},{... | collective-permute-start | bytes 1769480 | tf_op jit(solution)/shard_map/ppermute | solution.py:48
  61.7 10.4 %collective-permute-start.9 = (bf16[48,6144]{1,0:T(8,128)(2,1)S(1)}, bf16[48,6144]{1,0:T(8,128)(2,1)S(1)}, u32[]{:S(2)}, u32[]{:S(2)}) collective-permute-start(bf16[48,6144]{1,0:T(8,128)(2,1)S(1)} %slice.12), channel_id=1, source_target_pairs={{0,1},{1,2},{2,3},{3,0},{4,12},{5,13},{6,14},{7,15},{8,9},{9,10},{... | collective-permute-start | bytes 1769480 | tf_op jit(solution)/shard_map/ppermute | solution.py:48
  72.1 2.8 %copy-start = (bf16[1,256,6144]{2,1,0:T(8,128)(2,1)S(1)}, bf16[1,256,6144]{2,1,0:T(8,128)(2,1)}, u32[]{:S(2)}) copy-start(bf16[1,256,6144]{2,1,0:T(8,128)(2,1)} %param.18) | copy-start | bytes 9437188
  77.1 9.3 %collective-permute-start.11 = (bf16[48,6144]{1,0:T(8,128)(2,1)S(1)}, bf16[48,6144]{1,0:T(8,128)(2,1)S(1)}, u32[]{:S(2)}, u32[]{:S(2)}) collective-permute-start(bf16[48,6144]{1,0:T(8,128)(2,1)S(1)} %get-tuple-element.70), channel_id=1, source_target_pairs={{0,24},{1,25},{2,26},{3,27},{4,7},{5,4},{6,5},{7,6},{8,0},{9,1},{1... | collective-permute-start | bytes 1769480 | tf_op jit(solution)/shard_map/ppermute | solution.py:48
  78.9 10.2 %collective-permute-start.14 = (bf16[48,6144]{1,0:T(8,128)(2,1)S(1)}, bf16[48,6144]{1,0:T(8,128)(2,1)S(1)}, u32[]{:S(2)}, u32[]{:S(2)}) collective-permute-start(bf16[48,6144]{1,0:T(8,128)(2,1)S(1)} %get-tuple-element.76), channel_id=1, source_target_pairs={{0,8},{1,9},{2,10},{3,11},{4,5},{5,6},{6,7},{7,4},{8,16},{9,17},{1... | collective-permute-start | bytes 1769480 | tf_op jit(solution)/shard_map/ppermute | solution.py:48
  91.8 15.4 %collective-permute-start.15 = (bf16[96,6144]{1,0:T(8,128)(2,1)S(1)}, bf16[96,6144]{1,0:T(8,128)(2,1)S(1)}, u32[]{:S(2)}, u32[]{:S(2)}) collective-permute-start(bf16[96,6144]{1,0:T(8,128)(2,1)S(1)} %get-tuple-element.77), channel_id=1, source_target_pairs={{0,24},{1,25},{2,26},{3,27},{4,7},{5,4},{6,5},{7,6},{8,0},{9,1},{1... | collective-permute-start | bytes 3538952 | tf_op jit(solution)/shard_map/ppermute | solution.py:48
  91.9 16.6 %collective-permute-start.16 = (bf16[96,6144]{1,0:T(8,128)(2,1)S(1)}, bf16[96,6144]{1,0:T(8,128)(2,1)S(1)}, u32[]{:S(2)}, u32[]{:S(2)}) collective-permute-start(bf16[96,6144]{1,0:T(8,128)(2,1)S(1)} %get-tuple-element.78), channel_id=1, source_target_pairs={{0,8},{1,9},{2,10},{3,11},{4,5},{5,6},{6,7},{7,4},{8,16},{9,17},{1... | collective-permute-start | bytes 3538952 | tf_op jit(solution)/shard_map/ppermute | solution.py:48
  95.4 55.7 %collective-permute-start.26 = (bf16[128,6144]{1,0:T(8,128)(2,1)}, bf16[128,6144]{1,0:T(8,128)(2,1)}, u32[]{:S(2)}, u32[]{:S(2)}) collective-permute-start(bf16[128,6144]{1,0:T(8,128)(2,1)} %collective-permute-done.12.refs_2_), channel_id=1, source_target_pairs={{0,4},{4,0},{8,12},{12,8},{16,20},{20,16},{24,28},{28,24},{1,5},{5... | collective-permute-start | bytes 4718600 | tf_op jit(solution)/shard_map/ppermute | solution.py:60
  102.2 48.9 %collective-permute-start.27 = (bf16[128,6144]{1,0:T(8,128)(2,1)}, bf16[128,6144]{1,0:T(8,128)(2,1)}, u32[]{:S(2)}, u32[]{:S(2)}) collective-permute-start(bf16[128,6144]{1,0:T(8,128)(2,1)} %collective-permute-done.13.refs_4_), channel_id=1, source_target_pairs={{0,4},{4,0},{8,12},{12,8},{16,20},{20,16},{24,28},{28,24},{1,5},{5... | collective-permute-start | bytes 4718600 | tf_op jit(solution)/shard_map/ppermute | solution.py:60
  109.4 25.4 %copy-start.10 = (f32[6144]{0:T(1024)S(1)}, f32[6144]{0:T(1024)}, u32[]{:S(2)}) copy-start(f32[6144]{0:T(1024)} %param.14) | copy-start | bytes 73732
  109.4 7.3 %collective-permute-start.17 = (bf16[24,6144]{1,0:T(8,128)(2,1)S(1)}, bf16[24,6144]{1,0:T(8,128)(2,1)S(1)}, u32[]{:S(2)}, u32[]{:S(2)}) collective-permute-start(bf16[24,6144]{1,0:T(8,128)(2,1)S(1)} %get-tuple-element.80), channel_id=1, source_target_pairs={{0,3},{1,0},{2,1},{3,2},{4,28},{5,29},{6,30},{7,31},{8,11},{9,8},{... | collective-permute-start | bytes 884744 | tf_op jit(solution)/shard_map/ppermute | solution.py:48
  109.5 11.6 %collective-permute-start.18 = (bf16[24,6144]{1,0:T(8,128)(2,1)S(1)}, bf16[24,6144]{1,0:T(8,128)(2,1)S(1)}, u32[]{:S(2)}, u32[]{:S(2)}) collective-permute-start(bf16[24,6144]{1,0:T(8,128)(2,1)S(1)} %get-tuple-element.81), channel_id=1, source_target_pairs={{0,1},{1,2},{2,3},{3,0},{4,12},{5,13},{6,14},{7,15},{8,9},{9,10},{... | collective-permute-start | bytes 884744 | tf_op jit(solution)/shard_map/ppermute | solution.py:48
  111.0 10.2 %collective-permute-start.19 = (bf16[24,6144]{1,0:T(8,128)(2,1)S(1)}, bf16[24,6144]{1,0:T(8,128)(2,1)S(1)}, u32[]{:S(2)}, u32[]{:S(2)}) collective-permute-start(bf16[24,6144]{1,0:T(8,128)(2,1)S(1)} %get-tuple-element.82), channel_id=1, source_target_pairs={{0,2},{1,3},{2,0},{3,1},{4,20},{5,21},{6,22},{7,23},{8,10},{9,11},... | collective-permute-start | bytes 884744 | tf_op jit(solution)/shard_map/ppermute | solution.py:48
  121.2 29.9 %copy-start.2 = (bf16[256,6144]{1,0:T(8,128)(2,1)S(1)}, bf16[256,6144]{1,0:T(8,128)(2,1)}, u32[]{:S(2)}) copy-start(bf16[256,6144]{1,0:T(8,128)(2,1)} %refs_0_.1) | copy-start | bytes 9437188
  135.8 7.7 %collective-permute-start.20 = (bf16[8,6144]{1,0:T(8,128)(2,1)S(1)}, bf16[8,6144]{1,0:T(8,128)(2,1)S(1)}, u32[]{:S(2)}, u32[]{:S(2)}) collective-permute-start(bf16[8,6144]{1,0:T(8,128)(2,1)S(1)} %shard_map.142.refs_0_), channel_id=1, source_target_pairs={{0,64},{4,68},{8,72},{12,76},{16,80},{20,84},{24,88},{28,92},{32,9... | collective-permute-start | bytes 294920 | tf_op jit(solution)/shard_map/ppermute | solution.py:56
  135.9 8.3 %collective-permute-start.21 = (bf16[8,6144]{1,0:T(8,128)(2,1)S(1)}, bf16[8,6144]{1,0:T(8,128)(2,1)S(1)}, u32[]{:S(2)}, u32[]{:S(2)}) collective-permute-start(bf16[8,6144]{1,0:T(8,128)(2,1)S(1)} %shard_map.142.refs_0_), channel_id=1, source_target_pairs={{0,192},{4,196},{8,200},{12,204},{16,208},{20,212},{24,216},{28,22... | collective-permute-start | bytes 294920 | tf_op jit(solution)/shard_map/ppermute | solution.py:56
  139.5 7.9 %collective-permute-start.22 = (bf16[8,6144]{1,0:T(8,128)(2,1)S(1)}, bf16[8,6144]{1,0:T(8,128)(2,1)S(1)}, u32[]{:S(2)}, u32[]{:S(2)}) collective-permute-start(bf16[8,6144]{1,0:T(8,128)(2,1)S(1)} %shard_map.142.refs_0_), channel_id=1, source_target_pairs={{0,128},{4,132},{8,136},{12,140},{16,144},{20,148},{24,152},{28,15... | collective-permute-start | bytes 294920 | tf_op jit(solution)/shard_map/ppermute | solution.py:56
  147.4 12.4 %collective-permute-start.23 = (bf16[32,6144]{1,0:T(8,128)(2,1)S(1)}, bf16[32,6144]{1,0:T(8,128)(2,1)}, u32[]{:S(2)}, u32[]{:S(2)}) collective-permute-start(bf16[32,6144]{1,0:T(8,128)(2,1)S(1)} %shard_map.143.r0), channel_id=1, source_target_pairs={{0,8},{4,12},{8,16},{12,20},{16,24},{20,28},{24,0},{28,4},{32,40},... | collective-permute-start | bytes 1179656 | tf_op jit(solution)/shard_map/ppermute | solution.py:56
  147.5 12.3 %collective-permute-start.24 = (bf16[32,6144]{1,0:T(8,128)(2,1)S(1)}, bf16[32,6144]{1,0:T(8,128)(2,1)}, u32[]{:S(2)}, u32[]{:S(2)}) collective-permute-start(bf16[32,6144]{1,0:T(8,128)(2,1)S(1)} %shard_map.143.r0), channel_id=1, source_target_pairs={{0,24},{4,28},{8,0},{12,4},{16,8},{20,12},{24,16},{28,20},{32,56},... | collective-permute-start | bytes 1179656 | tf_op jit(solution)/shard_map/ppermute | solution.py:56
  150.2 9.7 %collective-permute-start.25 = (bf16[32,6144]{1,0:T(8,128)(2,1)S(1)}, bf16[32,6144]{1,0:T(8,128)(2,1)}, u32[]{:S(2)}, u32[]{:S(2)}) collective-permute-start(bf16[32,6144]{1,0:T(8,128)(2,1)S(1)} %shard_map.143.r0), channel_id=1, source_target_pairs={{0,16},{4,20},{8,24},{12,28},{16,0},{20,4},{24,8},{28,12},{32,48},... | collective-permute-start | bytes 1179656 | tf_op jit(solution)/shard_map/ppermute | solution.py:56
  151.1 8.8 %copy-start.11 = (s32[1,512]{1,0:T(1,128)S(1)}, s32[1,512]{1,0:T(1,128)}, u32[]{:S(2)}) copy-start(s32[1,512]{1,0:T(1,128)} %targets_ref.1) | copy-start | bytes 6148
  159.9 36.5 %copy-start.12 = (s32[1,16]{1,0:T(1,128)S(1)}, s32[1,16]{1,0:T(1,128)}, u32[]{:S(2)}) copy-start(s32[1,16]{1,0:T(1,128)} %lengths_ref.1) | copy-start | bytes 196
  159.9 36.4 %copy-start.13 = (s32[1,16]{1,0:T(1,128)S(1)}, s32[1,16]{1,0:T(1,128)}, u32[]{:S(2)}) copy-start(s32[1,16]{1,0:T(1,128)} %questions_ref.1) | copy-start | bytes 196

commit v8 on v7

--- a/solution.py
+++ b/solution.py
@@ -188,52 +188,37 @@
     )(*parts)
 
 
-def expand_kernel(*refs, count):
-    rows = [ref[...] for ref in refs[:count]]
+def expand_kernel(*refs, count, chunk):
+    rows = refs[:count]
     gate_a, up_a, gate_b, up_b, out_ref, total = refs[count:]
-    step = pl.program_id(0)
-
-    @pl.when(step == 0)
-    def _():
-        total[...] = jnp.zeros_like(total)
-
-    block = rows[0] if count == 1 else jnp.concatenate(rows)
-    for j, weight in enumerate((gate_a, up_a, gate_b, up_b)):
-        total[j] += jnp.dot(block, weight[...], preferred_element_type=f32)
-
-    @pl.when(step == pl.num_programs(0) - 1)
-    def _():
-        share = total.shape[2]
-        for j in range(2):
-            gate = total[2 * j]
-            out_ref[:, j * share : (j + 1) * share] = (
-                gate / (1.0 + jnp.exp(-gate)) * total[2 * j + 1]
-            ).astype(bf16)
+    total[...] = jnp.zeros_like(total)
+
+    @pl.loop(0, rows[0].shape[1] // chunk)
+    def _(step):
+        columns = pl.ds(pl.multiple_of(step * chunk, chunk), chunk)
+        block = jnp.concatenate([ref[:, columns] for ref in rows])
+        for j, weight in enumerate((gate_a, up_a, gate_b, up_b)):
+            total[j] += jnp.dot(block, weight[columns, :], preferred_element_type=f32)
+
+    share = total.shape[2]
+    for j in range(2):
+        gate = total[2 * j]
+        out_ref[:, j * share : (j + 1) * share] = (
+            gate / (1.0 + jnp.exp(-gate)) * total[2 * j + 1]
+        ).astype(bf16)
 
 
 def expand(rows, weights):
-    depth = 1536
     count = len(rows)
     each, width = rows[0].shape
     share = weights[0].shape[1]
     return pl.pallas_call(
-        functools.partial(expand_kernel, count=count),
-        grid=(width // depth,),
-        in_specs=[pl.BlockSpec((each, depth), lambda k: (0, k))] * count
-        + [pl.BlockSpec((depth, share), lambda k: (k, 0))] * 4,
-        out_specs=pl.BlockSpec((count * each, 2 * share), lambda k: (0, 0)),
+        functools.partial(expand_kernel, count=count, chunk=width if count == 2 else 1536),
         out_shape=shape((count * each, 2 * share), bf16),
         scratch_shapes=[pltpu.VMEM((4, count * each, share), f32)],
         compiler_params=params(),
         cost_estimate=cost(8 * count * each * width * share, 8 * width * share),
     )(*rows, *weights)
-
-
-def contract(hidden, down_a, down_b):
-    share = down_a.shape[0]
-    return jnp.dot(hidden[:, :share], down_a, preferred_element_type=f32) + jnp.dot(
-        hidden[:, share:], down_b, preferred_element_type=f32
-    )
 
 
 def rows_from(near_ref, far_ref, places):
@@ -248,46 +233,52 @@
     return jnp.concatenate(pieces).astype(bf16)
 
 
-def far_kernel(near_ref, far_ref, down_a, down_b, before_ref, after_ref):
-    part = contract(rows_from(near_ref, far_ref, (3,)), down_a[...], down_b[...]).astype(bf16)
-    half = before_ref.shape[0]
-    before_ref[...] = part[:half]
-    after_ref[...] = part[half:]
-
-
-def near_kernel(
-    near_ref, far_ref, down_a, down_b, got_before, got_after, before_ref, after_ref
-):
-    rows = before_ref.shape[0]
-    half = rows // 2
-    part = contract(rows_from(near_ref, far_ref, (1, 2)), down_a[...], down_b[...])
-    before_ref[:half] = (part[:half] + got_before[...].astype(f32)).astype(bf16)
-    before_ref[half:] = part[half:rows].astype(bf16)
-    after_ref[:half] = part[rows : rows + half].astype(bf16)
-    after_ref[half:] = (part[rows + half :] + got_after[...].astype(f32)).astype(bf16)
-
-
-def own_kernel(near_ref, far_ref, down_a, down_b, own_ref):
-    own_ref[...] = contract(
-        rows_from(near_ref, far_ref, (0,)), down_a[...], down_b[...]
-    ).astype(bf16)
-
-
-def down_call(kernel, hidden, downs, got, out_rows):
-    tile = 1536
+def down_kernel(near_ref, far_ref, down_a, down_b, *outs, places, chunk):
+    rows = rows_from(near_ref, far_ref, places)
+    share, width = down_a.shape
+
+    @pl.loop(0, width // chunk)
+    def _(step):
+        columns = pl.ds(pl.multiple_of(step * chunk, chunk), chunk)
+        part = jnp.dot(rows[:, :share], down_a[:, columns], preferred_element_type=f32)
+        part += jnp.dot(rows[:, share:], down_b[:, columns], preferred_element_type=f32)
+        at = 0
+        for out in outs:
+            out[:, columns] = part[at : at + out.shape[0]].astype(bf16)
+            at += out.shape[0]
+
+
+def down_parts(places, hidden, downs, out_rows):
     share, width = downs[0].shape
-    total = sum(out_rows)
-    return pl.pallas_call(
-        kernel,
-        grid=(width // tile,),
-        in_specs=[pl.BlockSpec(h.shape, lambda n: (0, 0)) for h in hidden]
-        + [pl.BlockSpec((share, tile), lambda n: (0, n))] * 2
-        + [pl.BlockSpec((g.shape[0], tile), lambda n: (0, n)) for g in got],
-        out_specs=[pl.BlockSpec((rows, tile), lambda n: (0, n)) for rows in out_rows],
+    return pl.pallas_call(
+        functools.partial(down_kernel, places=places, chunk=1536),
         out_shape=[shape((rows, width), bf16) for rows in out_rows],
         compiler_params=params(),
-        cost_estimate=cost(4 * total * share * width, 4 * share * width),
-    )(*hidden, *downs, *got)
+        cost_estimate=cost(4 * sum(out_rows) * share * width, 4 * share * width),
+    )(*hidden, *downs)
+
+
+def join_kernel(before, after, got_before, got_after, before_ref, after_ref, *, chunk):
+    half = got_before.shape[0]
+
+    @pl.loop(0, before.shape[1] // chunk)
+    def _(step):
+        columns = pl.ds(pl.multiple_of(step * chunk, chunk), chunk)
+        first_half = before[:half, columns].astype(f32) + got_before[:, columns].astype(f32)
+        before_ref[:half, columns] = first_half.astype(bf16)
+        before_ref[half:, columns] = before[half:, columns]
+        after_ref[:half, columns] = after[:half, columns]
+        second_half = after[half:, columns].astype(f32) + got_after[:, columns].astype(f32)
+        after_ref[half:, columns] = second_half.astype(bf16)
+
+
+def join(before, after, got_before, got_after):
+    return pl.pallas_call(
+        functools.partial(join_kernel, chunk=1024),
+        out_shape=[shape(before.shape, bf16)] * 2,
+        compiler_params=params(),
+        cost_estimate=cost(before.size, 10 * before.size),
+    )(before, after, got_before, got_after)
 
 
 def line_sum_kernel(own_ref, before_ref, after_ref, *outs):
@@ -356,83 +347,75 @@
     )(weights, rows, resid, gain)
 
 
-def head_kernel(place_ref, targets_ref, r0, r1, r2, r3, *refs):
+def head_kernel(place_ref, targets_ref, r0, r1, r2, r3, *refs, chunk):
     *tables, out_ref, total = refs
-    step = pl.program_id(0)
-
-    @pl.when(step == 0)
-    def _():
-        total[...] = jnp.zeros_like(total)
-
-    rows = jnp.concatenate([r0[...], r1[...], r2[...], r3[...]])
-    share = tables[0].shape[0]
-    at = 0
-    for table in tables:
-        total[at : at + table.shape[0]] += lax.dot_general(
-            table[...], rows, (((1,), (1,)), ((), ())), preferred_element_type=f32
-        )
-        at += table.shape[0]
-
-    @pl.when(step == pl.num_programs(0) - 1)
-    def _():
-        z, x, c = place_ref[0], place_ref[1], place_ref[2]
-        count = rows.shape[0]
-        row = iota((count, 1), 0)
-        outer, inner, token = rel_step(row // 32), rel_step(row // 8 % 4), row % 8
-        z_half = (z // 2 + 4 + inner) % 4
-        x_seen = (x + 4 + outer) % 4
-        place = (z_half * NX + x_seen) * 8 + token
-        position = ((2 * z_half + z % 2) * NX + x_seen) * (NC * 8) + c * 8 + token
-        targets = targets_ref[...]
-        wanted = jnp.sum(
-            jnp.where(position == iota((count, targets.shape[1]), 1), targets, 0),
-            axis=1,
-            keepdims=True,
-        )
-        same = iota((count, count), 0) == iota((count, count), 1)
-        here = place == iota((count, count), 1)
-        wanted = jnp.sum(jnp.where(same, wanted, 0), axis=0, keepdims=True)
-        logits = total[...]
-        half = share // 2
-        entry = iota((4 * share, 1), 0)
-        part = entry // half
-        shared, upper = part >= 4, part >= 6
-        z_of = jnp.where(shared, (z + NZ + jnp.where(upper, 1, -1)) % NZ, z)
-        other = jnp.where(shared, part % 2, jnp.where(part >= 2, 1, 0))
-        c_of = c + other * (1 - 2 * c)
-        offset = jnp.where(
-            shared, entry % half + jnp.where(upper, half, 0), entry % share
-        )
-        entry_id = ((z_of * NX + x) * NC + c_of) * share + offset
-        top = jnp.max(logits, axis=0, keepdims=True)
-        spread = jnp.sum(jnp.exp(logits - top), axis=0, keepdims=True)
-        hit = jnp.sum(jnp.where(wanted == entry_id, logits, 0.0), axis=0, keepdims=True)
-        figures = []
-        for value in (top + jnp.log(spread), hit):
-            column = jnp.sum(jnp.where(same, value, 0.0), axis=1, keepdims=True)
-            figures.append(jnp.sum(jnp.where(here, column, 0.0), axis=0, keepdims=True))
-        figures = jnp.concatenate(figures)
-        for peer in range(out_ref.shape[0]):
-            out_ref[peer] = figures
+    total[...] = jnp.zeros_like(total)
+    share, width = tables[0].shape
+    count = total.shape[1]
+
+    @pl.loop(0, width // chunk)
+    def _(step):
+        columns = pl.ds(pl.multiple_of(step * chunk, chunk), chunk)
+        rows = jnp.concatenate([r[:, columns] for r in (r0, r1, r2, r3)])
+        at = 0
+        for table in tables:
+            total[at : at + table.shape[0]] += lax.dot_general(
+                table[:, columns], rows, (((1,), (1,)), ((), ())), preferred_element_type=f32
+            )
+            at += table.shape[0]
+
+    z, x, c = place_ref[0], place_ref[1], place_ref[2]
+    row = iota((count, 1), 0)
+    outer, inner, token = rel_step(row // 32), rel_step(row // 8 % 4), row % 8
+    z_half = (z // 2 + 4 + inner) % 4
+    x_seen = (x + 4 + outer) % 4
+    place = (z_half * NX + x_seen) * 8 + token
+    position = ((2 * z_half + z % 2) * NX + x_seen) * (NC * 8) + c * 8 + token
+    targets = targets_ref[...]
+    wanted = jnp.sum(
+        jnp.where(position == iota((count, targets.shape[1]), 1), targets, 0),
+        axis=1,
+        keepdims=True,
+    )
+    same = iota((count, count), 0) == iota((count, count), 1)
+    here = place == iota((count, count), 1)
+    wanted = jnp.sum(jnp.where(same, wanted, 0), axis=0, keepdims=True)
+    logits = total[...]
+    half = share // 2
+    entry = iota((4 * share, 1), 0)
+    part = entry // half
+    shared, upper = part >= 4, part >= 6
+    z_of = jnp.where(shared, (z + NZ + jnp.where(upper, 1, -1)) % NZ, z)
+    other = jnp.where(shared, part % 2, jnp.where(part >= 2, 1, 0))
+    c_of = c + other * (1 - 2 * c)
+    offset = jnp.where(
+        shared, entry % half + jnp.where(upper, half, 0), entry % share
+    )
+    entry_id = ((z_of * NX + x) * NC + c_of) * share + offset
+    top = jnp.max(logits, axis=0, keepdims=True)
+    spread = jnp.sum(jnp.exp(logits - top), axis=0, keepdims=True)
+    hit = jnp.sum(jnp.where(wanted == entry_id, logits, 0.0), axis=0, keepdims=True)
+    figures = []
+    for value in (top + jnp.log(spread), hit):
+        column = jnp.sum(jnp.where(same, value, 0.0), axis=1, keepdims=True)
+        figures.append(jnp.sum(jnp.where(here, column, 0.0), axis=0, keepdims=True))
+    figures = jnp.concatenate(figures)
+    for peer in range(out_ref.shape[0]):
+        out_ref[peer] = figures
 
 
 def head(place, targets, rows, tables):
-    depth = 1536
     width = rows[0].shape[1]
-    share = tables[0].shape[0]
+    entries = sum(t.shape[0] for t in tables)
     count = sum(r.shape[0] for r in rows)
-    whole = pl.BlockSpec(memory_space=pltpu.SMEM)
-    return pl.pallas_call(
-        head_kernel,
-        grid=(width // depth,),
-        in_specs=[whole, pl.BlockSpec(targets.shape, lambda k: (0, 0))]
-        + [pl.BlockSpec((rows[0].shape[0], depth), lambda k: (0, k))] * 4
-        + [pl.BlockSpec((t.shape[0], depth), lambda k: (0, k)) for t in tables],
-        out_specs=pl.BlockSpec((NZ * NX * NC, 2, count), lambda k: (0, 0, 0)),
+    smem, vmem = (pl.BlockSpec(memory_space=space) for space in (pltpu.SMEM, pltpu.VMEM))
+    return pl.pallas_call(
+        functools.partial(head_kernel, chunk=3072),
+        in_specs=[smem] + [vmem] * (1 + len(rows) + len(tables)),
         out_shape=shape((NZ * NX * NC, 2, count), f32),
-        scratch_shapes=[pltpu.VMEM((4 * share, count), f32)],
-        compiler_params=params(),
-        cost_estimate=cost(8 * count * share * width, 8 * share * width),
+        scratch_shapes=[pltpu.VMEM((entries, count), f32)],
+        compiler_params=params(),
+        cost_estimate=cost(2 * count * entries * width, 2 * entries * width),
     )(place, targets, *rows, *tables)
 
 
@@ -586,20 +569,21 @@
     )
     far_before = second(from_before[:half], 1)
     far_after = second(from_after[half:], -1)
-    downs = (own_down, other_down)
     near_hidden = expand([line, from_before, from_after], weights)
-    near_hidden, far_before, far_after = tied(near_hidden, far_before, far_after)
+    downs = hold(tied(near_hidden, own_down, other_down)[1:])
+    near_hidden, far_before, far_after, *downs = tied(
+        near_hidden, far_before, far_after, *downs
+    )
     far_hidden = expand([far_before, far_after], weights)
 
     hidden = (near_hidden, far_hidden)
-    to_before, to_after = down_call(far_kernel, hidden, downs, (), (half, half))
+    to_before, to_after = down_parts((3,), hidden, downs, (half, half))
+    before_part, after_part = down_parts((1, 2), hidden, downs, (rows, rows))
     got_before = first(to_before, -1)
     got_after = first(to_after, 1)
     got_before, low_head, high_head = tied(got_before, low_head, high_head)
-    before_part, after_part = down_call(
-        near_kernel, hidden, downs, (got_before, got_after), (rows, rows)
-    )
-    (own_part,) = down_call(own_kernel, hidden, downs, (), (rows,))
+    before_part, after_part = join(before_part, after_part, got_before, got_after)
+    (own_part,) = down_parts((0,), hidden, downs, (rows,))
     own_part, low_head, high_head = tied(own_part, low_head, high_head)
     low_other = swap_cores(low_head)
     high_other = swap_cores(high_head)

time: 198 us -> 197 us (level)
  waiting for transfers between devices: 60.6 us -> 56.5 us
  starting transfers between devices: 36 us -> 38.3 us
    ppermute x14, waiting for transfers between devices: 47.8 us -> 37.9 us  [plane_shift(): return lax.ppermute(array, ('vocab', 'batch'), perm)]
    ppermute x6, waiting for transfers between devices: 12.4 us -> 16.1 us  [head_shift(): return lax.ppermute(array, ('expert', 'vocab'), perm)]
    pallas_call x6 -> x7, Pallas kernels: 20.9 us -> 17.7 us  [the longest x2 6.73 us: expand(): pl.pallas_call(functools.partial(expand_kernel, count=count, chunk=width...]
    ppermute x14, starting transfers between devices: 14.9 us -> 17.8 us  [plane_shift(): return lax.ppermute(array, ('vocab', 'batch'), perm)]
    pallas_call x2 -> x3, Pallas kernels: 7.3 us -> 9.42 us  [hold(): pl.pallas_call(functools.partial(hold_kernel, count=count), in_specs=[pl....]
    ppermute x2, waiting for transfers between devices: 0.45 us -> 2.53 us  [z_shift(): lax.ppermute(array, 'expert', [(z, (z + shift) % NZ) for z in range(NZ)])]
  transfers between devices with their start and end apart: 28 -> 28, of which waited for: 17 -> 16; matrix products, arithmetic and copies ran while one was open for 1% -> 1% of each run, Pallas kernels for 11% -> 12%
where the time goes in v8:
time: 197 us
  blocking collectives  65.5 us (33%)
  waiting for transfers between devices  56.5 us (29%)
  starting transfers between devices  38.3 us (19%)
  Pallas kernels  32.5 us (16%)
  local copies, waits for them, and re-layouts  2.74 us (1%)
    ppermute x14, waiting for transfers between devices, plane_shift(): return lax.ppermute(array, ('vocab', 'batch'), perm)  37.9 us
    all_to_all x1, blocking collectives, on_device(): gathered = lax.all_to_all(stats, ('expert', 'vocab'), 0, 0, tiled=True)  32.1 us
    all_to_all x1, blocking collectives, on_device(): lax.all_to_all(buckets, 'expert', split_axis=0, concat_axis=0, tiled=True)  20.3 us
    ppermute x14, starting transfers between devices, plane_shift(): return lax.ppermute(array, ('vocab', 'batch'), perm)  17.8 us
    ppermute x6, waiting for transfers between devices, head_shift(): return lax.ppermute(array, ('expert', 'vocab'), perm)  16.1 us
    all_to_all x1, blocking collectives, on_device(): lax.all_to_all(outgoing, 'expert', split_axis=0, concat_axis=0, tiled=True)  13.1 us
    ppermute x6, starting transfers between devices, swap_cores(): return lax.ppermute(array, 'vocab', [(v, v ^ 1) for v in range(NX * NC)])  11.2 us
    pallas_call x3, Pallas kernels, hold(): pl.pallas_call(functools.partial(hold_kernel, count=count), in_specs=[pl....  9.42 us
  transfers between devices with their start and end apart: 28, of which 16 were waited for; matrix products, arithmetic and copies ran while one was open for 1% of the time, Pallas kernels for 12%

profile of v8, /device:TPU:1, one launch (start us, length us, event | category | flops | bytes accessed | tf_op | source)
XLA Modules:
  0.0 196.5 jit_solution(9518241788069884513)
XLA Ops:
  0.6 3.3 %collective-permute-start = (bf16[6144,256]{1,0:T(8,128)(2,1)}, bf16[6144,256]{1,0:T(8,128)(2,1)}, u32[]{:S(2)}, u32[]{:S(2)}) collective-permute-start(bf16[6144,256]{1,0:T(8,128)(2,1)} %bitcast.13), channel_id=1, source_target_pairs={{0,4},{4,0},{8,12},{12,8},{16,20},{20,16},{24,28},{28,24},{1,5},{5... | collective-permute-start | bytes 9437192 | tf_op jit(solution)/shard_map/ppermute | solution.py:60
  4.6 0.8 copy.14.ids_ref
  5.3 0.9 copy-done.4
  7.5 20.3 %all_to_all.15.refs_0_ = bf16[8,3,6144]{2,1,0:T(4,128)(2,1)S(1)} all-to-all(bf16[8,3,6144]{2,1,0:T(4,128)(2,1)S(1)} %shard_map.131), channel_id=1, replica_groups=mesh['expert'=8,'vocab'=8,'batch'=4] {'expert'}, dimensions={0} | all-to-all | bytes 589824 | tf_op jit(solution)/shard_map/all_to_all | solution.py:546
  27.8 1.4 collective-permute-start.4
  29.2 1.5 collective-permute-start.5
  30.7 1.6 collective-permute-start.6
  32.3 3.8 %collective-permute-done.4.refs_1_ = bf16[8,3,6144]{2,1,0:T(4,128)(2,1)S(1)} collective-permute-done((bf16[8,3,6144]{2,1,0:T(4,128)(2,1)S(1)}, bf16[8,3,6144]{2,1,0:T(4,128)(2,1)S(1)}, u32[]{:S(2)}, u32[]{:S(2)}) %collective-permute-start.4) | collective-permute-done | bytes 294944 | tf_op jit(solution)/shard_map/ppermute | solution.py:48
  36.1 3.6 %collective-permute-done.5.refs_2_ = bf16[8,3,6144]{2,1,0:T(4,128)(2,1)S(1)} collective-permute-done((bf16[8,3,6144]{2,1,0:T(4,128)(2,1)S(1)}, bf16[8,3,6144]{2,1,0:T(4,128)(2,1)S(1)}, u32[]{:S(2)}, u32[]{:S(2)}) %collective-permute-start.5) | collective-permute-done | bytes 294944 | tf_op jit(solution)/shard_map/ppermute | solution.py:48
  39.6 1.8 collective-permute-done.6.refs_3_
  42.1 1.0 collective-permute-start.7
  43.2 1.7 collective-permute-start.8
  45.5 2.4 %collective-permute-start.13 = (bf16[128,6144]{1,0:T(8,128)(2,1)S(1)}, bf16[128,6144]{1,0:T(8,128)(2,1)}, u32[]{:S(2)}, u32[]{:S(2)}) collective-permute-start(bf16[128,6144]{1,0:T(8,128)(2,1)S(1)} %get-tuple-element.108), channel_id=1, source_target_pairs={{0,224},{32,0},{64,32},{96,64},{128,96},{160,128},{192,160},{224,1... | collective-permute-start | bytes 4718600 | tf_op jit(solution)/shard_map/ppermute | solution.py:64
  48.3 3.3 %shard_map.134 = (bf16[6144,256]{1,0:T(8,128)(2,1)S(1)}, bf16[6144,256]{1,0:T(8,128)(2,1)S(1)}, bf16[6144,256]{1,0:T(8,128)(2,1)S(1)}, bf16[6144,256]{1,0:T(8,128)(2,1)S(1)}) custom-call(bf16[6144,256]{1,0:T(8,128)(2,1)S(1)} %bitcast.14, bf16[6144,256]{1,0:T(8,128)(2,1)S(1)} %bitcast.16, bf16[6144,256]{1,0:T(8,128)(2,1)} %collective-permute-done.refs_2_, ...), custom_call_target="tpu_custom_call" | custom-call | bytes 12582912 | tf_op jit(solution)/shard_map/pallas_call | solution.py:436
  51.6 7.2 %collective-permute-done.7.refs_1_ = bf16[96,6144]{1,0:T(8,128)(2,1)S(1)} collective-permute-done((bf16[96,6144]{1,0:T(8,128)(2,1)S(1)}, bf16[96,6144]{1,0:T(8,128)(2,1)S(1)}, u32[]{:S(2)}, u32[]{:S(2)}) %collective-permute-start.7) | collective-permute-done | bytes 1179680 | tf_op jit(solution)/shard_map/ppermute | solution.py:48
  58.9 1.0 collective-permute-start.9
  59.9 2.1 %collective-permute-start.10 = (bf16[48,6144]{1,0:T(8,128)(2,1)S(1)}, bf16[48,6144]{1,0:T(8,128)(2,1)S(1)}, u32[]{:S(2)}, u32[]{:S(2)}) collective-permute-start(bf16[48,6144]{1,0:T(8,128)(2,1)S(1)} %slice.13), channel_id=1, source_target_pairs={{0,3},{1,0},{2,1},{3,2},{4,28},{5,29},{6,30},{7,31},{8,11},{9,8},{... | collective-permute-start | bytes 1769480 | tf_op jit(solution)/shard_map/ppermute | solution.py:48
  62.0 4.6 %shard_map.135.near_ref = bf16[288,512]{1,0:T(8,128)(2,1)S(1)} custom-call(bf16[96,6144]{1,0:T(8,128)(2,1)S(1)} %shard_map.132.refs_0_, bf16[96,6144]{1,0:T(8,128)(2,1)S(1)} %collective-permute-done.7.refs_1_, bf16[96,6144]{1,0:T(8,128)(2,1)S(1)} %collective-permute-done.8.refs_2_, bf16[6144,256]{1,0:T(8,128)(2,1)S(1)} %get-tuple-element.70.refs_3_.refs_2_, ...), custom_call_target="tpu_custom_call" | custom-call | flops 3623878656 | bytes 12582912 | tf_op jit(solution)/shard_map/pallas_call | solution.py:215
  66.6 2.1 %shard_map.136 = (bf16[256,6144]{1,0:T(8,128)(2,1)S(1)}, bf16[256,6144]{1,0:T(8,128)(2,1)S(1)}) custom-call(bf16[256,6144]{1,0:T(8,128)(2,1)S(1)} %bitcast.12, bf16[256,6144]{1,0:T(8,128)(2,1)} %collective-permute-done.2.refs_1_), custom_call_target="tpu_custom_call" | custom-call | bytes 6291456 | tf_op jit(solution)/shard_map/pallas_call | solution.py:436
  69.4 2.1 %shard_map.137.far_ref = bf16[96,512]{1,0:T(8,128)(2,1)S(1)} custom-call(bf16[48,6144]{1,0:T(8,128)(2,1)S(1)} %collective-permute-done.9.refs_0_, bf16[48,6144]{1,0:T(8,128)(2,1)S(1)} %collective-permute-done.10.refs_1_, bf16[6144,256]{1,0:T(8,128)(2,1)S(1)} %get-tuple-element.70.refs_3_.refs_2_, bf16[6144,256]{1,0:T(8,128)(2,1)S(1)} %get-tuple-element.71.refs_4_.refs_3_, ...), custom_call_target="tpu_custom_call" | custom-call | flops 1207959552 | bytes 12582912 | tf_op jit(solution)/shard_map/pallas_call | solution.py:215
  71.5 1.6 shard_map.139
  73.1 1.8 collective-permute-start.11
  74.8 1.9 shard_map.140
  76.8 2.5 %collective-permute-done.12.refs_2_ = bf16[128,6144]{1,0:T(8,128)(2,1)} collective-permute-done((bf16[128,6144]{1,0:T(8,128)(2,1)S(1)}, bf16[128,6144]{1,0:T(8,128)(2,1)}, u32[]{:S(2)}, u32[]{:S(2)}) %collective-permute-start.12) | collective-permute-done | bytes 1572896 | tf_op jit(solution)/shard_map/ppermute | solution.py:64
  79.3 2.9 %collective-permute-done.11.got_before = bf16[48,6144]{1,0:T(8,128)(2,1)S(1)} collective-permute-done((bf16[48,6144]{1,0:T(8,128)(2,1)S(1)}, bf16[48,6144]{1,0:T(8,128)(2,1)S(1)}, u32[]{:S(2)}, u32[]{:S(2)}) %collective-permute-start.11) | collective-permute-done | bytes 589856 | tf_op jit(solution)/shard_map/ppermute | solution.py:48
  82.3 2.8 %collective-permute-done.14.got_after = bf16[48,6144]{1,0:T(8,128)(2,1)S(1)} collective-permute-done((bf16[48,6144]{1,0:T(8,128)(2,1)S(1)}, bf16[48,6144]{1,0:T(8,128)(2,1)S(1)}, u32[]{:S(2)}, u32[]{:S(2)}) %collective-permute-start.14) | collective-permute-done | bytes 589856 | tf_op jit(solution)/shard_map/ppermute | solution.py:48
  85.5 1.5 collective-permute-start.16
  86.9 1.6 shard_map.138.own_ref
  88.5 7.1 %collective-permute-start.26 = (bf16[128,6144]{1,0:T(8,128)(2,1)}, bf16[128,6144]{1,0:T(8,128)(2,1)}, u32[]{:S(2)}, u32[]{:S(2)}) collective-permute-start(bf16[128,6144]{1,0:T(8,128)(2,1)} %collective-permute-done.12.refs_2_), channel_id=1, source_target_pairs={{0,4},{4,0},{8,12},{12,8},{16,20},{20,16},{24,28},{28,24},{1,5},{5... | collective-permute-start | bytes 4718600 | tf_op jit(solution)/shard_map/ppermute | solution.py:60
  95.7 5.1 %collective-permute-done.15.before_ref = bf16[96,6144]{1,0:T(8,128)(2,1)S(1)} collective-permute-done((bf16[96,6144]{1,0:T(8,128)(2,1)S(1)}, bf16[96,6144]{1,0:T(8,128)(2,1)S(1)}, u32[]{:S(2)}, u32[]{:S(2)}) %collective-permute-start.15) | collective-permute-done | bytes 1179680 | tf_op jit(solution)/shard_map/ppermute | solution.py:48
  100.8 1.3 collective-permute-done.16.after_ref
  102.1 0.9 shard_map.142
  103.0 3.0 %collective-permute-start.17 = (bf16[24,6144]{1,0:T(8,128)(2,1)S(1)}, bf16[24,6144]{1,0:T(8,128)(2,1)S(1)}, u32[]{:S(2)}, u32[]{:S(2)}) collective-permute-start(bf16[24,6144]{1,0:T(8,128)(2,1)S(1)} %get-tuple-element.96), channel_id=1, source_target_pairs={{0,3},{1,0},{2,1},{3,2},{4,28},{5,29},{6,30},{7,31},{8,11},{9,8},{... | collective-permute-start | bytes 884744 | tf_op jit(solution)/shard_map/ppermute | solution.py:48
  105.9 1.3 collective-permute-start.19
  107.2 3.4 %collective-permute-done.17.b = bf16[24,6144]{1,0:T(8,128)(2,1)S(1)} collective-permute-done((bf16[24,6144]{1,0:T(8,128)(2,1)S(1)}, bf16[24,6144]{1,0:T(8,128)(2,1)S(1)}, u32[]{:S(2)}, u32[]{:S(2)}) %collective-permute-start.17) | collective-permute-done | bytes 294944 | tf_op jit(solution)/shard_map/ppermute | solution.py:48
  110.6 5.3 %collective-permute-done.18.c = bf16[24,6144]{1,0:T(8,128)(2,1)S(1)} collective-permute-done((bf16[24,6144]{1,0:T(8,128)(2,1)S(1)}, bf16[24,6144]{1,0:T(8,128)(2,1)S(1)}, u32[]{:S(2)}, u32[]{:S(2)}) %collective-permute-start.18) | collective-permute-done | bytes 294944 | tf_op jit(solution)/shard_map/ppermute | solution.py:48
  116.3 13.1 %all_to_all.16.rows_ref = bf16[8,3,6144]{2,1,0:T(4,128)(2,1)S(1)} all-to-all(bf16[8,3,6144]{2,1,0:T(4,128)(2,1)S(1)} %shard_map.143), channel_id=1, replica_groups=mesh['expert'=8,'vocab'=8,'batch'=4] {'expert'}, dimensions={0} | all-to-all | bytes 589824 | tf_op jit(solution)/shard_map/all_to_all | solution.py:594
  129.4 1.0 shard_map.144.refs_0_
  130.5 3.6 %collective-permute-start.21 = (bf16[8,6144]{1,0:T(8,128)(2,1)S(1)}, bf16[8,6144]{1,0:T(8,128)(2,1)S(1)}, u32[]{:S(2)}, u32[]{:S(2)}) collective-permute-start(bf16[8,6144]{1,0:T(8,128)(2,1)S(1)} %shard_map.144.refs_0_), channel_id=1, source_target_pairs={{0,192},{4,196},{8,200},{12,204},{16,208},{20,212},{24,216},{28,22... | collective-permute-start | bytes 294920 | tf_op jit(solution)/shard_map/ppermute | solution.py:56
  134.4 1.8 collective-permute-done.20.refs_1_
  136.2 3.1 %collective-permute-done.21.refs_2_ = bf16[8,6144]{1,0:T(8,128)(2,1)S(1)} collective-permute-done((bf16[8,6144]{1,0:T(8,128)(2,1)S(1)}, bf16[8,6144]{1,0:T(8,128)(2,1)S(1)}, u32[]{:S(2)}, u32[]{:S(2)}) %collective-permute-start.21) | collective-permute-done | bytes 98336 | tf_op jit(solution)/shard_map/ppermute | solution.py:56
  139.3 5.8 %collective-permute-done.22.refs_3_ = bf16[8,6144]{1,0:T(8,128)(2,1)S(1)} collective-permute-done((bf16[8,6144]{1,0:T(8,128)(2,1)S(1)}, bf16[8,6144]{1,0:T(8,128)(2,1)S(1)}, u32[]{:S(2)}, u32[]{:S(2)}) %collective-permute-start.22) | collective-permute-done | bytes 98336 | tf_op jit(solution)/shard_map/ppermute | solution.py:56
  145.2 2.7 %collective-permute-start.24 = (bf16[32,6144]{1,0:T(8,128)(2,1)S(1)}, bf16[32,6144]{1,0:T(8,128)(2,1)}, u32[]{:S(2)}, u32[]{:S(2)}) collective-permute-start(bf16[32,6144]{1,0:T(8,128)(2,1)S(1)} %shard_map.145.r0), channel_id=1, source_target_pairs={{0,24},{4,28},{8,0},{12,4},{16,8},{20,12},{24,16},{28,20},{32,56},... | collective-permute-start | bytes 1179656 | tf_op jit(solution)/shard_map/ppermute | solution.py:56
  148.0 4.0 %shard_map.146 = (bf16[256,6144]{1,0:T(8,128)(2,1)S(1)}, bf16[256,6144]{1,0:T(8,128)(2,1)S(1)}, bf16[128,6144]{1,0:T(8,128)(2,1)S(1)}, bf16[128,6144]{1,0:T(8,12...) custom-call(bf16[256,6144]{1,0:T(8,128)(2,1)S(1)} %copy-done, ...), custom_call_target="tpu_custom_call" | custom-call | bytes 12582912 | tf_op jit(solution)/shard_map/pallas_call | solution.py:436
  152.0 5.4 %collective-permute-done.23.r1 = bf16[32,6144]{1,0:T(8,128)(2,1)} collective-permute-done((bf16[32,6144]{1,0:T(8,128)(2,1)S(1)}, bf16[32,6144]{1,0:T(8,128)(2,1)}, u32[]{:S(2)}, u32[]{:S(2)}) %collective-permute-start.23) | collective-permute-done | bytes 393248 | tf_op jit(solution)/shard_map/ppermute | solution.py:56
  157.4 5.6 %shard_map.147 = f32[64,2,128]{2,1,0:T(2,128)S(1)} custom-call(s32[3]{0:T(128)S(1)} %pad_add_fusion.place_ref, s32[1,512]{1,0:T(1,128)S(1)} %copy-done.10, bf16[32,6144]{1,0:T(8,128)(2,1)S(1)} %shard_map.145.r0, bf16[32,6144]{1,0:T(8,128)(2,1)} %collective-permute-done.23.r1, bf16[32,6144]{1,0:T(8,128)(2,1)} %collective-permute-done.24.r2, ...), custom_call_target="tpu_custom_call" | custom-call | flops 1610612736 | bytes 12582912 | tf_op jit(solution)/shard_map/pallas_call | solution.py:412
  163.0 32.1 %all_to_all.17.stats_ref = f32[64,2,128]{2,1,0:T(2,128)S(1)} all-to-all(f32[64,2,128]{2,1,0:T(2,128)S(1)} %shard_map.147), channel_id=1, replica_groups=mesh['expert'=8,'vocab'=8,'batch'=4] {'expert','vocab'}, dimensions={0} | all-to-all | bytes 131072 | tf_op jit(solution)/shard_map/all_to_all | solution.py:600
  195.1 1.4 shard_map.148
  (60 shorter events, 5.8 us)
Async XLA Ops:
  0.6 27.2 %collective-permute-start = (bf16[6144,256]{1,0:T(8,128)(2,1)}, bf16[6144,256]{1,0:T(8,128)(2,1)}, u32[]{:S(2)}, u32[]{:S(2)}) collective-permute-start(bf16[6144,256]{1,0:T(8,128)(2,1)} %bitcast.13), channel_id=1, source_target_pairs={{0,4},{4,0},{8,12},{12,8},{16,20},{20,16},{24,28},{28,24},{1,5},{5... | collective-permute-start | bytes 9437192 | tf_op jit(solution)/shard_map/ppermute | solution.py:60
  4.0 23.8 %collective-permute-start.1 = (bf16[6144,256]{1,0:T(8,128)(2,1)}, bf16[6144,256]{1,0:T(8,128)(2,1)}, u32[]{:S(2)}, u32[]{:S(2)}) collective-permute-start(bf16[6144,256]{1,0:T(8,128)(2,1)} %bitcast.15), channel_id=1, source_target_pairs={{0,4},{4,0},{8,12},{12,8},{16,20},{20,16},{24,28},{28,24},{1,5},{5... | collective-permute-start | bytes 9437192 | tf_op jit(solution)/shard_map/ppermute | solution.py:60
  4.1 23.7 %collective-permute-start.2 = (bf16[256,6144]{1,0:T(8,128)(2,1)}, bf16[256,6144]{1,0:T(8,128)(2,1)}, u32[]{:S(2)}, u32[]{:S(2)}) collective-permute-start(bf16[256,6144]{1,0:T(8,128)(2,1)} %bitcast.11), channel_id=1, source_target_pairs={{0,4},{4,0},{8,12},{12,8},{16,20},{20,16},{24,28},{28,24},{1,5},{5... | collective-permute-start | bytes 9437192 | tf_op jit(solution)/shard_map/ppermute | solution.py:60
  4.5 23.3 %collective-permute-start.3 = (bf16[256,6144]{1,0:T(8,128)(2,1)}, bf16[256,6144]{1,0:T(8,128)(2,1)}, u32[]{:S(2)}, u32[]{:S(2)}) collective-permute-start(bf16[256,6144]{1,0:T(8,128)(2,1)} %refs_0_.1), channel_id=1, source_target_pairs={{0,4},{4,0},{8,12},{12,8},{16,20},{20,16},{24,28},{28,24},{1,5},{5... | collective-permute-start | bytes 9437192 | tf_op jit(solution)/shard_map/ppermute | solution.py:60
  5.3 0.9 copy-start.4
  6.2 0.7 copy-start.6
  7.5 37.4 %copy-start = (bf16[256,6144]{1,0:T(8,128)(2,1)S(1)}, bf16[256,6144]{1,0:T(8,128)(2,1)}, u32[]{:S(2)}) copy-start(bf16[256,6144]{1,0:T(8,128)(2,1)} %refs_0_.1) | copy-start | bytes 9437188
  27.8 8.3 %collective-permute-start.4 = (bf16[8,3,6144]{2,1,0:T(4,128)(2,1)S(1)}, bf16[8,3,6144]{2,1,0:T(4,128)(2,1)S(1)}, u32[]{:S(2)}, u32[]{:S(2)}) collective-permute-start(bf16[8,3,6144]{2,1,0:T(4,128)(2,1)S(1)} %all_to_all.15.refs_0_), channel_id=1, source_target_pairs={{0,8},{1,9},{2,10},{3,11},{4,5},{5,6},{6,7},{7,4},{8,16},{9,17},{1... | collective-permute-start | bytes 884744 | tf_op jit(solution)/shard_map/ppermute | solution.py:48
  29.2 10.4 %collective-permute-start.5 = (bf16[8,3,6144]{2,1,0:T(4,128)(2,1)S(1)}, bf16[8,3,6144]{2,1,0:T(4,128)(2,1)S(1)}, u32[]{:S(2)}, u32[]{:S(2)}) collective-permute-start(bf16[8,3,6144]{2,1,0:T(4,128)(2,1)S(1)} %all_to_all.15.refs_0_), channel_id=1, source_target_pairs={{0,24},{1,25},{2,26},{3,27},{4,7},{5,4},{6,5},{7,6},{8,0},{9,1},{1... | collective-permute-start | bytes 884744 | tf_op jit(solution)/shard_map/ppermute | solution.py:48
  30.7 10.8 %collective-permute-start.6 = (bf16[8,3,6144]{2,1,0:T(4,128)(2,1)S(1)}, bf16[8,3,6144]{2,1,0:T(4,128)(2,1)S(1)}, u32[]{:S(2)}, u32[]{:S(2)}) collective-permute-start(bf16[8,3,6144]{2,1,0:T(4,128)(2,1)S(1)} %all_to_all.15.refs_0_), channel_id=1, source_target_pairs={{0,16},{1,17},{2,18},{3,19},{4,6},{5,7},{6,4},{7,5},{8,24},{9,25},... | collective-permute-start | bytes 884744 | tf_op jit(solution)/shard_map/ppermute | solution.py:48
  42.1 5.8 %copy-start.5 = (bf16[1,8,6144]{2,1,0:T(8,128)(2,1)S(1)}, bf16[1,8,6144]{2,1,0:T(8,128)(2,1)}, u32[]{:S(2)}) copy-start(bf16[1,8,6144]{2,1,0:T(8,128)(2,1)} %param.12) | copy-start | bytes 294916
  42.1 5.8 %copy-start.7 = (f32[6144]{0:T(1024)S(1)}, f32[6144]{0:T(1024)}, u32[]{:S(2)}) copy-start(f32[6144]{0:T(1024)} %param.13) | copy-start | bytes 73732
  42.1 5.7 %copy-start.8 = (bf16[6144,8]{0,1:T(8,128)(2,1)S(1)}, bf16[6144,8]{0,1:T(8,128)(2,1)}, u32[]{:S(2)}) copy-start(bf16[6144,8]{0,1:T(8,128)(2,1)} %param.15) | copy-start | bytes 294916
  42.1 16.7 %collective-permute-start.7 = (bf16[96,6144]{1,0:T(8,128)(2,1)S(1)}, bf16[96,6144]{1,0:T(8,128)(2,1)S(1)}, u32[]{:S(2)}, u32[]{:S(2)}) collective-permute-start(bf16[96,6144]{1,0:T(8,128)(2,1)S(1)} %shard_map.132.refs_0_), channel_id=1, source_target_pairs={{0,1},{1,2},{2,3},{3,0},{4,12},{5,13},{6,14},{7,15},{8,9},{9,10},{... | collective-permute-start | bytes 3538952 | tf_op jit(solution)/shard_map/ppermute | solution.py:48
  43.2 15.7 %collective-permute-start.8 = (bf16[96,6144]{1,0:T(8,128)(2,1)S(1)}, bf16[96,6144]{1,0:T(8,128)(2,1)S(1)}, u32[]{:S(2)}, u32[]{:S(2)}) collective-permute-start(bf16[96,6144]{1,0:T(8,128)(2,1)S(1)} %shard_map.132.refs_0_), channel_id=1, source_target_pairs={{0,3},{1,0},{2,1},{3,2},{4,28},{5,29},{6,30},{7,31},{8,11},{9,8},{... | collective-permute-start | bytes 3538952 | tf_op jit(solution)/shard_map/ppermute | solution.py:48
  44.9 3.4 %copy-start.2 = (bf16[1,6144,256]{2,1,0:T(8,128)(2,1)S(1)}, bf16[1,6144,256]{2,1,0:T(8,128)(2,1)}, u32[]{:S(2)}) copy-start(bf16[1,6144,256]{2,1,0:T(8,128)(2,1)} %param.16) | copy-start | bytes 9437188
  44.9 3.4 %copy-start.3 = (bf16[1,6144,256]{2,1,0:T(8,128)(2,1)S(1)}, bf16[1,6144,256]{2,1,0:T(8,128)(2,1)}, u32[]{:S(2)}) copy-start(bf16[1,6144,256]{2,1,0:T(8,128)(2,1)} %param.17) | copy-start | bytes 9437188
  45.1 34.2 %collective-permute-start.12 = (bf16[128,6144]{1,0:T(8,128)(2,1)S(1)}, bf16[128,6144]{1,0:T(8,128)(2,1)}, u32[]{:S(2)}, u32[]{:S(2)}) collective-permute-start(bf16[128,6144]{1,0:T(8,128)(2,1)S(1)} %get-tuple-element.109), channel_id=1, source_target_pairs={{0,32},{32,64},{64,96},{96,128},{128,160},{160,192},{192,224},{224... | collective-permute-start | bytes 4718600 | tf_op jit(solution)/shard_map/ppermute | solution.py:64
  45.5 33.9 %collective-permute-start.13 = (bf16[128,6144]{1,0:T(8,128)(2,1)S(1)}, bf16[128,6144]{1,0:T(8,128)(2,1)}, u32[]{:S(2)}, u32[]{:S(2)}) collective-permute-start(bf16[128,6144]{1,0:T(8,128)(2,1)S(1)} %get-tuple-element.108), channel_id=1, source_target_pairs={{0,224},{32,0},{64,32},{96,64},{128,96},{160,128},{192,160},{224,1... | collective-permute-start | bytes 4718600 | tf_op jit(solution)/shard_map/ppermute | solution.py:64
  58.9 10.4 %collective-permute-start.9 = (bf16[48,6144]{1,0:T(8,128)(2,1)S(1)}, bf16[48,6144]{1,0:T(8,128)(2,1)S(1)}, u32[]{:S(2)}, u32[]{:S(2)}) collective-permute-start(bf16[48,6144]{1,0:T(8,128)(2,1)S(1)} %slice.12), channel_id=1, source_target_pairs={{0,1},{1,2},{2,3},{3,0},{4,12},{5,13},{6,14},{7,15},{8,9},{9,10},{... | collective-permute-start | bytes 1769480 | tf_op jit(solution)/shard_map/ppermute | solution.py:48
  59.9 9.4 %collective-permute-start.10 = (bf16[48,6144]{1,0:T(8,128)(2,1)S(1)}, bf16[48,6144]{1,0:T(8,128)(2,1)S(1)}, u32[]{:S(2)}, u32[]{:S(2)}) collective-permute-start(bf16[48,6144]{1,0:T(8,128)(2,1)S(1)} %slice.13), channel_id=1, source_target_pairs={{0,3},{1,0},{2,1},{3,2},{4,28},{5,29},{6,30},{7,31},{8,11},{9,8},{... | collective-permute-start | bytes 1769480 | tf_op jit(solution)/shard_map/ppermute | solution.py:48
  62.0 4.6 %copy-start.1 = (bf16[1,256,6144]{2,1,0:T(8,128)(2,1)S(1)}, bf16[1,256,6144]{2,1,0:T(8,128)(2,1)}, u32[]{:S(2)}) copy-start(bf16[1,256,6144]{2,1,0:T(8,128)(2,1)} %param.18) | copy-start | bytes 9437188
  73.1 9.2 %collective-permute-start.11 = (bf16[48,6144]{1,0:T(8,128)(2,1)S(1)}, bf16[48,6144]{1,0:T(8,128)(2,1)S(1)}, u32[]{:S(2)}, u32[]{:S(2)}) collective-permute-start(bf16[48,6144]{1,0:T(8,128)(2,1)S(1)} %get-tuple-element.84), channel_id=1, source_target_pairs={{0,24},{1,25},{2,26},{3,27},{4,7},{5,4},{6,5},{7,6},{8,0},{9,1},{1... | collective-permute-start | bytes 1769480 | tf_op jit(solution)/shard_map/ppermute | solution.py:48
  74.8 10.2 %collective-permute-start.14 = (bf16[48,6144]{1,0:T(8,128)(2,1)S(1)}, bf16[48,6144]{1,0:T(8,128)(2,1)S(1)}, u32[]{:S(2)}, u32[]{:S(2)}) collective-permute-start(bf16[48,6144]{1,0:T(8,128)(2,1)S(1)} %get-tuple-element.92), channel_id=1, source_target_pairs={{0,8},{1,9},{2,10},{3,11},{4,5},{5,6},{6,7},{7,4},{8,16},{9,17},{1... | collective-permute-start | bytes 1769480 | tf_op jit(solution)/shard_map/ppermute | solution.py:48
  85.4 15.4 %collective-permute-start.15 = (bf16[96,6144]{1,0:T(8,128)(2,1)S(1)}, bf16[96,6144]{1,0:T(8,128)(2,1)S(1)}, u32[]{:S(2)}, u32[]{:S(2)}) collective-permute-start(bf16[96,6144]{1,0:T(8,128)(2,1)S(1)} %get-tuple-element.93), channel_id=1, source_target_pairs={{0,24},{1,25},{2,26},{3,27},{4,7},{5,4},{6,5},{7,6},{8,0},{9,1},{1... | collective-permute-start | bytes 3538952 | tf_op jit(solution)/shard_map/ppermute | solution.py:48
  85.5 16.6 %collective-permute-start.16 = (bf16[96,6144]{1,0:T(8,128)(2,1)S(1)}, bf16[96,6144]{1,0:T(8,128)(2,1)S(1)}, u32[]{:S(2)}, u32[]{:S(2)}) collective-permute-start(bf16[96,6144]{1,0:T(8,128)(2,1)S(1)} %get-tuple-element.94), channel_id=1, source_target_pairs={{0,8},{1,9},{2,10},{3,11},{4,5},{5,6},{6,7},{7,4},{8,16},{9,17},{1... | collective-permute-start | bytes 3538952 | tf_op jit(solution)/shard_map/ppermute | solution.py:48
  88.5 59.5 %collective-permute-start.26 = (bf16[128,6144]{1,0:T(8,128)(2,1)}, bf16[128,6144]{1,0:T(8,128)(2,1)}, u32[]{:S(2)}, u32[]{:S(2)}) collective-permute-start(bf16[128,6144]{1,0:T(8,128)(2,1)} %collective-permute-done.12.refs_2_), channel_id=1, source_target_pairs={{0,4},{4,0},{8,12},{12,8},{16,20},{20,16},{24,28},{28,24},{1,5},{5... | collective-permute-start | bytes 4718600 | tf_op jit(solution)/shard_map/ppermute | solution.py:60
  95.6 52.4 %collective-permute-start.27 = (bf16[128,6144]{1,0:T(8,128)(2,1)}, bf16[128,6144]{1,0:T(8,128)(2,1)}, u32[]{:S(2)}, u32[]{:S(2)}) collective-permute-start(bf16[128,6144]{1,0:T(8,128)(2,1)} %collective-permute-done.13.refs_4_), channel_id=1, source_target_pairs={{0,4},{4,0},{8,12},{12,8},{16,20},{20,16},{24,28},{28,24},{1,5},{5... | collective-permute-start | bytes 4718600 | tf_op jit(solution)/shard_map/ppermute | solution.py:60
  103.0 26.4 %copy-start.9 = (f32[6144]{0:T(1024)S(1)}, f32[6144]{0:T(1024)}, u32[]{:S(2)}) copy-start(f32[6144]{0:T(1024)} %param.14) | copy-start | bytes 73732
  103.0 7.6 %collective-permute-start.17 = (bf16[24,6144]{1,0:T(8,128)(2,1)S(1)}, bf16[24,6144]{1,0:T(8,128)(2,1)S(1)}, u32[]{:S(2)}, u32[]{:S(2)}) collective-permute-start(bf16[24,6144]{1,0:T(8,128)(2,1)S(1)} %get-tuple-element.96), channel_id=1, source_target_pairs={{0,3},{1,0},{2,1},{3,2},{4,28},{5,29},{6,30},{7,31},{8,11},{9,8},{... | collective-permute-start | bytes 884744 | tf_op jit(solution)/shard_map/ppermute | solution.py:48
  105.9 9.9 %collective-permute-start.18 = (bf16[24,6144]{1,0:T(8,128)(2,1)S(1)}, bf16[24,6144]{1,0:T(8,128)(2,1)S(1)}, u32[]{:S(2)}, u32[]{:S(2)}) collective-permute-start(bf16[24,6144]{1,0:T(8,128)(2,1)S(1)} %get-tuple-element.97), channel_id=1, source_target_pairs={{0,1},{1,2},{2,3},{3,0},{4,12},{5,13},{6,14},{7,15},{8,9},{9,10},{... | collective-permute-start | bytes 884744 | tf_op jit(solution)/shard_map/ppermute | solution.py:48
  105.9 9.9 %collective-permute-start.19 = (bf16[24,6144]{1,0:T(8,128)(2,1)S(1)}, bf16[24,6144]{1,0:T(8,128)(2,1)S(1)}, u32[]{:S(2)}, u32[]{:S(2)}) collective-permute-start(bf16[24,6144]{1,0:T(8,128)(2,1)S(1)} %get-tuple-element.98), channel_id=1, source_target_pairs={{0,2},{1,3},{2,0},{3,1},{4,20},{5,21},{6,22},{7,23},{8,10},{9,11},... | collective-permute-start | bytes 884744 | tf_op jit(solution)/shard_map/ppermute | solution.py:48
  130.4 5.8 %collective-permute-start.20 = (bf16[8,6144]{1,0:T(8,128)(2,1)S(1)}, bf16[8,6144]{1,0:T(8,128)(2,1)S(1)}, u32[]{:S(2)}, u32[]{:S(2)}) collective-permute-start(bf16[8,6144]{1,0:T(8,128)(2,1)S(1)} %shard_map.144.refs_0_), channel_id=1, source_target_pairs={{0,64},{4,68},{8,72},{12,76},{16,80},{20,84},{24,88},{28,92},{32,9... | collective-permute-start | bytes 294920 | tf_op jit(solution)/shard_map/ppermute | solution.py:56
  130.5 8.8 %collective-permute-start.21 = (bf16[8,6144]{1,0:T(8,128)(2,1)S(1)}, bf16[8,6144]{1,0:T(8,128)(2,1)S(1)}, u32[]{:S(2)}, u32[]{:S(2)}) collective-permute-start(bf16[8,6144]{1,0:T(8,128)(2,1)S(1)} %shard_map.144.refs_0_), channel_id=1, source_target_pairs={{0,192},{4,196},{8,200},{12,204},{16,208},{20,212},{24,216},{28,22... | collective-permute-start | bytes 294920 | tf_op jit(solution)/shard_map/ppermute | solution.py:56
  134.1 11.0 %collective-permute-start.22 = (bf16[8,6144]{1,0:T(8,128)(2,1)S(1)}, bf16[8,6144]{1,0:T(8,128)(2,1)S(1)}, u32[]{:S(2)}, u32[]{:S(2)}) collective-permute-start(bf16[8,6144]{1,0:T(8,128)(2,1)S(1)} %shard_map.144.refs_0_), channel_id=1, source_target_pairs={{0,128},{4,132},{8,136},{12,140},{16,144},{20,148},{24,152},{28,15... | collective-permute-start | bytes 294920 | tf_op jit(solution)/shard_map/ppermute | solution.py:56
  145.1 12.2 %collective-permute-start.23 = (bf16[32,6144]{1,0:T(8,128)(2,1)S(1)}, bf16[32,6144]{1,0:T(8,128)(2,1)}, u32[]{:S(2)}, u32[]{:S(2)}) collective-permute-start(bf16[32,6144]{1,0:T(8,128)(2,1)S(1)} %shard_map.145.r0), channel_id=1, source_target_pairs={{0,8},{4,12},{8,16},{12,20},{16,24},{20,28},{24,0},{28,4},{32,40},... | collective-permute-start | bytes 1179656 | tf_op jit(solution)/shard_map/ppermute | solution.py:56
  145.2 12.1 %collective-permute-start.24 = (bf16[32,6144]{1,0:T(8,128)(2,1)S(1)}, bf16[32,6144]{1,0:T(8,128)(2,1)}, u32[]{:S(2)}, u32[]{:S(2)}) collective-permute-start(bf16[32,6144]{1,0:T(8,128)(2,1)S(1)} %shard_map.145.r0), channel_id=1, source_target_pairs={{0,24},{4,28},{8,0},{12,4},{16,8},{20,12},{24,16},{28,20},{32,56},... | collective-permute-start | bytes 1179656 | tf_op jit(solution)/shard_map/ppermute | solution.py:56
  147.9 9.5 %collective-permute-start.25 = (bf16[32,6144]{1,0:T(8,128)(2,1)S(1)}, bf16[32,6144]{1,0:T(8,128)(2,1)}, u32[]{:S(2)}, u32[]{:S(2)}) collective-permute-start(bf16[32,6144]{1,0:T(8,128)(2,1)S(1)} %shard_map.145.r0), channel_id=1, source_target_pairs={{0,16},{4,20},{8,24},{12,28},{16,0},{20,4},{24,8},{28,12},{32,48},... | collective-permute-start | bytes 1179656 | tf_op jit(solution)/shard_map/ppermute | solution.py:56
  147.9 9.4 %copy-start.10 = (s32[1,512]{1,0:T(1,128)S(1)}, s32[1,512]{1,0:T(1,128)}, u32[]{:S(2)}) copy-start(s32[1,512]{1,0:T(1,128)} %targets_ref.1) | copy-start | bytes 6148
  157.4 37.8 %copy-start.11 = (s32[1,16]{1,0:T(1,128)S(1)}, s32[1,16]{1,0:T(1,128)}, u32[]{:S(2)}) copy-start(s32[1,16]{1,0:T(1,128)} %lengths_ref.1) | copy-start | bytes 196
  157.4 37.8 %copy-start.12 = (s32[1,16]{1,0:T(1,128)S(1)}, s32[1,16]{1,0:T(1,128)}, u32[]{:S(2)}) copy-start(s32[1,16]{1,0:T(1,128)} %questions_ref.1) | copy-start | bytes 196

commit v9 on v8

--- a/solution.py
+++ b/solution.py
@@ -244,15 +244,15 @@
         part += jnp.dot(rows[:, share:], down_b[:, columns], preferred_element_type=f32)
         at = 0
         for out in outs:
-            out[:, columns] = part[at : at + out.shape[0]].astype(bf16)
+            out[:, columns] = part[at : at + out.shape[0]].astype(out.dtype)
             at += out.shape[0]
 
 
-def down_parts(places, hidden, downs, out_rows):
+def down_parts(places, hidden, downs, out_rows, dtype):
     share, width = downs[0].shape
     return pl.pallas_call(
         functools.partial(down_kernel, places=places, chunk=1536),
-        out_shape=[shape((rows, width), bf16) for rows in out_rows],
+        out_shape=[shape((rows, width), dtype) for rows in out_rows],
         compiler_params=params(),
         cost_estimate=cost(4 * sum(out_rows) * share * width, 4 * share * width),
     )(*hidden, *downs)
@@ -264,11 +264,11 @@
     @pl.loop(0, before.shape[1] // chunk)
     def _(step):
         columns = pl.ds(pl.multiple_of(step * chunk, chunk), chunk)
-        first_half = before[:half, columns].astype(f32) + got_before[:, columns].astype(f32)
+        first_half = before[:half, columns] + got_before[:, columns].astype(f32)
         before_ref[:half, columns] = first_half.astype(bf16)
-        before_ref[half:, columns] = before[half:, columns]
-        after_ref[:half, columns] = after[:half, columns]
-        second_half = after[half:, columns].astype(f32) + got_after[:, columns].astype(f32)
+        before_ref[half:, columns] = before[half:, columns].astype(bf16)
+        after_ref[:half, columns] = after[:half, columns].astype(bf16)
+        second_half = after[half:, columns] + got_after[:, columns].astype(f32)
         after_ref[half:, columns] = second_half.astype(bf16)
 
 
@@ -577,13 +577,13 @@
     far_hidden = expand([far_before, far_after], weights)
 
     hidden = (near_hidden, far_hidden)
-    to_before, to_after = down_parts((3,), hidden, downs, (half, half))
-    before_part, after_part = down_parts((1, 2), hidden, downs, (rows, rows))
+    to_before, to_after = down_parts((3,), hidden, downs, (half, half), bf16)
+    before_part, after_part = down_parts((1, 2), hidden, downs, (rows, rows), f32)
     got_before = first(to_before, -1)
     got_after = first(to_after, 1)
     got_before, low_head, high_head = tied(got_before, low_head, high_head)
     before_part, after_part = join(before_part, after_part, got_before, got_after)
-    (own_part,) = down_parts((0,), hidden, downs, (rows,))
+    (own_part,) = down_parts((0,), hidden, downs, (rows,), f32)
     own_part, low_head, high_head = tied(own_part, low_head, high_head)
     low_other = swap_cores(low_head)
     high_other = swap_cores(high_head)

time: 197 us -> 197 us (level)
  no operation moved by 1% of the time
where the time goes in v9:
time: 197 us; the launch traced here: 196 us
  blocking collectives  65.2 us (33%)
  waiting for transfers between devices  56.4 us (29%)
  starting transfers between devices  38.5 us (20%)
  Pallas kernels  32.5 us (16%)
  local copies, waits for them, and re-layouts  2.74 us (1%)
    ppermute x14, waiting for transfers between devices, plane_shift(): return lax.ppermute(array, ('vocab', 'batch'), perm)  37.8 us
    all_to_all x1, blocking collectives, on_device(): gathered = lax.all_to_all(stats, ('expert', 'vocab'), 0, 0, tiled=True)  32.2 us
    all_to_all x1, blocking collectives, on_device(): lax.all_to_all(buckets, 'expert', split_axis=0, concat_axis=0, tiled=True)  19.9 us
    ppermute x14, starting transfers between devices, plane_shift(): return lax.ppermute(array, ('vocab', 'batch'), perm)  17.9 us
    ppermute x6, waiting for transfers between devices, head_shift(): return lax.ppermute(array, ('expert', 'vocab'), perm)  16 us
    all_to_all x1, blocking collectives, on_device(): lax.all_to_all(outgoing, 'expert', split_axis=0, concat_axis=0, tiled=True)  13.1 us
    ppermute x6, starting transfers between devices, swap_cores(): return lax.ppermute(array, 'vocab', [(v, v ^ 1) for v in range(NX * NC)])  11.2 us
    pallas_call x3, Pallas kernels, hold(): pl.pallas_call(functools.partial(hold_kernel, count=count), in_specs=[pl....  9.42 us
  transfers between devices with their start and end apart: 28, of which 16 were waited for; matrix products, arithmetic and copies ran while one was open for 1% of the time, Pallas kernels for 12%

profile of v9, /device:TPU:1, one launch (start us, length us, event | category | flops | bytes accessed | tf_op | source)
XLA Modules:
  0.0 196.3 jit_solution(10390508185086437928)
XLA Ops:
  0.6 3.3 %collective-permute-start = (bf16[6144,256]{1,0:T(8,128)(2,1)}, bf16[6144,256]{1,0:T(8,128)(2,1)}, u32[]{:S(2)}, u32[]{:S(2)}) collective-permute-start(bf16[6144,256]{1,0:T(8,128)(2,1)} %bitcast.13), channel_id=1, source_target_pairs={{0,4},{4,0},{8,12},{12,8},{16,20},{20,16},{24,28},{28,24},{1,5},{5... | collective-permute-start | bytes 9437192 | tf_op jit(solution)/shard_map/ppermute | solution.py:60
  4.6 0.8 copy.14.ids_ref
  5.3 0.9 copy-done.4
  7.5 19.9 %all_to_all.15.refs_0_ = bf16[8,3,6144]{2,1,0:T(4,128)(2,1)S(1)} all-to-all(bf16[8,3,6144]{2,1,0:T(4,128)(2,1)S(1)} %shard_map.131), channel_id=1, replica_groups=mesh['expert'=8,'vocab'=8,'batch'=4] {'expert'}, dimensions={0} | all-to-all | bytes 589824 | tf_op jit(solution)/shard_map/all_to_all | solution.py:546
  27.5 1.4 collective-permute-start.4
  28.9 1.6 collective-permute-start.5
  30.5 1.6 collective-permute-start.6
  32.0 3.8 %collective-permute-done.4.refs_1_ = bf16[8,3,6144]{2,1,0:T(4,128)(2,1)S(1)} collective-permute-done((bf16[8,3,6144]{2,1,0:T(4,128)(2,1)S(1)}, bf16[8,3,6144]{2,1,0:T(4,128)(2,1)S(1)}, u32[]{:S(2)}, u32[]{:S(2)}) %collective-permute-start.4) | collective-permute-done | bytes 294944 | tf_op jit(solution)/shard_map/ppermute | solution.py:48
  35.8 3.6 %collective-permute-done.5.refs_2_ = bf16[8,3,6144]{2,1,0:T(4,128)(2,1)S(1)} collective-permute-done((bf16[8,3,6144]{2,1,0:T(4,128)(2,1)S(1)}, bf16[8,3,6144]{2,1,0:T(4,128)(2,1)S(1)}, u32[]{:S(2)}, u32[]{:S(2)}) %collective-permute-start.5) | collective-permute-done | bytes 294944 | tf_op jit(solution)/shard_map/ppermute | solution.py:48
  39.4 1.8 collective-permute-done.6.refs_3_
  41.9 0.9 collective-permute-start.7
  42.8 1.8 collective-permute-start.8
  45.2 2.4 %collective-permute-start.13 = (bf16[128,6144]{1,0:T(8,128)(2,1)S(1)}, bf16[128,6144]{1,0:T(8,128)(2,1)}, u32[]{:S(2)}, u32[]{:S(2)}) collective-permute-start(bf16[128,6144]{1,0:T(8,128)(2,1)S(1)} %get-tuple-element.108), channel_id=1, source_target_pairs={{0,224},{32,0},{64,32},{96,64},{128,96},{160,128},{192,160},{224,1... | collective-permute-start | bytes 4718600 | tf_op jit(solution)/shard_map/ppermute | solution.py:64
  48.1 3.3 %shard_map.134 = (bf16[6144,256]{1,0:T(8,128)(2,1)S(1)}, bf16[6144,256]{1,0:T(8,128)(2,1)S(1)}, bf16[6144,256]{1,0:T(8,128)(2,1)S(1)}, bf16[6144,256]{1,0:T(8,128)(2,1)S(1)}) custom-call(bf16[6144,256]{1,0:T(8,128)(2,1)S(1)} %bitcast.14, bf16[6144,256]{1,0:T(8,128)(2,1)S(1)} %bitcast.16, bf16[6144,256]{1,0:T(8,128)(2,1)} %collective-permute-done.refs_2_, ...), custom_call_target="tpu_custom_call" | custom-call | bytes 12582912 | tf_op jit(solution)/shard_map/pallas_call | solution.py:436
  51.4 7.2 %collective-permute-done.7.refs_1_ = bf16[96,6144]{1,0:T(8,128)(2,1)S(1)} collective-permute-done((bf16[96,6144]{1,0:T(8,128)(2,1)S(1)}, bf16[96,6144]{1,0:T(8,128)(2,1)S(1)}, u32[]{:S(2)}, u32[]{:S(2)}) %collective-permute-start.7) | collective-permute-done | bytes 1179680 | tf_op jit(solution)/shard_map/ppermute | solution.py:48
  58.7 0.9 collective-permute-start.9
  59.7 2.1 %collective-permute-start.10 = (bf16[48,6144]{1,0:T(8,128)(2,1)S(1)}, bf16[48,6144]{1,0:T(8,128)(2,1)S(1)}, u32[]{:S(2)}, u32[]{:S(2)}) collective-permute-start(bf16[48,6144]{1,0:T(8,128)(2,1)S(1)} %slice.13), channel_id=1, source_target_pairs={{0,3},{1,0},{2,1},{3,2},{4,28},{5,29},{6,30},{7,31},{8,11},{9,8},{... | collective-permute-start | bytes 1769480 | tf_op jit(solution)/shard_map/ppermute | solution.py:48
  61.8 4.6 %shard_map.135.near_ref = bf16[288,512]{1,0:T(8,128)(2,1)S(1)} custom-call(bf16[96,6144]{1,0:T(8,128)(2,1)S(1)} %shard_map.132.refs_0_, bf16[96,6144]{1,0:T(8,128)(2,1)S(1)} %collective-permute-done.7.refs_1_, bf16[96,6144]{1,0:T(8,128)(2,1)S(1)} %collective-permute-done.8.refs_2_, bf16[6144,256]{1,0:T(8,128)(2,1)S(1)} %get-tuple-element.70.refs_3_.refs_2_, ...), custom_call_target="tpu_custom_call" | custom-call | flops 3623878656 | bytes 12582912 | tf_op jit(solution)/shard_map/pallas_call | solution.py:215
  66.4 2.1 %shard_map.136 = (bf16[256,6144]{1,0:T(8,128)(2,1)S(1)}, bf16[256,6144]{1,0:T(8,128)(2,1)S(1)}) custom-call(bf16[256,6144]{1,0:T(8,128)(2,1)S(1)} %bitcast.12, bf16[256,6144]{1,0:T(8,128)(2,1)} %collective-permute-done.2.refs_1_), custom_call_target="tpu_custom_call" | custom-call | bytes 6291456 | tf_op jit(solution)/shard_map/pallas_call | solution.py:436
  69.1 2.1 %shard_map.137.far_ref = bf16[96,512]{1,0:T(8,128)(2,1)S(1)} custom-call(bf16[48,6144]{1,0:T(8,128)(2,1)S(1)} %collective-permute-done.9.refs_0_, bf16[48,6144]{1,0:T(8,128)(2,1)S(1)} %collective-permute-done.10.refs_1_, bf16[6144,256]{1,0:T(8,128)(2,1)S(1)} %get-tuple-element.70.refs_3_.refs_2_, bf16[6144,256]{1,0:T(8,128)(2,1)S(1)} %get-tuple-element.71.refs_4_.refs_3_, ...), custom_call_target="tpu_custom_call" | custom-call | flops 1207959552 | bytes 12582912 | tf_op jit(solution)/shard_map/pallas_call | solution.py:215
  71.2 1.6 shard_map.139
  72.8 1.8 collective-permute-start.11
  74.6 1.9 shard_map.140
  76.5 2.6 %collective-permute-done.12.refs_2_ = bf16[128,6144]{1,0:T(8,128)(2,1)} collective-permute-done((bf16[128,6144]{1,0:T(8,128)(2,1)S(1)}, bf16[128,6144]{1,0:T(8,128)(2,1)}, u32[]{:S(2)}, u32[]{:S(2)}) %collective-permute-start.12) | collective-permute-done | bytes 1572896 | tf_op jit(solution)/shard_map/ppermute | solution.py:64
  79.1 2.9 %collective-permute-done.11.got_before = bf16[48,6144]{1,0:T(8,128)(2,1)S(1)} collective-permute-done((bf16[48,6144]{1,0:T(8,128)(2,1)S(1)}, bf16[48,6144]{1,0:T(8,128)(2,1)S(1)}, u32[]{:S(2)}, u32[]{:S(2)}) %collective-permute-start.11) | collective-permute-done | bytes 589856 | tf_op jit(solution)/shard_map/ppermute | solution.py:48
  82.0 2.8 %collective-permute-done.14.got_after = bf16[48,6144]{1,0:T(8,128)(2,1)S(1)} collective-permute-done((bf16[48,6144]{1,0:T(8,128)(2,1)S(1)}, bf16[48,6144]{1,0:T(8,128)(2,1)S(1)}, u32[]{:S(2)}, u32[]{:S(2)}) %collective-permute-start.14) | collective-permute-done | bytes 589856 | tf_op jit(solution)/shard_map/ppermute | solution.py:48
  85.2 1.5 collective-permute-start.16
  86.7 1.5 shard_map.138.own_ref
  88.2 7.1 %collective-permute-start.26 = (bf16[128,6144]{1,0:T(8,128)(2,1)}, bf16[128,6144]{1,0:T(8,128)(2,1)}, u32[]{:S(2)}, u32[]{:S(2)}) collective-permute-start(bf16[128,6144]{1,0:T(8,128)(2,1)} %collective-permute-done.12.refs_2_), channel_id=1, source_target_pairs={{0,4},{4,0},{8,12},{12,8},{16,20},{20,16},{24,28},{28,24},{1,5},{5... | collective-permute-start | bytes 4718600 | tf_op jit(solution)/shard_map/ppermute | solution.py:60
  95.5 5.1 %collective-permute-done.15.before_ref = bf16[96,6144]{1,0:T(8,128)(2,1)S(1)} collective-permute-done((bf16[96,6144]{1,0:T(8,128)(2,1)S(1)}, bf16[96,6144]{1,0:T(8,128)(2,1)S(1)}, u32[]{:S(2)}, u32[]{:S(2)}) %collective-permute-start.15) | collective-permute-done | bytes 1179680 | tf_op jit(solution)/shard_map/ppermute | solution.py:48
  100.6 1.3 collective-permute-done.16.after_ref
  101.9 0.9 shard_map.142
  102.7 3.0 %collective-permute-start.17 = (bf16[24,6144]{1,0:T(8,128)(2,1)S(1)}, bf16[24,6144]{1,0:T(8,128)(2,1)S(1)}, u32[]{:S(2)}, u32[]{:S(2)}) collective-permute-start(bf16[24,6144]{1,0:T(8,128)(2,1)S(1)} %get-tuple-element.96), channel_id=1, source_target_pairs={{0,3},{1,0},{2,1},{3,2},{4,28},{5,29},{6,30},{7,31},{8,11},{9,8},{... | collective-permute-start | bytes 884744 | tf_op jit(solution)/shard_map/ppermute | solution.py:48
  105.7 1.3 collective-permute-start.19
  107.0 3.4 %collective-permute-done.17.b = bf16[24,6144]{1,0:T(8,128)(2,1)S(1)} collective-permute-done((bf16[24,6144]{1,0:T(8,128)(2,1)S(1)}, bf16[24,6144]{1,0:T(8,128)(2,1)S(1)}, u32[]{:S(2)}, u32[]{:S(2)}) %collective-permute-start.17) | collective-permute-done | bytes 294944 | tf_op jit(solution)/shard_map/ppermute | solution.py:48
  110.4 5.3 %collective-permute-done.18.c = bf16[24,6144]{1,0:T(8,128)(2,1)S(1)} collective-permute-done((bf16[24,6144]{1,0:T(8,128)(2,1)S(1)}, bf16[24,6144]{1,0:T(8,128)(2,1)S(1)}, u32[]{:S(2)}, u32[]{:S(2)}) %collective-permute-start.18) | collective-permute-done | bytes 294944 | tf_op jit(solution)/shard_map/ppermute | solution.py:48
  116.0 13.1 %all_to_all.16.rows_ref = bf16[8,3,6144]{2,1,0:T(4,128)(2,1)S(1)} all-to-all(bf16[8,3,6144]{2,1,0:T(4,128)(2,1)S(1)} %shard_map.143), channel_id=1, replica_groups=mesh['expert'=8,'vocab'=8,'batch'=4] {'expert'}, dimensions={0} | all-to-all | bytes 589824 | tf_op jit(solution)/shard_map/all_to_all | solution.py:594
  129.2 1.0 shard_map.144.refs_0_
  130.3 3.6 %collective-permute-start.21 = (bf16[8,6144]{1,0:T(8,128)(2,1)S(1)}, bf16[8,6144]{1,0:T(8,128)(2,1)S(1)}, u32[]{:S(2)}, u32[]{:S(2)}) collective-permute-start(bf16[8,6144]{1,0:T(8,128)(2,1)S(1)} %shard_map.144.refs_0_), channel_id=1, source_target_pairs={{0,192},{4,196},{8,200},{12,204},{16,208},{20,212},{24,216},{28,22... | collective-permute-start | bytes 294920 | tf_op jit(solution)/shard_map/ppermute | solution.py:56
  134.2 1.8 collective-permute-done.20.refs_1_
  136.0 3.1 %collective-permute-done.21.refs_2_ = bf16[8,6144]{1,0:T(8,128)(2,1)S(1)} collective-permute-done((bf16[8,6144]{1,0:T(8,128)(2,1)S(1)}, bf16[8,6144]{1,0:T(8,128)(2,1)S(1)}, u32[]{:S(2)}, u32[]{:S(2)}) %collective-permute-start.21) | collective-permute-done | bytes 98336 | tf_op jit(solution)/shard_map/ppermute | solution.py:56
  139.1 5.7 %collective-permute-done.22.refs_3_ = bf16[8,6144]{1,0:T(8,128)(2,1)S(1)} collective-permute-done((bf16[8,6144]{1,0:T(8,128)(2,1)S(1)}, bf16[8,6144]{1,0:T(8,128)(2,1)S(1)}, u32[]{:S(2)}, u32[]{:S(2)}) %collective-permute-start.22) | collective-permute-done | bytes 98336 | tf_op jit(solution)/shard_map/ppermute | solution.py:56
  144.9 2.7 %collective-permute-start.24 = (bf16[32,6144]{1,0:T(8,128)(2,1)S(1)}, bf16[32,6144]{1,0:T(8,128)(2,1)}, u32[]{:S(2)}, u32[]{:S(2)}) collective-permute-start(bf16[32,6144]{1,0:T(8,128)(2,1)S(1)} %shard_map.145.r0), channel_id=1, source_target_pairs={{0,24},{4,28},{8,0},{12,4},{16,8},{20,12},{24,16},{28,20},{32,56},... | collective-permute-start | bytes 1179656 | tf_op jit(solution)/shard_map/ppermute | solution.py:56
  147.7 4.0 %shard_map.146 = (bf16[256,6144]{1,0:T(8,128)(2,1)S(1)}, bf16[256,6144]{1,0:T(8,128)(2,1)S(1)}, bf16[128,6144]{1,0:T(8,128)(2,1)S(1)}, bf16[128,6144]{1,0:T(8,12...) custom-call(bf16[256,6144]{1,0:T(8,128)(2,1)S(1)} %copy-done, ...), custom_call_target="tpu_custom_call" | custom-call | bytes 12582912 | tf_op jit(solution)/shard_map/pallas_call | solution.py:436
  151.7 5.4 %collective-permute-done.23.r1 = bf16[32,6144]{1,0:T(8,128)(2,1)} collective-permute-done((bf16[32,6144]{1,0:T(8,128)(2,1)S(1)}, bf16[32,6144]{1,0:T(8,128)(2,1)}, u32[]{:S(2)}, u32[]{:S(2)}) %collective-permute-start.23) | collective-permute-done | bytes 393248 | tf_op jit(solution)/shard_map/ppermute | solution.py:56
  157.1 5.6 %shard_map.147 = f32[64,2,128]{2,1,0:T(2,128)S(1)} custom-call(s32[3]{0:T(128)S(1)} %pad_add_fusion.place_ref, s32[1,512]{1,0:T(1,128)S(1)} %copy-done.10, bf16[32,6144]{1,0:T(8,128)(2,1)S(1)} %shard_map.145.r0, bf16[32,6144]{1,0:T(8,128)(2,1)} %collective-permute-done.23.r1, bf16[32,6144]{1,0:T(8,128)(2,1)} %collective-permute-done.24.r2, ...), custom_call_target="tpu_custom_call" | custom-call | flops 1610612736 | bytes 12582912 | tf_op jit(solution)/shard_map/pallas_call | solution.py:412
  162.7 32.2 %all_to_all.17.stats_ref = f32[64,2,128]{2,1,0:T(2,128)S(1)} all-to-all(f32[64,2,128]{2,1,0:T(2,128)S(1)} %shard_map.147), channel_id=1, replica_groups=mesh['expert'=8,'vocab'=8,'batch'=4] {'expert','vocab'}, dimensions={0} | all-to-all | bytes 131072 | tf_op jit(solution)/shard_map/all_to_all | solution.py:600
  194.9 1.4 shard_map.148
  (60 shorter events, 5.8 us)
Async XLA Ops:
  0.6 44.0 %copy-start = (bf16[256,6144]{1,0:T(8,128)(2,1)S(1)}, bf16[256,6144]{1,0:T(8,128)(2,1)}, u32[]{:S(2)}) copy-start(bf16[256,6144]{1,0:T(8,128)(2,1)} %refs_0_.1) | copy-start | bytes 9437188
  0.6 26.8 %collective-permute-start = (bf16[6144,256]{1,0:T(8,128)(2,1)}, bf16[6144,256]{1,0:T(8,128)(2,1)}, u32[]{:S(2)}, u32[]{:S(2)}) collective-permute-start(bf16[6144,256]{1,0:T(8,128)(2,1)} %bitcast.13), channel_id=1, source_target_pairs={{0,4},{4,0},{8,12},{12,8},{16,20},{20,16},{24,28},{28,24},{1,5},{5... | collective-permute-start | bytes 9437192 | tf_op jit(solution)/shard_map/ppermute | solution.py:60
  4.0 23.5 %collective-permute-start.1 = (bf16[6144,256]{1,0:T(8,128)(2,1)}, bf16[6144,256]{1,0:T(8,128)(2,1)}, u32[]{:S(2)}, u32[]{:S(2)}) collective-permute-start(bf16[6144,256]{1,0:T(8,128)(2,1)} %bitcast.15), channel_id=1, source_target_pairs={{0,4},{4,0},{8,12},{12,8},{16,20},{20,16},{24,28},{28,24},{1,5},{5... | collective-permute-start | bytes 9437192 | tf_op jit(solution)/shard_map/ppermute | solution.py:60
  4.1 23.4 %collective-permute-start.2 = (bf16[256,6144]{1,0:T(8,128)(2,1)}, bf16[256,6144]{1,0:T(8,128)(2,1)}, u32[]{:S(2)}, u32[]{:S(2)}) collective-permute-start(bf16[256,6144]{1,0:T(8,128)(2,1)} %bitcast.11), channel_id=1, source_target_pairs={{0,4},{4,0},{8,12},{12,8},{16,20},{20,16},{24,28},{28,24},{1,5},{5... | collective-permute-start | bytes 9437192 | tf_op jit(solution)/shard_map/ppermute | solution.py:60
  4.5 23.0 %collective-permute-start.3 = (bf16[256,6144]{1,0:T(8,128)(2,1)}, bf16[256,6144]{1,0:T(8,128)(2,1)}, u32[]{:S(2)}, u32[]{:S(2)}) collective-permute-start(bf16[256,6144]{1,0:T(8,128)(2,1)} %refs_0_.1), channel_id=1, source_target_pairs={{0,4},{4,0},{8,12},{12,8},{16,20},{20,16},{24,28},{28,24},{1,5},{5... | collective-permute-start | bytes 9437192 | tf_op jit(solution)/shard_map/ppermute | solution.py:60
  5.3 0.9 copy-start.4
  6.2 0.7 copy-start.6
  27.5 8.3 %collective-permute-start.4 = (bf16[8,3,6144]{2,1,0:T(4,128)(2,1)S(1)}, bf16[8,3,6144]{2,1,0:T(4,128)(2,1)S(1)}, u32[]{:S(2)}, u32[]{:S(2)}) collective-permute-start(bf16[8,3,6144]{2,1,0:T(4,128)(2,1)S(1)} %all_to_all.15.refs_0_), channel_id=1, source_target_pairs={{0,8},{1,9},{2,10},{3,11},{4,5},{5,6},{6,7},{7,4},{8,16},{9,17},{1... | collective-permute-start | bytes 884744 | tf_op jit(solution)/shard_map/ppermute | solution.py:48
  28.9 10.5 %collective-permute-start.5 = (bf16[8,3,6144]{2,1,0:T(4,128)(2,1)S(1)}, bf16[8,3,6144]{2,1,0:T(4,128)(2,1)S(1)}, u32[]{:S(2)}, u32[]{:S(2)}) collective-permute-start(bf16[8,3,6144]{2,1,0:T(4,128)(2,1)S(1)} %all_to_all.15.refs_0_), channel_id=1, source_target_pairs={{0,24},{1,25},{2,26},{3,27},{4,7},{5,4},{6,5},{7,6},{8,0},{9,1},{1... | collective-permute-start | bytes 884744 | tf_op jit(solution)/shard_map/ppermute | solution.py:48
  30.5 10.8 %collective-permute-start.6 = (bf16[8,3,6144]{2,1,0:T(4,128)(2,1)S(1)}, bf16[8,3,6144]{2,1,0:T(4,128)(2,1)S(1)}, u32[]{:S(2)}, u32[]{:S(2)}) collective-permute-start(bf16[8,3,6144]{2,1,0:T(4,128)(2,1)S(1)} %all_to_all.15.refs_0_), channel_id=1, source_target_pairs={{0,16},{1,17},{2,18},{3,19},{4,6},{5,7},{6,4},{7,5},{8,24},{9,25},... | collective-permute-start | bytes 884744 | tf_op jit(solution)/shard_map/ppermute | solution.py:48
  41.2 6.4 %copy-start.5 = (bf16[1,8,6144]{2,1,0:T(8,128)(2,1)S(1)}, bf16[1,8,6144]{2,1,0:T(8,128)(2,1)}, u32[]{:S(2)}) copy-start(bf16[1,8,6144]{2,1,0:T(8,128)(2,1)} %param.12) | copy-start | bytes 294916
  41.2 6.4 %copy-start.7 = (f32[6144]{0:T(1024)S(1)}, f32[6144]{0:T(1024)}, u32[]{:S(2)}) copy-start(f32[6144]{0:T(1024)} %param.13) | copy-start | bytes 73732
  41.2 6.4 %copy-start.8 = (bf16[6144,8]{0,1:T(8,128)(2,1)S(1)}, bf16[6144,8]{0,1:T(8,128)(2,1)}, u32[]{:S(2)}) copy-start(bf16[6144,8]{0,1:T(8,128)(2,1)} %param.15) | copy-start | bytes 294916
  41.9 6.2 %copy-start.2 = (bf16[1,6144,256]{2,1,0:T(8,128)(2,1)S(1)}, bf16[1,6144,256]{2,1,0:T(8,128)(2,1)}, u32[]{:S(2)}) copy-start(bf16[1,6144,256]{2,1,0:T(8,128)(2,1)} %param.16) | copy-start | bytes 9437188
  41.9 6.2 %copy-start.3 = (bf16[1,6144,256]{2,1,0:T(8,128)(2,1)S(1)}, bf16[1,6144,256]{2,1,0:T(8,128)(2,1)}, u32[]{:S(2)}) copy-start(bf16[1,6144,256]{2,1,0:T(8,128)(2,1)} %param.17) | copy-start | bytes 9437188
  41.9 16.7 %collective-permute-start.7 = (bf16[96,6144]{1,0:T(8,128)(2,1)S(1)}, bf16[96,6144]{1,0:T(8,128)(2,1)S(1)}, u32[]{:S(2)}, u32[]{:S(2)}) collective-permute-start(bf16[96,6144]{1,0:T(8,128)(2,1)S(1)} %shard_map.132.refs_0_), channel_id=1, source_target_pairs={{0,1},{1,2},{2,3},{3,0},{4,12},{5,13},{6,14},{7,15},{8,9},{9,10},{... | collective-permute-start | bytes 3538952 | tf_op jit(solution)/shard_map/ppermute | solution.py:48
  42.8 15.8 %collective-permute-start.8 = (bf16[96,6144]{1,0:T(8,128)(2,1)S(1)}, bf16[96,6144]{1,0:T(8,128)(2,1)S(1)}, u32[]{:S(2)}, u32[]{:S(2)}) collective-permute-start(bf16[96,6144]{1,0:T(8,128)(2,1)S(1)} %shard_map.132.refs_0_), channel_id=1, source_target_pairs={{0,3},{1,0},{2,1},{3,2},{4,28},{5,29},{6,30},{7,31},{8,11},{9,8},{... | collective-permute-start | bytes 3538952 | tf_op jit(solution)/shard_map/ppermute | solution.py:48
  44.9 34.2 %collective-permute-start.12 = (bf16[128,6144]{1,0:T(8,128)(2,1)S(1)}, bf16[128,6144]{1,0:T(8,128)(2,1)}, u32[]{:S(2)}, u32[]{:S(2)}) collective-permute-start(bf16[128,6144]{1,0:T(8,128)(2,1)S(1)} %get-tuple-element.109), channel_id=1, source_target_pairs={{0,32},{32,64},{64,96},{96,128},{128,160},{160,192},{192,224},{224... | collective-permute-start | bytes 4718600 | tf_op jit(solution)/shard_map/ppermute | solution.py:64
  45.2 33.9 %collective-permute-start.13 = (bf16[128,6144]{1,0:T(8,128)(2,1)S(1)}, bf16[128,6144]{1,0:T(8,128)(2,1)}, u32[]{:S(2)}, u32[]{:S(2)}) collective-permute-start(bf16[128,6144]{1,0:T(8,128)(2,1)S(1)} %get-tuple-element.108), channel_id=1, source_target_pairs={{0,224},{32,0},{64,32},{96,64},{128,96},{160,128},{192,160},{224,1... | collective-permute-start | bytes 4718600 | tf_op jit(solution)/shard_map/ppermute | solution.py:64
  58.7 10.4 %collective-permute-start.9 = (bf16[48,6144]{1,0:T(8,128)(2,1)S(1)}, bf16[48,6144]{1,0:T(8,128)(2,1)S(1)}, u32[]{:S(2)}, u32[]{:S(2)}) collective-permute-start(bf16[48,6144]{1,0:T(8,128)(2,1)S(1)} %slice.12), channel_id=1, source_target_pairs={{0,1},{1,2},{2,3},{3,0},{4,12},{5,13},{6,14},{7,15},{8,9},{9,10},{... | collective-permute-start | bytes 1769480 | tf_op jit(solution)/shard_map/ppermute | solution.py:48
  59.6 6.7 %copy-start.1 = (bf16[1,256,6144]{2,1,0:T(8,128)(2,1)S(1)}, bf16[1,256,6144]{2,1,0:T(8,128)(2,1)}, u32[]{:S(2)}) copy-start(bf16[1,256,6144]{2,1,0:T(8,128)(2,1)} %param.18) | copy-start | bytes 9437188
  59.7 9.5 %collective-permute-start.10 = (bf16[48,6144]{1,0:T(8,128)(2,1)S(1)}, bf16[48,6144]{1,0:T(8,128)(2,1)S(1)}, u32[]{:S(2)}, u32[]{:S(2)}) collective-permute-start(bf16[48,6144]{1,0:T(8,128)(2,1)S(1)} %slice.13), channel_id=1, source_target_pairs={{0,3},{1,0},{2,1},{3,2},{4,28},{5,29},{6,30},{7,31},{8,11},{9,8},{... | collective-permute-start | bytes 1769480 | tf_op jit(solution)/shard_map/ppermute | solution.py:48
  72.8 9.2 %collective-permute-start.11 = (bf16[48,6144]{1,0:T(8,128)(2,1)S(1)}, bf16[48,6144]{1,0:T(8,128)(2,1)S(1)}, u32[]{:S(2)}, u32[]{:S(2)}) collective-permute-start(bf16[48,6144]{1,0:T(8,128)(2,1)S(1)} %get-tuple-element.84), channel_id=1, source_target_pairs={{0,24},{1,25},{2,26},{3,27},{4,7},{5,4},{6,5},{7,6},{8,0},{9,1},{1... | collective-permute-start | bytes 1769480 | tf_op jit(solution)/shard_map/ppermute | solution.py:48
  74.6 10.2 %collective-permute-start.14 = (bf16[48,6144]{1,0:T(8,128)(2,1)S(1)}, bf16[48,6144]{1,0:T(8,128)(2,1)S(1)}, u32[]{:S(2)}, u32[]{:S(2)}) collective-permute-start(bf16[48,6144]{1,0:T(8,128)(2,1)S(1)} %get-tuple-element.92), channel_id=1, source_target_pairs={{0,8},{1,9},{2,10},{3,11},{4,5},{5,6},{6,7},{7,4},{8,16},{9,17},{1... | collective-permute-start | bytes 1769480 | tf_op jit(solution)/shard_map/ppermute | solution.py:48
  85.1 15.4 %collective-permute-start.15 = (bf16[96,6144]{1,0:T(8,128)(2,1)S(1)}, bf16[96,6144]{1,0:T(8,128)(2,1)S(1)}, u32[]{:S(2)}, u32[]{:S(2)}) collective-permute-start(bf16[96,6144]{1,0:T(8,128)(2,1)S(1)} %get-tuple-element.93), channel_id=1, source_target_pairs={{0,24},{1,25},{2,26},{3,27},{4,7},{5,4},{6,5},{7,6},{8,0},{9,1},{1... | collective-permute-start | bytes 3538952 | tf_op jit(solution)/shard_map/ppermute | solution.py:48
  85.2 16.6 %collective-permute-start.16 = (bf16[96,6144]{1,0:T(8,128)(2,1)S(1)}, bf16[96,6144]{1,0:T(8,128)(2,1)S(1)}, u32[]{:S(2)}, u32[]{:S(2)}) collective-permute-start(bf16[96,6144]{1,0:T(8,128)(2,1)S(1)} %get-tuple-element.94), channel_id=1, source_target_pairs={{0,8},{1,9},{2,10},{3,11},{4,5},{5,6},{6,7},{7,4},{8,16},{9,17},{1... | collective-permute-start | bytes 3538952 | tf_op jit(solution)/shard_map/ppermute | solution.py:48
  88.2 59.5 %collective-permute-start.26 = (bf16[128,6144]{1,0:T(8,128)(2,1)}, bf16[128,6144]{1,0:T(8,128)(2,1)}, u32[]{:S(2)}, u32[]{:S(2)}) collective-permute-start(bf16[128,6144]{1,0:T(8,128)(2,1)} %collective-permute-done.12.refs_2_), channel_id=1, source_target_pairs={{0,4},{4,0},{8,12},{12,8},{16,20},{20,16},{24,28},{28,24},{1,5},{5... | collective-permute-start | bytes 4718600 | tf_op jit(solution)/shard_map/ppermute | solution.py:60
  95.4 52.3 %collective-permute-start.27 = (bf16[128,6144]{1,0:T(8,128)(2,1)}, bf16[128,6144]{1,0:T(8,128)(2,1)}, u32[]{:S(2)}, u32[]{:S(2)}) collective-permute-start(bf16[128,6144]{1,0:T(8,128)(2,1)} %collective-permute-done.13.refs_4_), channel_id=1, source_target_pairs={{0,4},{4,0},{8,12},{12,8},{16,20},{20,16},{24,28},{28,24},{1,5},{5... | collective-permute-start | bytes 4718600 | tf_op jit(solution)/shard_map/ppermute | solution.py:60
  102.7 26.4 %copy-start.9 = (f32[6144]{0:T(1024)S(1)}, f32[6144]{0:T(1024)}, u32[]{:S(2)}) copy-start(f32[6144]{0:T(1024)} %param.14) | copy-start | bytes 73732
  102.7 7.6 %collective-permute-start.17 = (bf16[24,6144]{1,0:T(8,128)(2,1)S(1)}, bf16[24,6144]{1,0:T(8,128)(2,1)S(1)}, u32[]{:S(2)}, u32[]{:S(2)}) collective-permute-start(bf16[24,6144]{1,0:T(8,128)(2,1)S(1)} %get-tuple-element.96), channel_id=1, source_target_pairs={{0,3},{1,0},{2,1},{3,2},{4,28},{5,29},{6,30},{7,31},{8,11},{9,8},{... | collective-permute-start | bytes 884744 | tf_op jit(solution)/shard_map/ppermute | solution.py:48
  105.7 9.9 %collective-permute-start.18 = (bf16[24,6144]{1,0:T(8,128)(2,1)S(1)}, bf16[24,6144]{1,0:T(8,128)(2,1)S(1)}, u32[]{:S(2)}, u32[]{:S(2)}) collective-permute-start(bf16[24,6144]{1,0:T(8,128)(2,1)S(1)} %get-tuple-element.97), channel_id=1, source_target_pairs={{0,1},{1,2},{2,3},{3,0},{4,12},{5,13},{6,14},{7,15},{8,9},{9,10},{... | collective-permute-start | bytes 884744 | tf_op jit(solution)/shard_map/ppermute | solution.py:48
  105.7 9.9 %collective-permute-start.19 = (bf16[24,6144]{1,0:T(8,128)(2,1)S(1)}, bf16[24,6144]{1,0:T(8,128)(2,1)S(1)}, u32[]{:S(2)}, u32[]{:S(2)}) collective-permute-start(bf16[24,6144]{1,0:T(8,128)(2,1)S(1)} %get-tuple-element.98), channel_id=1, source_target_pairs={{0,2},{1,3},{2,0},{3,1},{4,20},{5,21},{6,22},{7,23},{8,10},{9,11},... | collective-permute-start | bytes 884744 | tf_op jit(solution)/shard_map/ppermute | solution.py:48
  130.2 5.8 %collective-permute-start.20 = (bf16[8,6144]{1,0:T(8,128)(2,1)S(1)}, bf16[8,6144]{1,0:T(8,128)(2,1)S(1)}, u32[]{:S(2)}, u32[]{:S(2)}) collective-permute-start(bf16[8,6144]{1,0:T(8,128)(2,1)S(1)} %shard_map.144.refs_0_), channel_id=1, source_target_pairs={{0,64},{4,68},{8,72},{12,76},{16,80},{20,84},{24,88},{28,92},{32,9... | collective-permute-start | bytes 294920 | tf_op jit(solution)/shard_map/ppermute | solution.py:56
  130.3 8.8 %collective-permute-start.21 = (bf16[8,6144]{1,0:T(8,128)(2,1)S(1)}, bf16[8,6144]{1,0:T(8,128)(2,1)S(1)}, u32[]{:S(2)}, u32[]{:S(2)}) collective-permute-start(bf16[8,6144]{1,0:T(8,128)(2,1)S(1)} %shard_map.144.refs_0_), channel_id=1, source_target_pairs={{0,192},{4,196},{8,200},{12,204},{16,208},{20,212},{24,216},{28,22... | collective-permute-start | bytes 294920 | tf_op jit(solution)/shard_map/ppermute | solution.py:56
  133.9 10.9 %collective-permute-start.22 = (bf16[8,6144]{1,0:T(8,128)(2,1)S(1)}, bf16[8,6144]{1,0:T(8,128)(2,1)S(1)}, u32[]{:S(2)}, u32[]{:S(2)}) collective-permute-start(bf16[8,6144]{1,0:T(8,128)(2,1)S(1)} %shard_map.144.refs_0_), channel_id=1, source_target_pairs={{0,128},{4,132},{8,136},{12,140},{16,144},{20,148},{24,152},{28,15... | collective-permute-start | bytes 294920 | tf_op jit(solution)/shard_map/ppermute | solution.py:56
  144.8 12.2 %collective-permute-start.23 = (bf16[32,6144]{1,0:T(8,128)(2,1)S(1)}, bf16[32,6144]{1,0:T(8,128)(2,1)}, u32[]{:S(2)}, u32[]{:S(2)}) collective-permute-start(bf16[32,6144]{1,0:T(8,128)(2,1)S(1)} %shard_map.145.r0), channel_id=1, source_target_pairs={{0,8},{4,12},{8,16},{12,20},{16,24},{20,28},{24,0},{28,4},{32,40},... | collective-permute-start | bytes 1179656 | tf_op jit(solution)/shard_map/ppermute | solution.py:56
  144.9 12.1 %collective-permute-start.24 = (bf16[32,6144]{1,0:T(8,128)(2,1)S(1)}, bf16[32,6144]{1,0:T(8,128)(2,1)}, u32[]{:S(2)}, u32[]{:S(2)}) collective-permute-start(bf16[32,6144]{1,0:T(8,128)(2,1)S(1)} %shard_map.145.r0), channel_id=1, source_target_pairs={{0,24},{4,28},{8,0},{12,4},{16,8},{20,12},{24,16},{28,20},{32,56},... | collective-permute-start | bytes 1179656 | tf_op jit(solution)/shard_map/ppermute | solution.py:56
  147.6 9.5 %collective-permute-start.25 = (bf16[32,6144]{1,0:T(8,128)(2,1)S(1)}, bf16[32,6144]{1,0:T(8,128)(2,1)}, u32[]{:S(2)}, u32[]{:S(2)}) collective-permute-start(bf16[32,6144]{1,0:T(8,128)(2,1)S(1)} %shard_map.145.r0), channel_id=1, source_target_pairs={{0,16},{4,20},{8,24},{12,28},{16,0},{20,4},{24,8},{28,12},{32,48},... | collective-permute-start | bytes 1179656 | tf_op jit(solution)/shard_map/ppermute | solution.py:56
  147.7 9.4 %copy-start.10 = (s32[1,512]{1,0:T(1,128)S(1)}, s32[1,512]{1,0:T(1,128)}, u32[]{:S(2)}) copy-start(s32[1,512]{1,0:T(1,128)} %targets_ref.1) | copy-start | bytes 6148
  157.1 37.8 %copy-start.11 = (s32[1,16]{1,0:T(1,128)S(1)}, s32[1,16]{1,0:T(1,128)}, u32[]{:S(2)}) copy-start(s32[1,16]{1,0:T(1,128)} %lengths_ref.1) | copy-start | bytes 196
  157.1 37.8 %copy-start.12 = (s32[1,16]{1,0:T(1,128)S(1)}, s32[1,16]{1,0:T(1,128)}, u32[]{:S(2)}) copy-start(s32[1,16]{1,0:T(1,128)} %questions_ref.1) | copy-start | bytes 196
